TPU v7x, 32 devices: a whole 2x2x4 slice. The times are simulated.
32 devices in a mesh: dom: 2 (over x), energy: 16 (over z, y, core).
Axes of the slice: x: 2, y: 2, z: 4, core: 2. Of those that a mesh axis runs over, the one named last changes fastest.
Arguments:
- lesser: bfloat16 [1024, 2, 128, 128], P(('dom', 'energy')), parts along dimension 0, may hold values from -6 to 6
- greater: bfloat16 [1024, 2, 128, 128], P(('dom', 'energy')), parts along dimension 0, may hold values from -6 to 6
- dipole: bfloat16 [2, 128, 128], replicated, may hold values from -0.375 to 0.375
- shifts: int32 [16], replicated, may hold values from 1 to 64, as said below
- window: int32 [4], P('dom'), parts along dimension 0, may hold values from 0 to 512, as said below
Outputs:
- polarization: float32 [256, 16, 2, 128], P(('dom', 'energy')), parts along dimension 0
There are 2 independent parts, one for each index of `dom`. A program takes and returns all parts, laid end to end along the dimension named above; an argument that names none is the same for every part. Nothing has to cross between parts.
Inputs may be any that keep to these rules, and one draw needn't show every extreme that they name: `shifts`: every photon energy is at least one bin; one of them is exactly 32 bins and another exactly 64 bins. window[0] < 16 and window[1] >= 384.
All inputs are finite; a program needn't handle non-finite values.
Results may differ from a plain program's by a relative error of at most 0.0029.
Values may be sent and summed in bfloat16 or wider, within the bound.
No kernel may reach another device: no remote copies, remote signals or barrier semaphores. Data moves between devices by JAX's collectives and lax.ppermute only.
A program may use at most 64 MiB of HBM per device.

v0:
```python
import math

import jax
import jax.numpy as jnp
from jax import lax
from jax.sharding import PartitionSpec as P


def passed_along(block, axis, distance):
    devices = range(lax.axis_size(axis))
    route = [(i - distance, i) for i in devices if i - distance in devices]
    return lax.ppermute(block, axis, route)


def lower_blocks(blocks):
    near = passed_along((blocks[0], blocks[1]), "energy", 1)
    far = passed_along((blocks[0], blocks[1]), "energy", 2)
    return (near, far)


def complex_sum(left_real, left_imag, right_real, right_imag):
    real = jnp.einsum(
        "eij,ejk->ik", left_real, right_real, preferred_element_type=jnp.float32
    ) - jnp.einsum("eij,ejk->ik", left_imag, right_imag, preferred_element_type=jnp.float32)
    imag = jnp.einsum(
        "eij,ejk->ik", left_real, right_imag, preferred_element_type=jnp.float32
    ) + jnp.einsum("eij,ejk->ik", left_imag, right_real, preferred_element_type=jnp.float32)
    return jnp.stack([real, imag], 1)


def on_device(lesser, greater, dipole, shifts, window):
    hp = lax.Precision.HIGHEST
    e_dev = lesser.shape[0]
    orbitals = lesser.shape[2]
    devices = lax.axis_size("energy")
    total = e_dev * devices
    base = lax.axis_index("energy") * e_dev
    mreal, mimag = (dipole[0], dipole[1])
    mg_real = jnp.einsum(
        "ij,ejk->eik", mreal, lesser[:, 0], preferred_element_type=jnp.float32
    ) - jnp.einsum("ij,ejk->eik", mimag, lesser[:, 1], preferred_element_type=jnp.float32)
    mg_imag = jnp.einsum(
        "ij,ejk->eik", mreal, lesser[:, 1], preferred_element_type=jnp.float32
    ) + jnp.einsum("ij,ejk->eik", mimag, lesser[:, 0], preferred_element_type=jnp.float32)
    freal = mreal.astype(jnp.float32)
    fimag = mimag.astype(jnp.float32)
    c_real = jnp.einsum("eij,kj->eik", mg_real, freal, precision=hp) + jnp.einsum(
        "eij,kj->eik", mg_imag, fimag, precision=hp
    )
    c_imag = jnp.einsum("eij,kj->eik", mg_imag, freal, precision=hp) - jnp.einsum(
        "eij,kj->eik", mg_real, fimag, precision=hp
    )
    energy = base + jnp.arange(e_dev)
    inside = ((energy >= window[0]) & (energy < window[1])).astype(jnp.bfloat16)[:, None, None]
    proj_real = c_real.astype(jnp.bfloat16) * inside
    proj_imag = c_imag.astype(jnp.bfloat16) * inside
    green_real = greater[:, 0] * inside
    green_imag = greater[:, 1] * inside
    near, far = lower_blocks((green_real, green_imag))
    ext_real = jnp.concatenate([far[0], near[0], green_real], 0)
    ext_imag = jnp.concatenate([far[1], near[1], green_imag], 0)

    def single(shift_bins):
        start = 2 * e_dev - shift_bins
        piece_real = lax.dynamic_slice_in_dim(ext_real, start, e_dev, 0)
        piece_imag = lax.dynamic_slice_in_dim(ext_imag, start, e_dev, 0)
        return complex_sum(proj_real, proj_imag, piece_real, piece_imag)

    full_term = jnp.transpose(lax.map(single, shifts), (1, 0, 2, 3))
    summed = lax.psum_scatter(full_term, "energy", scatter_dimension=0, tiled=True)
    scale = 1.0 / math.sqrt(2.0 * orbitals * total)
    return summed * scale


def solution(mesh):
    placed = (
        P(("dom", "energy"), None, None, None),
        P(("dom", "energy"), None, None, None),
        P(),
        P(),
        P("dom"),
    )
    return jax.shard_map(
        on_device,
        mesh=mesh,
        in_specs=placed,
        out_specs=P(("dom", "energy"), None, None, None),
        check_vma=False,
    )
```

profile of v0, /device:TPU:0, one launch (start us, length us, event | category | flops | bytes accessed | tf_op | source)
XLA Modules:
  0.0 375.6 jit_solution(8166383505669656663)
XLA Ops:
  9.2 3.3 bitcast_multiply_fusion
  12.5 3.4 collective-permute-start.3
  15.9 4.4 %collective-permute-start.2 = (bf16[32,128,128]{2,1,0:T(8,128)(2,1)}, bf16[32,128,128]{2,1,0:T(8,128)(2,1)}, u32[]{:S(2)}, u32[]{:S(2)}) collective-permute-start(bf16[32,128,128]{2,1,0:T(8,128)(2,1)} %get-tuple-element.123), channel_id=1, source_target_pairs={{0,2},{1,3},{2,4},{3,5},{4,6},{5,7},{6,8},{7,9},{8,10},{9,11},{10,... | collective-permute-start | bytes 3145736 | tf_op jit(solution)/shard_map/ppermute | solution.py:12
  20.2 4.2 %collective-permute-start.1 = (bf16[32,128,128]{2,1,0:T(8,128)(2,1)}, bf16[32,128,128]{2,1,0:T(8,128)(2,1)}, u32[]{:S(2)}, u32[]{:S(2)}) collective-permute-start(bf16[32,128,128]{2,1,0:T(8,128)(2,1)} %get-tuple-element.124), channel_id=1, source_target_pairs={{0,1},{1,2},{2,3},{3,4},{4,5},{5,6},{6,7},{7,8},{8,9},{9,10},{10,1... | collective-permute-start | bytes 3145736 | tf_op jit(solution)/shard_map/ppermute | solution.py:12
  24.5 2.5 collective-permute-start
  28.9 3.2 fusion.12
  32.1 3.2 fusion.14
  35.2 3.7 fusion.27
  39.0 3.6 fusion.24
  43.2 3.2 pad_maximum_fusion.1
  46.4 19.2 %collective-permute-done = bf16[32,128,128]{2,1,0:T(8,128)(2,1)} collective-permute-done((bf16[32,128,128]{2,1,0:T(8,128)(2,1)}, bf16[32,128,128]{2,1,0:T(8,128)(2,1)}, u32[]{:S(2)}, u32[]{:S(2)}) %collective-permute-start) | collective-permute-done | bytes 1048608 | tf_op jit(solution)/shard_map/ppermute | solution.py:12
  65.7 3.3 pad_maximum_fusion
  68.9 214.8 %while.12 = (s32[]{:T(128)}, f32[16,128,2,128]{3,0,2,1:T(8,128)}, s32[16]{0:T(128)S(1)}, bf16[96,128,128]{2,1,0:T(8,128)(2,1)}, bf16[32,128,128]{2,1,0:T(8,128)(...) while((s32[]{:T(128)}, f32[16,128,2,128]{3,0,2,1:T(8,128)}, ...), condition=%wide.region_1.2_spmd, body=%wide.region_0.1_spmd.sunk | while | flops 536936448 | bytes 9568451 | solution.py:69
  72.5 1.7 fusion.80
  75.9 1.7 fusion.79
  77.8 4.6 %dynamic_update_slice.8 = f32[16,128,2,128]{3,0,2,1:T(8,128)} dynamic-update-slice(f32[16,128,2,128]{3,0,2,1:T(8,128)} %get-tuple-element.182, f32[1,128,2,128]{3,0,2,1:T(1,128)S(1)} %copy.42, s32[]{:T(128)S(6)} %copy.46, s32[]{:T(128)} %constant.37.clone.1..sunk, s32[]{:T(128)} %constant.37.clone.1..sunk, s32[]{:T(128)} %constant.37.clone.1..sunk) | dynamic-update-slice | bytes 262148 | tf_op jit(solution)/shard_map/while/body/jit(dynamic_update_index_in_dim)/dynamic_update_slice | solution.py:69
  85.9 1.7 fusion.80
  89.3 1.7 fusion.79
  91.2 4.6 %dynamic_update_slice.8 = f32[16,128,2,128]{3,0,2,1:T(8,128)} dynamic-update-slice(f32[16,128,2,128]{3,0,2,1:T(8,128)} %get-tuple-element.182, f32[1,128,2,128]{3,0,2,1:T(1,128)S(1)} %copy.42, s32[]{:T(128)S(6)} %copy.46, s32[]{:T(128)} %constant.37.clone.1..sunk, s32[]{:T(128)} %constant.37.clone.1..sunk, s32[]{:T(128)} %constant.37.clone.1..sunk) | dynamic-update-slice | bytes 262148 | tf_op jit(solution)/shard_map/while/body/jit(dynamic_update_index_in_dim)/dynamic_update_slice | solution.py:69
  99.3 1.7 fusion.80
  101.0 1.7 convolution_bitcast_fusion.6
  102.7 1.7 fusion.79
  104.6 4.6 %dynamic_update_slice.8 = f32[16,128,2,128]{3,0,2,1:T(8,128)} dynamic-update-slice(f32[16,128,2,128]{3,0,2,1:T(8,128)} %get-tuple-element.182, f32[1,128,2,128]{3,0,2,1:T(1,128)S(1)} %copy.42, s32[]{:T(128)S(6)} %copy.46, s32[]{:T(128)} %constant.37.clone.1..sunk, s32[]{:T(128)} %constant.37.clone.1..sunk, s32[]{:T(128)} %constant.37.clone.1..sunk) | dynamic-update-slice | bytes 262148 | tf_op jit(solution)/shard_map/while/body/jit(dynamic_update_index_in_dim)/dynamic_update_slice | solution.py:69
  116.1 1.7 fusion.79
  118.0 4.6 %dynamic_update_slice.8 = f32[16,128,2,128]{3,0,2,1:T(8,128)} dynamic-update-slice(f32[16,128,2,128]{3,0,2,1:T(8,128)} %get-tuple-element.182, f32[1,128,2,128]{3,0,2,1:T(1,128)S(1)} %copy.42, s32[]{:T(128)S(6)} %copy.46, s32[]{:T(128)} %constant.37.clone.1..sunk, s32[]{:T(128)} %constant.37.clone.1..sunk, s32[]{:T(128)} %constant.37.clone.1..sunk) | dynamic-update-slice | bytes 262148 | tf_op jit(solution)/shard_map/while/body/jit(dynamic_update_index_in_dim)/dynamic_update_slice | solution.py:69
  126.2 1.7 fusion.80
  129.6 1.7 fusion.79
  131.4 4.6 %dynamic_update_slice.8 = f32[16,128,2,128]{3,0,2,1:T(8,128)} dynamic-update-slice(f32[16,128,2,128]{3,0,2,1:T(8,128)} %get-tuple-element.182, f32[1,128,2,128]{3,0,2,1:T(1,128)S(1)} %copy.42, s32[]{:T(128)S(6)} %copy.46, s32[]{:T(128)} %constant.37.clone.1..sunk, s32[]{:T(128)} %constant.37.clone.1..sunk, s32[]{:T(128)} %constant.37.clone.1..sunk) | dynamic-update-slice | bytes 262148 | tf_op jit(solution)/shard_map/while/body/jit(dynamic_update_index_in_dim)/dynamic_update_slice | solution.py:69
  139.6 1.7 fusion.80
  141.3 1.7 convolution_bitcast_fusion.6
  143.0 1.7 fusion.79
  144.8 4.6 %dynamic_update_slice.8 = f32[16,128,2,128]{3,0,2,1:T(8,128)} dynamic-update-slice(f32[16,128,2,128]{3,0,2,1:T(8,128)} %get-tuple-element.182, f32[1,128,2,128]{3,0,2,1:T(1,128)S(1)} %copy.42, s32[]{:T(128)S(6)} %copy.46, s32[]{:T(128)} %constant.37.clone.1..sunk, s32[]{:T(128)} %constant.37.clone.1..sunk, s32[]{:T(128)} %constant.37.clone.1..sunk) | dynamic-update-slice | bytes 262148 | tf_op jit(solution)/shard_map/while/body/jit(dynamic_update_index_in_dim)/dynamic_update_slice | solution.py:69
  156.4 1.7 fusion.79
  158.2 4.6 %dynamic_update_slice.8 = f32[16,128,2,128]{3,0,2,1:T(8,128)} dynamic-update-slice(f32[16,128,2,128]{3,0,2,1:T(8,128)} %get-tuple-element.182, f32[1,128,2,128]{3,0,2,1:T(1,128)S(1)} %copy.42, s32[]{:T(128)S(6)} %copy.46, s32[]{:T(128)} %constant.37.clone.1..sunk, s32[]{:T(128)} %constant.37.clone.1..sunk, s32[]{:T(128)} %constant.37.clone.1..sunk) | dynamic-update-slice | bytes 262148 | tf_op jit(solution)/shard_map/while/body/jit(dynamic_update_index_in_dim)/dynamic_update_slice | solution.py:69
  166.4 1.7 fusion.80
  169.8 1.7 fusion.79
  171.6 4.6 %dynamic_update_slice.8 = f32[16,128,2,128]{3,0,2,1:T(8,128)} dynamic-update-slice(f32[16,128,2,128]{3,0,2,1:T(8,128)} %get-tuple-element.182, f32[1,128,2,128]{3,0,2,1:T(1,128)S(1)} %copy.42, s32[]{:T(128)S(6)} %copy.46, s32[]{:T(128)} %constant.37.clone.1..sunk, s32[]{:T(128)} %constant.37.clone.1..sunk, s32[]{:T(128)} %constant.37.clone.1..sunk) | dynamic-update-slice | bytes 262148 | tf_op jit(solution)/shard_map/while/body/jit(dynamic_update_index_in_dim)/dynamic_update_slice | solution.py:69
  179.8 1.7 fusion.80
  181.5 1.7 convolution_bitcast_fusion.6
  183.2 1.7 fusion.79
  185.0 4.6 %dynamic_update_slice.8 = f32[16,128,2,128]{3,0,2,1:T(8,128)} dynamic-update-slice(f32[16,128,2,128]{3,0,2,1:T(8,128)} %get-tuple-element.182, f32[1,128,2,128]{3,0,2,1:T(1,128)S(1)} %copy.42, s32[]{:T(128)S(6)} %copy.46, s32[]{:T(128)} %constant.37.clone.1..sunk, s32[]{:T(128)} %constant.37.clone.1..sunk, s32[]{:T(128)} %constant.37.clone.1..sunk) | dynamic-update-slice | bytes 262148 | tf_op jit(solution)/shard_map/while/body/jit(dynamic_update_index_in_dim)/dynamic_update_slice | solution.py:69
  193.2 1.7 fusion.80
  194.9 1.7 convolution_bitcast_fusion.6
  196.6 1.7 fusion.79
  198.5 4.6 %dynamic_update_slice.8 = f32[16,128,2,128]{3,0,2,1:T(8,128)} dynamic-update-slice(f32[16,128,2,128]{3,0,2,1:T(8,128)} %get-tuple-element.182, f32[1,128,2,128]{3,0,2,1:T(1,128)S(1)} %copy.42, s32[]{:T(128)S(6)} %copy.46, s32[]{:T(128)} %constant.37.clone.1..sunk, s32[]{:T(128)} %constant.37.clone.1..sunk, s32[]{:T(128)} %constant.37.clone.1..sunk) | dynamic-update-slice | bytes 262148 | tf_op jit(solution)/shard_map/while/body/jit(dynamic_update_index_in_dim)/dynamic_update_slice | solution.py:69
  206.7 1.7 fusion.80
  210.1 1.7 fusion.79
  211.9 4.6 %dynamic_update_slice.8 = f32[16,128,2,128]{3,0,2,1:T(8,128)} dynamic-update-slice(f32[16,128,2,128]{3,0,2,1:T(8,128)} %get-tuple-element.182, f32[1,128,2,128]{3,0,2,1:T(1,128)S(1)} %copy.42, s32[]{:T(128)S(6)} %copy.46, s32[]{:T(128)} %constant.37.clone.1..sunk, s32[]{:T(128)} %constant.37.clone.1..sunk, s32[]{:T(128)} %constant.37.clone.1..sunk) | dynamic-update-slice | bytes 262148 | tf_op jit(solution)/shard_map/while/body/jit(dynamic_update_index_in_dim)/dynamic_update_slice | solution.py:69
  220.1 1.7 fusion.80
  223.5 1.7 fusion.79
  225.4 4.6 %dynamic_update_slice.8 = f32[16,128,2,128]{3,0,2,1:T(8,128)} dynamic-update-slice(f32[16,128,2,128]{3,0,2,1:T(8,128)} %get-tuple-element.182, f32[1,128,2,128]{3,0,2,1:T(1,128)S(1)} %copy.42, s32[]{:T(128)S(6)} %copy.46, s32[]{:T(128)} %constant.37.clone.1..sunk, s32[]{:T(128)} %constant.37.clone.1..sunk, s32[]{:T(128)} %constant.37.clone.1..sunk) | dynamic-update-slice | bytes 262148 | tf_op jit(solution)/shard_map/while/body/jit(dynamic_update_index_in_dim)/dynamic_update_slice | solution.py:69
  233.6 1.7 fusion.80
  237.0 1.7 fusion.79
  238.8 4.6 %dynamic_update_slice.8 = f32[16,128,2,128]{3,0,2,1:T(8,128)} dynamic-update-slice(f32[16,128,2,128]{3,0,2,1:T(8,128)} %get-tuple-element.182, f32[1,128,2,128]{3,0,2,1:T(1,128)S(1)} %copy.42, s32[]{:T(128)S(6)} %copy.46, s32[]{:T(128)} %constant.37.clone.1..sunk, s32[]{:T(128)} %constant.37.clone.1..sunk, s32[]{:T(128)} %constant.37.clone.1..sunk) | dynamic-update-slice | bytes 262148 | tf_op jit(solution)/shard_map/while/body/jit(dynamic_update_index_in_dim)/dynamic_update_slice | solution.py:69
  247.0 1.7 fusion.80
  250.4 1.7 fusion.79
  252.3 4.6 %dynamic_update_slice.8 = f32[16,128,2,128]{3,0,2,1:T(8,128)} dynamic-update-slice(f32[16,128,2,128]{3,0,2,1:T(8,128)} %get-tuple-element.182, f32[1,128,2,128]{3,0,2,1:T(1,128)S(1)} %copy.42, s32[]{:T(128)S(6)} %copy.46, s32[]{:T(128)} %constant.37.clone.1..sunk, s32[]{:T(128)} %constant.37.clone.1..sunk, s32[]{:T(128)} %constant.37.clone.1..sunk) | dynamic-update-slice | bytes 262148 | tf_op jit(solution)/shard_map/while/body/jit(dynamic_update_index_in_dim)/dynamic_update_slice | solution.py:69
  260.5 1.7 fusion.80
  263.9 1.7 fusion.79
  265.7 4.6 %dynamic_update_slice.8 = f32[16,128,2,128]{3,0,2,1:T(8,128)} dynamic-update-slice(f32[16,128,2,128]{3,0,2,1:T(8,128)} %get-tuple-element.182, f32[1,128,2,128]{3,0,2,1:T(1,128)S(1)} %copy.42, s32[]{:T(128)S(6)} %copy.46, s32[]{:T(128)} %constant.37.clone.1..sunk, s32[]{:T(128)} %constant.37.clone.1..sunk, s32[]{:T(128)} %constant.37.clone.1..sunk) | dynamic-update-slice | bytes 262148 | tf_op jit(solution)/shard_map/while/body/jit(dynamic_update_index_in_dim)/dynamic_update_slice | solution.py:69
  273.9 1.7 fusion.80
  277.3 1.7 fusion.79
  279.2 4.6 %dynamic_update_slice.8 = f32[16,128,2,128]{3,0,2,1:T(8,128)} dynamic-update-slice(f32[16,128,2,128]{3,0,2,1:T(8,128)} %get-tuple-element.182, f32[1,128,2,128]{3,0,2,1:T(1,128)S(1)} %copy.42, s32[]{:T(128)S(6)} %copy.46, s32[]{:T(128)} %constant.37.clone.1..sunk, s32[]{:T(128)} %constant.37.clone.1..sunk, s32[]{:T(128)} %constant.37.clone.1..sunk) | dynamic-update-slice | bytes 262148 | tf_op jit(solution)/shard_map/while/body/jit(dynamic_update_index_in_dim)/dynamic_update_slice | solution.py:69
  283.8 83.3 %reduce-scatter.2.cloned.1.call-done = f32[8,16,2,128]{3,1,2,0:T(8,128)} async-done(((f32[128,16,2,128]{3,1,2,0:T(8,128)}), f32[8,16,2,128]{3,1,2,0:T(8,128)}) %reduce-scatter.2.cloned.1.call-update) | async-done | bytes 131088 | tf_op jit(solution)/shard_map/reduce_scatter | solution.py:70
  (102 shorter events, 69.7 us)
Async XLA Ops:
  6.5 360.6 %reduce-scatter.2.cloned.1.call-start = ((), (), s32[]{:S(2)}) async-start(), calls=%async_computation.1 | async-start | bytes 2228224 | tf_op jit(solution)/shard_map/reduce_scatter | solution.py:70
  9.2 17.8 %copy-start.1 = (bf16[32,2,128,128]{3,2,1,0:T(8,128)(2,1)S(1)}, bf16[32,2,128,128]{3,2,1,0:T(8,128)(2,1)}, u32[]{:S(2)}) copy-start(bf16[32,2,128,128]{3,2,1,0:T(8,128)(2,1)} %param.7) | copy-start | bytes 6291460
  9.2 17.8 %copy-start.3 = (bf16[2,128,128]{2,1,0:T(8,128)(2,1)S(1)}, bf16[2,128,128]{2,1,0:T(8,128)(2,1)}, u32[]{:S(2)}) copy-start(bf16[2,128,128]{2,1,0:T(8,128)(2,1)} %param.9) | copy-start | bytes 196612
  12.5 30.2 %collective-permute-start.3 = (bf16[32,128,128]{2,1,0:T(8,128)(2,1)}, bf16[32,128,128]{2,1,0:T(8,128)(2,1)}, u32[]{:S(2)}, u32[]{:S(2)}) collective-permute-start(bf16[32,128,128]{2,1,0:T(8,128)(2,1)} %get-tuple-element.123), channel_id=1, source_target_pairs={{0,1},{1,2},{2,3},{3,4},{4,5},{5,6},{6,7},{7,8},{8,9},{9,10},{10,1... | collective-permute-start | bytes 3145736 | tf_op jit(solution)/shard_map/ppermute | solution.py:12
  15.9 27.3 %collective-permute-start.2 = (bf16[32,128,128]{2,1,0:T(8,128)(2,1)}, bf16[32,128,128]{2,1,0:T(8,128)(2,1)}, u32[]{:S(2)}, u32[]{:S(2)}) collective-permute-start(bf16[32,128,128]{2,1,0:T(8,128)(2,1)} %get-tuple-element.123), channel_id=1, source_target_pairs={{0,2},{1,3},{2,4},{3,5},{4,6},{5,7},{6,8},{7,9},{8,10},{9,11},{10,... | collective-permute-start | bytes 3145736 | tf_op jit(solution)/shard_map/ppermute | solution.py:12
  20.2 26.2 %collective-permute-start.1 = (bf16[32,128,128]{2,1,0:T(8,128)(2,1)}, bf16[32,128,128]{2,1,0:T(8,128)(2,1)}, u32[]{:S(2)}, u32[]{:S(2)}) collective-permute-start(bf16[32,128,128]{2,1,0:T(8,128)(2,1)} %get-tuple-element.124), channel_id=1, source_target_pairs={{0,1},{1,2},{2,3},{3,4},{4,5},{5,6},{6,7},{7,8},{8,9},{9,10},{10,1... | collective-permute-start | bytes 3145736 | tf_op jit(solution)/shard_map/ppermute | solution.py:12
  24.5 41.2 %collective-permute-start = (bf16[32,128,128]{2,1,0:T(8,128)(2,1)}, bf16[32,128,128]{2,1,0:T(8,128)(2,1)}, u32[]{:S(2)}, u32[]{:S(2)}) collective-permute-start(bf16[32,128,128]{2,1,0:T(8,128)(2,1)} %get-tuple-element.124), channel_id=1, source_target_pairs={{0,2},{1,3},{2,4},{3,5},{4,6},{5,7},{6,8},{7,9},{8,10},{9,11},{10,... | collective-permute-start | bytes 3145736 | tf_op jit(solution)/shard_map/ppermute | solution.py:12
  28.9 6.3 %copy-start = (f32[32,128,128]{2,1,0:T(8,128)}, f32[32,128,128]{2,1,0:T(8,128)S(1)}, u32[]{:S(2)}) copy-start(f32[32,128,128]{2,1,0:T(8,128)S(1)} %convolution_subtract_fusion) | copy-start | bytes 6291460
  35.2 3.8 %copy-start.2 = (f32[32,128,128]{2,1,0:T(8,128)S(1)}, f32[32,128,128]{2,1,0:T(8,128)}, u32[]{:S(2)}) copy-start(f32[32,128,128]{2,1,0:T(8,128)} %fusion.14) | copy-start | bytes 6291460
  46.4 22.5 %copy-start.4 = (s32[16]{0:T(128)S(1)}, s32[16]{0:T(128)}, u32[]{:S(2)}) copy-start(s32[16]{0:T(128)} %param.10) | copy-start | bytes 196
Sparse Core Ops, SparseCore 0:
  283.9 83.1 reduce-scatter.1
where the time goes:
time: 380 us; the launch traced here: 376 us
  matrix products  124 us (33%)
  waiting for transfers between devices  103 us (27%)
  local copies, waits for them, and re-layouts  87.7 us (23%)
  loops' own time  20.5 us (5%)
  starting transfers between devices  14.5 us (4%)
  between operations  13.5 us (4%)
  other arithmetic  12.2 us (3%)
    reduce_scatter x1, waiting for transfers between devices, on_device(): lax.psum_scatter(full_term, 'energy', scatter_dimension=0, tiled=True)  83.3 us
    dynamic_update_slice x32, local copies, waits for them, and re-layouts, on_device(): full_term = jnp.transpose(lax.map(single, shifts), (1, 0, 2, 3))  75.3 us
    dot_general x16, matrix products, complex_sum(): jnp.einsum('eij,ejk->ik', left_real, right_imag, preferred_element_type=j...  27.2 us
    dot_general x16, matrix products, complex_sum(): jnp.einsum('eij,ejk->ik', left_real, right_real, preferred_element_type=j...  27.2 us
    dot_general x16, matrix products, complex_sum(): jnp.einsum('eij,ejk->ik', left_imag, right_real, preferred_element_type=j...  27.1 us
    dot_general x16, matrix products, complex_sum(): jnp.einsum('eij,ejk->ik', left_imag, right_imag, preferred_element_type=j...  27 us
    another operation x1, loops' own time, on_device(): full_term = jnp.transpose(lax.map(single, shifts), (1, 0, 2, 3))  20.5 us
    ppermute x4, waiting for transfers between devices, passed_along(): return lax.ppermute(block, axis, route)  19.8 us
  transfers between devices with their start and end apart: 5, of which 3 were waited for; matrix products, arithmetic and copies ran while one was open for 5% of the time, Pallas kernels for 0%

commit v1 on v0

v1 whole, which is shorter than its diff:
```python
import functools
import math

import jax
import jax.numpy as jnp
from jax import lax
from jax.experimental import pallas as pl
from jax.experimental.pallas import tpu as pltpu
from jax.sharding import PartitionSpec as P

STEP = 8
PAIR = 2
PARTS = 4
MIB = 1 << 20


def rotated(real, imag):
    top = jnp.concatenate([real, imag], 1)
    bottom = jnp.concatenate([-imag, real], 1)
    return jnp.concatenate([top, bottom], 0)


def project_kernel(left_ref, right_ref, lesser_ref, out_ref):
    left = left_ref[...]
    right = right_ref[...]
    for u in range(lesser_ref.shape[0]):
        block = rotated(lesser_ref[u, 0], lesser_ref[u, 1])
        inner = jnp.dot(left, block, preferred_element_type=jnp.float32)
        high = inner.astype(jnp.bfloat16)
        low = (inner - high.astype(jnp.float32)).astype(jnp.bfloat16)
        outer = jnp.dot(high, right, preferred_element_type=jnp.float32)
        outer += jnp.dot(low, right, preferred_element_type=jnp.float32)
        out_ref[u] = outer.astype(jnp.bfloat16)


def project(left, right, lesser):
    energies, _, orbitals, _ = lesser.shape
    width = 2 * orbitals
    flops = energies * 2 * orbitals * width * width * 3
    return pl.pallas_call(
        project_kernel,
        out_shape=jax.ShapeDtypeStruct((energies, orbitals, width), jnp.bfloat16),
        grid=(energies // STEP,),
        in_specs=[
            pl.BlockSpec((orbitals, width), lambda t: (0, 0)),
            pl.BlockSpec((width, width), lambda t: (0, 0)),
            pl.BlockSpec((STEP, 2, orbitals, orbitals), lambda t: (t, 0, 0, 0)),
        ],
        out_specs=pl.BlockSpec((STEP, orbitals, width), lambda t: (t, 0, 0)),
        compiler_params=pltpu.CompilerParams(vmem_limit_bytes=16 * MIB),
        cost_estimate=pl.CostEstimate(
            flops=flops, bytes_accessed=lesser.size * 4, transcendentals=0
        ),
    )(left, right, lesser)


def add_products(place_ref, proj_ref, green_ref, total_ref):
    first = pl.program_id(0) * STEP
    photons, rows, width = total_ref.shape
    for w in range(0, photons, PAIR):
        total = total_ref[w : w + PAIR].reshape(PAIR * rows, width)
        for u in range(STEP):
            left = jnp.concatenate(
                [proj_ref[place_ref[first + u, w + v]] for v in range(PAIR)], 0
            )
            right = rotated(green_ref[u, 0], green_ref[u, 1])
            total += jnp.dot(left, right, preferred_element_type=jnp.float32)
        total_ref[w : w + PAIR] = total.reshape(PAIR, rows, width)


def first_kernel(place_ref, proj_ref, green_ref, total_ref):
    @pl.when(pl.program_id(0) == 0)
    def _():
        total_ref[...] = jnp.zeros_like(total_ref)

    add_products(place_ref, proj_ref, green_ref, total_ref)


def next_kernel(place_ref, proj_ref, green_ref, before_ref, total_ref):
    @pl.when(pl.program_id(0) == 0)
    def _():
        total_ref[...] = before_ref[...]

    add_products(place_ref, proj_ref, green_ref, total_ref)


def last_kernel(place_ref, core_ref, proj_ref, green_ref, before_ref, keep_ref, send_ref, total_ref):
    @pl.when(pl.program_id(0) == 0)
    def _():
        total_ref[...] = before_ref[...]

    add_products(place_ref, proj_ref, green_ref, total_ref)

    @pl.when(pl.program_id(0) == pl.num_programs(0) - 1)
    def _():
        half = keep_ref.shape[1]
        core = core_ref[0]
        own = pl.multiple_of(core * half, half)
        other = pl.multiple_of((1 - core) * half, half)
        keep_ref[...] = total_ref[:, pl.ds(own, half), :]
        send_ref[...] = total_ref[:, pl.ds(other, half), :].astype(send_ref.dtype)


def products(place, proj, green, before=None, core=None):
    slots, rows, width = proj.shape
    energies, _, orbitals, _ = green.shape
    photons = place.shape[1]
    smem = pl.BlockSpec(memory_space=pltpu.SMEM)
    total_spec = pl.BlockSpec((photons, rows, width), lambda t: (0, 0, 0))
    total_shape = jax.ShapeDtypeStruct((photons, rows, width), jnp.float32)
    operands, specs = [place], [smem]
    if core is not None:
        operands.append(core)
        specs.append(smem)
    operands += [proj, green]
    specs += [
        pl.BlockSpec((slots, rows, width), lambda t: (0, 0, 0), pipeline_mode=pl.Buffered(1)),
        pl.BlockSpec((STEP, 2, orbitals, orbitals), lambda t: (t, 0, 0, 0)),
    ]
    if before is not None:
        operands.append(before)
        specs.append(
            pl.BlockSpec((photons, rows, width), lambda t: (0, 0, 0), pipeline_mode=pl.Buffered(1))
        )
    scratch = []
    if core is not None:
        half = rows // 2
        half_spec = pl.BlockSpec((photons, half, width), lambda t: (0, 0, 0))
        kernel = last_kernel
        out_specs = [half_spec, half_spec]
        out_shape = [
            jax.ShapeDtypeStruct((photons, half, width), jnp.float32),
            jax.ShapeDtypeStruct((photons, half, width), jnp.bfloat16),
        ]
        scratch = [pltpu.VMEM((photons, rows, width), jnp.float32)]
    else:
        kernel = first_kernel if before is None else next_kernel
        out_specs, out_shape = total_spec, total_shape
    flops = 2 * energies * photons * rows * width * width
    return pl.pallas_call(
        kernel,
        out_shape=out_shape,
        grid=(energies // STEP,),
        in_specs=specs,
        out_specs=out_specs,
        scratch_shapes=scratch,
        compiler_params=pltpu.CompilerParams(vmem_limit_bytes=24 * MIB),
        cost_estimate=pl.CostEstimate(
            flops=flops,
            bytes_accessed=2 * proj.size + 2 * green.size + 8 * photons * rows * width,
            transcendentals=0,
        ),
    )(*operands)


def places(shifts, window, first_energy, core, e_dev):
    zero_slot = 2 * e_dev
    offset = jnp.arange(e_dev, dtype=jnp.int32)[:, None]
    reach = offset + shifts[None, :]
    limit = jnp.where(core == 0, 2 * e_dev, e_dev)

    def inside(energy):
        return (energy >= window[0]) & (energy < window[1])

    own = first_energy + offset
    near = inside(own) & inside(own + shifts[None, :]) & (reach < limit)
    far = inside(own - 2 * e_dev) & inside(own - 2 * e_dev + shifts[None, :]) & (reach >= limit)
    wrapped = jnp.where(reach >= 2 * e_dev, reach - 2 * e_dev, reach)
    return jnp.where(near, reach, zero_slot), jnp.where(far, wrapped, zero_slot)


def on_device(lesser, greater, dipole, shifts, window):
    e_dev, _, orbitals, _ = lesser.shape
    photons = shifts.shape[0]
    devices = lax.axis_size("energy")
    index = lax.axis_index("energy")
    core = index % 2
    chips = devices // 2
    share = orbitals // devices
    total = e_dev * devices

    up = [(i, i + 2) for i in range(devices - 2)]
    across = [(i, i ^ 1) for i in range(devices)]
    piece = e_dev // PARTS
    far = [
        lax.ppermute(greater[k * piece : (k + 1) * piece], "energy", up) for k in range(PARTS)
    ]

    rows = dipole.reshape(2, chips, 2, share, orbitals)
    rows = jnp.transpose(rows, (0, 2, 1, 3, 4)).reshape(2, orbitals, orbitals)
    left = jnp.concatenate([rows[0], rows[1]], 1)
    real, imag = dipole[0].T, dipole[1].T
    right = jnp.concatenate(
        [jnp.concatenate([real, -imag], 1), jnp.concatenate([imag, real], 1)], 0
    )
    proj = project(left, right, lesser)
    other = lax.ppermute(proj, "energy", across)
    zeros = jnp.zeros((1,) + proj.shape[1:], proj.dtype)
    proj = jnp.concatenate([proj, other, zeros], 0)

    near_place, far_place = places(shifts, window, index * e_dev, core, e_dev)
    result = products(near_place, proj, greater)
    for k in range(PARTS):
        place = far_place[k * piece : (k + 1) * piece]
        if k < PARTS - 1:
            result = products(place, proj, far[k], before=result)
    keep, send = products(
        place, proj, far[-1], before=result, core=jnp.reshape(core, (1,)).astype(jnp.int32)
    )
    got = lax.ppermute(send, "energy", across)
    chip_sum = keep + got.astype(jnp.float32)
    chip_sum = chip_sum.reshape(photons, chips, share, 2 * orbitals)
    chip_sum = jnp.transpose(chip_sum, (1, 0, 2, 3)).astype(jnp.bfloat16)
    groups = [[i for i in range(devices) if i % 2 == c] for c in range(2)]
    shares = lax.all_to_all(chip_sum, "energy", 0, 0, axis_index_groups=groups, tiled=True)
    scale = 1.0 / math.sqrt(2.0 * orbitals * total)
    summed = jnp.sum(shares.astype(jnp.float32), 0) * scale
    summed = jnp.transpose(summed, (1, 0, 2))
    return summed.reshape(share, photons, 2, orbitals)


def solution(mesh):
    placed = (
        P(("dom", "energy"), None, None, None),
        P(("dom", "energy"), None, None, None),
        P(),
        P(),
        P("dom"),
    )
    return jax.shard_map(
        on_device,
        mesh=mesh,
        in_specs=placed,
        out_specs=P(("dom", "energy"), None, None, None),
        check_vma=False,
    )
```

time: 380 us -> 98.4 us (0.26); the launches traced: 376 us -> 97.9 us
  matrix products: 124 us -> 0 us
  waiting for transfers between devices: 103 us -> 20.4 us
  local copies, waits for them, and re-layouts: 87.7 us -> 6.25 us
  Pallas kernels: 0 us -> 28.3 us
  blocking collectives: 0 us -> 21.4 us
  loops' own time: 20.5 us -> 0 us
  between operations: 13.5 us -> 0.21 us
  other arithmetic: 12.2 us -> 5.34 us
    dot_general x72 -> x0, matrix products: 124 us -> none  [the longest x16 27.2 us: complex_sum(): jnp.einsum('eij,ejk->ik', left_real, right_imag, preferred_element_type=j...]
    reduce_scatter x1 -> x0, waiting for transfers between devices: 83.3 us -> none  [on_device(): lax.psum_scatter(full_term, 'energy', scatter_dimension=0, tiled=True)]
    dynamic_update_slice x32 -> x0, local copies, waits for them, and re-layouts: 75.3 us -> none  [on_device(): full_term = jnp.transpose(lax.map(single, shifts), (1, 0, 2, 3))]
    pallas_call x0 -> x6, Pallas kernels: none -> 28.3 us  [the longest x5 23.3 us: products(): pl.pallas_call(kernel, out_shape=out_shape, grid=(energies // STEP,), in_...]
    all_to_all x0 -> x1, blocking collectives: none -> 21.4 us  [on_device(): lax.all_to_all(chip_sum, 'energy', 0, 0, axis_index_groups=groups, tiled=...]
    another operation x1 -> x0, loops' own time: 20.5 us -> none  [on_device(): full_term = jnp.transpose(lax.map(single, shifts), (1, 0, 2, 3))]
    dynamic_slice x16 -> x0, local copies, waits for them, and re-layouts: 10.3 us -> none  [on_device(): full_term = jnp.transpose(lax.map(single, shifts), (1, 0, 2, 3))]
    mul x2 -> x0, other arithmetic: 4.2 us -> none  [the longest x1 3.29 us: on_device(): green_imag = greater[:, 1] * inside]
  transfers between devices with their start and end apart: 5 -> 6, of which waited for: 3 -> 2; matrix products, arithmetic and copies ran while one was open for 5% -> 7% of each run, Pallas kernels for 0% -> 20%
where the time goes in v1:
time: 98.4 us; the launch traced here: 97.9 us
  Pallas kernels  28.3 us (29%)
  blocking collectives  21.4 us (22%)
  waiting for transfers between devices  20.4 us (21%)
  starting transfers between devices  16 us (16%)
  local copies, waits for them, and re-layouts  6.25 us (6%)
  other arithmetic  5.34 us (5%)
    pallas_call x5, Pallas kernels, products(): pl.pallas_call(kernel, out_shape=out_shape, grid=(energies // STEP,), in_...  23.3 us
    all_to_all x1, blocking collectives, on_device(): lax.all_to_all(chip_sum, 'energy', 0, 0, axis_index_groups=groups, tiled=...  21.4 us
    ppermute x4, waiting for transfers between devices, on_device(): lax.ppermute(greater[k * piece:(k + 1) * piece], 'energy', up)  18.5 us
    ppermute x4, starting transfers between devices, on_device(): lax.ppermute(greater[k * piece:(k + 1) * piece], 'energy', up)  15.5 us
    pallas_call x1, Pallas kernels, project(): pl.pallas_call(project_kernel, out_shape=jax.ShapeDtypeStruct((energies,...  4.95 us
    concatenate x1, other arithmetic, on_device(): proj = jnp.concatenate([proj, other, zeros], 0)  2.46 us
  transfers between devices with their start and end apart: 6, of which 2 were waited for; matrix products, arithmetic and copies ran while one was open for 7% of the time, Pallas kernels for 20%

profile of v1, /device:TPU:0, one launch (start us, length us, event | category | flops | bytes accessed | tf_op | source)
XLA Modules:
  0.0 97.9 jit_solution(5209116301182213902)
XLA Ops:
  0.0 0.8 fusion.12
  0.8 0.8 copy.20
  1.6 0.1 copy.16
  1.8 0.1 copy.17
  1.9 0.0 copy-start.1
  2.0 1.6 %copy-done.1 = bf16[32,2,128,128]{3,2,1,0:T(8,128)(2,1)S(1)} copy-done((bf16[32,2,128,128]{3,2,1,0:T(8,128)(2,1)S(1)}, bf16[32,2,128,128]{3,2,1,0:T(8,128)(2,1)}, u32[]{:S(2)}) %copy-start.1) | copy-done | bytes 2097176
  3.5 0.0 copy-start
  3.5 5.0 %shard_map.55 = bf16[32,128,256]{2,1,0:T(8,128)(2,1)} custom-call(bf16[128,256]{1,0:T(8,128)(2,1)S(1)} %pad_maximum_fusion.left_ref, bf16[256,256]{1,0:T(8,128)(2,1)S(1)} %maximum_maximum_fusion.1.right_ref, bf16[32,2,128,128]{3,2,1,0:T(8,128)(2,1)S(1)} %copy-done.1), custom_call_target="tpu_custom_call" | custom-call | flops 1610612736 | bytes 4194304 | tf_op jit(solution)/shard_map/pallas_call | solution.py:40
  8.5 0.0 copy-start.2
  8.5 0.0 copy-start.3
  8.5 0.5 collective-permute-start
  9.0 0.0 copy-done
  9.0 1.4 %fusion.11 = (bf16[8,2,128,128]{3,2,1,0:T(8,128)(2,1)}, bf16[8,2,128,128]{3,2,1,0:T(8,128)(2,1)}, bf16[8,2,128,128]{3,2,1,0:T(8,128)(2,1)}, bf16[8,2,128,128]{3,2,1,0:T(8,128)(2,1)}) fusion(bf16[32,2,128,128]{3,2,1,0:T(8,128)(2,1)S(1)} %copy-done), kind=kLoop, calls=%fused_computation.30 | loop fusion | bytes 4194304 | tf_op jit(solution)/shard_map/slice | solution.py:186
  10.3 5.2 %collective-permute-start.1 = (bf16[8,2,128,128]{3,2,1,0:T(8,128)(2,1)}, bf16[8,2,128,128]{3,2,1,0:T(8,128)(2,1)}, u32[]{:S(2)}, u32[]{:S(2)}) collective-permute-start(bf16[8,2,128,128]{3,2,1,0:T(8,128)(2,1)} %get-tuple-element.12), channel_id=1, source_target_pairs={{0,2},{1,3},{2,4},{3,5},{4,6},{5,7},{6,8},{7,9},{8,10},{9,11},{10,... | collective-permute-start | bytes 1572872 | tf_op jit(solution)/shard_map/ppermute | solution.py:186
  15.6 2.6 %collective-permute-start.2 = (bf16[8,2,128,128]{3,2,1,0:T(8,128)(2,1)}, bf16[8,2,128,128]{3,2,1,0:T(8,128)(2,1)S(1)}, u32[]{:S(2)}, u32[]{:S(2)}) collective-permute-start(bf16[8,2,128,128]{3,2,1,0:T(8,128)(2,1)} %get-tuple-element.11), channel_id=1, source_target_pairs={{0,2},{1,3},{2,4},{3,5},{4,6},{5,7},{6,8},{7,9},{8,10},{9,11},{10,... | collective-permute-start | bytes 1572872 | tf_op jit(solution)/shard_map/ppermute | solution.py:186
  18.2 3.4 %collective-permute-start.3 = (bf16[8,2,128,128]{3,2,1,0:T(8,128)(2,1)}, bf16[8,2,128,128]{3,2,1,0:T(8,128)(2,1)S(1)}, u32[]{:S(2)}, u32[]{:S(2)}) collective-permute-start(bf16[8,2,128,128]{3,2,1,0:T(8,128)(2,1)} %get-tuple-element.10), channel_id=1, source_target_pairs={{0,2},{1,3},{2,4},{3,5},{4,6},{5,7},{6,8},{7,9},{8,10},{9,11},{10,... | collective-permute-start | bytes 1572872 | tf_op jit(solution)/shard_map/ppermute | solution.py:186
  21.7 4.2 %collective-permute-start.4 = (bf16[8,2,128,128]{3,2,1,0:T(8,128)(2,1)}, bf16[8,2,128,128]{3,2,1,0:T(8,128)(2,1)}, u32[]{:S(2)}, u32[]{:S(2)}) collective-permute-start(bf16[8,2,128,128]{3,2,1,0:T(8,128)(2,1)} %get-tuple-element.9), channel_id=1, source_target_pairs={{0,2},{1,3},{2,4},{3,5},{4,6},{5,7},{6,8},{7,9},{8,10},{9,11},{10,... | collective-permute-start | bytes 1572872 | tf_op jit(solution)/shard_map/ppermute | solution.py:186
  25.8 0.1 pad.2.clone
  25.9 0.0 copy-done.2
  25.9 0.6 fusion.15
  26.5 1.3 %compare_and_fusion = (pred[32]{0:T(512)(128)(4,1)S(1)}, pred[32]{0:T(512)(128)(4,1)S(1)}) fusion(s32[]{:T(128)} %bitcast.1, s32[]{:T(128)} %bitcast, s32[]{:T(128)S(6)} %mul.13), kind=kLoop, calls=%fused_computation.25 | loop fusion | flops 256 | bytes 76 | tf_op jit(solution)/shard_map/and | solution.py:163
  27.8 0.0 copy-done.3
  27.8 1.3 %fusion.3 = (s32[32,16]{1,0:T(8,128)S(1)}, s32[32,16]{1,0:T(8,128)S(1)}) fusion(s32[32]{0:T(128)S(1)} %get-tuple-element.27, s32[]{:T(128)S(6)} %select_n.23, s32[]{:T(128)} %bitcast.1, s32[]{:T(128)} %bitcast, s32[16]{0:T(128)S(1)} %copy-done.3, pred[32]{0:T(512)(128)(4,1)S(1)} %get-tuple-element.25, s32[32]{0:T(128)S(1)} %get-tuple-element.28, ...), kind=kLoop, calls=%fused_computation.17 | loop fusion | flops 10240 | bytes 4492 | tf_op jit(solution)/shard_map/jit(_where)/select_n | solution.py:169
  29.2 0.0 collective-permute-done
  29.2 2.5 %maximum_maximum_fusion.proj_ref = bf16[65,128,256]{2,1,0:T(8,128)(2,1)S(1)} fusion(bf16[32,128,256]{2,1,0:T(8,128)(2,1)} %collective-permute-done, bf16[32,128,256]{2,1,0:T(8,128)(2,1)} %shard_map.55, bf16[65]{0:T(256)(128)(2,1)S(1)} %pad.2.clone), kind=kLoop, calls=%fused_computation | loop fusion | flops 4259840 | bytes 8454274 | tf_op jit(solution)/shard_map/concatenate | solution.py:199
  31.6 10.5 %shard_map.56.before_ref = f32[16,128,256]{2,1,0:T(8,128)S(1)} custom-call(s32[32,16]{1,0:T(8,128)S(1)} %get-tuple-element.21.place_ref, bf16[65,128,256]{2,1,0:T(8,128)(2,1)S(1)} %maximum_maximum_fusion.proj_ref, bf16[32,2,128,128]{3,2,1,0:T(8,128)(2,1)S(1)} %copy-done), custom_call_target="tpu_custom_call" | custom-call | flops 8589934592 | bytes 10551296 | tf_op jit(solution)/shard_map/pallas_call | solution.py:140
  42.1 18.5 %collective-permute-done.4.green_ref = bf16[8,2,128,128]{3,2,1,0:T(8,128)(2,1)} collective-permute-done((bf16[8,2,128,128]{3,2,1,0:T(8,128)(2,1)}, bf16[8,2,128,128]{3,2,1,0:T(8,128)(2,1)}, u32[]{:S(2)}, u32[]{:S(2)}) %collective-permute-start.4) | collective-permute-done | bytes 524320 | tf_op jit(solution)/shard_map/ppermute | solution.py:186
  60.6 3.4 %shard_map.57.before_ref = f32[16,128,256]{2,1,0:T(8,128)S(1)} custom-call(s32[8,16]{1,0:T(8,128)S(1)} %get-tuple-element.17.place_ref, bf16[65,128,256]{2,1,0:T(8,128)(2,1)S(1)} %maximum_maximum_fusion.proj_ref, bf16[8,2,128,128]{3,2,1,0:T(8,128)(2,1)} %collective-permute-done.4.green_ref, f32[16,128,256]{2,1,0:T(8,128)S(1)} %shard_map.56.before_ref), custom_call_target="tpu_custom_call" | custom-call | flops 2147483648 | bytes 8978432 | tf_op jit(solution)/shard_map/pallas_call | solution.py:140
  64.0 0.0 collective-permute-done.3.green_ref
  64.0 3.0 %shard_map.58.before_ref = f32[16,128,256]{2,1,0:T(8,128)S(1)} custom-call(s32[8,16]{1,0:T(8,128)S(1)} %get-tuple-element.18.place_ref, bf16[65,128,256]{2,1,0:T(8,128)(2,1)S(1)} %maximum_maximum_fusion.proj_ref, bf16[8,2,128,128]{3,2,1,0:T(8,128)(2,1)S(1)} %collective-permute-done.3.green_ref, f32[16,128,256]{2,1,0:T(8,128)S(1)} %shard_map.57.before_ref), custom_call_target="tpu_custom_call" | custom-call | flops 2147483648 | bytes 8978432 | tf_op jit(solution)/shard_map/pallas_call | solution.py:140
  67.0 0.0 collective-permute-done.2.green_ref
  67.0 3.0 %shard_map.59.before_ref = f32[16,128,256]{2,1,0:T(8,128)S(1)} custom-call(s32[8,16]{1,0:T(8,128)S(1)} %get-tuple-element.19.place_ref, bf16[65,128,256]{2,1,0:T(8,128)(2,1)S(1)} %maximum_maximum_fusion.proj_ref, bf16[8,2,128,128]{3,2,1,0:T(8,128)(2,1)S(1)} %collective-permute-done.2.green_ref, f32[16,128,256]{2,1,0:T(8,128)S(1)} %shard_map.58.before_ref), custom_call_target="tpu_custom_call" | custom-call | flops 2147483648 | bytes 8978432 | tf_op jit(solution)/shard_map/pallas_call | solution.py:140
  70.0 0.0 collective-permute-done.1.green_ref
  70.0 3.5 %shard_map.60 = (f32[16,64,256]{2,1,0:T(8,128)S(1)}, bf16[16,64,256]{2,1,0:T(8,128)(2,1)S(1)}) custom-call(s32[8,16]{1,0:T(8,128)S(1)} %get-tuple-element.20.place_ref, s32[1]{0:T(128)} %bitcast.2.core_ref, bf16[65,128,256]{2,1,0:T(8,128)(2,1)S(1)} %maximum_maximum_fusion.proj_ref, bf16[8,2,128,128]{3,2,1,0:T(8,128)(2,1)} %collective-permute-done.1.green_ref, ...), custom_call_target="tpu_custom_call" | custom-call | flops 2147483648 | bytes 8978432 | tf_op jit(solution)/shard_map/pallas_call | solution.py:140
  73.5 0.1 collective-permute-start.5
  73.6 1.9 %collective-permute-done.5 = bf16[16,64,256]{2,1,0:T(8,128)(2,1)S(1)} collective-permute-done((bf16[16,64,256]{2,1,0:T(8,128)(2,1)S(1)}, bf16[16,64,256]{2,1,0:T(8,128)(2,1)S(1)}, u32[]{:S(2)}, u32[]{:S(2)}) %collective-permute-start.5) | collective-permute-done | bytes 524320 | tf_op jit(solution)/shard_map/ppermute | solution.py:210
  75.5 0.2 copy_bitcast_fusion
  75.7 21.4 %all_to_all.5 = bf16[8,16,8,256]{3,2,1,0:T(8,128)(2,1)S(1)} all-to-all(bf16[8,16,8,256]{3,2,1,0:T(8,128)(2,1)S(1)} %copy_bitcast_fusion), channel_id=1, replica_groups={{0,2,4,6,8,10,12,14},{1,3,5,7,9,11,13,15},{16,18,20,22,24,26,28,30},{17..., dimensions={0} | all-to-all | bytes 1048576 | tf_op jit(solution)/shard_map/all_to_all | solution.py:215
  97.1 0.1 convert_reduce_fusion
  97.2 0.7 copy.14
  (7 shorter events, 0.1 us)
Async XLA Ops:
  1.9 1.6 %copy-start.1 = (bf16[32,2,128,128]{3,2,1,0:T(8,128)(2,1)S(1)}, bf16[32,2,128,128]{3,2,1,0:T(8,128)(2,1)}, u32[]{:S(2)}) copy-start(bf16[32,2,128,128]{3,2,1,0:T(8,128)(2,1)} %lesser_ref.1) | copy-start | bytes 6291460
  3.5 5.4 %copy-start = (bf16[32,2,128,128]{3,2,1,0:T(8,128)(2,1)S(1)}, bf16[32,2,128,128]{3,2,1,0:T(8,128)(2,1)}, u32[]{:S(2)}) copy-start(bf16[32,2,128,128]{3,2,1,0:T(8,128)(2,1)} %green_ref.1) | copy-start | bytes 6291460
  8.5 17.4 %copy-start.2 = (s32[2]{0:T(128)S(1)}, s32[2]{0:T(128)}, u32[]{:S(2)}) copy-start(s32[2]{0:T(128)} %param.9) | copy-start | bytes 28
  8.5 19.3 %copy-start.3 = (s32[16]{0:T(128)S(1)}, s32[16]{0:T(128)}, u32[]{:S(2)}) copy-start(s32[16]{0:T(128)} %param.8) | copy-start | bytes 196
  8.5 20.7 %collective-permute-start = (bf16[32,128,256]{2,1,0:T(8,128)(2,1)}, bf16[32,128,256]{2,1,0:T(8,128)(2,1)}, u32[]{:S(2)}, u32[]{:S(2)}) collective-permute-start(bf16[32,128,256]{2,1,0:T(8,128)(2,1)} %shard_map.55), channel_id=1, source_target_pairs={{0,1},{1,0},{2,3},{3,2},{4,5},{5,4},{6,7},{7,6},{8,9},{9,8},{10,11... | collective-permute-start | bytes 6291464 | tf_op jit(solution)/shard_map/ppermute | solution.py:197
  10.3 59.7 %collective-permute-start.1 = (bf16[8,2,128,128]{3,2,1,0:T(8,128)(2,1)}, bf16[8,2,128,128]{3,2,1,0:T(8,128)(2,1)}, u32[]{:S(2)}, u32[]{:S(2)}) collective-permute-start(bf16[8,2,128,128]{3,2,1,0:T(8,128)(2,1)} %get-tuple-element.12), channel_id=1, source_target_pairs={{0,2},{1,3},{2,4},{3,5},{4,6},{5,7},{6,8},{7,9},{8,10},{9,11},{10,... | collective-permute-start | bytes 1572872 | tf_op jit(solution)/shard_map/ppermute | solution.py:186
  15.6 51.4 %collective-permute-start.2 = (bf16[8,2,128,128]{3,2,1,0:T(8,128)(2,1)}, bf16[8,2,128,128]{3,2,1,0:T(8,128)(2,1)S(1)}, u32[]{:S(2)}, u32[]{:S(2)}) collective-permute-start(bf16[8,2,128,128]{3,2,1,0:T(8,128)(2,1)} %get-tuple-element.11), channel_id=1, source_target_pairs={{0,2},{1,3},{2,4},{3,5},{4,6},{5,7},{6,8},{7,9},{8,10},{9,11},{10,... | collective-permute-start | bytes 1572872 | tf_op jit(solution)/shard_map/ppermute | solution.py:186
  18.2 45.8 %collective-permute-start.3 = (bf16[8,2,128,128]{3,2,1,0:T(8,128)(2,1)}, bf16[8,2,128,128]{3,2,1,0:T(8,128)(2,1)S(1)}, u32[]{:S(2)}, u32[]{:S(2)}) collective-permute-start(bf16[8,2,128,128]{3,2,1,0:T(8,128)(2,1)} %get-tuple-element.10), channel_id=1, source_target_pairs={{0,2},{1,3},{2,4},{3,5},{4,6},{5,7},{6,8},{7,9},{8,10},{9,11},{10,... | collective-permute-start | bytes 1572872 | tf_op jit(solution)/shard_map/ppermute | solution.py:186
  21.7 38.9 %collective-permute-start.4 = (bf16[8,2,128,128]{3,2,1,0:T(8,128)(2,1)}, bf16[8,2,128,128]{3,2,1,0:T(8,128)(2,1)}, u32[]{:S(2)}, u32[]{:S(2)}) collective-permute-start(bf16[8,2,128,128]{3,2,1,0:T(8,128)(2,1)} %get-tuple-element.9), channel_id=1, source_target_pairs={{0,2},{1,3},{2,4},{3,5},{4,6},{5,7},{6,8},{7,9},{8,10},{9,11},{10,... | collective-permute-start | bytes 1572872 | tf_op jit(solution)/shard_map/ppermute | solution.py:186
  73.5 2.0 %collective-permute-start.5 = (bf16[16,64,256]{2,1,0:T(8,128)(2,1)S(1)}, bf16[16,64,256]{2,1,0:T(8,128)(2,1)S(1)}, u32[]{:S(2)}, u32[]{:S(2)}) collective-permute-start(bf16[16,64,256]{2,1,0:T(8,128)(2,1)S(1)} %get-tuple-element.8), channel_id=1, source_target_pairs={{0,1},{1,0},{2,3},{3,2},{4,5},{5,4},{6,7},{7,6},{8,9},{9,8},{10,11... | collective-permute-start | bytes 1572872 | tf_op jit(solution)/shard_map/ppermute | solution.py:210

commit v2 on v1

--- a/solution.py
+++ b/solution.py
@@ -20,38 +20,63 @@
     return jnp.concatenate([top, bottom], 0)
 
 
-def project_kernel(left_ref, right_ref, lesser_ref, out_ref):
-    left = left_ref[...]
-    right = right_ref[...]
-    for u in range(lesser_ref.shape[0]):
-        block = rotated(lesser_ref[u, 0], lesser_ref[u, 1])
-        inner = jnp.dot(left, block, preferred_element_type=jnp.float32)
-        high = inner.astype(jnp.bfloat16)
-        low = (inner - high.astype(jnp.float32)).astype(jnp.bfloat16)
-        outer = jnp.dot(high, right, preferred_element_type=jnp.float32)
-        outer += jnp.dot(low, right, preferred_element_type=jnp.float32)
-        out_ref[u] = outer.astype(jnp.bfloat16)
-
-
-def project(left, right, lesser):
-    energies, _, orbitals, _ = lesser.shape
+def project_blocks(left, right, lesser_ref, out_ref):
+    count, rows, width = out_ref.shape
+    inner = [
+        jnp.dot(
+            left,
+            rotated(lesser_ref[u, 0], lesser_ref[u, 1]),
+            preferred_element_type=jnp.float32,
+        )
+        for u in range(count)
+    ]
+    inner = jnp.concatenate(inner, 0)
+    high = inner.astype(jnp.bfloat16)
+    low = (inner - high.astype(jnp.float32)).astype(jnp.bfloat16)
+    outer = jnp.dot(high, right, preferred_element_type=jnp.float32)
+    outer += jnp.dot(low, right, preferred_element_type=jnp.float32)
+    out_ref[...] = outer.astype(jnp.bfloat16).reshape(count, rows, width)
+
+
+def project_kernel(steps, left_ref, right_ref, own_ref, other_ref, out_ref):
+    t = pl.program_id(0)
+
+    @pl.when(t < steps)
+    def _():
+        project_blocks(left_ref[...], right_ref[...], own_ref, out_ref)
+
+    @pl.when((t >= steps) & (t < 2 * steps))
+    def _():
+        project_blocks(left_ref[...], right_ref[...], other_ref, out_ref)
+
+    @pl.when(t == 2 * steps)
+    def _():
+        out_ref[...] = jnp.zeros_like(out_ref)
+
+
+def project(left, right, own, other):
+    energies, _, orbitals, _ = own.shape
     width = 2 * orbitals
-    flops = energies * 2 * orbitals * width * width * 3
+    steps = energies // STEP
+    slots = 2 * energies + STEP
     return pl.pallas_call(
-        project_kernel,
-        out_shape=jax.ShapeDtypeStruct((energies, orbitals, width), jnp.bfloat16),
-        grid=(energies // STEP,),
+        functools.partial(project_kernel, steps),
+        out_shape=jax.ShapeDtypeStruct((slots, orbitals, width), jnp.bfloat16),
+        grid=(2 * steps + 1,),
         in_specs=[
             pl.BlockSpec((orbitals, width), lambda t: (0, 0)),
             pl.BlockSpec((width, width), lambda t: (0, 0)),
-            pl.BlockSpec((STEP, 2, orbitals, orbitals), lambda t: (t, 0, 0, 0)),
+            pl.BlockSpec(
+                (STEP, 2, orbitals, orbitals), lambda t: (jnp.minimum(t, steps - 1), 0, 0, 0)
+            ),
+            pl.BlockSpec(
+                (STEP, 2, orbitals, orbitals),
+                lambda t: (jnp.clip(t - steps, 0, steps - 1), 0, 0, 0),
+            ),
         ],
         out_specs=pl.BlockSpec((STEP, orbitals, width), lambda t: (t, 0, 0)),
         compiler_params=pltpu.CompilerParams(vmem_limit_bytes=16 * MIB),
-        cost_estimate=pl.CostEstimate(
-            flops=flops, bytes_accessed=lesser.size * 4, transcendentals=0
-        ),
-    )(left, right, lesser)
+    )(left, right, own, other)
 
 
 def add_products(place_ref, proj_ref, green_ref, total_ref):
@@ -136,7 +161,6 @@
     else:
         kernel = first_kernel if before is None else next_kernel
         out_specs, out_shape = total_spec, total_shape
-    flops = 2 * energies * photons * rows * width * width
     return pl.pallas_call(
         kernel,
         out_shape=out_shape,
@@ -145,11 +169,6 @@
         out_specs=out_specs,
         scratch_shapes=scratch,
         compiler_params=pltpu.CompilerParams(vmem_limit_bytes=24 * MIB),
-        cost_estimate=pl.CostEstimate(
-            flops=flops,
-            bytes_accessed=2 * proj.size + 2 * green.size + 8 * photons * rows * width,
-            transcendentals=0,
-        ),
     )(*operands)
 
 
@@ -182,9 +201,8 @@
     up = [(i, i + 2) for i in range(devices - 2)]
     across = [(i, i ^ 1) for i in range(devices)]
     piece = e_dev // PARTS
-    far = [
-        lax.ppermute(greater[k * piece : (k + 1) * piece], "energy", up) for k in range(PARTS)
-    ]
+    pieces = [greater[k * piece : (k + 1) * piece] for k in range(PARTS)]
+    far = [lax.ppermute(pieces[k], "energy", up) for k in range(2)]
 
     rows = dipole.reshape(2, chips, 2, share, orbitals)
     rows = jnp.transpose(rows, (0, 2, 1, 3, 4)).reshape(2, orbitals, orbitals)
@@ -193,10 +211,7 @@
     right = jnp.concatenate(
         [jnp.concatenate([real, -imag], 1), jnp.concatenate([imag, real], 1)], 0
     )
-    proj = project(left, right, lesser)
-    other = lax.ppermute(proj, "energy", across)
-    zeros = jnp.zeros((1,) + proj.shape[1:], proj.dtype)
-    proj = jnp.concatenate([proj, other, zeros], 0)
+    proj = project(left, right, lesser, lax.ppermute(lesser, "energy", across))
 
     near_place, far_place = places(shifts, window, index * e_dev, core, e_dev)
     result = products(near_place, proj, greater)
@@ -204,6 +219,9 @@
         place = far_place[k * piece : (k + 1) * piece]
         if k < PARTS - 1:
             result = products(place, proj, far[k], before=result)
+        if k + 2 < PARTS:
+            leaving, result = lax.optimization_barrier((pieces[k + 2], result))
+            far.append(lax.ppermute(leaving, "energy", up))
     keep, send = products(
         place, proj, far[-1], before=result, core=jnp.reshape(core, (1,)).astype(jnp.int32)
     )

time: 98.4 us -> 88.3 us (0.90)
  waiting for transfers between devices: 20.4 us -> 14.8 us
  other arithmetic: 5.34 us -> 2.91 us
  local copies, waits for them, and re-layouts: 6.25 us -> 4.59 us
  Pallas kernels: 28.3 us -> 29.5 us
  blocking collectives: 21.4 us -> 20.4 us
    ppermute x5, waiting for transfers between devices: 18.5 us -> 12.9 us  [the longest x2 12.9 us: on_device(): far.append(lax.ppermute(leaving, 'energy', up))]
    concatenate x1 -> x0, other arithmetic: 2.46 us -> none  [on_device(): proj = jnp.concatenate([proj, other, zeros], 0)]
    pallas_call x1, Pallas kernels: 4.95 us -> 7 us  [project(): pl.pallas_call(functools.partial(project_kernel, steps), out_shape=jax.Sh...]
    unnamed x10 -> x16, local copies, waits for them, and re-layouts: 1.83 us -> 0.26 us
    slice x1, local copies, waits for them, and re-layouts: 1.38 us -> 2.92 us  [on_device(): pieces = [greater[k * piece:(k + 1) * piece] for k in range(PARTS)]]
    all_to_all x1, blocking collectives: 21.4 us -> 20.4 us  [on_device(): lax.all_to_all(chip_sum, 'energy', 0, 0, axis_index_groups=groups, tiled=...]
  transfers between devices with their start and end apart: 6 -> 6, of which waited for: 2 -> 3; matrix products, arithmetic and copies ran while one was open for 7% -> 7% of each run, Pallas kernels for 20% -> 30%
where the time goes in v2:
time: 88.3 us; the launch traced here: 87.9 us
  Pallas kernels  29.5 us (33%)
  blocking collectives  20.4 us (23%)
  starting transfers between devices  15.5 us (18%)
  waiting for transfers between devices  14.8 us (17%)
  local copies, waits for them, and re-layouts  4.59 us (5%)
  other arithmetic  2.91 us (3%)
    pallas_call x5, Pallas kernels, products(): pl.pallas_call(kernel, out_shape=out_shape, grid=(energies // STEP,), in_...  22.5 us
    all_to_all x1, blocking collectives, on_device(): lax.all_to_all(chip_sum, 'energy', 0, 0, axis_index_groups=groups, tiled=...  20.4 us
    ppermute x2, waiting for transfers between devices, on_device(): far.append(lax.ppermute(leaving, 'energy', up))  12.9 us
    ppermute x2, starting transfers between devices, on_device(): far = [lax.ppermute(pieces[k], 'energy', up) for k in range(2)]  8.01 us
    pallas_call x1, Pallas kernels, project(): pl.pallas_call(functools.partial(project_kernel, steps), out_shape=jax.Sh...  7 us
    ppermute x2, starting transfers between devices, on_device(): far.append(lax.ppermute(leaving, 'energy', up))  6.86 us
    slice x1, local copies, waits for them, and re-layouts, on_device(): pieces = [greater[k * piece:(k + 1) * piece] for k in range(PARTS)]  2.92 us
    ppermute x1, waiting for transfers between devices, on_device(): got = lax.ppermute(send, 'energy', across)  1.9 us
  transfers between devices with their start and end apart: 6, of which 3 were waited for; matrix products, arithmetic and copies ran while one was open for 7% of the time, Pallas kernels for 30%

profile of v2, /device:TPU:0, one launch (start us, length us, event | category | flops | bytes accessed | tf_op | source)
XLA Modules:
  0.0 87.9 jit_solution(17714540460171458754)
XLA Ops:
  0.0 0.0 copy-start.1
  0.0 0.0 copy-start.4
  0.0 0.0 copy-start.5
  0.0 0.0 copy-start.6
  0.0 0.5 collective-permute-start
  0.5 2.9 %fusion.11 = (bf16[8,2,128,128]{3,2,1,0:T(8,128)(2,1)}, bf16[8,2,128,128]{3,2,1,0:T(8,128)(2,1)}, bf16[8,2,128,128]{3,2,1,0:T(8,128)(2,1)}, bf16[8,2,128,128]{3,2,1,0:T(8,128)(2,1)}) fusion(bf16[32,2,128,128]{3,2,1,0:T(8,128)(2,1)} %green_ref.1), kind=kLoop, calls=%fused_computation.29 | loop fusion | bytes 4194304 | tf_op jit(solution)/shard_map/slice | solution.py:204
  3.5 4.6 %collective-permute-start.2 = (bf16[8,2,128,128]{3,2,1,0:T(8,128)(2,1)}, bf16[8,2,128,128]{3,2,1,0:T(8,128)(2,1)S(1)}, u32[]{:S(2)}, u32[]{:S(2)}) collective-permute-start(bf16[8,2,128,128]{3,2,1,0:T(8,128)(2,1)} %get-tuple-element.17), channel_id=1, source_target_pairs={{0,2},{1,3},{2,4},{3,5},{4,6},{5,7},{6,8},{7,9},{8,10},{9,11},{10,... | collective-permute-start | bytes 1572872 | tf_op jit(solution)/shard_map/ppermute | solution.py:205
  8.1 3.4 %collective-permute-start.1 = (bf16[8,2,128,128]{3,2,1,0:T(8,128)(2,1)}, bf16[8,2,128,128]{3,2,1,0:T(8,128)(2,1)S(1)}, u32[]{:S(2)}, u32[]{:S(2)}) collective-permute-start(bf16[8,2,128,128]{3,2,1,0:T(8,128)(2,1)} %get-tuple-element.19), channel_id=1, source_target_pairs={{0,2},{1,3},{2,4},{3,5},{4,6},{5,7},{6,8},{7,9},{8,10},{9,11},{10,... | collective-permute-start | bytes 1572872 | tf_op jit(solution)/shard_map/ppermute | solution.py:205
  11.5 0.0 copy-done.4
  11.6 0.1 copy.17
  11.7 0.1 copy.16
  11.8 0.0 copy-done.5
  11.8 0.6 fusion.15
  12.5 1.3 %compare_and_fusion = (pred[32]{0:T(512)(128)(4,1)S(1)}, pred[32]{0:T(512)(128)(4,1)S(1)}) fusion(s32[]{:T(128)} %bitcast.1, s32[]{:T(128)} %bitcast, s32[]{:T(128)S(6)} %mul.13), kind=kLoop, calls=%fused_computation.24 | loop fusion | flops 256 | bytes 76 | tf_op jit(solution)/shard_map/and | solution.py:182
  13.8 0.0 copy-done.6
  13.8 1.3 %fusion.3 = (s32[32,16]{1,0:T(8,128)S(1)}, s32[32,16]{1,0:T(8,128)S(1)}) fusion(s32[32]{0:T(128)S(1)} %get-tuple-element.35, s32[]{:T(128)S(6)} %select_n.23, s32[]{:T(128)} %bitcast.1, s32[]{:T(128)} %bitcast, s32[16]{0:T(128)S(1)} %copy-done.6, pred[32]{0:T(512)(128)(4,1)S(1)} %get-tuple-element.33, s32[32]{0:T(128)S(1)} %get-tuple-element.36, ...), kind=kLoop, calls=%fused_computation.16 | loop fusion | flops 10240 | bytes 4492 | tf_op jit(solution)/shard_map/jit(_where)/select_n | solution.py:188
  15.2 0.0 copy-start
  15.2 0.0 collective-permute-done.other_ref
  15.2 0.0 copy-done.1
  15.2 7.0 %shard_map.55.proj_ref = bf16[72,128,256]{2,1,0:T(8,128)(2,1)S(1)} custom-call(bf16[128,256]{1,0:T(8,128)(2,1)S(1)} %pad_maximum_fusion.left_ref, bf16[256,256]{1,0:T(8,128)(2,1)S(1)} %maximum_maximum_fusion.right_ref, bf16[32,2,128,128]{3,2,1,0:T(8,128)(2,1)S(1)} %copy-done.1, bf16[32,2,128,128]{3,2,1,0:T(8,128)(2,1)} %collective-permute-done.other_ref), custom_call_target="tpu_custom_call" | custom-call | tf_op jit(solution)/shard_map/pallas_call | solution.py:62
  22.2 0.0 copy-done
  22.2 10.5 %shard_map.56.before_ref = f32[16,128,256]{2,1,0:T(8,128)S(1)} custom-call(s32[32,16]{1,0:T(8,128)S(1)} %get-tuple-element.29.place_ref, bf16[72,128,256]{2,1,0:T(8,128)(2,1)S(1)} %shard_map.55.proj_ref, bf16[32,2,128,128]{3,2,1,0:T(8,128)(2,1)S(1)} %copy-done), custom_call_target="tpu_custom_call" | custom-call | tf_op jit(solution)/shard_map/pallas_call | solution.py:164
  32.7 0.0 collective-permute-done.2.green_ref
  32.7 0.0 copy-start.3
  32.8 3.0 %shard_map.57.before_ref = f32[16,128,256]{2,1,0:T(8,128)S(1)} custom-call(s32[8,16]{1,0:T(8,128)S(1)} %get-tuple-element.26.place_ref, bf16[72,128,256]{2,1,0:T(8,128)(2,1)S(1)} %shard_map.55.proj_ref, bf16[8,2,128,128]{3,2,1,0:T(8,128)(2,1)S(1)} %collective-permute-done.2.green_ref, f32[16,128,256]{2,1,0:T(8,128)S(1)} %shard_map.56.before_ref), custom_call_target="tpu_custom_call" | custom-call | tf_op jit(solution)/shard_map/pallas_call | solution.py:164
  35.7 0.0 copy-done.3
  35.7 3.4 %collective-permute-start.4 = (bf16[8,2,128,128]{3,2,1,0:T(8,128)(2,1)S(1)}, bf16[8,2,128,128]{3,2,1,0:T(8,128)(2,1)S(1)}, u32[]{:S(2)}, u32[]{:S(2)}) collective-permute-start(bf16[8,2,128,128]{3,2,1,0:T(8,128)(2,1)S(1)} %copy-done.3), channel_id=1, source_target_pairs={{0,2},{1,3},{2,4},{3,5},{4,6},{5,7},{6,8},{7,9},{8,10},{9,11},{10,... | collective-permute-start | bytes 1572872 | tf_op jit(solution)/shard_map/ppermute | solution.py:224
  39.2 0.0 collective-permute-done.1.green_ref
  39.2 0.0 copy-start.2
  39.2 3.0 %shard_map.58.before_ref = f32[16,128,256]{2,1,0:T(8,128)S(1)} custom-call(s32[8,16]{1,0:T(8,128)S(1)} %get-tuple-element.27.place_ref, bf16[72,128,256]{2,1,0:T(8,128)(2,1)S(1)} %shard_map.55.proj_ref, bf16[8,2,128,128]{3,2,1,0:T(8,128)(2,1)S(1)} %collective-permute-done.1.green_ref, f32[16,128,256]{2,1,0:T(8,128)S(1)} %shard_map.57.before_ref), custom_call_target="tpu_custom_call" | custom-call | tf_op jit(solution)/shard_map/pallas_call | solution.py:164
  42.2 0.0 copy-done.2
  42.2 3.4 %collective-permute-start.3 = (bf16[8,2,128,128]{3,2,1,0:T(8,128)(2,1)S(1)}, bf16[8,2,128,128]{3,2,1,0:T(8,128)(2,1)S(1)}, u32[]{:S(2)}, u32[]{:S(2)}) collective-permute-start(bf16[8,2,128,128]{3,2,1,0:T(8,128)(2,1)S(1)} %copy-done.2), channel_id=1, source_target_pairs={{0,2},{1,3},{2,4},{3,5},{4,6},{5,7},{6,8},{7,9},{8,10},{9,11},{10,... | collective-permute-start | bytes 1572872 | tf_op jit(solution)/shard_map/ppermute | solution.py:224
  45.6 5.8 %collective-permute-done.4.green_ref = bf16[8,2,128,128]{3,2,1,0:T(8,128)(2,1)S(1)} collective-permute-done((bf16[8,2,128,128]{3,2,1,0:T(8,128)(2,1)S(1)}, bf16[8,2,128,128]{3,2,1,0:T(8,128)(2,1)S(1)}, u32[]{:S(2)}, u32[]{:S(2)}) %collective-permute-start.4) | collective-permute-done | bytes 524320 | tf_op jit(solution)/shard_map/ppermute | solution.py:224
  51.5 3.0 %shard_map.59.before_ref = f32[16,128,256]{2,1,0:T(8,128)S(1)} custom-call(s32[8,16]{1,0:T(8,128)S(1)} %get-tuple-element.25.place_ref, bf16[72,128,256]{2,1,0:T(8,128)(2,1)S(1)} %shard_map.55.proj_ref, bf16[8,2,128,128]{3,2,1,0:T(8,128)(2,1)S(1)} %collective-permute-done.4.green_ref, f32[16,128,256]{2,1,0:T(8,128)S(1)} %shard_map.58.before_ref), custom_call_target="tpu_custom_call" | custom-call | tf_op jit(solution)/shard_map/pallas_call | solution.py:164
  54.4 7.1 %collective-permute-done.3.green_ref = bf16[8,2,128,128]{3,2,1,0:T(8,128)(2,1)S(1)} collective-permute-done((bf16[8,2,128,128]{3,2,1,0:T(8,128)(2,1)S(1)}, bf16[8,2,128,128]{3,2,1,0:T(8,128)(2,1)S(1)}, u32[]{:S(2)}, u32[]{:S(2)}) %collective-permute-start.3) | collective-permute-done | bytes 524320 | tf_op jit(solution)/shard_map/ppermute | solution.py:224
  61.5 3.1 %shard_map.60 = (f32[16,64,256]{2,1,0:T(8,128)S(1)}, bf16[16,64,256]{2,1,0:T(8,128)(2,1)S(1)}) custom-call(s32[8,16]{1,0:T(8,128)S(1)} %get-tuple-element.28.place_ref, s32[1]{0:T(128)} %bitcast.2.core_ref, bf16[72,128,256]{2,1,0:T(8,128)(2,1)S(1)} %shard_map.55.proj_ref, bf16[8,2,128,128]{3,2,1,0:T(8,128)(2,1)S(1)} %collective-permute-done.3.green_ref, ...), custom_call_target="tpu_custom_call" | custom-call | tf_op jit(solution)/shard_map/pallas_call | solution.py:164
  64.6 0.1 collective-permute-start.5
  64.7 1.9 %collective-permute-done.5 = bf16[16,64,256]{2,1,0:T(8,128)(2,1)S(1)} collective-permute-done((bf16[16,64,256]{2,1,0:T(8,128)(2,1)S(1)}, bf16[16,64,256]{2,1,0:T(8,128)(2,1)S(1)}, u32[]{:S(2)}, u32[]{:S(2)}) %collective-permute-start.5) | collective-permute-done | bytes 524320 | tf_op jit(solution)/shard_map/ppermute | solution.py:228
  66.6 0.2 copy_bitcast_fusion
  66.7 20.4 %all_to_all.5 = bf16[8,16,8,256]{3,2,1,0:T(8,128)(2,1)S(1)} all-to-all(bf16[8,16,8,256]{3,2,1,0:T(8,128)(2,1)S(1)} %copy_bitcast_fusion), channel_id=1, replica_groups={{0,2,4,6,8,10,12,14},{1,3,5,7,9,11,13,15},{16,18,20,22,24,26,28,30},{17..., dimensions={0} | all-to-all | bytes 1048576 | tf_op jit(solution)/shard_map/all_to_all | solution.py:233
  87.1 0.1 convert_reduce_fusion
  87.2 0.7 copy.14
  (9 shorter events, 0.1 us)
Async XLA Ops:
  0.0 15.2 %copy-start.1 = (bf16[32,2,128,128]{3,2,1,0:T(8,128)(2,1)S(1)}, bf16[32,2,128,128]{3,2,1,0:T(8,128)(2,1)}, u32[]{:S(2)}) copy-start(bf16[32,2,128,128]{3,2,1,0:T(8,128)(2,1)} %own_ref.1) | copy-start | bytes 6291460
  0.0 11.5 %copy-start.4 = (bf16[2,128,128]{2,1,0:T(8,128)(2,1)S(1)}, bf16[2,128,128]{2,1,0:T(8,128)(2,1)}, u32[]{:S(2)}) copy-start(bf16[2,128,128]{2,1,0:T(8,128)(2,1)} %param.7) | copy-start | bytes 196612
  0.0 11.8 %copy-start.5 = (s32[2]{0:T(128)S(1)}, s32[2]{0:T(128)}, u32[]{:S(2)}) copy-start(s32[2]{0:T(128)} %param.9) | copy-start | bytes 28
  0.0 13.8 %copy-start.6 = (s32[16]{0:T(128)S(1)}, s32[16]{0:T(128)}, u32[]{:S(2)}) copy-start(s32[16]{0:T(128)} %param.8) | copy-start | bytes 196
  0.0 15.2 %collective-permute-start = (bf16[32,2,128,128]{3,2,1,0:T(8,128)(2,1)}, bf16[32,2,128,128]{3,2,1,0:T(8,128)(2,1)}, u32[]{:S(2)}, u32[]{:S(2)}) collective-permute-start(bf16[32,2,128,128]{3,2,1,0:T(8,128)(2,1)} %own_ref.1), channel_id=1, source_target_pairs={{0,1},{1,0},{2,3},{3,2},{4,5},{5,4},{6,7},{7,6},{8,9},{9,8},{10,11... | collective-permute-start | bytes 6291464 | tf_op jit(solution)/shard_map/ppermute | solution.py:214
  3.5 29.3 %collective-permute-start.2 = (bf16[8,2,128,128]{3,2,1,0:T(8,128)(2,1)}, bf16[8,2,128,128]{3,2,1,0:T(8,128)(2,1)S(1)}, u32[]{:S(2)}, u32[]{:S(2)}) collective-permute-start(bf16[8,2,128,128]{3,2,1,0:T(8,128)(2,1)} %get-tuple-element.17), channel_id=1, source_target_pairs={{0,2},{1,3},{2,4},{3,5},{4,6},{5,7},{6,8},{7,9},{8,10},{9,11},{10,... | collective-permute-start | bytes 1572872 | tf_op jit(solution)/shard_map/ppermute | solution.py:205
  8.1 31.1 %collective-permute-start.1 = (bf16[8,2,128,128]{3,2,1,0:T(8,128)(2,1)}, bf16[8,2,128,128]{3,2,1,0:T(8,128)(2,1)S(1)}, u32[]{:S(2)}, u32[]{:S(2)}) collective-permute-start(bf16[8,2,128,128]{3,2,1,0:T(8,128)(2,1)} %get-tuple-element.19), channel_id=1, source_target_pairs={{0,2},{1,3},{2,4},{3,5},{4,6},{5,7},{6,8},{7,9},{8,10},{9,11},{10,... | collective-permute-start | bytes 1572872 | tf_op jit(solution)/shard_map/ppermute | solution.py:205
  15.2 7.0 %copy-start = (bf16[32,2,128,128]{3,2,1,0:T(8,128)(2,1)S(1)}, bf16[32,2,128,128]{3,2,1,0:T(8,128)(2,1)}, u32[]{:S(2)}) copy-start(bf16[32,2,128,128]{3,2,1,0:T(8,128)(2,1)} %green_ref.1) | copy-start | bytes 6291460
  32.7 3.0 %copy-start.3 = (bf16[8,2,128,128]{3,2,1,0:T(8,128)(2,1)S(1)}, bf16[8,2,128,128]{3,2,1,0:T(8,128)(2,1)}, u32[]{:S(2)}) copy-start(bf16[8,2,128,128]{3,2,1,0:T(8,128)(2,1)} %get-tuple-element.13) | copy-start | bytes 1572868
  35.7 15.7 %collective-permute-start.4 = (bf16[8,2,128,128]{3,2,1,0:T(8,128)(2,1)S(1)}, bf16[8,2,128,128]{3,2,1,0:T(8,128)(2,1)S(1)}, u32[]{:S(2)}, u32[]{:S(2)}) collective-permute-start(bf16[8,2,128,128]{3,2,1,0:T(8,128)(2,1)S(1)} %copy-done.3), channel_id=1, source_target_pairs={{0,2},{1,3},{2,4},{3,5},{4,6},{5,7},{6,8},{7,9},{8,10},{9,11},{10,... | collective-permute-start | bytes 1572872 | tf_op jit(solution)/shard_map/ppermute | solution.py:224
  39.2 3.0 %copy-start.2 = (bf16[8,2,128,128]{3,2,1,0:T(8,128)(2,1)S(1)}, bf16[8,2,128,128]{3,2,1,0:T(8,128)(2,1)}, u32[]{:S(2)}) copy-start(bf16[8,2,128,128]{3,2,1,0:T(8,128)(2,1)} %get-tuple-element.12) | copy-start | bytes 1572868
  42.2 19.3 %collective-permute-start.3 = (bf16[8,2,128,128]{3,2,1,0:T(8,128)(2,1)S(1)}, bf16[8,2,128,128]{3,2,1,0:T(8,128)(2,1)S(1)}, u32[]{:S(2)}, u32[]{:S(2)}) collective-permute-start(bf16[8,2,128,128]{3,2,1,0:T(8,128)(2,1)S(1)} %copy-done.2), channel_id=1, source_target_pairs={{0,2},{1,3},{2,4},{3,5},{4,6},{5,7},{6,8},{7,9},{8,10},{9,11},{10,... | collective-permute-start | bytes 1572872 | tf_op jit(solution)/shard_map/ppermute | solution.py:224
  64.6 2.0 %collective-permute-start.5 = (bf16[16,64,256]{2,1,0:T(8,128)(2,1)S(1)}, bf16[16,64,256]{2,1,0:T(8,128)(2,1)S(1)}, u32[]{:S(2)}, u32[]{:S(2)}) collective-permute-start(bf16[16,64,256]{2,1,0:T(8,128)(2,1)S(1)} %get-tuple-element.16), channel_id=1, source_target_pairs={{0,1},{1,0},{2,3},{3,2},{4,5},{5,4},{6,7},{7,6},{8,9},{9,8},{10,11... | collective-permute-start | bytes 1572872 | tf_op jit(solution)/shard_map/ppermute | solution.py:228

commit v3 on v2

--- a/solution.py
+++ b/solution.py
@@ -201,8 +201,11 @@
     up = [(i, i + 2) for i in range(devices - 2)]
     across = [(i, i ^ 1) for i in range(devices)]
     piece = e_dev // PARTS
-    pieces = [greater[k * piece : (k + 1) * piece] for k in range(PARTS)]
-    far = [lax.ppermute(pieces[k], "energy", up) for k in range(2)]
+    pieces = []
+    for k in range(PARTS):
+        source = lax.optimization_barrier(greater) if k else greater
+        pieces.append(source[k * piece : (k + 1) * piece])
+    far = [lax.ppermute(block, "energy", up) for block in pieces[:-1]]
 
     rows = dipole.reshape(2, chips, 2, share, orbitals)
     rows = jnp.transpose(rows, (0, 2, 1, 3, 4)).reshape(2, orbitals, orbitals)
@@ -219,8 +222,8 @@
         place = far_place[k * piece : (k + 1) * piece]
         if k < PARTS - 1:
             result = products(place, proj, far[k], before=result)
-        if k + 2 < PARTS:
-            leaving, result = lax.optimization_barrier((pieces[k + 2], result))
+        if k == 0:
+            leaving, result = lax.optimization_barrier((pieces[-1], result))
             far.append(lax.ppermute(leaving, "energy", up))
     keep, send = products(
         place, proj, far[-1], before=result, core=jnp.reshape(core, (1,)).astype(jnp.int32)

time: 88.3 us -> 82.3 us (0.932)
  waiting for transfers between devices: 14.8 us -> 6.87 us
  local copies, waits for them, and re-layouts: 4.59 us -> 6.11 us
    ppermute x2 -> x1, waiting for transfers between devices: 12.9 us -> 4.97 us  [on_device(): far.append(lax.ppermute(leaving, 'energy', up))]
    ppermute x2 -> x3, starting transfers between devices: 8.01 us -> 11.5 us  [on_device(): far = [lax.ppermute(block, 'energy', up) for block in pieces[:-1]]]
    ppermute x2 -> x1, starting transfers between devices: 6.86 us -> 3.42 us  [on_device(): far.append(lax.ppermute(leaving, 'energy', up))]
    slice x1 -> x2, local copies, waits for them, and re-layouts: 2.92 us -> 4.44 us  [on_device(): pieces.append(source[k * piece:(k + 1) * piece])]
  transfers between devices with their start and end apart: 6 -> 6, of which waited for: 3 -> 2; matrix products, arithmetic and copies ran while one was open for 7% -> 10% of each run, Pallas kernels for 30% -> 33%
where the time goes in v3:
time: 82.3 us; the launch traced here: 81.9 us
  Pallas kernels  30 us (36%)
  blocking collectives  20.3 us (25%)
  starting transfers between devices  15.4 us (19%)
  waiting for transfers between devices  6.87 us (8%)
  local copies, waits for them, and re-layouts  6.11 us (7%)
  other arithmetic  2.88 us (3%)
    pallas_call x5, Pallas kernels, products(): pl.pallas_call(kernel, out_shape=out_shape, grid=(energies // STEP,), in_...  23 us
    all_to_all x1, blocking collectives, on_device(): lax.all_to_all(chip_sum, 'energy', 0, 0, axis_index_groups=groups, tiled=...  20.3 us
    ppermute x3, starting transfers between devices, on_device(): far = [lax.ppermute(block, 'energy', up) for block in pieces[:-1]]  11.5 us
    pallas_call x1, Pallas kernels, project(): pl.pallas_call(functools.partial(project_kernel, steps), out_shape=jax.Sh...  7.01 us
    ppermute x1, waiting for transfers between devices, on_device(): far.append(lax.ppermute(leaving, 'energy', up))  4.97 us
    slice x2, local copies, waits for them, and re-layouts, on_device(): pieces.append(source[k * piece:(k + 1) * piece])  4.44 us
    ppermute x1, starting transfers between devices, on_device(): far.append(lax.ppermute(leaving, 'energy', up))  3.42 us
    ppermute x1, waiting for transfers between devices, on_device(): got = lax.ppermute(send, 'energy', across)  1.9 us
  transfers between devices with their start and end apart: 6, of which 2 were waited for; matrix products, arithmetic and copies ran while one was open for 10% of the time, Pallas kernels for 33%

profile of v3, /device:TPU:0, one launch (start us, length us, event | category | flops | bytes accessed | tf_op | source)
XLA Modules:
  0.0 81.9 jit_solution(6703984516536382305)
XLA Ops:
  0.0 0.0 copy-start.3
  0.0 0.0 copy-start.4
  0.0 0.5 collective-permute-start
  0.5 1.9 %slice.59 = bf16[8,2,128,128]{3,2,1,0:T(8,128)(2,1)} slice(bf16[32,2,128,128]{3,2,1,0:T(8,128)(2,1)} %green_ref.1), slice={[0:8], [0:2], [0:128], [0:128]} | slice | bytes 1048576 | tf_op jit(solution)/shard_map/slice | solution.py:207
  2.3 0.0 copy-start.5
  2.3 0.0 copy-start.1
  2.4 5.4 %collective-permute-start.1 = (bf16[8,2,128,128]{3,2,1,0:T(8,128)(2,1)}, bf16[8,2,128,128]{3,2,1,0:T(8,128)(2,1)}, u32[]{:S(2)}, u32[]{:S(2)}) collective-permute-start(bf16[8,2,128,128]{3,2,1,0:T(8,128)(2,1)} %slice.59), channel_id=1, source_target_pairs={{0,2},{1,3},{2,4},{3,5},{4,6},{5,7},{6,8},{7,9},{8,10},{9,11},{10,... | collective-permute-start | bytes 1572872 | tf_op jit(solution)/shard_map/ppermute | solution.py:208
  7.7 2.5 %fusion.11 = (bf16[8,2,128,128]{3,2,1,0:T(8,128)(2,1)}, bf16[8,2,128,128]{3,2,1,0:T(8,128)(2,1)}, bf16[8,2,128,128]{3,2,1,0:T(8,128)(2,1)}) fusion(bf16[32,2,128,128]{3,2,1,0:T(8,128)(2,1)} %green_ref.1), kind=kLoop, calls=%fused_computation.29 | loop fusion | bytes 3145728 | tf_op jit(solution)/shard_map/slice | solution.py:207
  10.3 2.6 %collective-permute-start.4 = (bf16[8,2,128,128]{3,2,1,0:T(8,128)(2,1)}, bf16[8,2,128,128]{3,2,1,0:T(8,128)(2,1)S(1)}, u32[]{:S(2)}, u32[]{:S(2)}) collective-permute-start(bf16[8,2,128,128]{3,2,1,0:T(8,128)(2,1)} %get-tuple-element.13), channel_id=1, source_target_pairs={{0,2},{1,3},{2,4},{3,5},{4,6},{5,7},{6,8},{7,9},{8,10},{9,11},{10,... | collective-permute-start | bytes 1572872 | tf_op jit(solution)/shard_map/ppermute | solution.py:208
  13.0 3.4 %collective-permute-start.3 = (bf16[8,2,128,128]{3,2,1,0:T(8,128)(2,1)}, bf16[8,2,128,128]{3,2,1,0:T(8,128)(2,1)S(1)}, u32[]{:S(2)}, u32[]{:S(2)}) collective-permute-start(bf16[8,2,128,128]{3,2,1,0:T(8,128)(2,1)} %get-tuple-element.14), channel_id=1, source_target_pairs={{0,2},{1,3},{2,4},{3,5},{4,6},{5,7},{6,8},{7,9},{8,10},{9,11},{10,... | collective-permute-start | bytes 1572872 | tf_op jit(solution)/shard_map/ppermute | solution.py:208
  16.4 0.0 copy-done.3
  16.4 0.1 copy.17
  16.5 0.1 copy.16
  16.7 0.0 copy-done.4
  16.7 0.7 fusion.15
  17.4 1.3 %compare_and_fusion = (pred[32]{0:T(512)(128)(4,1)S(1)}, pred[32]{0:T(512)(128)(4,1)S(1)}) fusion(s32[]{:T(128)} %bitcast.1, s32[]{:T(128)} %bitcast, s32[]{:T(128)S(6)} %mul.13), kind=kLoop, calls=%fused_computation.24 | loop fusion | flops 256 | bytes 76 | tf_op jit(solution)/shard_map/and | solution.py:182
  18.7 0.0 copy-done.5
  18.7 1.3 %fusion.3 = (s32[32,16]{1,0:T(8,128)S(1)}, s32[32,16]{1,0:T(8,128)S(1)}) fusion(s32[32]{0:T(128)S(1)} %get-tuple-element.30, s32[]{:T(128)S(6)} %select_n.23, s32[]{:T(128)} %bitcast.1, s32[]{:T(128)} %bitcast, s32[16]{0:T(128)S(1)} %copy-done.5, pred[32]{0:T(512)(128)(4,1)S(1)} %get-tuple-element.28, s32[32]{0:T(128)S(1)} %get-tuple-element.31, ...), kind=kLoop, calls=%fused_computation.16 | loop fusion | flops 10240 | bytes 4492 | tf_op jit(solution)/shard_map/jit(_where)/select_n | solution.py:188
  20.1 0.0 copy-start
  20.1 0.0 collective-permute-done.other_ref
  20.1 0.0 copy-done.1
  20.1 7.0 %shard_map.55.proj_ref = bf16[72,128,256]{2,1,0:T(8,128)(2,1)S(1)} custom-call(bf16[128,256]{1,0:T(8,128)(2,1)S(1)} %pad_maximum_fusion.left_ref, bf16[256,256]{1,0:T(8,128)(2,1)S(1)} %maximum_maximum_fusion.right_ref, bf16[32,2,128,128]{3,2,1,0:T(8,128)(2,1)S(1)} %copy-done.1, bf16[32,2,128,128]{3,2,1,0:T(8,128)(2,1)} %collective-permute-done.other_ref), custom_call_target="tpu_custom_call" | custom-call | tf_op jit(solution)/shard_map/pallas_call | solution.py:62
  27.1 0.0 copy-done
  27.1 10.5 %shard_map.56.before_ref = f32[16,128,256]{2,1,0:T(8,128)S(1)} custom-call(s32[32,16]{1,0:T(8,128)S(1)} %get-tuple-element.24.place_ref, bf16[72,128,256]{2,1,0:T(8,128)(2,1)S(1)} %shard_map.55.proj_ref, bf16[32,2,128,128]{3,2,1,0:T(8,128)(2,1)S(1)} %copy-done), custom_call_target="tpu_custom_call" | custom-call | tf_op jit(solution)/shard_map/pallas_call | solution.py:164
  37.6 0.0 collective-permute-done.1.green_ref
  37.6 0.0 copy-start.2
  37.6 3.5 %shard_map.57.before_ref = f32[16,128,256]{2,1,0:T(8,128)S(1)} custom-call(s32[8,16]{1,0:T(8,128)S(1)} %get-tuple-element.22.place_ref, bf16[72,128,256]{2,1,0:T(8,128)(2,1)S(1)} %shard_map.55.proj_ref, bf16[8,2,128,128]{3,2,1,0:T(8,128)(2,1)} %collective-permute-done.1.green_ref, f32[16,128,256]{2,1,0:T(8,128)S(1)} %shard_map.56.before_ref), custom_call_target="tpu_custom_call" | custom-call | tf_op jit(solution)/shard_map/pallas_call | solution.py:164
  41.1 0.0 copy-done.2
  41.1 3.4 %collective-permute-start.2 = (bf16[8,2,128,128]{3,2,1,0:T(8,128)(2,1)S(1)}, bf16[8,2,128,128]{3,2,1,0:T(8,128)(2,1)S(1)}, u32[]{:S(2)}, u32[]{:S(2)}) collective-permute-start(bf16[8,2,128,128]{3,2,1,0:T(8,128)(2,1)S(1)} %copy-done.2), channel_id=1, source_target_pairs={{0,2},{1,3},{2,4},{3,5},{4,6},{5,7},{6,8},{7,9},{8,10},{9,11},{10,... | collective-permute-start | bytes 1572872 | tf_op jit(solution)/shard_map/ppermute | solution.py:227
  44.6 0.0 collective-permute-done.4.green_ref
  44.6 3.0 %shard_map.58.before_ref = f32[16,128,256]{2,1,0:T(8,128)S(1)} custom-call(s32[8,16]{1,0:T(8,128)S(1)} %get-tuple-element.20.place_ref, bf16[72,128,256]{2,1,0:T(8,128)(2,1)S(1)} %shard_map.55.proj_ref, bf16[8,2,128,128]{3,2,1,0:T(8,128)(2,1)S(1)} %collective-permute-done.4.green_ref, f32[16,128,256]{2,1,0:T(8,128)S(1)} %shard_map.57.before_ref), custom_call_target="tpu_custom_call" | custom-call | tf_op jit(solution)/shard_map/pallas_call | solution.py:164
  47.6 0.0 collective-permute-done.3.green_ref
  47.6 3.0 %shard_map.59.before_ref = f32[16,128,256]{2,1,0:T(8,128)S(1)} custom-call(s32[8,16]{1,0:T(8,128)S(1)} %get-tuple-element.21.place_ref, bf16[72,128,256]{2,1,0:T(8,128)(2,1)S(1)} %shard_map.55.proj_ref, bf16[8,2,128,128]{3,2,1,0:T(8,128)(2,1)S(1)} %collective-permute-done.3.green_ref, f32[16,128,256]{2,1,0:T(8,128)S(1)} %shard_map.58.before_ref), custom_call_target="tpu_custom_call" | custom-call | tf_op jit(solution)/shard_map/pallas_call | solution.py:164
  50.5 5.0 %collective-permute-done.2.green_ref = bf16[8,2,128,128]{3,2,1,0:T(8,128)(2,1)S(1)} collective-permute-done((bf16[8,2,128,128]{3,2,1,0:T(8,128)(2,1)S(1)}, bf16[8,2,128,128]{3,2,1,0:T(8,128)(2,1)S(1)}, u32[]{:S(2)}, u32[]{:S(2)}) %collective-permute-start.2) | collective-permute-done | bytes 524320 | tf_op jit(solution)/shard_map/ppermute | solution.py:227
  55.5 3.1 %shard_map.60 = (f32[16,64,256]{2,1,0:T(8,128)S(1)}, bf16[16,64,256]{2,1,0:T(8,128)(2,1)S(1)}) custom-call(s32[8,16]{1,0:T(8,128)S(1)} %get-tuple-element.23.place_ref, s32[1]{0:T(128)} %bitcast.2.core_ref, bf16[72,128,256]{2,1,0:T(8,128)(2,1)S(1)} %shard_map.55.proj_ref, bf16[8,2,128,128]{3,2,1,0:T(8,128)(2,1)S(1)} %collective-permute-done.2.green_ref, ...), custom_call_target="tpu_custom_call" | custom-call | tf_op jit(solution)/shard_map/pallas_call | solution.py:164
  58.6 0.1 collective-permute-start.5
  58.7 1.9 %collective-permute-done.5 = bf16[16,64,256]{2,1,0:T(8,128)(2,1)S(1)} collective-permute-done((bf16[16,64,256]{2,1,0:T(8,128)(2,1)S(1)}, bf16[16,64,256]{2,1,0:T(8,128)(2,1)S(1)}, u32[]{:S(2)}, u32[]{:S(2)}) %collective-permute-start.5) | collective-permute-done | bytes 524320 | tf_op jit(solution)/shard_map/ppermute | solution.py:231
  60.6 0.2 copy_bitcast_fusion
  60.7 20.3 %all_to_all.5 = bf16[8,16,8,256]{3,2,1,0:T(8,128)(2,1)S(1)} all-to-all(bf16[8,16,8,256]{3,2,1,0:T(8,128)(2,1)S(1)} %copy_bitcast_fusion), channel_id=1, replica_groups={{0,2,4,6,8,10,12,14},{1,3,5,7,9,11,13,15},{16,18,20,22,24,26,28,30},{17..., dimensions={0} | all-to-all | bytes 1048576 | tf_op jit(solution)/shard_map/all_to_all | solution.py:236
  81.0 0.1 convert_reduce_fusion
  81.1 0.7 copy.14
  (9 shorter events, 0.1 us)
Async XLA Ops:
  0.0 16.4 %copy-start.3 = (bf16[2,128,128]{2,1,0:T(8,128)(2,1)S(1)}, bf16[2,128,128]{2,1,0:T(8,128)(2,1)}, u32[]{:S(2)}) copy-start(bf16[2,128,128]{2,1,0:T(8,128)(2,1)} %param.7) | copy-start | bytes 196612
  0.0 16.7 %copy-start.4 = (s32[2]{0:T(128)S(1)}, s32[2]{0:T(128)}, u32[]{:S(2)}) copy-start(s32[2]{0:T(128)} %param.9) | copy-start | bytes 28
  0.0 20.1 %collective-permute-start = (bf16[32,2,128,128]{3,2,1,0:T(8,128)(2,1)}, bf16[32,2,128,128]{3,2,1,0:T(8,128)(2,1)}, u32[]{:S(2)}, u32[]{:S(2)}) collective-permute-start(bf16[32,2,128,128]{3,2,1,0:T(8,128)(2,1)} %own_ref.1), channel_id=1, source_target_pairs={{0,1},{1,0},{2,3},{3,2},{4,5},{5,4},{6,7},{7,6},{8,9},{9,8},{10,11... | collective-permute-start | bytes 6291464 | tf_op jit(solution)/shard_map/ppermute | solution.py:217
  2.3 16.4 %copy-start.5 = (s32[16]{0:T(128)S(1)}, s32[16]{0:T(128)}, u32[]{:S(2)}) copy-start(s32[16]{0:T(128)} %param.8) | copy-start | bytes 196
  2.3 17.7 %copy-start.1 = (bf16[32,2,128,128]{3,2,1,0:T(8,128)(2,1)S(1)}, bf16[32,2,128,128]{3,2,1,0:T(8,128)(2,1)}, u32[]{:S(2)}) copy-start(bf16[32,2,128,128]{3,2,1,0:T(8,128)(2,1)} %own_ref.1) | copy-start | bytes 6291460
  2.4 35.3 %collective-permute-start.1 = (bf16[8,2,128,128]{3,2,1,0:T(8,128)(2,1)}, bf16[8,2,128,128]{3,2,1,0:T(8,128)(2,1)}, u32[]{:S(2)}, u32[]{:S(2)}) collective-permute-start(bf16[8,2,128,128]{3,2,1,0:T(8,128)(2,1)} %slice.59), channel_id=1, source_target_pairs={{0,2},{1,3},{2,4},{3,5},{4,6},{5,7},{6,8},{7,9},{8,10},{9,11},{10,... | collective-permute-start | bytes 1572872 | tf_op jit(solution)/shard_map/ppermute | solution.py:208
  10.3 34.3 %collective-permute-start.4 = (bf16[8,2,128,128]{3,2,1,0:T(8,128)(2,1)}, bf16[8,2,128,128]{3,2,1,0:T(8,128)(2,1)S(1)}, u32[]{:S(2)}, u32[]{:S(2)}) collective-permute-start(bf16[8,2,128,128]{3,2,1,0:T(8,128)(2,1)} %get-tuple-element.13), channel_id=1, source_target_pairs={{0,2},{1,3},{2,4},{3,5},{4,6},{5,7},{6,8},{7,9},{8,10},{9,11},{10,... | collective-permute-start | bytes 1572872 | tf_op jit(solution)/shard_map/ppermute | solution.py:208
  13.0 34.6 %collective-permute-start.3 = (bf16[8,2,128,128]{3,2,1,0:T(8,128)(2,1)}, bf16[8,2,128,128]{3,2,1,0:T(8,128)(2,1)S(1)}, u32[]{:S(2)}, u32[]{:S(2)}) collective-permute-start(bf16[8,2,128,128]{3,2,1,0:T(8,128)(2,1)} %get-tuple-element.14), channel_id=1, source_target_pairs={{0,2},{1,3},{2,4},{3,5},{4,6},{5,7},{6,8},{7,9},{8,10},{9,11},{10,... | collective-permute-start | bytes 1572872 | tf_op jit(solution)/shard_map/ppermute | solution.py:208
  20.1 7.0 %copy-start = (bf16[32,2,128,128]{3,2,1,0:T(8,128)(2,1)S(1)}, bf16[32,2,128,128]{3,2,1,0:T(8,128)(2,1)}, u32[]{:S(2)}) copy-start(bf16[32,2,128,128]{3,2,1,0:T(8,128)(2,1)} %green_ref.1) | copy-start | bytes 6291460
  37.6 3.5 %copy-start.2 = (bf16[8,2,128,128]{3,2,1,0:T(8,128)(2,1)S(1)}, bf16[8,2,128,128]{3,2,1,0:T(8,128)(2,1)}, u32[]{:S(2)}) copy-start(bf16[8,2,128,128]{3,2,1,0:T(8,128)(2,1)} %get-tuple-element.9) | copy-start | bytes 1572868
  41.1 14.4 %collective-permute-start.2 = (bf16[8,2,128,128]{3,2,1,0:T(8,128)(2,1)S(1)}, bf16[8,2,128,128]{3,2,1,0:T(8,128)(2,1)S(1)}, u32[]{:S(2)}, u32[]{:S(2)}) collective-permute-start(bf16[8,2,128,128]{3,2,1,0:T(8,128)(2,1)S(1)} %copy-done.2), channel_id=1, source_target_pairs={{0,2},{1,3},{2,4},{3,5},{4,6},{5,7},{6,8},{7,9},{8,10},{9,11},{10,... | collective-permute-start | bytes 1572872 | tf_op jit(solution)/shard_map/ppermute | solution.py:227
  58.6 2.0 %collective-permute-start.5 = (bf16[16,64,256]{2,1,0:T(8,128)(2,1)S(1)}, bf16[16,64,256]{2,1,0:T(8,128)(2,1)S(1)}, u32[]{:S(2)}, u32[]{:S(2)}) collective-permute-start(bf16[16,64,256]{2,1,0:T(8,128)(2,1)S(1)} %get-tuple-element.12), channel_id=1, source_target_pairs={{0,1},{1,0},{2,3},{3,2},{4,5},{5,4},{6,7},{7,6},{8,9},{9,8},{10,11... | collective-permute-start | bytes 1572872 | tf_op jit(solution)/shard_map/ppermute | solution.py:231

commit v4 on v3

--- a/solution.py
+++ b/solution.py
@@ -205,7 +205,7 @@
     for k in range(PARTS):
         source = lax.optimization_barrier(greater) if k else greater
         pieces.append(source[k * piece : (k + 1) * piece])
-    far = [lax.ppermute(block, "energy", up) for block in pieces[:-1]]
+    far = [lax.ppermute(block, "energy", up) for block in pieces]
 
     rows = dipole.reshape(2, chips, 2, share, orbitals)
     rows = jnp.transpose(rows, (0, 2, 1, 3, 4)).reshape(2, orbitals, orbitals)
@@ -222,9 +222,6 @@
         place = far_place[k * piece : (k + 1) * piece]
         if k < PARTS - 1:
             result = products(place, proj, far[k], before=result)
-        if k == 0:
-            leaving, result = lax.optimization_barrier((pieces[-1], result))
-            far.append(lax.ppermute(leaving, "energy", up))
     keep, send = products(
         place, proj, far[-1], before=result, core=jnp.reshape(core, (1,)).astype(jnp.int32)
     )

time: 82.3 us -> 80.6 us (0.979)
  waiting for transfers between devices: 6.87 us -> 3.8 us
  blocking collectives: 20.3 us -> 21.3 us
    ppermute x4, waiting for transfers between devices: 4.97 us -> 1.9 us  [on_device(): far = [lax.ppermute(block, 'energy', up) for block in pieces]]
    all_to_all x1, blocking collectives: 20.3 us -> 21.3 us  [on_device(): lax.all_to_all(chip_sum, 'energy', 0, 0, axis_index_groups=groups, tiled=...]
  transfers between devices with their start and end apart: 6 -> 6, of which waited for: 2 -> 2; matrix products, arithmetic and copies ran while one was open for 10% -> 10% of each run, Pallas kernels for 33% -> 34%
where the time goes in v4:
time: 80.6 us; the launch traced here: 80.1 us
  Pallas kernels  30.4 us (38%)
  blocking collectives  21.3 us (26%)
  starting transfers between devices  15.4 us (19%)
  local copies, waits for them, and re-layouts  6.1 us (8%)
  waiting for transfers between devices  3.8 us (5%)
  other arithmetic  2.86 us (4%)
    pallas_call x5, Pallas kernels, products(): pl.pallas_call(kernel, out_shape=out_shape, grid=(energies // STEP,), in_...  23.4 us
    all_to_all x1, blocking collectives, on_device(): lax.all_to_all(chip_sum, 'energy', 0, 0, axis_index_groups=groups, tiled=...  21.3 us
    ppermute x4, starting transfers between devices, on_device(): far = [lax.ppermute(block, 'energy', up) for block in pieces]  14.9 us
    pallas_call x1, Pallas kernels, project(): pl.pallas_call(functools.partial(project_kernel, steps), out_shape=jax.Sh...  7 us
    slice x2, local copies, waits for them, and re-layouts, on_device(): pieces.append(source[k * piece:(k + 1) * piece])  4.46 us
    ppermute x4, waiting for transfers between devices, on_device(): far = [lax.ppermute(block, 'energy', up) for block in pieces]  1.9 us
    ppermute x1, waiting for transfers between devices, on_device(): got = lax.ppermute(send, 'energy', across)  1.9 us
  transfers between devices with their start and end apart: 6, of which 2 were waited for; matrix products, arithmetic and copies ran while one was open for 10% of the time, Pallas kernels for 34%

profile of v4, /device:TPU:0, one launch (start us, length us, event | category | flops | bytes accessed | tf_op | source)
XLA Modules:
  0.0 80.1 jit_solution(16751562558667820736)
XLA Ops:
  0.0 0.0 copy-start.2
  0.0 0.0 copy-start.3
  0.0 0.5 collective-permute-start
  0.5 1.9 %slice.63 = bf16[8,2,128,128]{3,2,1,0:T(8,128)(2,1)} slice(bf16[32,2,128,128]{3,2,1,0:T(8,128)(2,1)} %green_ref.1), slice={[0:8], [0:2], [0:128], [0:128]} | slice | bytes 1048576 | tf_op jit(solution)/shard_map/slice | solution.py:207
  2.4 0.0 copy-start.4
  2.4 0.0 copy-start.1
  2.4 5.4 %collective-permute-start.4 = (bf16[8,2,128,128]{3,2,1,0:T(8,128)(2,1)}, bf16[8,2,128,128]{3,2,1,0:T(8,128)(2,1)}, u32[]{:S(2)}, u32[]{:S(2)}) collective-permute-start(bf16[8,2,128,128]{3,2,1,0:T(8,128)(2,1)} %slice.63), channel_id=1, source_target_pairs={{0,2},{1,3},{2,4},{3,5},{4,6},{5,7},{6,8},{7,9},{8,10},{9,11},{10,... | collective-permute-start | bytes 1572872 | tf_op jit(solution)/shard_map/ppermute | solution.py:208
  7.7 2.6 %fusion.11 = (bf16[8,2,128,128]{3,2,1,0:T(8,128)(2,1)}, bf16[8,2,128,128]{3,2,1,0:T(8,128)(2,1)}, bf16[8,2,128,128]{3,2,1,0:T(8,128)(2,1)}) fusion(bf16[32,2,128,128]{3,2,1,0:T(8,128)(2,1)} %green_ref.1), kind=kLoop, calls=%fused_computation.29 | loop fusion | bytes 3145728 | tf_op jit(solution)/shard_map/slice | solution.py:207
  10.3 3.4 %collective-permute-start.3 = (bf16[8,2,128,128]{3,2,1,0:T(8,128)(2,1)}, bf16[8,2,128,128]{3,2,1,0:T(8,128)(2,1)}, u32[]{:S(2)}, u32[]{:S(2)}) collective-permute-start(bf16[8,2,128,128]{3,2,1,0:T(8,128)(2,1)} %get-tuple-element.9), channel_id=1, source_target_pairs={{0,2},{1,3},{2,4},{3,5},{4,6},{5,7},{6,8},{7,9},{8,10},{9,11},{10,... | collective-permute-start | bytes 1572872 | tf_op jit(solution)/shard_map/ppermute | solution.py:208
  13.8 2.6 %collective-permute-start.2 = (bf16[8,2,128,128]{3,2,1,0:T(8,128)(2,1)}, bf16[8,2,128,128]{3,2,1,0:T(8,128)(2,1)S(1)}, u32[]{:S(2)}, u32[]{:S(2)}) collective-permute-start(bf16[8,2,128,128]{3,2,1,0:T(8,128)(2,1)} %get-tuple-element.10), channel_id=1, source_target_pairs={{0,2},{1,3},{2,4},{3,5},{4,6},{5,7},{6,8},{7,9},{8,10},{9,11},{10,... | collective-permute-start | bytes 1572872 | tf_op jit(solution)/shard_map/ppermute | solution.py:208
  16.4 3.4 %collective-permute-start.1 = (bf16[8,2,128,128]{3,2,1,0:T(8,128)(2,1)}, bf16[8,2,128,128]{3,2,1,0:T(8,128)(2,1)S(1)}, u32[]{:S(2)}, u32[]{:S(2)}) collective-permute-start(bf16[8,2,128,128]{3,2,1,0:T(8,128)(2,1)} %get-tuple-element.11), channel_id=1, source_target_pairs={{0,2},{1,3},{2,4},{3,5},{4,6},{5,7},{6,8},{7,9},{8,10},{9,11},{10,... | collective-permute-start | bytes 1572872 | tf_op jit(solution)/shard_map/ppermute | solution.py:208
  19.9 0.0 copy-done.2
  19.9 0.1 copy.17
  20.0 0.1 copy.16
  20.2 0.0 copy-done.3
  20.2 0.6 fusion.15
  20.9 1.2 %compare_and_fusion = (pred[32]{0:T(512)(128)(4,1)S(1)}, pred[32]{0:T(512)(128)(4,1)S(1)}) fusion(s32[]{:T(128)} %bitcast.1, s32[]{:T(128)} %bitcast, s32[]{:T(128)S(6)} %mul.13), kind=kLoop, calls=%fused_computation.24 | loop fusion | flops 256 | bytes 76 | tf_op jit(solution)/shard_map/and | solution.py:182
  22.1 0.0 copy-done.4
  22.1 1.3 %fusion.3 = (s32[32,16]{1,0:T(8,128)S(1)}, s32[32,16]{1,0:T(8,128)S(1)}) fusion(s32[32]{0:T(128)S(1)} %get-tuple-element.26, s32[]{:T(128)S(6)} %select_n.23, s32[]{:T(128)} %bitcast.1, s32[]{:T(128)} %bitcast, s32[16]{0:T(128)S(1)} %copy-done.4, pred[32]{0:T(512)(128)(4,1)S(1)} %get-tuple-element.24, s32[32]{0:T(128)S(1)} %get-tuple-element.27, ...), kind=kLoop, calls=%fused_computation.16 | loop fusion | flops 10240 | bytes 4492 | tf_op jit(solution)/shard_map/jit(_where)/select_n | solution.py:188
  23.5 0.0 copy-start
  23.5 0.0 collective-permute-done.other_ref
  23.5 0.0 copy-done.1
  23.5 7.0 %shard_map.55.proj_ref = bf16[72,128,256]{2,1,0:T(8,128)(2,1)S(1)} custom-call(bf16[128,256]{1,0:T(8,128)(2,1)S(1)} %pad_maximum_fusion.left_ref, bf16[256,256]{1,0:T(8,128)(2,1)S(1)} %maximum_maximum_fusion.right_ref, bf16[32,2,128,128]{3,2,1,0:T(8,128)(2,1)S(1)} %copy-done.1, bf16[32,2,128,128]{3,2,1,0:T(8,128)(2,1)} %collective-permute-done.other_ref), custom_call_target="tpu_custom_call" | custom-call | tf_op jit(solution)/shard_map/pallas_call | solution.py:62
  30.5 0.0 copy-done
  30.5 10.5 %shard_map.56.before_ref = f32[16,128,256]{2,1,0:T(8,128)S(1)} custom-call(s32[32,16]{1,0:T(8,128)S(1)} %get-tuple-element.20.place_ref, bf16[72,128,256]{2,1,0:T(8,128)(2,1)S(1)} %shard_map.55.proj_ref, bf16[32,2,128,128]{3,2,1,0:T(8,128)(2,1)S(1)} %copy-done), custom_call_target="tpu_custom_call" | custom-call | tf_op jit(solution)/shard_map/pallas_call | solution.py:164
  41.0 0.0 collective-permute-done.4.green_ref
  41.0 3.4 %shard_map.57.before_ref = f32[16,128,256]{2,1,0:T(8,128)S(1)} custom-call(s32[8,16]{1,0:T(8,128)S(1)} %get-tuple-element.16.place_ref, bf16[72,128,256]{2,1,0:T(8,128)(2,1)S(1)} %shard_map.55.proj_ref, bf16[8,2,128,128]{3,2,1,0:T(8,128)(2,1)} %collective-permute-done.4.green_ref, f32[16,128,256]{2,1,0:T(8,128)S(1)} %shard_map.56.before_ref), custom_call_target="tpu_custom_call" | custom-call | tf_op jit(solution)/shard_map/pallas_call | solution.py:164
  44.5 0.0 collective-permute-done.3.green_ref
  44.5 3.4 %shard_map.58.before_ref = f32[16,128,256]{2,1,0:T(8,128)S(1)} custom-call(s32[8,16]{1,0:T(8,128)S(1)} %get-tuple-element.17.place_ref, bf16[72,128,256]{2,1,0:T(8,128)(2,1)S(1)} %shard_map.55.proj_ref, bf16[8,2,128,128]{3,2,1,0:T(8,128)(2,1)} %collective-permute-done.3.green_ref, f32[16,128,256]{2,1,0:T(8,128)S(1)} %shard_map.57.before_ref), custom_call_target="tpu_custom_call" | custom-call | tf_op jit(solution)/shard_map/pallas_call | solution.py:164
  47.9 0.0 collective-permute-done.2.green_ref
  47.9 3.0 %shard_map.59.before_ref = f32[16,128,256]{2,1,0:T(8,128)S(1)} custom-call(s32[8,16]{1,0:T(8,128)S(1)} %get-tuple-element.18.place_ref, bf16[72,128,256]{2,1,0:T(8,128)(2,1)S(1)} %shard_map.55.proj_ref, bf16[8,2,128,128]{3,2,1,0:T(8,128)(2,1)S(1)} %collective-permute-done.2.green_ref, f32[16,128,256]{2,1,0:T(8,128)S(1)} %shard_map.58.before_ref), custom_call_target="tpu_custom_call" | custom-call | tf_op jit(solution)/shard_map/pallas_call | solution.py:164
  50.9 1.9 %collective-permute-done.1.green_ref = bf16[8,2,128,128]{3,2,1,0:T(8,128)(2,1)S(1)} collective-permute-done((bf16[8,2,128,128]{3,2,1,0:T(8,128)(2,1)}, bf16[8,2,128,128]{3,2,1,0:T(8,128)(2,1)S(1)}, u32[]{:S(2)}, u32[]{:S(2)}) %collective-permute-start.1) | collective-permute-done | bytes 524320 | tf_op jit(solution)/shard_map/ppermute | solution.py:208
  52.8 3.1 %shard_map.60 = (f32[16,64,256]{2,1,0:T(8,128)S(1)}, bf16[16,64,256]{2,1,0:T(8,128)(2,1)S(1)}) custom-call(s32[8,16]{1,0:T(8,128)S(1)} %get-tuple-element.19.place_ref, s32[1]{0:T(128)} %bitcast.2.core_ref, bf16[72,128,256]{2,1,0:T(8,128)(2,1)S(1)} %shard_map.55.proj_ref, bf16[8,2,128,128]{3,2,1,0:T(8,128)(2,1)S(1)} %collective-permute-done.1.green_ref, ...), custom_call_target="tpu_custom_call" | custom-call | tf_op jit(solution)/shard_map/pallas_call | solution.py:164
  55.9 0.1 collective-permute-start.5
  55.9 1.9 %collective-permute-done.5 = bf16[16,64,256]{2,1,0:T(8,128)(2,1)S(1)} collective-permute-done((bf16[16,64,256]{2,1,0:T(8,128)(2,1)S(1)}, bf16[16,64,256]{2,1,0:T(8,128)(2,1)S(1)}, u32[]{:S(2)}, u32[]{:S(2)}) %collective-permute-start.5) | collective-permute-done | bytes 524320 | tf_op jit(solution)/shard_map/ppermute | solution.py:228
  57.8 0.2 copy_bitcast_fusion
  58.0 21.3 %all_to_all.5 = bf16[8,16,8,256]{3,2,1,0:T(8,128)(2,1)S(1)} all-to-all(bf16[8,16,8,256]{3,2,1,0:T(8,128)(2,1)S(1)} %copy_bitcast_fusion), channel_id=1, replica_groups={{0,2,4,6,8,10,12,14},{1,3,5,7,9,11,13,15},{16,18,20,22,24,26,28,30},{17..., dimensions={0} | all-to-all | bytes 1048576 | tf_op jit(solution)/shard_map/all_to_all | solution.py:233
  79.3 0.1 convert_reduce_fusion
  79.4 0.7 copy.14
  (9 shorter events, 0.1 us)
Async XLA Ops:
  0.0 19.9 %copy-start.2 = (bf16[2,128,128]{2,1,0:T(8,128)(2,1)S(1)}, bf16[2,128,128]{2,1,0:T(8,128)(2,1)}, u32[]{:S(2)}) copy-start(bf16[2,128,128]{2,1,0:T(8,128)(2,1)} %param.7) | copy-start | bytes 196612
  0.0 20.2 %copy-start.3 = (s32[2]{0:T(128)S(1)}, s32[2]{0:T(128)}, u32[]{:S(2)}) copy-start(s32[2]{0:T(128)} %param.9) | copy-start | bytes 28
  0.0 23.5 %collective-permute-start = (bf16[32,2,128,128]{3,2,1,0:T(8,128)(2,1)}, bf16[32,2,128,128]{3,2,1,0:T(8,128)(2,1)}, u32[]{:S(2)}, u32[]{:S(2)}) collective-permute-start(bf16[32,2,128,128]{3,2,1,0:T(8,128)(2,1)} %own_ref.1), channel_id=1, source_target_pairs={{0,1},{1,0},{2,3},{3,2},{4,5},{5,4},{6,7},{7,6},{8,9},{9,8},{10,11... | collective-permute-start | bytes 6291464 | tf_op jit(solution)/shard_map/ppermute | solution.py:217
  2.4 19.8 %copy-start.4 = (s32[16]{0:T(128)S(1)}, s32[16]{0:T(128)}, u32[]{:S(2)}) copy-start(s32[16]{0:T(128)} %param.8) | copy-start | bytes 196
  2.4 21.1 %copy-start.1 = (bf16[32,2,128,128]{3,2,1,0:T(8,128)(2,1)S(1)}, bf16[32,2,128,128]{3,2,1,0:T(8,128)(2,1)}, u32[]{:S(2)}) copy-start(bf16[32,2,128,128]{3,2,1,0:T(8,128)(2,1)} %own_ref.1) | copy-start | bytes 6291460
  2.4 38.7 %collective-permute-start.4 = (bf16[8,2,128,128]{3,2,1,0:T(8,128)(2,1)}, bf16[8,2,128,128]{3,2,1,0:T(8,128)(2,1)}, u32[]{:S(2)}, u32[]{:S(2)}) collective-permute-start(bf16[8,2,128,128]{3,2,1,0:T(8,128)(2,1)} %slice.63), channel_id=1, source_target_pairs={{0,2},{1,3},{2,4},{3,5},{4,6},{5,7},{6,8},{7,9},{8,10},{9,11},{10,... | collective-permute-start | bytes 1572872 | tf_op jit(solution)/shard_map/ppermute | solution.py:208
  10.3 34.2 %collective-permute-start.3 = (bf16[8,2,128,128]{3,2,1,0:T(8,128)(2,1)}, bf16[8,2,128,128]{3,2,1,0:T(8,128)(2,1)}, u32[]{:S(2)}, u32[]{:S(2)}) collective-permute-start(bf16[8,2,128,128]{3,2,1,0:T(8,128)(2,1)} %get-tuple-element.9), channel_id=1, source_target_pairs={{0,2},{1,3},{2,4},{3,5},{4,6},{5,7},{6,8},{7,9},{8,10},{9,11},{10,... | collective-permute-start | bytes 1572872 | tf_op jit(solution)/shard_map/ppermute | solution.py:208
  13.8 34.2 %collective-permute-start.2 = (bf16[8,2,128,128]{3,2,1,0:T(8,128)(2,1)}, bf16[8,2,128,128]{3,2,1,0:T(8,128)(2,1)S(1)}, u32[]{:S(2)}, u32[]{:S(2)}) collective-permute-start(bf16[8,2,128,128]{3,2,1,0:T(8,128)(2,1)} %get-tuple-element.10), channel_id=1, source_target_pairs={{0,2},{1,3},{2,4},{3,5},{4,6},{5,7},{6,8},{7,9},{8,10},{9,11},{10,... | collective-permute-start | bytes 1572872 | tf_op jit(solution)/shard_map/ppermute | solution.py:208
  16.4 36.4 %collective-permute-start.1 = (bf16[8,2,128,128]{3,2,1,0:T(8,128)(2,1)}, bf16[8,2,128,128]{3,2,1,0:T(8,128)(2,1)S(1)}, u32[]{:S(2)}, u32[]{:S(2)}) collective-permute-start(bf16[8,2,128,128]{3,2,1,0:T(8,128)(2,1)} %get-tuple-element.11), channel_id=1, source_target_pairs={{0,2},{1,3},{2,4},{3,5},{4,6},{5,7},{6,8},{7,9},{8,10},{9,11},{10,... | collective-permute-start | bytes 1572872 | tf_op jit(solution)/shard_map/ppermute | solution.py:208
  23.5 7.0 %copy-start = (bf16[32,2,128,128]{3,2,1,0:T(8,128)(2,1)S(1)}, bf16[32,2,128,128]{3,2,1,0:T(8,128)(2,1)}, u32[]{:S(2)}) copy-start(bf16[32,2,128,128]{3,2,1,0:T(8,128)(2,1)} %green_ref.1) | copy-start | bytes 6291460
  55.9 2.0 %collective-permute-start.5 = (bf16[16,64,256]{2,1,0:T(8,128)(2,1)S(1)}, bf16[16,64,256]{2,1,0:T(8,128)(2,1)S(1)}, u32[]{:S(2)}, u32[]{:S(2)}) collective-permute-start(bf16[16,64,256]{2,1,0:T(8,128)(2,1)S(1)} %get-tuple-element.8), channel_id=1, source_target_pairs={{0,1},{1,0},{2,3},{3,2},{4,5},{5,4},{6,7},{7,6},{8,9},{9,8},{10,11... | collective-permute-start | bytes 1572872 | tf_op jit(solution)/shard_map/ppermute | solution.py:228

commit v5 on v4

--- a/solution.py
+++ b/solution.py
@@ -9,7 +9,7 @@
 from jax.sharding import PartitionSpec as P
 
 STEP = 8
-PAIR = 2
+GROUPS = 2
 PARTS = 4
 MIB = 1 << 20
 
@@ -79,42 +79,57 @@
     )(left, right, own, other)
 
 
-def add_products(place_ref, proj_ref, green_ref, total_ref):
+def add_products(reach_ref, place_ref, proj_ref, green_ref, total_ref, start, far):
     first = pl.program_id(0) * STEP
-    photons, rows, width = total_ref.shape
-    for w in range(0, photons, PAIR):
-        total = total_ref[w : w + PAIR].reshape(PAIR * rows, width)
-        for u in range(STEP):
-            left = jnp.concatenate(
-                [proj_ref[place_ref[first + u, w + v]] for v in range(PAIR)], 0
-            )
-            right = rotated(green_ref[u, 0], green_ref[u, 1])
-            total += jnp.dot(left, right, preferred_element_type=jnp.float32)
-        total_ref[w : w + PAIR] = total.reshape(PAIR, rows, width)
-
-
-def first_kernel(place_ref, proj_ref, green_ref, total_ref):
+    photons = total_ref.shape[0]
+    for w in range(photons):
+        lowest = reach_ref[start + w] + first
+        limit = reach_ref[reach_ref.shape[0] - 1]
+        needed = lowest + STEP - 1 >= limit if far else lowest < limit
+
+        @pl.when(needed)
+        def _():
+            total = total_ref[w]
+            for u in range(STEP):
+                right = rotated(green_ref[u, 0], green_ref[u, 1])
+                left = proj_ref[place_ref[first + u, start + w]]
+                total += jnp.dot(left, right, preferred_element_type=jnp.float32)
+            total_ref[w] = total
+
+
+def near_kernel(reach_ref, place_ref, proj_ref, green_ref, total_ref):
     @pl.when(pl.program_id(0) == 0)
     def _():
         total_ref[...] = jnp.zeros_like(total_ref)
 
-    add_products(place_ref, proj_ref, green_ref, total_ref)
-
-
-def next_kernel(place_ref, proj_ref, green_ref, before_ref, total_ref):
+    add_products(reach_ref, place_ref, proj_ref, green_ref, total_ref, 0, False)
+
+
+def far_kernel(reach_ref, place_ref, proj_ref, green_ref, before_ref, total_ref):
     @pl.when(pl.program_id(0) == 0)
     def _():
         total_ref[...] = before_ref[...]
 
-    add_products(place_ref, proj_ref, green_ref, total_ref)
-
-
-def last_kernel(place_ref, core_ref, proj_ref, green_ref, before_ref, keep_ref, send_ref, total_ref):
+    add_products(reach_ref, place_ref, proj_ref, green_ref, total_ref, 0, True)
+
+
+def last_kernel(
+    start,
+    reach_ref,
+    place_ref,
+    core_ref,
+    proj_ref,
+    green_ref,
+    before_ref,
+    keep_ref,
+    send_ref,
+    total_ref,
+):
     @pl.when(pl.program_id(0) == 0)
     def _():
         total_ref[...] = before_ref[...]
 
-    add_products(place_ref, proj_ref, green_ref, total_ref)
+    add_products(reach_ref, place_ref, proj_ref, green_ref, total_ref, start, True)
 
     @pl.when(pl.program_id(0) == pl.num_programs(0) - 1)
     def _():
@@ -126,14 +141,15 @@
         send_ref[...] = total_ref[:, pl.ds(other, half), :].astype(send_ref.dtype)
 
 
-def products(place, proj, green, before=None, core=None):
+def products(reach, place, proj, green, before=None, core=None, group=0):
     slots, rows, width = proj.shape
     energies, _, orbitals, _ = green.shape
     photons = place.shape[1]
     smem = pl.BlockSpec(memory_space=pltpu.SMEM)
-    total_spec = pl.BlockSpec((photons, rows, width), lambda t: (0, 0, 0))
-    total_shape = jax.ShapeDtypeStruct((photons, rows, width), jnp.float32)
-    operands, specs = [place], [smem]
+    if core is not None:
+        photons //= GROUPS
+    block = (photons, rows, width)
+    operands, specs = [reach, place], [smem, smem]
     if core is not None:
         operands.append(core)
         specs.append(smem)
@@ -145,22 +161,22 @@
     if before is not None:
         operands.append(before)
         specs.append(
-            pl.BlockSpec((photons, rows, width), lambda t: (0, 0, 0), pipeline_mode=pl.Buffered(1))
+            pl.BlockSpec(block, lambda t: (group, 0, 0), pipeline_mode=pl.Buffered(1))
         )
     scratch = []
     if core is not None:
-        half = rows // 2
-        half_spec = pl.BlockSpec((photons, half, width), lambda t: (0, 0, 0))
-        kernel = last_kernel
-        out_specs = [half_spec, half_spec]
+        half = (photons, rows // 2, width)
+        kernel = functools.partial(last_kernel, group * photons)
+        out_specs = [pl.BlockSpec(half, lambda t: (0, 0, 0))] * 2
         out_shape = [
-            jax.ShapeDtypeStruct((photons, half, width), jnp.float32),
-            jax.ShapeDtypeStruct((photons, half, width), jnp.bfloat16),
+            jax.ShapeDtypeStruct(half, jnp.float32),
+            jax.ShapeDtypeStruct(half, jnp.bfloat16),
         ]
-        scratch = [pltpu.VMEM((photons, rows, width), jnp.float32)]
+        scratch = [pltpu.VMEM(block, jnp.float32)]
     else:
-        kernel = first_kernel if before is None else next_kernel
-        out_specs, out_shape = total_spec, total_shape
+        kernel = near_kernel if before is None else far_kernel
+        out_specs = pl.BlockSpec(block, lambda t: (0, 0, 0))
+        out_shape = jax.ShapeDtypeStruct(block, jnp.float32)
     return pl.pallas_call(
         kernel,
         out_shape=out_shape,
@@ -188,27 +204,50 @@
     return jnp.where(near, reach, zero_slot), jnp.where(far, wrapped, zero_slot)
 
 
+def pick(blocks, place):
+    return lax.dynamic_index_in_dim(blocks, place, 0, keepdims=False)
+
+
+def reduced(keep, send, planes, share):
+    devices = 4 * planes
+    index = lax.axis_index("energy")
+    plane, chip = index // 4, (index // 2) % 2
+    photons, half, width = keep.shape
+    got = lax.ppermute(send, "energy", [(i, i ^ 1) for i in range(devices)])
+    both = keep + got.astype(jnp.float32)
+    both = both.reshape(photons, 2, planes, share, width)
+    both = jnp.transpose(both, (1, 2, 0, 3, 4))
+    send = pick(both, 1 - chip).astype(jnp.bfloat16)
+    got = lax.ppermute(send, "energy", [(i, i ^ 2) for i in range(devices)])
+    both = pick(both, chip) + got.astype(jnp.float32)
+    total = pick(both, plane)
+    for step in range(1, planes):
+        send = pick(both, (plane + step) % planes).astype(jnp.bfloat16)
+        route = [(i, (i + 4 * step) % devices) for i in range(devices)]
+        total = total + lax.ppermute(send, "energy", route).astype(jnp.float32)
+    return total
+
+
 def on_device(lesser, greater, dipole, shifts, window):
     e_dev, _, orbitals, _ = lesser.shape
     photons = shifts.shape[0]
     devices = lax.axis_size("energy")
     index = lax.axis_index("energy")
     core = index % 2
-    chips = devices // 2
     share = orbitals // devices
     total = e_dev * devices
 
     up = [(i, i + 2) for i in range(devices - 2)]
     across = [(i, i ^ 1) for i in range(devices)]
     piece = e_dev // PARTS
-    pieces = []
-    for k in range(PARTS):
-        source = lax.optimization_barrier(greater) if k else greater
-        pieces.append(source[k * piece : (k + 1) * piece])
+    pieces = [greater[:piece]]
+    lesser, greater, pieces[0] = lax.optimization_barrier((lesser, greater, pieces[0]))
+    pieces += [greater[k * piece : (k + 1) * piece] for k in range(1, PARTS)]
     far = [lax.ppermute(block, "energy", up) for block in pieces]
 
-    rows = dipole.reshape(2, chips, 2, share, orbitals)
-    rows = jnp.transpose(rows, (0, 2, 1, 3, 4)).reshape(2, orbitals, orbitals)
+    planes = devices // 4
+    rows = dipole.reshape(2, planes, 2, 2, share, orbitals)
+    rows = jnp.transpose(rows, (0, 3, 2, 1, 4, 5)).reshape(2, orbitals, orbitals)
     left = jnp.concatenate([rows[0], rows[1]], 1)
     real, imag = dipole[0].T, dipole[1].T
     right = jnp.concatenate(
@@ -217,22 +256,20 @@
     proj = project(left, right, lesser, lax.ppermute(lesser, "energy", across))
 
     near_place, far_place = places(shifts, window, index * e_dev, core, e_dev)
-    result = products(near_place, proj, greater)
+    limit = jnp.where(core == 0, 2 * e_dev, e_dev)[None]
+    result = products(jnp.concatenate([shifts, limit]), near_place, proj, greater)
+    core = core[None]
     for k in range(PARTS):
         place = far_place[k * piece : (k + 1) * piece]
+        reach = jnp.concatenate([shifts, limit - k * piece])
         if k < PARTS - 1:
-            result = products(place, proj, far[k], before=result)
-    keep, send = products(
-        place, proj, far[-1], before=result, core=jnp.reshape(core, (1,)).astype(jnp.int32)
-    )
-    got = lax.ppermute(send, "energy", across)
-    chip_sum = keep + got.astype(jnp.float32)
-    chip_sum = chip_sum.reshape(photons, chips, share, 2 * orbitals)
-    chip_sum = jnp.transpose(chip_sum, (1, 0, 2, 3)).astype(jnp.bfloat16)
-    groups = [[i for i in range(devices) if i % 2 == c] for c in range(2)]
-    shares = lax.all_to_all(chip_sum, "energy", 0, 0, axis_index_groups=groups, tiled=True)
+            result = products(reach, place, proj, far[k], before=result)
+    sums = []
+    for group in range(GROUPS):
+        keep, send = products(reach, place, proj, far[-1], before=result, core=core, group=group)
+        sums.append(reduced(keep, send, planes, share))
     scale = 1.0 / math.sqrt(2.0 * orbitals * total)
-    summed = jnp.sum(shares.astype(jnp.float32), 0) * scale
+    summed = jnp.concatenate(sums, 0) * scale
     summed = jnp.transpose(summed, (1, 0, 2))
     return summed.reshape(share, photons, 2, orbitals)
 

time: 80.6 us -> 84 us (1.042)
  blocking collectives: 21.3 us -> 0 us
  starting transfers between devices: 15.4 us -> 28.4 us
  Pallas kernels: 30.4 us -> 35.6 us
  local copies, waits for them, and re-layouts: 6.1 us -> 8.66 us
  waiting for transfers between devices: 3.8 us -> 6.16 us
  other arithmetic: 2.86 us -> 4.14 us
    all_to_all x1 -> x0, blocking collectives: 21.3 us -> none  [on_device(): lax.all_to_all(chip_sum, 'energy', 0, 0, axis_index_groups=groups, tiled=...]
    ppermute x1 -> x10, starting transfers between devices: 0.07 us -> 13.1 us  [the longest x6 8.88 us: reduced(): total = total + lax.ppermute(send, 'energy', route).astype(jnp.float32)]
    pallas_call x5 -> x6, Pallas kernels: 23.4 us -> 28.6 us  [products(): pl.pallas_call(kernel, out_shape=out_shape, grid=(energies // STEP,), in_...]
    ppermute x1 -> x10, waiting for transfers between devices: 1.9 us -> 6.15 us  [the longest x2 4.17 us: reduced(): got = lax.ppermute(send, 'energy', [(i, i ^ 2) for i in range(devices)])]
    unnamed x12 -> x16, local copies, waits for them, and re-layouts: 0.25 us -> 2.59 us
    ppermute x4, waiting for transfers between devices: 1.9 us -> 0.01 us  [on_device(): far = [lax.ppermute(block, 'energy', up) for block in pieces]]
    add x0 -> x6, other arithmetic: none -> 1.15 us  [the longest x2 1.07 us: reduced(): both = keep + got.astype(jnp.float32)]
  transfers between devices with their start and end apart: 6 -> 15, of which waited for: 2 -> 4; matrix products, arithmetic and copies ran while one was open for 10% -> 9% of each run, Pallas kernels for 34% -> 40%
where the time goes in v5:
time: 84 us; the launch traced here: 83.4 us
  Pallas kernels  35.6 us (42%)
  starting transfers between devices  28.4 us (34%)
  local copies, waits for them, and re-layouts  8.66 us (10%)
  waiting for transfers between devices  6.16 us (7%)
  other arithmetic  4.14 us (5%)
    pallas_call x6, Pallas kernels, products(): pl.pallas_call(kernel, out_shape=out_shape, grid=(energies // STEP,), in_...  28.6 us
    ppermute x4, starting transfers between devices, on_device(): far = [lax.ppermute(block, 'energy', up) for block in pieces]  14.9 us
    ppermute x6, starting transfers between devices, reduced(): total = total + lax.ppermute(send, 'energy', route).astype(jnp.float32)  8.88 us
    pallas_call x1, Pallas kernels, project(): pl.pallas_call(functools.partial(project_kernel, steps), out_shape=jax.Sh...  7.01 us
    ppermute x2, waiting for transfers between devices, reduced(): got = lax.ppermute(send, 'energy', [(i, i ^ 2) for i in range(devices)])  4.17 us
    slice x1, local copies, waits for them, and re-layouts, on_device(): pieces += [greater[k * piece:(k + 1) * piece] for k in range(1, PARTS)]  2.59 us
    unnamed x16, local copies, waits for them, and re-layouts  2.59 us
    ppermute x2, starting transfers between devices, reduced(): got = lax.ppermute(send, 'energy', [(i, i ^ 2) for i in range(devices)])  2.16 us
  transfers between devices with their start and end apart: 15, of which 4 were waited for; matrix products, arithmetic and copies ran while one was open for 9% of the time, Pallas kernels for 40%

profile of v5, /device:TPU:0, one launch (start us, length us, event | category | flops | bytes accessed | tf_op | source)
XLA Modules:
  0.0 83.4 jit_solution(6184221010461602149)
XLA Ops:
  0.0 0.0 copy-start.4
  0.0 0.0 copy-start.5
  0.0 0.0 copy-start.6
  0.0 1.9 %slice.57 = bf16[8,2,128,128]{3,2,1,0:T(8,128)(2,1)} slice(bf16[32,2,128,128]{3,2,1,0:T(8,128)(2,1)} %green_ref), slice={[0:8], [0:2], [0:128], [0:128]} | slice | bytes 1048576 | tf_op jit(solution)/shard_map/slice | solution.py:243
  1.9 0.0 copy-start.3
  1.9 0.5 collective-permute-start
  2.4 5.3 %collective-permute-start.4 = (bf16[8,2,128,128]{3,2,1,0:T(8,128)(2,1)}, bf16[8,2,128,128]{3,2,1,0:T(8,128)(2,1)}, u32[]{:S(2)}, u32[]{:S(2)}) collective-permute-start(bf16[8,2,128,128]{3,2,1,0:T(8,128)(2,1)} %slice.57), channel_id=1, source_target_pairs={{0,2},{1,3},{2,4},{3,5},{4,6},{5,7},{6,8},{7,9},{8,10},{9,11},{10,... | collective-permute-start | bytes 1572872 | tf_op jit(solution)/shard_map/ppermute | solution.py:246
  7.7 2.6 %fusion.24 = (bf16[8,2,128,128]{3,2,1,0:T(8,128)(2,1)}, bf16[8,2,128,128]{3,2,1,0:T(8,128)(2,1)}, bf16[8,2,128,128]{3,2,1,0:T(8,128)(2,1)}) fusion(bf16[32,2,128,128]{3,2,1,0:T(8,128)(2,1)} %green_ref), kind=kLoop, calls=%fused_computation.59 | loop fusion | bytes 3145728 | tf_op jit(solution)/shard_map/slice | solution.py:245
  10.3 3.5 %collective-permute-start.3 = (bf16[8,2,128,128]{3,2,1,0:T(8,128)(2,1)}, bf16[8,2,128,128]{3,2,1,0:T(8,128)(2,1)}, u32[]{:S(2)}, u32[]{:S(2)}) collective-permute-start(bf16[8,2,128,128]{3,2,1,0:T(8,128)(2,1)} %get-tuple-element.19), channel_id=1, source_target_pairs={{0,2},{1,3},{2,4},{3,5},{4,6},{5,7},{6,8},{7,9},{8,10},{9,11},{10,... | collective-permute-start | bytes 1572872 | tf_op jit(solution)/shard_map/ppermute | solution.py:246
  13.8 2.6 %collective-permute-start.2 = (bf16[8,2,128,128]{3,2,1,0:T(8,128)(2,1)}, bf16[8,2,128,128]{3,2,1,0:T(8,128)(2,1)S(1)}, u32[]{:S(2)}, u32[]{:S(2)}) collective-permute-start(bf16[8,2,128,128]{3,2,1,0:T(8,128)(2,1)} %get-tuple-element.20), channel_id=1, source_target_pairs={{0,2},{1,3},{2,4},{3,5},{4,6},{5,7},{6,8},{7,9},{8,10},{9,11},{10,... | collective-permute-start | bytes 1572872 | tf_op jit(solution)/shard_map/ppermute | solution.py:246
  16.4 3.4 %collective-permute-start.1 = (bf16[8,2,128,128]{3,2,1,0:T(8,128)(2,1)}, bf16[8,2,128,128]{3,2,1,0:T(8,128)(2,1)S(1)}, u32[]{:S(2)}, u32[]{:S(2)}) collective-permute-start(bf16[8,2,128,128]{3,2,1,0:T(8,128)(2,1)} %get-tuple-element.21), channel_id=1, source_target_pairs={{0,2},{1,3},{2,4},{3,5},{4,6},{5,7},{6,8},{7,9},{8,10},{9,11},{10,... | collective-permute-start | bytes 1572872 | tf_op jit(solution)/shard_map/ppermute | solution.py:246
  19.9 0.0 copy-done.4
  19.9 0.1 copy.17
  20.0 0.1 copy.16
  20.2 0.0 copy-done.5
  20.2 0.1 pad_add_fusion.3
  20.3 0.0 copy-done.6
  20.3 0.7 fusion.28
  21.0 1.4 %compare_and_fusion = (pred[32]{0:T(512)(128)(4,1)S(1)}, pred[32]{0:T(512)(128)(4,1)S(1)}) fusion(s32[]{:T(128)} %bitcast.2, s32[]{:T(128)} %bitcast.1, s32[]{:T(128)S(6)} %mul.9), kind=kLoop, calls=%fused_computation.50 | loop fusion | flops 256 | bytes 76 | tf_op jit(solution)/shard_map/and | solution.py:198
  22.4 1.5 %fusion.16 = (s32[32,16]{1,0:T(8,128)S(1)}, s32[32,16]{1,0:T(8,128)S(1)}) fusion(s32[32]{0:T(128)S(1)} %get-tuple-element.46, s32[]{:T(128)} %select_n.83, s32[]{:T(128)} %bitcast.2, s32[]{:T(128)} %bitcast.1, s32[16]{0:T(128)S(1)} %copy-done.5, pred[32]{0:T(512)(128)(4,1)S(1)} %get-tuple-element.44, s32[32]{0:T(128)S(1)} %get-tuple-element.47, ...), kind=kLoop, calls=%fused_computation.40 | loop fusion | flops 10240 | bytes 4492 | tf_op jit(solution)/shard_map/jit(_where)/select_n | solution.py:204
  23.9 0.0 copy-start.2
  23.9 0.0 collective-permute-done.other_ref
  23.9 0.0 copy-done.3
  23.9 7.0 %shard_map.55.proj_ref = bf16[72,128,256]{2,1,0:T(8,128)(2,1)S(1)} custom-call(bf16[128,256]{1,0:T(8,128)(2,1)S(1)} %pad_maximum_fusion.left_ref, bf16[256,256]{1,0:T(8,128)(2,1)S(1)} %maximum_maximum_fusion.right_ref, bf16[32,2,128,128]{3,2,1,0:T(8,128)(2,1)S(1)} %copy-done.3, bf16[32,2,128,128]{3,2,1,0:T(8,128)(2,1)} %collective-permute-done.other_ref), custom_call_target="tpu_custom_call" | custom-call | tf_op jit(solution)/shard_map/pallas_call | solution.py:62
  30.9 0.0 copy-start
  30.9 0.0 copy-done.2
  31.0 15.9 %shard_map.56.before_ref = f32[16,128,256]{2,1,0:T(8,128)S(1)} custom-call(s32[17]{0:T(128)S(1)} %get-tuple-element.38.reach_ref, s32[32,16]{1,0:T(8,128)S(1)} %get-tuple-element.36.place_ref, bf16[72,128,256]{2,1,0:T(8,128)(2,1)S(1)} %shard_map.55.proj_ref, bf16[32,2,128,128]{3,2,1,0:T(8,128)(2,1)S(1)} %copy-done.2), custom_call_target="tpu_custom_call" | custom-call | tf_op jit(solution)/shard_map/pallas_call | solution.py:180
  46.8 0.0 collective-permute-done.4.green_ref
  46.8 2.3 %shard_map.57.before_ref = f32[16,128,256]{2,1,0:T(8,128)S(1)} custom-call(s32[17]{0:T(128)S(1)} %get-tuple-element.38.reach_ref, s32[8,16]{1,0:T(8,128)S(1)} %get-tuple-element.32.place_ref, bf16[72,128,256]{2,1,0:T(8,128)(2,1)S(1)} %shard_map.55.proj_ref, bf16[8,2,128,128]{3,2,1,0:T(8,128)(2,1)} %collective-permute-done.4.green_ref, ...), custom_call_target="tpu_custom_call" | custom-call | tf_op jit(solution)/shard_map/pallas_call | solution.py:180
  49.1 0.0 collective-permute-done.3.green_ref
  49.1 3.4 %shard_map.58.before_ref = f32[16,128,256]{2,1,0:T(8,128)S(1)} custom-call(s32[17]{0:T(128)S(1)} %get-tuple-element.40.reach_ref, s32[8,16]{1,0:T(8,128)S(1)} %get-tuple-element.33.place_ref, bf16[72,128,256]{2,1,0:T(8,128)(2,1)S(1)} %shard_map.55.proj_ref, bf16[8,2,128,128]{3,2,1,0:T(8,128)(2,1)} %collective-permute-done.3.green_ref, ...), custom_call_target="tpu_custom_call" | custom-call | tf_op jit(solution)/shard_map/pallas_call | solution.py:180
  52.5 0.0 collective-permute-done.2.green_ref
  52.5 3.0 %shard_map.59.before_ref = f32[16,128,256]{2,1,0:T(8,128)S(1)} custom-call(s32[17]{0:T(128)S(1)} %get-tuple-element.39.reach_ref, s32[8,16]{1,0:T(8,128)S(1)} %get-tuple-element.34.place_ref, bf16[72,128,256]{2,1,0:T(8,128)(2,1)S(1)} %shard_map.55.proj_ref, bf16[8,2,128,128]{3,2,1,0:T(8,128)(2,1)S(1)} %collective-permute-done.2.green_ref, ...), custom_call_target="tpu_custom_call" | custom-call | tf_op jit(solution)/shard_map/pallas_call | solution.py:180
  55.6 0.0 collective-permute-done.1.green_ref
  55.6 0.0 copy-done
  55.6 2.4 %shard_map.60 = (f32[8,64,256]{2,1,0:T(8,128)S(1)}, bf16[8,64,256]{2,1,0:T(8,128)(2,1)S(1)}) custom-call(s32[17]{0:T(128)S(1)} %get-tuple-element.41.reach_ref, s32[8,16]{1,0:T(8,128)S(1)} %get-tuple-element.35.place_ref, s32[1]{0:T(128)} %bitcast.3.core_ref, bf16[72,128,256]{2,1,0:T(8,128)(2,1)S(1)} %shard_map.55.proj_ref, ...), custom_call_target="tpu_custom_call" | custom-call | tf_op jit(solution)/shard_map/pallas_call | solution.py:180
  57.9 0.1 collective-permute-start.5
  58.1 0.0 copy-start.1
  58.1 2.3 %copy-done.1 = bf16[72,128,256]{2,1,0:T(8,128)(2,1)S(1)} copy-done((bf16[72,128,256]{2,1,0:T(8,128)(2,1)S(1)}, bf16[72,128,256]{2,1,0:T(8,128)(2,1)}, u32[]{:S(2)}) %copy-start.1) | copy-done | bytes 4718616
  60.5 1.7 %shard_map.61 = (f32[8,64,256]{2,1,0:T(8,128)S(1)}, bf16[8,64,256]{2,1,0:T(8,128)(2,1)S(1)}) custom-call(s32[17]{0:T(128)S(1)} %get-tuple-element.41.reach_ref, s32[8,16]{1,0:T(8,128)S(1)} %get-tuple-element.35.place_ref, s32[1]{0:T(128)} %bitcast.3.core_ref, bf16[72,128,256]{2,1,0:T(8,128)(2,1)S(1)} %copy-done.1, ...), custom_call_target="tpu_custom_call" | custom-call | tf_op jit(solution)/shard_map/pallas_call | solution.py:180
  62.2 2.0 %collective-permute-start.10 = (bf16[8,64,256]{2,1,0:T(8,128)(2,1)S(1)}, bf16[8,64,256]{2,1,0:T(8,128)(2,1)S(1)}, u32[]{:S(2)}, u32[]{:S(2)}) collective-permute-start(bf16[8,64,256]{2,1,0:T(8,128)(2,1)S(1)} %get-tuple-element.18), channel_id=1, source_target_pairs={{0,1},{1,0},{2,3},{3,2},{4,5},{5,4},{6,7},{7,6},{8,9},{9,8},{10,11... | collective-permute-start | bytes 786440 | tf_op jit(solution)/shard_map/ppermute | solution.py:216
  64.1 0.0 collective-permute-done.5
  64.1 1.0 %convert_add_fusion.1 = f32[8,64,256]{2,1,0:T(8,128)S(1)} fusion(f32[8,64,256]{2,1,0:T(8,128)S(1)} %get-tuple-element.15, bf16[8,64,256]{2,1,0:T(8,128)(2,1)} %collective-permute-done.5), kind=kLoop, calls=%fused_computation.1 | loop fusion | flops 262144 | bytes 1310720 | tf_op jit(solution)/shard_map/add | solution.py:217
  65.2 1.6 %collective-permute-start.6 = (bf16[4,8,8,256]{3,2,1,0:T(8,128)(2,1)S(1)}, bf16[4,8,8,256]{3,2,1,0:T(8,128)(2,1)S(1)}, u32[]{:S(2)}, u32[]{:S(2)}) collective-permute-start(bf16[4,8,8,256]{3,2,1,0:T(8,128)(2,1)S(1)} %fusion.2), channel_id=1, source_target_pairs={{0,2},{1,3},{2,0},{3,1},{4,6},{5,7},{6,4},{7,5},{8,10},{9,11},{10,... | collective-permute-start | bytes 393224 | tf_op jit(solution)/shard_map/ppermute | solution.py:221
  66.7 0.0 collective-permute-done.10
  66.7 0.1 convert_add_fusion
  66.8 0.6 collective-permute-start.11
  67.4 4.2 %collective-permute-done.6 = bf16[4,8,8,256]{3,2,1,0:T(8,128)(2,1)S(1)} collective-permute-done((bf16[4,8,8,256]{3,2,1,0:T(8,128)(2,1)S(1)}, bf16[4,8,8,256]{3,2,1,0:T(8,128)(2,1)S(1)}, u32[]{:S(2)}, u32[]{:S(2)}) %collective-permute-start.6) | collective-permute-done | bytes 131104 | tf_op jit(solution)/shard_map/ppermute | solution.py:221
  71.7 1.6 %collective-permute-start.7 = (bf16[8,8,256]{2,1,0:T(8,128)(2,1)S(1)}, bf16[8,8,256]{2,1,0:T(8,128)(2,1)S(1)}, u32[]{:S(2)}, u32[]{:S(2)}) collective-permute-start(bf16[8,8,256]{2,1,0:T(8,128)(2,1)S(1)} %get-tuple-element.22), channel_id=1, source_target_pairs={{0,4},{1,5},{2,6},{3,7},{4,8},{5,9},{6,10},{7,11},{8,12},{9,13},{1... | collective-permute-start | bytes 98312 | tf_op jit(solution)/shard_map/ppermute | solution.py:227
  73.3 1.6 %collective-permute-start.8 = (bf16[8,8,256]{2,1,0:T(8,128)(2,1)S(1)}, bf16[8,8,256]{2,1,0:T(8,128)(2,1)S(1)}, u32[]{:S(2)}, u32[]{:S(2)}) collective-permute-start(bf16[8,8,256]{2,1,0:T(8,128)(2,1)S(1)} %get-tuple-element.24), channel_id=1, source_target_pairs={{0,8},{1,9},{2,10},{3,11},{4,12},{5,13},{6,14},{7,15},{8,0},{9,1},... | collective-permute-start | bytes 98312 | tf_op jit(solution)/shard_map/ppermute | solution.py:227
  74.9 1.3 %collective-permute-start.9 = (bf16[8,8,256]{2,1,0:T(8,128)(2,1)S(1)}, bf16[8,8,256]{2,1,0:T(8,128)(2,1)S(1)}, u32[]{:S(2)}, u32[]{:S(2)}) collective-permute-start(bf16[8,8,256]{2,1,0:T(8,128)(2,1)S(1)} %get-tuple-element.23), channel_id=1, source_target_pairs={{0,12},{1,13},{2,14},{3,15},{4,0},{5,1},{6,2},{7,3},{8,4},{9,5},{1... | collective-permute-start | bytes 98312 | tf_op jit(solution)/shard_map/ppermute | solution.py:227
  76.2 0.0 collective-permute-done.11
  76.3 0.7 collective-permute-start.12
  77.0 1.3 %collective-permute-start.13 = (bf16[8,8,256]{2,1,0:T(8,128)(2,1)S(1)}, bf16[8,8,256]{2,1,0:T(8,128)(2,1)S(1)}, u32[]{:S(2)}, u32[]{:S(2)}) collective-permute-start(bf16[8,8,256]{2,1,0:T(8,128)(2,1)S(1)} %get-tuple-element.27), channel_id=1, source_target_pairs={{0,8},{1,9},{2,10},{3,11},{4,12},{5,13},{6,14},{7,15},{8,0},{9,1},... | collective-permute-start | bytes 98312 | tf_op jit(solution)/shard_map/ppermute | solution.py:227
  78.3 0.0 collective-permute-done.7
  78.3 2.3 %collective-permute-start.14 = (bf16[8,8,256]{2,1,0:T(8,128)(2,1)S(1)}, bf16[8,8,256]{2,1,0:T(8,128)(2,1)S(1)}, u32[]{:S(2)}, u32[]{:S(2)}) collective-permute-start(bf16[8,8,256]{2,1,0:T(8,128)(2,1)S(1)} %get-tuple-element.26), channel_id=1, source_target_pairs={{0,12},{1,13},{2,14},{3,15},{4,0},{5,1},{6,2},{7,3},{8,4},{9,5},{1... | collective-permute-start | bytes 98312 | tf_op jit(solution)/shard_map/ppermute | solution.py:227
  80.6 0.0 collective-permute-done.8
  80.6 0.0 collective-permute-done.9
  80.7 1.5 %collective-permute-done.12 = bf16[8,8,256]{2,1,0:T(8,128)(2,1)S(1)} collective-permute-done((bf16[8,8,256]{2,1,0:T(8,128)(2,1)S(1)}, bf16[8,8,256]{2,1,0:T(8,128)(2,1)S(1)}, u32[]{:S(2)}, u32[]{:S(2)}) %collective-permute-start.12) | collective-permute-done | bytes 32800 | tf_op jit(solution)/shard_map/ppermute | solution.py:227
  82.1 0.4 collective-permute-done.13
  82.5 0.1 collective-permute-done.14
  82.7 0.1 reshape.52
  82.7 0.7 copy.15
  (17 shorter events, 0.3 us)
Async XLA Ops:
  0.0 19.9 %copy-start.4 = (bf16[2,128,128]{2,1,0:T(8,128)(2,1)S(1)}, bf16[2,128,128]{2,1,0:T(8,128)(2,1)}, u32[]{:S(2)}) copy-start(bf16[2,128,128]{2,1,0:T(8,128)(2,1)} %param.7) | copy-start | bytes 196612
  0.0 20.2 %copy-start.5 = (s32[16]{0:T(128)S(1)}, s32[16]{0:T(128)}, u32[]{:S(2)}) copy-start(s32[16]{0:T(128)} %param.8) | copy-start | bytes 196
  0.0 20.3 %copy-start.6 = (s32[2]{0:T(128)S(1)}, s32[2]{0:T(128)}, u32[]{:S(2)}) copy-start(s32[2]{0:T(128)} %param.9) | copy-start | bytes 28
  1.9 22.0 %copy-start.3 = (bf16[32,2,128,128]{3,2,1,0:T(8,128)(2,1)S(1)}, bf16[32,2,128,128]{3,2,1,0:T(8,128)(2,1)}, u32[]{:S(2)}) copy-start(bf16[32,2,128,128]{3,2,1,0:T(8,128)(2,1)} %own_ref) | copy-start | bytes 6291460
  1.9 22.0 %collective-permute-start = (bf16[32,2,128,128]{3,2,1,0:T(8,128)(2,1)}, bf16[32,2,128,128]{3,2,1,0:T(8,128)(2,1)}, u32[]{:S(2)}, u32[]{:S(2)}) collective-permute-start(bf16[32,2,128,128]{3,2,1,0:T(8,128)(2,1)} %own_ref), channel_id=1, source_target_pairs={{0,1},{1,0},{2,3},{3,2},{4,5},{5,4},{6,7},{7,6},{8,9},{9,8},{10,11... | collective-permute-start | bytes 6291464 | tf_op jit(solution)/shard_map/ppermute | solution.py:256
  2.4 44.4 %collective-permute-start.4 = (bf16[8,2,128,128]{3,2,1,0:T(8,128)(2,1)}, bf16[8,2,128,128]{3,2,1,0:T(8,128)(2,1)}, u32[]{:S(2)}, u32[]{:S(2)}) collective-permute-start(bf16[8,2,128,128]{3,2,1,0:T(8,128)(2,1)} %slice.57), channel_id=1, source_target_pairs={{0,2},{1,3},{2,4},{3,5},{4,6},{5,7},{6,8},{7,9},{8,10},{9,11},{10,... | collective-permute-start | bytes 1572872 | tf_op jit(solution)/shard_map/ppermute | solution.py:246
  10.3 38.8 %collective-permute-start.3 = (bf16[8,2,128,128]{3,2,1,0:T(8,128)(2,1)}, bf16[8,2,128,128]{3,2,1,0:T(8,128)(2,1)}, u32[]{:S(2)}, u32[]{:S(2)}) collective-permute-start(bf16[8,2,128,128]{3,2,1,0:T(8,128)(2,1)} %get-tuple-element.19), channel_id=1, source_target_pairs={{0,2},{1,3},{2,4},{3,5},{4,6},{5,7},{6,8},{7,9},{8,10},{9,11},{10,... | collective-permute-start | bytes 1572872 | tf_op jit(solution)/shard_map/ppermute | solution.py:246
  13.8 38.7 %collective-permute-start.2 = (bf16[8,2,128,128]{3,2,1,0:T(8,128)(2,1)}, bf16[8,2,128,128]{3,2,1,0:T(8,128)(2,1)S(1)}, u32[]{:S(2)}, u32[]{:S(2)}) collective-permute-start(bf16[8,2,128,128]{3,2,1,0:T(8,128)(2,1)} %get-tuple-element.20), channel_id=1, source_target_pairs={{0,2},{1,3},{2,4},{3,5},{4,6},{5,7},{6,8},{7,9},{8,10},{9,11},{10,... | collective-permute-start | bytes 1572872 | tf_op jit(solution)/shard_map/ppermute | solution.py:246
  16.4 39.1 %collective-permute-start.1 = (bf16[8,2,128,128]{3,2,1,0:T(8,128)(2,1)}, bf16[8,2,128,128]{3,2,1,0:T(8,128)(2,1)S(1)}, u32[]{:S(2)}, u32[]{:S(2)}) collective-permute-start(bf16[8,2,128,128]{3,2,1,0:T(8,128)(2,1)} %get-tuple-element.21), channel_id=1, source_target_pairs={{0,2},{1,3},{2,4},{3,5},{4,6},{5,7},{6,8},{7,9},{8,10},{9,11},{10,... | collective-permute-start | bytes 1572872 | tf_op jit(solution)/shard_map/ppermute | solution.py:246
  23.9 7.1 %copy-start.2 = (bf16[32,2,128,128]{3,2,1,0:T(8,128)(2,1)S(1)}, bf16[32,2,128,128]{3,2,1,0:T(8,128)(2,1)}, u32[]{:S(2)}) copy-start(bf16[32,2,128,128]{3,2,1,0:T(8,128)(2,1)} %green_ref) | copy-start | bytes 6291460
  30.9 24.6 %copy-start = (bf16[72,128,256]{2,1,0:T(8,128)(2,1)}, bf16[72,128,256]{2,1,0:T(8,128)(2,1)S(1)}, u32[]{:S(2)}) copy-start(bf16[72,128,256]{2,1,0:T(8,128)(2,1)S(1)} %shard_map.55.proj_ref) | copy-start | bytes 14155780
  57.9 6.2 %collective-permute-start.5 = (bf16[8,64,256]{2,1,0:T(8,128)(2,1)S(1)}, bf16[8,64,256]{2,1,0:T(8,128)(2,1)}, u32[]{:S(2)}, u32[]{:S(2)}) collective-permute-start(bf16[8,64,256]{2,1,0:T(8,128)(2,1)S(1)} %get-tuple-element.16), channel_id=1, source_target_pairs={{0,1},{1,0},{2,3},{3,2},{4,5},{5,4},{6,7},{7,6},{8,9},{9,8},{10,11... | collective-permute-start | bytes 786440 | tf_op jit(solution)/shard_map/ppermute | solution.py:216
  58.1 2.3 %copy-start.1 = (bf16[72,128,256]{2,1,0:T(8,128)(2,1)S(1)}, bf16[72,128,256]{2,1,0:T(8,128)(2,1)}, u32[]{:S(2)}) copy-start(bf16[72,128,256]{2,1,0:T(8,128)(2,1)} %copy-done) | copy-start | bytes 14155780
  62.2 4.6 %collective-permute-start.10 = (bf16[8,64,256]{2,1,0:T(8,128)(2,1)S(1)}, bf16[8,64,256]{2,1,0:T(8,128)(2,1)S(1)}, u32[]{:S(2)}, u32[]{:S(2)}) collective-permute-start(bf16[8,64,256]{2,1,0:T(8,128)(2,1)S(1)} %get-tuple-element.18), channel_id=1, source_target_pairs={{0,1},{1,0},{2,3},{3,2},{4,5},{5,4},{6,7},{7,6},{8,9},{9,8},{10,11... | collective-permute-start | bytes 786440 | tf_op jit(solution)/shard_map/ppermute | solution.py:216
  65.2 6.4 %collective-permute-start.6 = (bf16[4,8,8,256]{3,2,1,0:T(8,128)(2,1)S(1)}, bf16[4,8,8,256]{3,2,1,0:T(8,128)(2,1)S(1)}, u32[]{:S(2)}, u32[]{:S(2)}) collective-permute-start(bf16[4,8,8,256]{3,2,1,0:T(8,128)(2,1)S(1)} %fusion.2), channel_id=1, source_target_pairs={{0,2},{1,3},{2,0},{3,1},{4,6},{5,7},{6,4},{7,5},{8,10},{9,11},{10,... | collective-permute-start | bytes 393224 | tf_op jit(solution)/shard_map/ppermute | solution.py:221
  66.8 9.4 %collective-permute-start.11 = (bf16[4,8,8,256]{3,2,0,1:T(8,128)(2,1)S(1)}, bf16[4,8,8,256]{3,2,0,1:T(8,128)(2,1)S(1)}, u32[]{:S(2)}, u32[]{:S(2)}) collective-permute-start(bf16[4,8,8,256]{3,2,0,1:T(8,128)(2,1)S(1)} %fusion.1), channel_id=1, source_target_pairs={{0,2},{1,3},{2,0},{3,1},{4,6},{5,7},{6,4},{7,5},{8,10},{9,11},{10,... | collective-permute-start | bytes 393224 | tf_op jit(solution)/shard_map/ppermute | solution.py:221
  71.7 6.7 %collective-permute-start.7 = (bf16[8,8,256]{2,1,0:T(8,128)(2,1)S(1)}, bf16[8,8,256]{2,1,0:T(8,128)(2,1)S(1)}, u32[]{:S(2)}, u32[]{:S(2)}) collective-permute-start(bf16[8,8,256]{2,1,0:T(8,128)(2,1)S(1)} %get-tuple-element.22), channel_id=1, source_target_pairs={{0,4},{1,5},{2,6},{3,7},{4,8},{5,9},{6,10},{7,11},{8,12},{9,13},{1... | collective-permute-start | bytes 98312 | tf_op jit(solution)/shard_map/ppermute | solution.py:227
  73.3 7.4 %collective-permute-start.8 = (bf16[8,8,256]{2,1,0:T(8,128)(2,1)S(1)}, bf16[8,8,256]{2,1,0:T(8,128)(2,1)S(1)}, u32[]{:S(2)}, u32[]{:S(2)}) collective-permute-start(bf16[8,8,256]{2,1,0:T(8,128)(2,1)S(1)} %get-tuple-element.24), channel_id=1, source_target_pairs={{0,8},{1,9},{2,10},{3,11},{4,12},{5,13},{6,14},{7,15},{8,0},{9,1},... | collective-permute-start | bytes 98312 | tf_op jit(solution)/shard_map/ppermute | solution.py:227
  74.9 5.8 %collective-permute-start.9 = (bf16[8,8,256]{2,1,0:T(8,128)(2,1)S(1)}, bf16[8,8,256]{2,1,0:T(8,128)(2,1)S(1)}, u32[]{:S(2)}, u32[]{:S(2)}) collective-permute-start(bf16[8,8,256]{2,1,0:T(8,128)(2,1)S(1)} %get-tuple-element.23), channel_id=1, source_target_pairs={{0,12},{1,13},{2,14},{3,15},{4,0},{5,1},{6,2},{7,3},{8,4},{9,5},{1... | collective-permute-start | bytes 98312 | tf_op jit(solution)/shard_map/ppermute | solution.py:227
  76.3 5.9 %collective-permute-start.12 = (bf16[8,8,256]{2,1,0:T(8,128)(2,1)S(1)}, bf16[8,8,256]{2,1,0:T(8,128)(2,1)S(1)}, u32[]{:S(2)}, u32[]{:S(2)}) collective-permute-start(bf16[8,8,256]{2,1,0:T(8,128)(2,1)S(1)} %get-tuple-element.25), channel_id=1, source_target_pairs={{0,4},{1,5},{2,6},{3,7},{4,8},{5,9},{6,10},{7,11},{8,12},{9,13},{1... | collective-permute-start | bytes 98312 | tf_op jit(solution)/shard_map/ppermute | solution.py:227
  77.0 5.5 %collective-permute-start.13 = (bf16[8,8,256]{2,1,0:T(8,128)(2,1)S(1)}, bf16[8,8,256]{2,1,0:T(8,128)(2,1)S(1)}, u32[]{:S(2)}, u32[]{:S(2)}) collective-permute-start(bf16[8,8,256]{2,1,0:T(8,128)(2,1)S(1)} %get-tuple-element.27), channel_id=1, source_target_pairs={{0,8},{1,9},{2,10},{3,11},{4,12},{5,13},{6,14},{7,15},{8,0},{9,1},... | collective-permute-start | bytes 98312 | tf_op jit(solution)/shard_map/ppermute | solution.py:227
  78.3 4.3 %collective-permute-start.14 = (bf16[8,8,256]{2,1,0:T(8,128)(2,1)S(1)}, bf16[8,8,256]{2,1,0:T(8,128)(2,1)S(1)}, u32[]{:S(2)}, u32[]{:S(2)}) collective-permute-start(bf16[8,8,256]{2,1,0:T(8,128)(2,1)S(1)} %get-tuple-element.26), channel_id=1, source_target_pairs={{0,12},{1,13},{2,14},{3,15},{4,0},{5,1},{6,2},{7,3},{8,4},{9,5},{1... | collective-permute-start | bytes 98312 | tf_op jit(solution)/shard_map/ppermute | solution.py:227

commit v6 on v5

--- a/solution.py
+++ b/solution.py
@@ -9,8 +9,9 @@
 from jax.sharding import PartitionSpec as P
 
 STEP = 8
-GROUPS = 2
-PARTS = 4
+PAIR = 2
+GROUPS = 1
+PARTS = (24, 4, 4)
 MIB = 1 << 20
 
 
@@ -18,6 +19,30 @@
     top = jnp.concatenate([real, imag], 1)
     bottom = jnp.concatenate([-imag, real], 1)
     return jnp.concatenate([top, bottom], 0)
+
+
+def cut_kernel(sizes, source_ref, *refs):
+    sems = refs[-1]
+    copies = []
+    first = 0
+    for k, size in enumerate(sizes):
+        copies.append(
+            pltpu.make_async_copy(source_ref.at[pl.ds(first, size)], refs[k], sems.at[k])
+        )
+        copies[-1].start()
+        first += size
+    for copy in copies:
+        copy.wait()
+
+
+def cut(blocks, sizes):
+    return pl.pallas_call(
+        functools.partial(cut_kernel, sizes),
+        out_shape=[jax.ShapeDtypeStruct((size,) + blocks.shape[1:], blocks.dtype) for size in sizes],
+        in_specs=[pl.BlockSpec(memory_space=pl.ANY)],
+        out_specs=[pl.BlockSpec(memory_space=pl.ANY)] * len(sizes),
+        scratch_shapes=[pltpu.SemaphoreType.DMA((len(sizes),))],
+    )(blocks)
 
 
 def project_blocks(left, right, lesser_ref, out_ref):
@@ -79,43 +104,39 @@
     )(left, right, own, other)
 
 
-def add_products(reach_ref, place_ref, proj_ref, green_ref, total_ref, start, far):
-    first = pl.program_id(0) * STEP
-    photons = total_ref.shape[0]
-    for w in range(photons):
-        lowest = reach_ref[start + w] + first
-        limit = reach_ref[reach_ref.shape[0] - 1]
-        needed = lowest + STEP - 1 >= limit if far else lowest < limit
-
-        @pl.when(needed)
-        def _():
-            total = total_ref[w]
-            for u in range(STEP):
-                right = rotated(green_ref[u, 0], green_ref[u, 1])
-                left = proj_ref[place_ref[first + u, start + w]]
-                total += jnp.dot(left, right, preferred_element_type=jnp.float32)
-            total_ref[w] = total
-
-
-def near_kernel(reach_ref, place_ref, proj_ref, green_ref, total_ref):
+def add_products(place_ref, proj_ref, green_ref, total_ref, start):
+    step = green_ref.shape[0]
+    first = pl.program_id(0) * step
+    photons, rows, width = total_ref.shape
+    for w in range(0, photons, PAIR):
+        total = total_ref[w : w + PAIR].reshape(PAIR * rows, width)
+        for u in range(step):
+            left = jnp.concatenate(
+                [proj_ref[place_ref[first + u, start + w + v]] for v in range(PAIR)], 0
+            )
+            right = rotated(green_ref[u, 0], green_ref[u, 1])
+            total += jnp.dot(left, right, preferred_element_type=jnp.float32)
+        total_ref[w : w + PAIR] = total.reshape(PAIR, rows, width)
+
+
+def near_kernel(place_ref, proj_ref, green_ref, total_ref):
     @pl.when(pl.program_id(0) == 0)
     def _():
         total_ref[...] = jnp.zeros_like(total_ref)
 
-    add_products(reach_ref, place_ref, proj_ref, green_ref, total_ref, 0, False)
-
-
-def far_kernel(reach_ref, place_ref, proj_ref, green_ref, before_ref, total_ref):
+    add_products(place_ref, proj_ref, green_ref, total_ref, 0)
+
+
+def far_kernel(place_ref, proj_ref, green_ref, before_ref, total_ref):
     @pl.when(pl.program_id(0) == 0)
     def _():
         total_ref[...] = before_ref[...]
 
-    add_products(reach_ref, place_ref, proj_ref, green_ref, total_ref, 0, True)
+    add_products(place_ref, proj_ref, green_ref, total_ref, 0)
 
 
 def last_kernel(
     start,
-    reach_ref,
     place_ref,
     core_ref,
     proj_ref,
@@ -129,7 +150,7 @@
     def _():
         total_ref[...] = before_ref[...]
 
-    add_products(reach_ref, place_ref, proj_ref, green_ref, total_ref, start, True)
+    add_products(place_ref, proj_ref, green_ref, total_ref, start)
 
     @pl.when(pl.program_id(0) == pl.num_programs(0) - 1)
     def _():
@@ -141,22 +162,23 @@
         send_ref[...] = total_ref[:, pl.ds(other, half), :].astype(send_ref.dtype)
 
 
-def products(reach, place, proj, green, before=None, core=None, group=0):
+def products(place, proj, green, before=None, core=None, group=0):
     slots, rows, width = proj.shape
     energies, _, orbitals, _ = green.shape
+    step = min(STEP, energies)
     photons = place.shape[1]
     smem = pl.BlockSpec(memory_space=pltpu.SMEM)
     if core is not None:
         photons //= GROUPS
     block = (photons, rows, width)
-    operands, specs = [reach, place], [smem, smem]
+    operands, specs = [place], [smem]
     if core is not None:
         operands.append(core)
         specs.append(smem)
     operands += [proj, green]
     specs += [
         pl.BlockSpec((slots, rows, width), lambda t: (0, 0, 0), pipeline_mode=pl.Buffered(1)),
-        pl.BlockSpec((STEP, 2, orbitals, orbitals), lambda t: (t, 0, 0, 0)),
+        pl.BlockSpec((step, 2, orbitals, orbitals), lambda t: (t, 0, 0, 0)),
     ]
     if before is not None:
         operands.append(before)
@@ -180,7 +202,7 @@
     return pl.pallas_call(
         kernel,
         out_shape=out_shape,
-        grid=(energies // STEP,),
+        grid=(energies // step,),
         in_specs=specs,
         out_specs=out_specs,
         scratch_shapes=scratch,
@@ -239,11 +261,9 @@
 
     up = [(i, i + 2) for i in range(devices - 2)]
     across = [(i, i ^ 1) for i in range(devices)]
-    piece = e_dev // PARTS
-    pieces = [greater[:piece]]
-    lesser, greater, pieces[0] = lax.optimization_barrier((lesser, greater, pieces[0]))
-    pieces += [greater[k * piece : (k + 1) * piece] for k in range(1, PARTS)]
-    far = [lax.ppermute(block, "energy", up) for block in pieces]
+    sizes = [e_dev * part // 32 for part in PARTS]
+    pieces = list(cut(greater, sizes))
+    far = [lax.ppermute(pieces[0], "energy", up)]
 
     planes = devices // 4
     rows = dipole.reshape(2, planes, 2, 2, share, orbitals)
@@ -255,18 +275,23 @@
     )
     proj = project(left, right, lesser, lax.ppermute(lesser, "energy", across))
 
+    pieces[1], proj = lax.optimization_barrier((pieces[1], proj))
+    far.append(lax.ppermute(pieces[1], "energy", up))
+
     near_place, far_place = places(shifts, window, index * e_dev, core, e_dev)
-    limit = jnp.where(core == 0, 2 * e_dev, e_dev)[None]
-    result = products(jnp.concatenate([shifts, limit]), near_place, proj, greater)
+    result = products(near_place, proj, greater)
+    pieces[2], result = lax.optimization_barrier((pieces[2], result))
+    far.append(lax.ppermute(pieces[2], "energy", up))
     core = core[None]
-    for k in range(PARTS):
-        place = far_place[k * piece : (k + 1) * piece]
-        reach = jnp.concatenate([shifts, limit - k * piece])
-        if k < PARTS - 1:
-            result = products(reach, place, proj, far[k], before=result)
+    first = 0
+    for k, size in enumerate(sizes):
+        place = far_place[first : first + size]
+        first += size
+        if k < len(sizes) - 1:
+            result = products(place, proj, far[k], before=result)
     sums = []
     for group in range(GROUPS):
-        keep, send = products(reach, place, proj, far[-1], before=result, core=core, group=group)
+        keep, send = products(place, proj, far[-1], before=result, core=core, group=group)
         sums.append(reduced(keep, send, planes, share))
     scale = 1.0 / math.sqrt(2.0 * orbitals * total)
     summed = jnp.concatenate(sums, 0) * scale

time: 84 us -> 141 us (1.68)
  Pallas kernels: 35.6 us -> 94.1 us
  waiting for transfers between devices: 6.16 us -> 20.4 us
  starting transfers between devices: 28.4 us -> 20.3 us
  local copies, waits for them, and re-layouts: 8.66 us -> 2.56 us
    pallas_call x6 -> x5, Pallas kernels: 28.6 us -> 87.1 us  [the longest x1 64.7 us: cut(): pl.pallas_call(functools.partial(cut_kernel, sizes), out_shape=[jax.Shape...]
    ppermute x4 -> x3, waiting for transfers between devices: 0.01 us -> 6.88 us  [the longest x1 6.31 us: on_device(): far = [lax.ppermute(pieces[0], 'energy', up)]]
    slice x3 -> x2, local copies, waits for them, and re-layouts: 4.52 us -> 0.01 us  [on_device(): place = far_place[first:first + size]]
    ppermute x4 -> x3, starting transfers between devices: 14.9 us -> 11.3 us  [the longest x1 5.62 us: on_device(): far = [lax.ppermute(pieces[0], 'energy', up)]]
    ppermute x6 -> x3, starting transfers between devices: 8.88 us -> 5.79 us  [reduced(): total = total + lax.ppermute(send, 'energy', route).astype(jnp.float32)]
    ppermute x6 -> x3, waiting for transfers between devices: 1.97 us -> 5.05 us  [reduced(): total = total + lax.ppermute(send, 'energy', route).astype(jnp.float32)]
    ppermute x2 -> x1, waiting for transfers between devices: 4.17 us -> 6.61 us  [reduced(): got = lax.ppermute(send, 'energy', [(i, i ^ 2) for i in range(devices)])]
    unnamed x16, local copies, waits for them, and re-layouts: 2.59 us -> 0.26 us
  transfers between devices with their start and end apart: 15 -> 9, of which waited for: 4 -> 7; matrix products, arithmetic and copies ran while one was open for 9% -> 3% of each run, Pallas kernels for 40% -> 66%
where the time goes in v6:
time: 141 us; the launch traced here: 140 us
  Pallas kernels  94.1 us (67%)
  waiting for transfers between devices  20.4 us (14%)
  starting transfers between devices  20.3 us (14%)
  other arithmetic  2.79 us (2%)
  local copies, waits for them, and re-layouts  2.56 us (2%)
    pallas_call x1, Pallas kernels, cut(): pl.pallas_call(functools.partial(cut_kernel, sizes), out_shape=[jax.Shape...  64.7 us
    pallas_call x4, Pallas kernels, products(): pl.pallas_call(kernel, out_shape=out_shape, grid=(energies // step,), in_...  22.4 us
    pallas_call x1, Pallas kernels, project(): pl.pallas_call(functools.partial(project_kernel, steps), out_shape=jax.Sh...  7.01 us
    ppermute x1, waiting for transfers between devices, reduced(): got = lax.ppermute(send, 'energy', [(i, i ^ 2) for i in range(devices)])  6.61 us
    ppermute x1, waiting for transfers between devices, on_device(): far = [lax.ppermute(pieces[0], 'energy', up)]  6.31 us
    ppermute x3, starting transfers between devices, reduced(): total = total + lax.ppermute(send, 'energy', route).astype(jnp.float32)  5.79 us
    ppermute x1, starting transfers between devices, on_device(): far = [lax.ppermute(pieces[0], 'energy', up)]  5.62 us
    ppermute x3, waiting for transfers between devices, reduced(): total = total + lax.ppermute(send, 'energy', route).astype(jnp.float32)  5.05 us
  transfers between devices with their start and end apart: 9, of which 7 were waited for; matrix products, arithmetic and copies ran while one was open for 3% of the time, Pallas kernels for 66%

profile of v6, /device:TPU:0, one launch (start us, length us, event | category | flops | bytes accessed | tf_op | source)
XLA Modules:
  0.0 140.4 jit_solution(13842141707910874204)
XLA Ops:
  0.0 0.0 copy-start.1
  0.0 0.0 copy-start.2
  0.0 0.0 copy-start.3
  0.0 0.0 copy-start.4
  0.0 0.5 collective-permute-start
  0.5 64.7 %shard_map.55 = (bf16[24,2,128,128]{3,2,1,0:T(8,128)(2,1)}, bf16[4,2,128,128]{3,2,1,0:T(8,128)(2,1)}, bf16[4,2,128,128]{3,2,1,0:T(8,128)(2,1)}) custom-call(bf16[32,2,128,128]{3,2,1,0:T(8,128)(2,1)} %green_ref.1), custom_call_target="tpu_custom_call" | custom-call | tf_op jit(solution)/shard_map/pallas_call | solution.py:39
  65.2 5.6 %collective-permute-start.3 = (bf16[24,2,128,128]{3,2,1,0:T(8,128)(2,1)}, bf16[24,2,128,128]{3,2,1,0:T(8,128)(2,1)}, u32[]{:S(2)}, u32[]{:S(2)}) collective-permute-start(bf16[24,2,128,128]{3,2,1,0:T(8,128)(2,1)} %get-tuple-element.19), channel_id=1, source_target_pairs={{0,2},{1,3},{2,4},{3,5},{4,6},{5,7},{6,8},{7,9},{8,10},{9,11},{10,... | collective-permute-start | bytes 4718600 | tf_op jit(solution)/shard_map/ppermute | solution.py:266
  70.8 0.8 fusion.18
  71.6 0.0 copy-done.2
  71.6 0.1 copy.14
  71.7 0.1 copy.15
  71.9 0.0 copy-done.3
  71.9 0.6 fusion.21
  72.5 1.2 compare_and_fusion
  73.8 0.0 copy-done.4
  73.9 1.3 fusion.10
  75.2 0.0 copy-start.6
  75.2 0.0 copy-start
  75.2 0.0 collective-permute-done.other_ref
  75.2 0.0 copy-done.1
  75.2 7.0 %shard_map.56.proj_ref = bf16[72,128,256]{2,1,0:T(8,128)(2,1)S(1)} custom-call(bf16[128,256]{1,0:T(8,128)(2,1)S(1)} %pad_maximum_fusion.left_ref, bf16[256,256]{1,0:T(8,128)(2,1)S(1)} %maximum_maximum_fusion.right_ref, bf16[32,2,128,128]{3,2,1,0:T(8,128)(2,1)S(1)} %copy-done.1, bf16[32,2,128,128]{3,2,1,0:T(8,128)(2,1)} %collective-permute-done.other_ref), custom_call_target="tpu_custom_call" | custom-call | tf_op jit(solution)/shard_map/pallas_call | solution.py:87
  82.2 0.0 copy-done.6
  82.2 2.3 %collective-permute-start.2 = (bf16[4,2,128,128]{3,2,1,0:T(8,128)(2,1)S(1)}, bf16[4,2,128,128]{3,2,1,0:T(8,128)(2,1)S(1)}, u32[]{:S(2)}, u32[]{:S(2)}) collective-permute-start(bf16[4,2,128,128]{3,2,1,0:T(8,128)(2,1)S(1)} %copy-done.6), channel_id=1, source_target_pairs={{0,2},{1,3},{2,4},{3,5},{4,6},{5,7},{6,8},{7,9},{8,10},{9,11},{10,... | collective-permute-start | bytes 786440 | tf_op jit(solution)/shard_map/ppermute | solution.py:279
  84.5 0.0 copy-done
  84.5 0.0 copy-start.5
  84.5 10.3 %shard_map.57.before_ref = f32[16,128,256]{2,1,0:T(8,128)S(1)} custom-call(s32[32,16]{1,0:T(8,128)S(1)} %get-tuple-element.32.place_ref, bf16[72,128,256]{2,1,0:T(8,128)(2,1)S(1)} %shard_map.56.proj_ref, bf16[32,2,128,128]{3,2,1,0:T(8,128)(2,1)S(1)} %copy-done), custom_call_target="tpu_custom_call" | custom-call | tf_op jit(solution)/shard_map/pallas_call | solution.py:202
  94.9 0.0 copy-done.5
  94.9 3.4 %collective-permute-start.1 = (bf16[4,2,128,128]{3,2,1,0:T(8,128)(2,1)S(1)}, bf16[4,2,128,128]{3,2,1,0:T(8,128)(2,1)S(1)}, u32[]{:S(2)}, u32[]{:S(2)}) collective-permute-start(bf16[4,2,128,128]{3,2,1,0:T(8,128)(2,1)S(1)} %copy-done.5), channel_id=1, source_target_pairs={{0,2},{1,3},{2,4},{3,5},{4,6},{5,7},{6,8},{7,9},{8,10},{9,11},{10,... | collective-permute-start | bytes 786440 | tf_op jit(solution)/shard_map/ppermute | solution.py:284
  98.3 6.3 %collective-permute-done.3.green_ref = bf16[24,2,128,128]{3,2,1,0:T(8,128)(2,1)} collective-permute-done((bf16[24,2,128,128]{3,2,1,0:T(8,128)(2,1)}, bf16[24,2,128,128]{3,2,1,0:T(8,128)(2,1)}, u32[]{:S(2)}, u32[]{:S(2)}) %collective-permute-start.3) | collective-permute-done | bytes 1572896 | tf_op jit(solution)/shard_map/ppermute | solution.py:266
  104.7 8.3 %shard_map.58.before_ref = f32[16,128,256]{2,1,0:T(8,128)S(1)} custom-call(s32[24,16]{1,0:T(8,128)S(1)} %slice.48.place_ref, bf16[72,128,256]{2,1,0:T(8,128)(2,1)S(1)} %shard_map.56.proj_ref, bf16[24,2,128,128]{3,2,1,0:T(8,128)(2,1)} %collective-permute-done.3.green_ref, f32[16,128,256]{2,1,0:T(8,128)S(1)} %shard_map.57.before_ref), custom_call_target="tpu_custom_call" | custom-call | tf_op jit(solution)/shard_map/pallas_call | solution.py:202
  113.0 0.0 collective-permute-done.2.green_ref
  113.0 1.8 %shard_map.59.before_ref = f32[16,128,256]{2,1,0:T(8,128)S(1)} custom-call(s32[4,16]{1,0:T(4,128)S(1)} %get-tuple-element.30.place_ref, bf16[72,128,256]{2,1,0:T(8,128)(2,1)S(1)} %shard_map.56.proj_ref, bf16[4,2,128,128]{3,2,1,0:T(8,128)(2,1)S(1)} %collective-permute-done.2.green_ref, f32[16,128,256]{2,1,0:T(8,128)S(1)} %shard_map.58.before_ref), custom_call_target="tpu_custom_call" | custom-call | tf_op jit(solution)/shard_map/pallas_call | solution.py:202
  114.8 0.6 collective-permute-done.1.green_ref
  115.4 1.9 %shard_map.60 = (f32[16,64,256]{2,1,0:T(8,128)S(1)}, bf16[16,64,256]{2,1,0:T(8,128)(2,1)S(1)}) custom-call(s32[4,16]{1,0:T(4,128)S(1)} %get-tuple-element.31.place_ref, s32[1]{0:T(128)} %bitcast.2.core_ref, bf16[72,128,256]{2,1,0:T(8,128)(2,1)S(1)} %shard_map.56.proj_ref, bf16[4,2,128,128]{3,2,1,0:T(8,128)(2,1)S(1)} %collective-permute-done.1.green_ref, ...), custom_call_target="tpu_custom_call" | custom-call | tf_op jit(solution)/shard_map/pallas_call | solution.py:202
  117.3 0.1 collective-permute-start.4
  117.4 1.9 %collective-permute-done.4 = bf16[16,64,256]{2,1,0:T(8,128)(2,1)S(1)} collective-permute-done((bf16[16,64,256]{2,1,0:T(8,128)(2,1)S(1)}, bf16[16,64,256]{2,1,0:T(8,128)(2,1)S(1)}, u32[]{:S(2)}, u32[]{:S(2)}) %collective-permute-start.4) | collective-permute-done | bytes 524320 | tf_op jit(solution)/shard_map/ppermute | solution.py:238
  119.3 0.1 convert_add_fusion
  119.5 2.5 %collective-permute-start.5 = (bf16[4,16,8,256]{3,2,0,1:T(8,128)(2,1)S(1)}, bf16[4,16,8,256]{3,2,0,1:T(8,128)(2,1)S(1)}, u32[]{:S(2)}, u32[]{:S(2)}) collective-permute-start(bf16[4,16,8,256]{3,2,0,1:T(8,128)(2,1)S(1)} %fusion), channel_id=1, source_target_pairs={{0,2},{1,3},{2,0},{3,1},{4,6},{5,7},{6,4},{7,5},{8,10},{9,11},{10,... | collective-permute-start | bytes 786440 | tf_op jit(solution)/shard_map/ppermute | solution.py:243
  122.0 6.6 %collective-permute-done.5 = bf16[4,16,8,256]{3,2,0,1:T(8,128)(2,1)S(1)} collective-permute-done((bf16[4,16,8,256]{3,2,0,1:T(8,128)(2,1)S(1)}, bf16[4,16,8,256]{3,2,0,1:T(8,128)(2,1)S(1)}, u32[]{:S(2)}, u32[]{:S(2)}) %collective-permute-start.5) | collective-permute-done | bytes 262176 | tf_op jit(solution)/shard_map/ppermute | solution.py:243
  128.6 0.1 bitcast_add_fusion
  128.8 4.8 %collective-permute-start.8 = (bf16[16,8,256]{2,1,0:T(8,128)(2,1)S(1)}, bf16[16,8,256]{2,1,0:T(8,128)(2,1)S(1)}, u32[]{:S(2)}, u32[]{:S(2)}) collective-permute-start(bf16[16,8,256]{2,1,0:T(8,128)(2,1)S(1)} %get-tuple-element.24), channel_id=1, source_target_pairs={{0,12},{1,13},{2,14},{3,15},{4,0},{5,1},{6,2},{7,3},{8,4},{9,5},{1... | collective-permute-start | bytes 196616 | tf_op jit(solution)/shard_map/ppermute | solution.py:249
  133.5 0.0 collective-permute-start.7
  133.5 1.0 collective-permute-start.6
  134.5 1.2 collective-permute-done.8
  135.8 3.1 %collective-permute-done.7 = bf16[16,8,256]{2,1,0:T(8,128)(2,1)S(1)} collective-permute-done((bf16[16,8,256]{2,1,0:T(8,128)(2,1)S(1)}, bf16[16,8,256]{2,1,0:T(8,128)(2,1)S(1)}, u32[]{:S(2)}, u32[]{:S(2)}) %collective-permute-start.7) | collective-permute-done | bytes 65568 | tf_op jit(solution)/shard_map/ppermute | solution.py:249
  138.9 0.7 collective-permute-done.6
  139.6 0.1 reshape.44
  139.7 0.7 copy.13
  (11 shorter events, 0.2 us)
Async XLA Ops:
  0.0 75.2 %copy-start.1 = (bf16[32,2,128,128]{3,2,1,0:T(8,128)(2,1)S(1)}, bf16[32,2,128,128]{3,2,1,0:T(8,128)(2,1)}, u32[]{:S(2)}) copy-start(bf16[32,2,128,128]{3,2,1,0:T(8,128)(2,1)} %own_ref.1) | copy-start | bytes 6291460
  0.0 71.6 %copy-start.2 = (bf16[2,128,128]{2,1,0:T(8,128)(2,1)S(1)}, bf16[2,128,128]{2,1,0:T(8,128)(2,1)}, u32[]{:S(2)}) copy-start(bf16[2,128,128]{2,1,0:T(8,128)(2,1)} %param.7) | copy-start | bytes 196612
  0.0 71.9 %copy-start.3 = (s32[2]{0:T(128)S(1)}, s32[2]{0:T(128)}, u32[]{:S(2)}) copy-start(s32[2]{0:T(128)} %param.9) | copy-start | bytes 28
  0.0 73.8 %copy-start.4 = (s32[16]{0:T(128)S(1)}, s32[16]{0:T(128)}, u32[]{:S(2)}) copy-start(s32[16]{0:T(128)} %param.8) | copy-start | bytes 196
  0.0 75.2 %collective-permute-start = (bf16[32,2,128,128]{3,2,1,0:T(8,128)(2,1)}, bf16[32,2,128,128]{3,2,1,0:T(8,128)(2,1)}, u32[]{:S(2)}, u32[]{:S(2)}) collective-permute-start(bf16[32,2,128,128]{3,2,1,0:T(8,128)(2,1)} %own_ref.1), channel_id=1, source_target_pairs={{0,1},{1,0},{2,3},{3,2},{4,5},{5,4},{6,7},{7,6},{8,9},{9,8},{10,11... | collective-permute-start | bytes 6291464 | tf_op jit(solution)/shard_map/ppermute | solution.py:276
  65.2 39.5 %collective-permute-start.3 = (bf16[24,2,128,128]{3,2,1,0:T(8,128)(2,1)}, bf16[24,2,128,128]{3,2,1,0:T(8,128)(2,1)}, u32[]{:S(2)}, u32[]{:S(2)}) collective-permute-start(bf16[24,2,128,128]{3,2,1,0:T(8,128)(2,1)} %get-tuple-element.19), channel_id=1, source_target_pairs={{0,2},{1,3},{2,4},{3,5},{4,6},{5,7},{6,8},{7,9},{8,10},{9,11},{10,... | collective-permute-start | bytes 4718600 | tf_op jit(solution)/shard_map/ppermute | solution.py:266
  75.2 7.1 %copy-start.6 = (bf16[4,2,128,128]{3,2,1,0:T(8,128)(2,1)S(1)}, bf16[4,2,128,128]{3,2,1,0:T(8,128)(2,1)}, u32[]{:S(2)}) copy-start(bf16[4,2,128,128]{3,2,1,0:T(8,128)(2,1)} %get-tuple-element.18) | copy-start | bytes 786436
  75.2 9.3 %copy-start = (bf16[32,2,128,128]{3,2,1,0:T(8,128)(2,1)S(1)}, bf16[32,2,128,128]{3,2,1,0:T(8,128)(2,1)}, u32[]{:S(2)}) copy-start(bf16[32,2,128,128]{3,2,1,0:T(8,128)(2,1)} %green_ref.1) | copy-start | bytes 6291460
  82.2 30.7 %collective-permute-start.2 = (bf16[4,2,128,128]{3,2,1,0:T(8,128)(2,1)S(1)}, bf16[4,2,128,128]{3,2,1,0:T(8,128)(2,1)S(1)}, u32[]{:S(2)}, u32[]{:S(2)}) collective-permute-start(bf16[4,2,128,128]{3,2,1,0:T(8,128)(2,1)S(1)} %copy-done.6), channel_id=1, source_target_pairs={{0,2},{1,3},{2,4},{3,5},{4,6},{5,7},{6,8},{7,9},{8,10},{9,11},{10,... | collective-permute-start | bytes 786440 | tf_op jit(solution)/shard_map/ppermute | solution.py:279
  84.5 10.4 %copy-start.5 = (bf16[4,2,128,128]{3,2,1,0:T(8,128)(2,1)S(1)}, bf16[4,2,128,128]{3,2,1,0:T(8,128)(2,1)}, u32[]{:S(2)}) copy-start(bf16[4,2,128,128]{3,2,1,0:T(8,128)(2,1)} %get-tuple-element.17) | copy-start | bytes 786436
  94.9 20.5 %collective-permute-start.1 = (bf16[4,2,128,128]{3,2,1,0:T(8,128)(2,1)S(1)}, bf16[4,2,128,128]{3,2,1,0:T(8,128)(2,1)S(1)}, u32[]{:S(2)}, u32[]{:S(2)}) collective-permute-start(bf16[4,2,128,128]{3,2,1,0:T(8,128)(2,1)S(1)} %copy-done.5), channel_id=1, source_target_pairs={{0,2},{1,3},{2,4},{3,5},{4,6},{5,7},{6,8},{7,9},{8,10},{9,11},{10,... | collective-permute-start | bytes 786440 | tf_op jit(solution)/shard_map/ppermute | solution.py:284
  117.3 2.0 %collective-permute-start.4 = (bf16[16,64,256]{2,1,0:T(8,128)(2,1)S(1)}, bf16[16,64,256]{2,1,0:T(8,128)(2,1)S(1)}, u32[]{:S(2)}, u32[]{:S(2)}) collective-permute-start(bf16[16,64,256]{2,1,0:T(8,128)(2,1)S(1)} %get-tuple-element.22), channel_id=1, source_target_pairs={{0,1},{1,0},{2,3},{3,2},{4,5},{5,4},{6,7},{7,6},{8,9},{9,8},{10,11... | collective-permute-start | bytes 1572872 | tf_op jit(solution)/shard_map/ppermute | solution.py:238
  119.5 9.2 %collective-permute-start.5 = (bf16[4,16,8,256]{3,2,0,1:T(8,128)(2,1)S(1)}, bf16[4,16,8,256]{3,2,0,1:T(8,128)(2,1)S(1)}, u32[]{:S(2)}, u32[]{:S(2)}) collective-permute-start(bf16[4,16,8,256]{3,2,0,1:T(8,128)(2,1)S(1)} %fusion), channel_id=1, source_target_pairs={{0,2},{1,3},{2,0},{3,1},{4,6},{5,7},{6,4},{7,5},{8,10},{9,11},{10,... | collective-permute-start | bytes 786440 | tf_op jit(solution)/shard_map/ppermute | solution.py:243
  128.8 7.0 %collective-permute-start.8 = (bf16[16,8,256]{2,1,0:T(8,128)(2,1)S(1)}, bf16[16,8,256]{2,1,0:T(8,128)(2,1)S(1)}, u32[]{:S(2)}, u32[]{:S(2)}) collective-permute-start(bf16[16,8,256]{2,1,0:T(8,128)(2,1)S(1)} %get-tuple-element.24), channel_id=1, source_target_pairs={{0,12},{1,13},{2,14},{3,15},{4,0},{5,1},{6,2},{7,3},{8,4},{9,5},{1... | collective-permute-start | bytes 196616 | tf_op jit(solution)/shard_map/ppermute | solution.py:249
  133.5 5.3 %collective-permute-start.7 = (bf16[16,8,256]{2,1,0:T(8,128)(2,1)S(1)}, bf16[16,8,256]{2,1,0:T(8,128)(2,1)S(1)}, u32[]{:S(2)}, u32[]{:S(2)}) collective-permute-start(bf16[16,8,256]{2,1,0:T(8,128)(2,1)S(1)} %get-tuple-element.25), channel_id=1, source_target_pairs={{0,8},{1,9},{2,10},{3,11},{4,12},{5,13},{6,14},{7,15},{8,0},{9,1},... | collective-permute-start | bytes 196616 | tf_op jit(solution)/shard_map/ppermute | solution.py:249
  133.5 6.1 %collective-permute-start.6 = (bf16[16,8,256]{2,1,0:T(8,128)(2,1)S(1)}, bf16[16,8,256]{2,1,0:T(8,128)(2,1)S(1)}, u32[]{:S(2)}, u32[]{:S(2)}) collective-permute-start(bf16[16,8,256]{2,1,0:T(8,128)(2,1)S(1)} %get-tuple-element.23), channel_id=1, source_target_pairs={{0,4},{1,5},{2,6},{3,7},{4,8},{5,9},{6,10},{7,11},{8,12},{9,13},{1... | collective-permute-start | bytes 196616 | tf_op jit(solution)/shard_map/ppermute | solution.py:249

commit v7 on v6

--- a/solution.py
+++ b/solution.py
@@ -9,6 +9,7 @@
 from jax.sharding import PartitionSpec as P
 
 STEP = 8
+WIDE = 16
 PAIR = 2
 GROUPS = 1
 PARTS = (24, 4, 4)
@@ -38,10 +39,11 @@
 def cut(blocks, sizes):
     return pl.pallas_call(
         functools.partial(cut_kernel, sizes),
-        out_shape=[jax.ShapeDtypeStruct((size,) + blocks.shape[1:], blocks.dtype) for size in sizes],
+        out_shape=[pltpu.VMEM((size,) + blocks.shape[1:], blocks.dtype) for size in sizes],
         in_specs=[pl.BlockSpec(memory_space=pl.ANY)],
-        out_specs=[pl.BlockSpec(memory_space=pl.ANY)] * len(sizes),
+        out_specs=[pl.BlockSpec(memory_space=pltpu.VMEM)] * len(sizes),
         scratch_shapes=[pltpu.SemaphoreType.DMA((len(sizes),))],
+        compiler_params=pltpu.CompilerParams(vmem_limit_bytes=8 * MIB),
     )(blocks)
 
 
@@ -82,8 +84,8 @@
 def project(left, right, own, other):
     energies, _, orbitals, _ = own.shape
     width = 2 * orbitals
-    steps = energies // STEP
-    slots = 2 * energies + STEP
+    steps = energies // WIDE
+    slots = 2 * energies + WIDE
     return pl.pallas_call(
         functools.partial(project_kernel, steps),
         out_shape=jax.ShapeDtypeStruct((slots, orbitals, width), jnp.bfloat16),
@@ -92,52 +94,68 @@
             pl.BlockSpec((orbitals, width), lambda t: (0, 0)),
             pl.BlockSpec((width, width), lambda t: (0, 0)),
             pl.BlockSpec(
-                (STEP, 2, orbitals, orbitals), lambda t: (jnp.minimum(t, steps - 1), 0, 0, 0)
+                (WIDE, 2, orbitals, orbitals), lambda t: (jnp.minimum(t, steps - 1), 0, 0, 0)
             ),
             pl.BlockSpec(
-                (STEP, 2, orbitals, orbitals),
+                (WIDE, 2, orbitals, orbitals),
                 lambda t: (jnp.clip(t - steps, 0, steps - 1), 0, 0, 0),
             ),
         ],
-        out_specs=pl.BlockSpec((STEP, orbitals, width), lambda t: (t, 0, 0)),
+        out_specs=pl.BlockSpec((WIDE, orbitals, width), lambda t: (t, 0, 0)),
         compiler_params=pltpu.CompilerParams(vmem_limit_bytes=16 * MIB),
     )(left, right, own, other)
 
 
-def add_products(place_ref, proj_ref, green_ref, total_ref, start):
+def pair_place(shift, offset, far, facts_ref, zero_place):
+    low, high, base, limit, e_dev = (facts_ref[i] for i in range(5))
+    reach = offset + shift
+    energy = base + offset
+    if far:
+        energy = energy - 2 * e_dev
+    met = reach >= limit if far else reach < limit
+    met = met & (energy >= low) & (energy + shift < high)
+    if far:
+        reach = jnp.where(reach >= 2 * e_dev, reach - 2 * e_dev, reach)
+    return jnp.where(met, reach, zero_place)
+
+
+def add_products(shifts_ref, facts_ref, proj_ref, green_ref, total_ref, start, far, offset):
     step = green_ref.shape[0]
-    first = pl.program_id(0) * step
+    first = pl.program_id(0) * step + offset
     photons, rows, width = total_ref.shape
+    zero_place = proj_ref.shape[0] - 1
     for w in range(0, photons, PAIR):
+        shifts = [shifts_ref[start + w + v] for v in range(PAIR)]
         total = total_ref[w : w + PAIR].reshape(PAIR * rows, width)
         for u in range(step):
-            left = jnp.concatenate(
-                [proj_ref[place_ref[first + u, start + w + v]] for v in range(PAIR)], 0
-            )
+            places = [pair_place(shift, first + u, far, facts_ref, zero_place) for shift in shifts]
+            left = jnp.concatenate([proj_ref[place] for place in places], 0)
             right = rotated(green_ref[u, 0], green_ref[u, 1])
             total += jnp.dot(left, right, preferred_element_type=jnp.float32)
         total_ref[w : w + PAIR] = total.reshape(PAIR, rows, width)
 
 
-def near_kernel(place_ref, proj_ref, green_ref, total_ref):
+def near_kernel(shifts_ref, facts_ref, proj_ref, green_ref, total_ref):
     @pl.when(pl.program_id(0) == 0)
     def _():
         total_ref[...] = jnp.zeros_like(total_ref)
 
-    add_products(place_ref, proj_ref, green_ref, total_ref, 0)
-
-
-def far_kernel(place_ref, proj_ref, green_ref, before_ref, total_ref):
+    add_products(shifts_ref, facts_ref, proj_ref, green_ref, total_ref, 0, False, 0)
+
+
+def far_kernel(offset, shifts_ref, facts_ref, proj_ref, green_ref, before_ref, total_ref):
     @pl.when(pl.program_id(0) == 0)
     def _():
         total_ref[...] = before_ref[...]
 
-    add_products(place_ref, proj_ref, green_ref, total_ref, 0)
+    add_products(shifts_ref, facts_ref, proj_ref, green_ref, total_ref, 0, True, offset)
 
 
 def last_kernel(
     start,
-    place_ref,
+    offset,
+    shifts_ref,
+    facts_ref,
     core_ref,
     proj_ref,
     green_ref,
@@ -150,7 +168,7 @@
     def _():
         total_ref[...] = before_ref[...]
 
-    add_products(place_ref, proj_ref, green_ref, total_ref, start)
+    add_products(shifts_ref, facts_ref, proj_ref, green_ref, total_ref, start, True, offset)
 
     @pl.when(pl.program_id(0) == pl.num_programs(0) - 1)
     def _():
@@ -162,16 +180,16 @@
         send_ref[...] = total_ref[:, pl.ds(other, half), :].astype(send_ref.dtype)
 
 
-def products(place, proj, green, before=None, core=None, group=0):
+def products(shifts, facts, proj, green, offset=0, before=None, core=None, group=0):
     slots, rows, width = proj.shape
     energies, _, orbitals, _ = green.shape
-    step = min(STEP, energies)
-    photons = place.shape[1]
+    step = math.gcd(STEP, energies)
+    photons = shifts.shape[0]
     smem = pl.BlockSpec(memory_space=pltpu.SMEM)
     if core is not None:
         photons //= GROUPS
     block = (photons, rows, width)
-    operands, specs = [place], [smem]
+    operands, specs = [shifts, facts], [smem, smem]
     if core is not None:
         operands.append(core)
         specs.append(smem)
@@ -188,7 +206,7 @@
     scratch = []
     if core is not None:
         half = (photons, rows // 2, width)
-        kernel = functools.partial(last_kernel, group * photons)
+        kernel = functools.partial(last_kernel, group * photons, offset)
         out_specs = [pl.BlockSpec(half, lambda t: (0, 0, 0))] * 2
         out_shape = [
             jax.ShapeDtypeStruct(half, jnp.float32),
@@ -196,7 +214,7 @@
         ]
         scratch = [pltpu.VMEM(block, jnp.float32)]
     else:
-        kernel = near_kernel if before is None else far_kernel
+        kernel = near_kernel if before is None else functools.partial(far_kernel, offset)
         out_specs = pl.BlockSpec(block, lambda t: (0, 0, 0))
         out_shape = jax.ShapeDtypeStruct(block, jnp.float32)
     return pl.pallas_call(
@@ -208,22 +226,6 @@
         scratch_shapes=scratch,
         compiler_params=pltpu.CompilerParams(vmem_limit_bytes=24 * MIB),
     )(*operands)
-
-
-def places(shifts, window, first_energy, core, e_dev):
-    zero_slot = 2 * e_dev
-    offset = jnp.arange(e_dev, dtype=jnp.int32)[:, None]
-    reach = offset + shifts[None, :]
-    limit = jnp.where(core == 0, 2 * e_dev, e_dev)
-
-    def inside(energy):
-        return (energy >= window[0]) & (energy < window[1])
-
-    own = first_energy + offset
-    near = inside(own) & inside(own + shifts[None, :]) & (reach < limit)
-    far = inside(own - 2 * e_dev) & inside(own - 2 * e_dev + shifts[None, :]) & (reach >= limit)
-    wrapped = jnp.where(reach >= 2 * e_dev, reach - 2 * e_dev, reach)
-    return jnp.where(near, reach, zero_slot), jnp.where(far, wrapped, zero_slot)
 
 
 def pick(blocks, place):
@@ -278,20 +280,22 @@
     pieces[1], proj = lax.optimization_barrier((pieces[1], proj))
     far.append(lax.ppermute(pieces[1], "energy", up))
 
-    near_place, far_place = places(shifts, window, index * e_dev, core, e_dev)
-    result = products(near_place, proj, greater)
+    limit = jnp.where(core == 0, 2 * e_dev, e_dev)
+    facts = jnp.stack([window[0], window[1], index * e_dev, limit, jnp.int32(e_dev)])
+    facts = facts.astype(jnp.int32)
+    result = products(shifts, facts, proj, greater)
     pieces[2], result = lax.optimization_barrier((pieces[2], result))
     far.append(lax.ppermute(pieces[2], "energy", up))
     core = core[None]
     first = 0
-    for k, size in enumerate(sizes):
-        place = far_place[first : first + size]
+    for block, size in zip(far[:-1], sizes):
+        result = products(shifts, facts, proj, block, offset=first, before=result)
         first += size
-        if k < len(sizes) - 1:
-            result = products(place, proj, far[k], before=result)
     sums = []
     for group in range(GROUPS):
-        keep, send = products(place, proj, far[-1], before=result, core=core, group=group)
+        keep, send = products(
+            shifts, facts, proj, far[-1], offset=first, before=result, core=core, group=group
+        )
         sums.append(reduced(keep, send, planes, share))
     scale = 1.0 / math.sqrt(2.0 * orbitals * total)
     summed = jnp.concatenate(sums, 0) * scale

time: 141 us -> 78.9 us (0.56)
  Pallas kernels: 94.1 us -> 29.6 us
  waiting for transfers between devices: 20.4 us -> 24.7 us
  other arithmetic: 2.79 us -> 0.34 us
    pallas_call x1, Pallas kernels: 64.7 us -> 1.32 us  [cut(): pl.pallas_call(functools.partial(cut_kernel, sizes), out_shape=[pltpu.VME...]
    ppermute x1, waiting for transfers between devices: 6.31 us -> 10.7 us  [on_device(): far = [lax.ppermute(pieces[0], 'energy', up)]]
    unnamed x16 -> x14, local copies, waits for them, and re-layouts: 0.26 us -> 1.85 us
  transfers between devices with their start and end apart: 9 -> 9, of which waited for: 7 -> 7; matrix products, arithmetic and copies ran while one was open for 3% -> 2% of each run, Pallas kernels for 66% -> 35%
where the time goes in v7:
time: 78.9 us; the launch traced here: 78.6 us
  Pallas kernels  29.6 us (38%)
  waiting for transfers between devices  24.7 us (31%)
  starting transfers between devices  20.2 us (26%)
  local copies, waits for them, and re-layouts  3.56 us (5%)
    pallas_call x4, Pallas kernels, products(): pl.pallas_call(kernel, out_shape=out_shape, grid=(energies // step,), in_...  22.5 us
    ppermute x1, waiting for transfers between devices, on_device(): far = [lax.ppermute(pieces[0], 'energy', up)]  10.7 us
    ppermute x1, waiting for transfers between devices, reduced(): got = lax.ppermute(send, 'energy', [(i, i ^ 2) for i in range(devices)])  6.61 us
    ppermute x3, starting transfers between devices, reduced(): total = total + lax.ppermute(send, 'energy', route).astype(jnp.float32)  5.79 us
    pallas_call x1, Pallas kernels, project(): pl.pallas_call(functools.partial(project_kernel, steps), out_shape=jax.Sh...  5.77 us
    ppermute x1, starting transfers between devices, on_device(): far = [lax.ppermute(pieces[0], 'energy', up)]  5.59 us
    ppermute x3, waiting for transfers between devices, reduced(): total = total + lax.ppermute(send, 'energy', route).astype(jnp.float32)  5.05 us
    ppermute x1, starting transfers between devices, on_device(): far.append(lax.ppermute(pieces[2], 'energy', up))  3.43 us
  transfers between devices with their start and end apart: 9, of which 7 were waited for; matrix products, arithmetic and copies ran while one was open for 2% of the time, Pallas kernels for 35%

profile of v7, /device:TPU:0, one launch (start us, length us, event | category | flops | bytes accessed | tf_op | source)
XLA Modules:
  0.0 78.6 jit_solution(5703270434103070811)
XLA Ops:
  0.0 0.5 collective-permute-start
  0.5 0.0 copy-start
  0.5 1.6 %copy-done = bf16[32,2,128,128]{3,2,1,0:T(8,128)(2,1)S(1)} copy-done((bf16[32,2,128,128]{3,2,1,0:T(8,128)(2,1)S(1)}, bf16[32,2,128,128]{3,2,1,0:T(8,128)(2,1)}, u32[]{:S(2)}) %copy-start) | copy-done | bytes 2097176
  2.0 0.0 copy-start.4
  2.0 0.0 copy-start.5
  2.0 0.0 copy-start.2
  2.1 1.3 %shard_map.55 = (bf16[24,2,128,128]{3,2,1,0:T(8,128)(2,1)}, bf16[4,2,128,128]{3,2,1,0:T(8,128)(2,1)S(1)}, bf16[4,2,128,128]{3,2,1,0:T(8,128)(2,1)S(1)}) custom-call(bf16[32,2,128,128]{3,2,1,0:T(8,128)(2,1)S(1)} %copy-done), custom_call_target="tpu_custom_call" | custom-call | tf_op jit(solution)/shard_map/pallas_call | solution.py:40
  3.4 5.6 %collective-permute-start.3 = (bf16[24,2,128,128]{3,2,1,0:T(8,128)(2,1)}, bf16[24,2,128,128]{3,2,1,0:T(8,128)(2,1)}, u32[]{:S(2)}, u32[]{:S(2)}) collective-permute-start(bf16[24,2,128,128]{3,2,1,0:T(8,128)(2,1)} %get-tuple-element.19), channel_id=1, source_target_pairs={{0,2},{1,3},{2,4},{3,5},{4,6},{5,7},{6,8},{7,9},{8,10},{9,11},{10,... | collective-permute-start | bytes 4718600 | tf_op jit(solution)/shard_map/ppermute | solution.py:268
  9.0 0.8 %copy.20 = bf16[2,4,2,2,8,128]{5,4,1,2,3,0:T(8,128)(2,1)S(1)} copy(bf16[2,4,2,2,8,128]{5,4,3,2,1,0:T(8,128)(2,1)} %bitcast.58) | data formatting | bytes 131072 | tf_op jit(solution)/shard_map/reshape | solution.py:271
  9.8 0.0 copy-done.4
  9.8 0.1 copy.14
  10.0 0.1 copy.15
  10.1 0.0 copy-done.5
  10.1 0.1 pad_add_fusion.facts_ref
  10.2 0.0 copy-start.1
  10.3 0.0 copy-start.3
  10.3 0.0 collective-permute-done.other_ref
  10.3 0.0 copy-done.2
  10.3 5.8 %shard_map.56.proj_ref = bf16[80,128,256]{2,1,0:T(8,128)(2,1)S(1)} custom-call(bf16[128,256]{1,0:T(8,128)(2,1)S(1)} %pad_maximum_fusion.left_ref, bf16[256,256]{1,0:T(8,128)(2,1)S(1)} %maximum_maximum_fusion.right_ref, bf16[32,2,128,128]{3,2,1,0:T(8,128)(2,1)S(1)} %copy-done.2, bf16[32,2,128,128]{3,2,1,0:T(8,128)(2,1)} %collective-permute-done.other_ref), custom_call_target="tpu_custom_call" | custom-call | tf_op jit(solution)/shard_map/pallas_call | solution.py:89
  16.1 0.0 copy-done.1
  16.1 0.0 copy-done.3
  16.1 10.3 %shard_map.57.before_ref = f32[16,128,256]{2,1,0:T(8,128)S(1)} custom-call(s32[16]{0:T(128)S(1)} %copy-done.3, s32[5]{0:T(128)S(1)} %pad_add_fusion.facts_ref, bf16[80,128,256]{2,1,0:T(8,128)(2,1)S(1)} %shard_map.56.proj_ref, bf16[32,2,128,128]{3,2,1,0:T(8,128)(2,1)S(1)} %copy-done.1), custom_call_target="tpu_custom_call" | custom-call | tf_op jit(solution)/shard_map/pallas_call | solution.py:220
  26.4 2.3 %collective-permute-start.2 = (bf16[4,2,128,128]{3,2,1,0:T(8,128)(2,1)S(1)}, bf16[4,2,128,128]{3,2,1,0:T(8,128)(2,1)S(1)}, u32[]{:S(2)}, u32[]{:S(2)}) collective-permute-start(bf16[4,2,128,128]{3,2,1,0:T(8,128)(2,1)S(1)} %get-tuple-element.18), channel_id=1, source_target_pairs={{0,2},{1,3},{2,4},{3,5},{4,6},{5,7},{6,8},{7,9},{8,10},{9,11},{10,... | collective-permute-start | bytes 786440 | tf_op jit(solution)/shard_map/ppermute | solution.py:281
  28.7 3.4 %collective-permute-start.1 = (bf16[4,2,128,128]{3,2,1,0:T(8,128)(2,1)S(1)}, bf16[4,2,128,128]{3,2,1,0:T(8,128)(2,1)S(1)}, u32[]{:S(2)}, u32[]{:S(2)}) collective-permute-start(bf16[4,2,128,128]{3,2,1,0:T(8,128)(2,1)S(1)} %get-tuple-element.17), channel_id=1, source_target_pairs={{0,2},{1,3},{2,4},{3,5},{4,6},{5,7},{6,8},{7,9},{8,10},{9,11},{10,... | collective-permute-start | bytes 786440 | tf_op jit(solution)/shard_map/ppermute | solution.py:288
  32.1 10.7 %collective-permute-done.3.green_ref = bf16[24,2,128,128]{3,2,1,0:T(8,128)(2,1)} collective-permute-done((bf16[24,2,128,128]{3,2,1,0:T(8,128)(2,1)}, bf16[24,2,128,128]{3,2,1,0:T(8,128)(2,1)}, u32[]{:S(2)}, u32[]{:S(2)}) %collective-permute-start.3) | collective-permute-done | bytes 1572896 | tf_op jit(solution)/shard_map/ppermute | solution.py:268
  42.8 8.4 %shard_map.58.before_ref = f32[16,128,256]{2,1,0:T(8,128)S(1)} custom-call(s32[16]{0:T(128)S(1)} %copy-done.3, s32[5]{0:T(128)S(1)} %pad_add_fusion.facts_ref, bf16[80,128,256]{2,1,0:T(8,128)(2,1)S(1)} %shard_map.56.proj_ref, bf16[24,2,128,128]{3,2,1,0:T(8,128)(2,1)} %collective-permute-done.3.green_ref, f32[16,128,256]{2,1,0:T(8,128)S(1)} %shard_map.57.before_ref), custom_call_target="tpu_custom_call" | custom-call | tf_op jit(solution)/shard_map/pallas_call | solution.py:220
  51.3 0.0 collective-permute-done.2.green_ref
  51.3 1.8 %shard_map.59.before_ref = f32[16,128,256]{2,1,0:T(8,128)S(1)} custom-call(s32[16]{0:T(128)S(1)} %copy-done.3, s32[5]{0:T(128)S(1)} %pad_add_fusion.facts_ref, bf16[80,128,256]{2,1,0:T(8,128)(2,1)S(1)} %shard_map.56.proj_ref, bf16[4,2,128,128]{3,2,1,0:T(8,128)(2,1)S(1)} %collective-permute-done.2.green_ref, f32[16,128,256]{2,1,0:T(8,128)S(1)} %shard_map.58.before_ref), custom_call_target="tpu_custom_call" | custom-call | tf_op jit(solution)/shard_map/pallas_call | solution.py:220
  53.1 0.5 collective-permute-done.1.green_ref
  53.6 2.0 %shard_map.60 = (f32[16,64,256]{2,1,0:T(8,128)S(1)}, bf16[16,64,256]{2,1,0:T(8,128)(2,1)S(1)}) custom-call(s32[16]{0:T(128)S(1)} %copy-done.3, s32[5]{0:T(128)S(1)} %pad_add_fusion.facts_ref, s32[1]{0:T(128)} %bitcast.2.core_ref, bf16[80,128,256]{2,1,0:T(8,128)(2,1)S(1)} %shard_map.56.proj_ref, ...), custom_call_target="tpu_custom_call" | custom-call | tf_op jit(solution)/shard_map/pallas_call | solution.py:220
  55.5 0.1 collective-permute-start.4
  55.6 1.9 %collective-permute-done.4 = bf16[16,64,256]{2,1,0:T(8,128)(2,1)S(1)} collective-permute-done((bf16[16,64,256]{2,1,0:T(8,128)(2,1)S(1)}, bf16[16,64,256]{2,1,0:T(8,128)(2,1)S(1)}, u32[]{:S(2)}, u32[]{:S(2)}) %collective-permute-start.4) | collective-permute-done | bytes 524320 | tf_op jit(solution)/shard_map/ppermute | solution.py:240
  57.5 0.1 convert_add_fusion
  57.7 2.5 %collective-permute-start.5 = (bf16[4,16,8,256]{3,2,0,1:T(8,128)(2,1)S(1)}, bf16[4,16,8,256]{3,2,0,1:T(8,128)(2,1)S(1)}, u32[]{:S(2)}, u32[]{:S(2)}) collective-permute-start(bf16[4,16,8,256]{3,2,0,1:T(8,128)(2,1)S(1)} %fusion), channel_id=1, source_target_pairs={{0,2},{1,3},{2,0},{3,1},{4,6},{5,7},{6,4},{7,5},{8,10},{9,11},{10,... | collective-permute-start | bytes 786440 | tf_op jit(solution)/shard_map/ppermute | solution.py:245
  60.2 6.6 %collective-permute-done.5 = bf16[4,16,8,256]{3,2,0,1:T(8,128)(2,1)S(1)} collective-permute-done((bf16[4,16,8,256]{3,2,0,1:T(8,128)(2,1)S(1)}, bf16[4,16,8,256]{3,2,0,1:T(8,128)(2,1)S(1)}, u32[]{:S(2)}, u32[]{:S(2)}) %collective-permute-start.5) | collective-permute-done | bytes 262176 | tf_op jit(solution)/shard_map/ppermute | solution.py:245
  66.8 0.1 bitcast_add_fusion
  67.0 4.8 %collective-permute-start.8 = (bf16[16,8,256]{2,1,0:T(8,128)(2,1)S(1)}, bf16[16,8,256]{2,1,0:T(8,128)(2,1)S(1)}, u32[]{:S(2)}, u32[]{:S(2)}) collective-permute-start(bf16[16,8,256]{2,1,0:T(8,128)(2,1)S(1)} %get-tuple-element.24), channel_id=1, source_target_pairs={{0,12},{1,13},{2,14},{3,15},{4,0},{5,1},{6,2},{7,3},{8,4},{9,5},{1... | collective-permute-start | bytes 196616 | tf_op jit(solution)/shard_map/ppermute | solution.py:251
  71.7 0.0 collective-permute-start.7
  71.7 1.0 %collective-permute-start.6 = (bf16[16,8,256]{2,1,0:T(8,128)(2,1)S(1)}, bf16[16,8,256]{2,1,0:T(8,128)(2,1)S(1)}, u32[]{:S(2)}, u32[]{:S(2)}) collective-permute-start(bf16[16,8,256]{2,1,0:T(8,128)(2,1)S(1)} %get-tuple-element.23), channel_id=1, source_target_pairs={{0,4},{1,5},{2,6},{3,7},{4,8},{5,9},{6,10},{7,11},{8,12},{9,13},{1... | collective-permute-start | bytes 196616 | tf_op jit(solution)/shard_map/ppermute | solution.py:251
  72.7 1.2 %collective-permute-done.8 = bf16[16,8,256]{2,1,0:T(8,128)(2,1)S(1)} collective-permute-done((bf16[16,8,256]{2,1,0:T(8,128)(2,1)S(1)}, bf16[16,8,256]{2,1,0:T(8,128)(2,1)S(1)}, u32[]{:S(2)}, u32[]{:S(2)}) %collective-permute-start.8) | collective-permute-done | bytes 65568 | tf_op jit(solution)/shard_map/ppermute | solution.py:251
  74.0 3.1 %collective-permute-done.7 = bf16[16,8,256]{2,1,0:T(8,128)(2,1)S(1)} collective-permute-done((bf16[16,8,256]{2,1,0:T(8,128)(2,1)S(1)}, bf16[16,8,256]{2,1,0:T(8,128)(2,1)S(1)}, u32[]{:S(2)}, u32[]{:S(2)}) %collective-permute-start.7) | collective-permute-done | bytes 65568 | tf_op jit(solution)/shard_map/ppermute | solution.py:251
  77.1 0.7 collective-permute-done.6
  77.8 0.1 reshape.21
  77.9 0.7 copy.13
  (8 shorter events, 0.2 us)
Async XLA Ops:
  0.0 10.3 %collective-permute-start = (bf16[32,2,128,128]{3,2,1,0:T(8,128)(2,1)}, bf16[32,2,128,128]{3,2,1,0:T(8,128)(2,1)}, u32[]{:S(2)}, u32[]{:S(2)}) collective-permute-start(bf16[32,2,128,128]{3,2,1,0:T(8,128)(2,1)} %own_ref.1), channel_id=1, source_target_pairs={{0,1},{1,0},{2,3},{3,2},{4,5},{5,4},{6,7},{7,6},{8,9},{9,8},{10,11... | collective-permute-start | bytes 6291464 | tf_op jit(solution)/shard_map/ppermute | solution.py:278
  0.5 1.6 %copy-start = (bf16[32,2,128,128]{3,2,1,0:T(8,128)(2,1)S(1)}, bf16[32,2,128,128]{3,2,1,0:T(8,128)(2,1)}, u32[]{:S(2)}) copy-start(bf16[32,2,128,128]{3,2,1,0:T(8,128)(2,1)} %green_ref.1) | copy-start | bytes 6291460
  2.0 7.8 %copy-start.4 = (bf16[2,128,128]{2,1,0:T(8,128)(2,1)S(1)}, bf16[2,128,128]{2,1,0:T(8,128)(2,1)}, u32[]{:S(2)}) copy-start(bf16[2,128,128]{2,1,0:T(8,128)(2,1)} %param.7) | copy-start | bytes 196612
  2.0 8.0 %copy-start.5 = (s32[2]{0:T(128)S(1)}, s32[2]{0:T(128)}, u32[]{:S(2)}) copy-start(s32[2]{0:T(128)} %param.9) | copy-start | bytes 28
  2.0 8.2 %copy-start.2 = (bf16[32,2,128,128]{3,2,1,0:T(8,128)(2,1)S(1)}, bf16[32,2,128,128]{3,2,1,0:T(8,128)(2,1)}, u32[]{:S(2)}) copy-start(bf16[32,2,128,128]{3,2,1,0:T(8,128)(2,1)} %own_ref.1) | copy-start | bytes 6291460
  3.4 39.4 %collective-permute-start.3 = (bf16[24,2,128,128]{3,2,1,0:T(8,128)(2,1)}, bf16[24,2,128,128]{3,2,1,0:T(8,128)(2,1)}, u32[]{:S(2)}, u32[]{:S(2)}) collective-permute-start(bf16[24,2,128,128]{3,2,1,0:T(8,128)(2,1)} %get-tuple-element.19), channel_id=1, source_target_pairs={{0,2},{1,3},{2,4},{3,5},{4,6},{5,7},{6,8},{7,9},{8,10},{9,11},{10,... | collective-permute-start | bytes 4718600 | tf_op jit(solution)/shard_map/ppermute | solution.py:268
  10.2 5.8 %copy-start.1 = (bf16[32,2,128,128]{3,2,1,0:T(8,128)(2,1)S(1)}, bf16[32,2,128,128]{3,2,1,0:T(8,128)(2,1)}, u32[]{:S(2)}) copy-start(bf16[32,2,128,128]{3,2,1,0:T(8,128)(2,1)} %green_ref.1) | copy-start | bytes 6291460
  10.3 5.8 %copy-start.3 = (s32[16]{0:T(128)S(1)}, s32[16]{0:T(128)}, u32[]{:S(2)}) copy-start(s32[16]{0:T(128)} %shifts_ref.7) | copy-start | bytes 196
  26.4 24.9 %collective-permute-start.2 = (bf16[4,2,128,128]{3,2,1,0:T(8,128)(2,1)S(1)}, bf16[4,2,128,128]{3,2,1,0:T(8,128)(2,1)S(1)}, u32[]{:S(2)}, u32[]{:S(2)}) collective-permute-start(bf16[4,2,128,128]{3,2,1,0:T(8,128)(2,1)S(1)} %get-tuple-element.18), channel_id=1, source_target_pairs={{0,2},{1,3},{2,4},{3,5},{4,6},{5,7},{6,8},{7,9},{8,10},{9,11},{10,... | collective-permute-start | bytes 786440 | tf_op jit(solution)/shard_map/ppermute | solution.py:281
  28.7 24.9 %collective-permute-start.1 = (bf16[4,2,128,128]{3,2,1,0:T(8,128)(2,1)S(1)}, bf16[4,2,128,128]{3,2,1,0:T(8,128)(2,1)S(1)}, u32[]{:S(2)}, u32[]{:S(2)}) collective-permute-start(bf16[4,2,128,128]{3,2,1,0:T(8,128)(2,1)S(1)} %get-tuple-element.17), channel_id=1, source_target_pairs={{0,2},{1,3},{2,4},{3,5},{4,6},{5,7},{6,8},{7,9},{8,10},{9,11},{10,... | collective-permute-start | bytes 786440 | tf_op jit(solution)/shard_map/ppermute | solution.py:288
  55.5 2.0 %collective-permute-start.4 = (bf16[16,64,256]{2,1,0:T(8,128)(2,1)S(1)}, bf16[16,64,256]{2,1,0:T(8,128)(2,1)S(1)}, u32[]{:S(2)}, u32[]{:S(2)}) collective-permute-start(bf16[16,64,256]{2,1,0:T(8,128)(2,1)S(1)} %get-tuple-element.22), channel_id=1, source_target_pairs={{0,1},{1,0},{2,3},{3,2},{4,5},{5,4},{6,7},{7,6},{8,9},{9,8},{10,11... | collective-permute-start | bytes 1572872 | tf_op jit(solution)/shard_map/ppermute | solution.py:240
  57.7 9.2 %collective-permute-start.5 = (bf16[4,16,8,256]{3,2,0,1:T(8,128)(2,1)S(1)}, bf16[4,16,8,256]{3,2,0,1:T(8,128)(2,1)S(1)}, u32[]{:S(2)}, u32[]{:S(2)}) collective-permute-start(bf16[4,16,8,256]{3,2,0,1:T(8,128)(2,1)S(1)} %fusion), channel_id=1, source_target_pairs={{0,2},{1,3},{2,0},{3,1},{4,6},{5,7},{6,4},{7,5},{8,10},{9,11},{10,... | collective-permute-start | bytes 786440 | tf_op jit(solution)/shard_map/ppermute | solution.py:245
  67.0 7.0 %collective-permute-start.8 = (bf16[16,8,256]{2,1,0:T(8,128)(2,1)S(1)}, bf16[16,8,256]{2,1,0:T(8,128)(2,1)S(1)}, u32[]{:S(2)}, u32[]{:S(2)}) collective-permute-start(bf16[16,8,256]{2,1,0:T(8,128)(2,1)S(1)} %get-tuple-element.24), channel_id=1, source_target_pairs={{0,12},{1,13},{2,14},{3,15},{4,0},{5,1},{6,2},{7,3},{8,4},{9,5},{1... | collective-permute-start | bytes 196616 | tf_op jit(solution)/shard_map/ppermute | solution.py:251
  71.7 5.3 %collective-permute-start.7 = (bf16[16,8,256]{2,1,0:T(8,128)(2,1)S(1)}, bf16[16,8,256]{2,1,0:T(8,128)(2,1)S(1)}, u32[]{:S(2)}, u32[]{:S(2)}) collective-permute-start(bf16[16,8,256]{2,1,0:T(8,128)(2,1)S(1)} %get-tuple-element.25), channel_id=1, source_target_pairs={{0,8},{1,9},{2,10},{3,11},{4,12},{5,13},{6,14},{7,15},{8,0},{9,1},... | collective-permute-start | bytes 196616 | tf_op jit(solution)/shard_map/ppermute | solution.py:251
  71.7 6.1 %collective-permute-start.6 = (bf16[16,8,256]{2,1,0:T(8,128)(2,1)S(1)}, bf16[16,8,256]{2,1,0:T(8,128)(2,1)S(1)}, u32[]{:S(2)}, u32[]{:S(2)}) collective-permute-start(bf16[16,8,256]{2,1,0:T(8,128)(2,1)S(1)} %get-tuple-element.23), channel_id=1, source_target_pairs={{0,4},{1,5},{2,6},{3,7},{4,8},{5,9},{6,10},{7,11},{8,12},{9,13},{1... | collective-permute-start | bytes 196616 | tf_op jit(solution)/shard_map/ppermute | solution.py:251

commit v8 on v7

--- a/solution.py
+++ b/solution.py
@@ -12,7 +12,7 @@
 WIDE = 16
 PAIR = 2
 GROUPS = 1
-PARTS = (24, 4, 4)
+PARTS = (16, 8, 6, 2)
 MIB = 1 << 20
 
 
@@ -22,10 +22,9 @@
     return jnp.concatenate([top, bottom], 0)
 
 
-def cut_kernel(sizes, source_ref, *refs):
+def cut_kernel(first, sizes, source_ref, *refs):
     sems = refs[-1]
     copies = []
-    first = 0
     for k, size in enumerate(sizes):
         copies.append(
             pltpu.make_async_copy(source_ref.at[pl.ds(first, size)], refs[k], sems.at[k])
@@ -36,14 +35,14 @@
         copy.wait()
 
 
-def cut(blocks, sizes):
+def cut(blocks, first, sizes, limit):
     return pl.pallas_call(
-        functools.partial(cut_kernel, sizes),
+        functools.partial(cut_kernel, first, sizes),
         out_shape=[pltpu.VMEM((size,) + blocks.shape[1:], blocks.dtype) for size in sizes],
         in_specs=[pl.BlockSpec(memory_space=pl.ANY)],
         out_specs=[pl.BlockSpec(memory_space=pltpu.VMEM)] * len(sizes),
         scratch_shapes=[pltpu.SemaphoreType.DMA((len(sizes),))],
-        compiler_params=pltpu.CompilerParams(vmem_limit_bytes=8 * MIB),
+        compiler_params=pltpu.CompilerParams(vmem_limit_bytes=limit * MIB),
     )(blocks)
 
 
@@ -264,7 +263,7 @@
     up = [(i, i + 2) for i in range(devices - 2)]
     across = [(i, i ^ 1) for i in range(devices)]
     sizes = [e_dev * part // 32 for part in PARTS]
-    pieces = list(cut(greater, sizes))
+    pieces = list(cut(greater, 0, sizes[:1], 50))
     far = [lax.ppermute(pieces[0], "energy", up)]
 
     planes = devices // 4
@@ -277,19 +276,21 @@
     )
     proj = project(left, right, lesser, lax.ppermute(lesser, "energy", across))
 
-    pieces[1], proj = lax.optimization_barrier((pieces[1], proj))
+    rest, proj = lax.optimization_barrier((greater, proj))
+    pieces += list(cut(rest, sizes[0], sizes[1:], 8))
     far.append(lax.ppermute(pieces[1], "energy", up))
 
     limit = jnp.where(core == 0, 2 * e_dev, e_dev)
     facts = jnp.stack([window[0], window[1], index * e_dev, limit, jnp.int32(e_dev)])
     facts = facts.astype(jnp.int32)
     result = products(shifts, facts, proj, greater)
-    pieces[2], result = lax.optimization_barrier((pieces[2], result))
-    far.append(lax.ppermute(pieces[2], "energy", up))
     core = core[None]
     first = 0
-    for block, size in zip(far[:-1], sizes):
-        result = products(shifts, facts, proj, block, offset=first, before=result)
+    for k, size in enumerate(sizes[:-1]):
+        if k + 2 < len(sizes):
+            pieces[k + 2], result = lax.optimization_barrier((pieces[k + 2], result))
+            far.append(lax.ppermute(pieces[k + 2], "energy", up))
+        result = products(shifts, facts, proj, far[k], offset=first, before=result)
         first += size
     sums = []
     for group in range(GROUPS):

time: 78.9 us -> 76.7 us (0.972)
  waiting for transfers between devices: 24.7 us -> 12 us
  local copies, waits for them, and re-layouts: 3.56 us -> 9.94 us
  starting transfers between devices: 20.2 us -> 22.8 us
  Pallas kernels: 29.6 us -> 31 us
    ppermute x1, waiting for transfers between devices: 10.7 us -> 0.01 us  [on_device(): far = [lax.ppermute(pieces[0], 'energy', up)]]
    unnamed x14 -> x22, local copies, waits for them, and re-layouts: 1.85 us -> 9.06 us
    ppermute x1 -> x2, starting transfers between devices: 3.43 us -> 6.23 us  [on_device(): far.append(lax.ppermute(pieces[k + 2], 'energy', up))]
    ppermute x3, waiting for transfers between devices: 5.05 us -> 3.25 us  [reduced(): total = total + lax.ppermute(send, 'energy', route).astype(jnp.float32)]
    pallas_call x4 -> x5, Pallas kernels: 22.5 us -> 24.1 us  [products(): pl.pallas_call(kernel, out_shape=out_shape, grid=(energies // step,), in_...]
    ppermute x1, starting transfers between devices: 2.55 us -> 1.58 us  [reduced(): got = lax.ppermute(send, 'energy', [(i, i ^ 2) for i in range(devices)])]
    ppermute x1, starting transfers between devices: 2.3 us -> 3.24 us  [on_device(): far.append(lax.ppermute(pieces[1], 'energy', up))]
    reshape x1, local copies, waits for them, and re-layouts: 0.85 us -> 0.02 us  [on_device(): rows = dipole.reshape(2, planes, 2, 2, share, orbitals)]
  transfers between devices with their start and end apart: 9 -> 10, of which waited for: 7 -> 4; matrix products, arithmetic and copies ran while one was open for 2% -> 0% of each run, Pallas kernels for 35% -> 39%
where the time goes in v8:
time: 76.7 us; the launch traced here: 76.3 us
  Pallas kernels  31 us (40%)
  starting transfers between devices  22.8 us (30%)
  waiting for transfers between devices  12 us (16%)
  local copies, waits for them, and re-layouts  9.94 us (13%)
    pallas_call x5, Pallas kernels, products(): pl.pallas_call(kernel, out_shape=out_shape, grid=(energies // step,), in_...  24.1 us
    unnamed x22, local copies, waits for them, and re-layouts  9.06 us
    ppermute x1, waiting for transfers between devices, reduced(): got = lax.ppermute(send, 'energy', [(i, i ^ 2) for i in range(devices)])  6.83 us
    ppermute x2, starting transfers between devices, on_device(): far.append(lax.ppermute(pieces[k + 2], 'energy', up))  6.23 us
    ppermute x3, starting transfers between devices, reduced(): total = total + lax.ppermute(send, 'energy', route).astype(jnp.float32)  5.76 us
    pallas_call x1, Pallas kernels, project(): pl.pallas_call(functools.partial(project_kernel, steps), out_shape=jax.Sh...  5.62 us
    ppermute x1, starting transfers between devices, on_device(): far = [lax.ppermute(pieces[0], 'energy', up)]  5.41 us
    ppermute x3, waiting for transfers between devices, reduced(): total = total + lax.ppermute(send, 'energy', route).astype(jnp.float32)  3.25 us
  transfers between devices with their start and end apart: 10, of which 4 were waited for; matrix products, arithmetic and copies ran while one was open for 0% of the time, Pallas kernels for 39%

profile of v8, /device:TPU:0, one launch (start us, length us, event | category | flops | bytes accessed | tf_op | source)
XLA Modules:
  0.0 76.3 jit_solution(15572877709997965432)
XLA Ops:
  0.0 0.5 collective-permute-start
  0.5 0.0 copy-start.2
  0.5 1.6 %copy-done.2 = bf16[32,2,128,128]{3,2,1,0:T(8,128)(2,1)S(1)} copy-done((bf16[32,2,128,128]{3,2,1,0:T(8,128)(2,1)S(1)}, bf16[32,2,128,128]{3,2,1,0:T(8,128)(2,1)}, u32[]{:S(2)}) %copy-start.2) | copy-done | bytes 2097176
  2.0 0.0 copy-start.8
  2.0 0.1 shard_map.57
  2.1 5.4 %collective-permute-start.1 = (bf16[16,2,128,128]{3,2,1,0:T(8,128)(2,1)S(1)}, bf16[16,2,128,128]{3,2,1,0:T(8,128)(2,1)}, u32[]{:S(2)}, u32[]{:S(2)}) collective-permute-start(bf16[16,2,128,128]{3,2,1,0:T(8,128)(2,1)S(1)} %shard_map.57), channel_id=1, source_target_pairs={{0,2},{1,3},{2,4},{3,5},{4,6},{5,7},{6,8},{7,9},{8,10},{9,11},{10,... | collective-permute-start | bytes 3145736 | tf_op jit(solution)/shard_map/ppermute | solution.py:267
  7.5 0.0 copy-done.8
  7.6 0.1 copy.15
  7.7 0.1 copy.14
  7.9 0.0 copy-start.3
  7.9 0.0 collective-permute-done.other_ref
  7.9 0.0 copy-start.4
  7.9 1.7 %copy-done.4 = bf16[32,2,128,128]{3,2,1,0:T(8,128)(2,1)S(1)} copy-done((bf16[32,2,128,128]{3,2,1,0:T(8,128)(2,1)S(1)}, bf16[32,2,128,128]{3,2,1,0:T(8,128)(2,1)}, u32[]{:S(2)}) %copy-start.4) | copy-done | bytes 2097176
  9.7 5.6 %shard_map.55.proj_ref = bf16[80,128,256]{2,1,0:T(8,128)(2,1)S(1)} custom-call(bf16[128,256]{1,0:T(8,128)(2,1)S(1)} %pad_maximum_fusion.left_ref, bf16[256,256]{1,0:T(8,128)(2,1)S(1)} %maximum_maximum_fusion.right_ref, bf16[32,2,128,128]{3,2,1,0:T(8,128)(2,1)S(1)} %copy-done.4, bf16[32,2,128,128]{3,2,1,0:T(8,128)(2,1)} %collective-permute-done.other_ref), custom_call_target="tpu_custom_call" | custom-call | tf_op jit(solution)/shard_map/pallas_call | solution.py:88
  15.3 0.0 copy-start
  15.3 2.3 %copy-done = bf16[80,128,256]{2,1,0:T(8,128)(2,1)} copy-done((bf16[80,128,256]{2,1,0:T(8,128)(2,1)}, bf16[80,128,256]{2,1,0:T(8,128)(2,1)S(1)}, u32[]{:S(2)}) %copy-start) | copy-done | bytes 5242904
  17.6 0.0 copy-done.3
  17.6 0.0 copy-start.9
  17.7 0.0 copy-start.5
  17.7 1.2 %shard_map.56 = (bf16[8,2,128,128]{3,2,1,0:T(8,128)(2,1)}, bf16[6,2,128,128]{3,2,1,0:T(8,128)(2,1)S(1)}, bf16[2,2,128,128]{3,2,1,0:T(8,128)(2,1)S(1)}) custom-call(bf16[32,2,128,128]{3,2,1,0:T(8,128)(2,1)S(1)} %copy-done.3), custom_call_target="tpu_custom_call" | custom-call | tf_op jit(solution)/shard_map/pallas_call | solution.py:39
  18.9 0.0 copy-start.6
  18.9 0.6 copy-done.6
  19.5 3.2 %collective-permute-start.4 = (bf16[8,2,128,128]{3,2,1,0:T(8,128)(2,1)}, bf16[8,2,128,128]{3,2,1,0:T(8,128)(2,1)}, u32[]{:S(2)}, u32[]{:S(2)}) collective-permute-start(bf16[8,2,128,128]{3,2,1,0:T(8,128)(2,1)} %get-tuple-element.23), channel_id=1, source_target_pairs={{0,2},{1,3},{2,4},{3,5},{4,6},{5,7},{6,8},{7,9},{8,10},{9,11},{10,... | collective-permute-start | bytes 1572872 | tf_op jit(solution)/shard_map/ppermute | solution.py:281
  22.8 0.0 copy-done.9
  22.8 0.1 pad_add_fusion.facts_ref
  22.9 0.0 copy-done.5
  22.9 0.0 copy-start.1
  22.9 2.5 %copy-done.1 = bf16[80,128,256]{2,1,0:T(8,128)(2,1)S(1)} copy-done((bf16[80,128,256]{2,1,0:T(8,128)(2,1)S(1)}, bf16[80,128,256]{2,1,0:T(8,128)(2,1)}, u32[]{:S(2)}) %copy-start.1) | copy-done | bytes 5242904
  25.4 10.2 %shard_map.58.before_ref = f32[16,128,256]{2,1,0:T(8,128)S(1)} custom-call(s32[16]{0:T(128)S(1)} %copy-done.5, s32[5]{0:T(128)S(1)} %pad_add_fusion.facts_ref, bf16[80,128,256]{2,1,0:T(8,128)(2,1)S(1)} %copy-done.1, bf16[32,2,128,128]{3,2,1,0:T(8,128)(2,1)S(1)} %copy-done.3), custom_call_target="tpu_custom_call" | custom-call | tf_op jit(solution)/shard_map/pallas_call | solution.py:219
  35.6 0.0 copy-start.7
  35.6 2.8 %collective-permute-start.3 = (bf16[6,2,128,128]{3,2,1,0:T(8,128)(2,1)S(1)}, bf16[6,2,128,128]{3,2,1,0:T(8,128)(2,1)S(1)}, u32[]{:S(2)}, u32[]{:S(2)}) collective-permute-start(bf16[6,2,128,128]{3,2,1,0:T(8,128)(2,1)S(1)} %get-tuple-element.22), channel_id=1, source_target_pairs={{0,2},{1,3},{2,4},{3,5},{4,6},{5,7},{6,8},{7,9},{8,10},{9,11},{10,... | collective-permute-start | bytes 1179656 | tf_op jit(solution)/shard_map/ppermute | solution.py:292
  38.4 0.0 collective-permute-done.1.green_ref
  38.5 6.0 %shard_map.59.before_ref = f32[16,128,256]{2,1,0:T(8,128)S(1)} custom-call(s32[16]{0:T(128)S(1)} %copy-done.5, s32[5]{0:T(128)S(1)} %pad_add_fusion.facts_ref, bf16[80,128,256]{2,1,0:T(8,128)(2,1)S(1)} %copy-done.1, bf16[16,2,128,128]{3,2,1,0:T(8,128)(2,1)} %collective-permute-done.1.green_ref, f32[16,128,256]{2,1,0:T(8,128)S(1)} %shard_map.58.before_ref), custom_call_target="tpu_custom_call" | custom-call | tf_op jit(solution)/shard_map/pallas_call | solution.py:219
  44.5 0.0 copy-done.7
  44.5 3.4 %collective-permute-start.2 = (bf16[2,2,128,128]{3,2,1,0:T(8,128)(2,1)S(1)}, bf16[2,2,128,128]{3,2,1,0:T(8,128)(2,1)S(1)}, u32[]{:S(2)}, u32[]{:S(2)}) collective-permute-start(bf16[2,2,128,128]{3,2,1,0:T(8,128)(2,1)S(1)} %copy-done.7), channel_id=1, source_target_pairs={{0,2},{1,3},{2,4},{3,5},{4,6},{5,7},{6,8},{7,9},{8,10},{9,11},{10,... | collective-permute-start | bytes 393224 | tf_op jit(solution)/shard_map/ppermute | solution.py:292
  47.9 0.0 collective-permute-done.4.green_ref
  47.9 3.4 %shard_map.60.before_ref = f32[16,128,256]{2,1,0:T(8,128)S(1)} custom-call(s32[16]{0:T(128)S(1)} %copy-done.5, s32[5]{0:T(128)S(1)} %pad_add_fusion.facts_ref, bf16[80,128,256]{2,1,0:T(8,128)(2,1)S(1)} %copy-done.1, bf16[8,2,128,128]{3,2,1,0:T(8,128)(2,1)} %collective-permute-done.4.green_ref, f32[16,128,256]{2,1,0:T(8,128)S(1)} %shard_map.59.before_ref), custom_call_target="tpu_custom_call" | custom-call | tf_op jit(solution)/shard_map/pallas_call | solution.py:219
  51.3 0.0 collective-permute-done.3.green_ref
  51.3 3.0 %shard_map.61.before_ref = f32[16,128,256]{2,1,0:T(8,128)S(1)} custom-call(s32[16]{0:T(128)S(1)} %copy-done.5, s32[5]{0:T(128)S(1)} %pad_add_fusion.facts_ref, bf16[80,128,256]{2,1,0:T(8,128)(2,1)S(1)} %copy-done.1, bf16[6,2,128,128]{3,2,1,0:T(8,128)(2,1)S(1)} %collective-permute-done.3.green_ref, f32[16,128,256]{2,1,0:T(8,128)S(1)} %shard_map.60.before_ref), custom_call_target="tpu_custom_call" | custom-call | tf_op jit(solution)/shard_map/pallas_call | solution.py:219
  54.3 0.0 collective-permute-done.2.green_ref
  54.4 1.4 %shard_map.62 = (f32[16,64,256]{2,1,0:T(8,128)S(1)}, bf16[16,64,256]{2,1,0:T(8,128)(2,1)S(1)}) custom-call(s32[16]{0:T(128)S(1)} %copy-done.5, s32[5]{0:T(128)S(1)} %pad_add_fusion.facts_ref, s32[1]{0:T(128)} %bitcast.2.core_ref, bf16[80,128,256]{2,1,0:T(8,128)(2,1)S(1)} %copy-done.1, bf16[2,2,128,128]{3,2,1,0:T(8,128)(2,1)S(1)} %collective-permute-done.2.green_ref, ...), custom_call_target="tpu_custom_call" | custom-call | tf_op jit(solution)/shard_map/pallas_call | solution.py:219
  55.8 0.1 collective-permute-start.5
  55.9 1.9 %collective-permute-done.5 = bf16[16,64,256]{2,1,0:T(8,128)(2,1)S(1)} collective-permute-done((bf16[16,64,256]{2,1,0:T(8,128)(2,1)S(1)}, bf16[16,64,256]{2,1,0:T(8,128)(2,1)S(1)}, u32[]{:S(2)}, u32[]{:S(2)}) %collective-permute-start.5) | collective-permute-done | bytes 524320 | tf_op jit(solution)/shard_map/ppermute | solution.py:239
  57.7 0.1 convert_add_fusion
  57.9 1.6 %collective-permute-start.6 = (bf16[4,16,8,256]{3,2,0,1:T(8,128)(2,1)S(1)}, bf16[4,16,8,256]{3,2,0,1:T(8,128)(2,1)S(1)}, u32[]{:S(2)}, u32[]{:S(2)}) collective-permute-start(bf16[4,16,8,256]{3,2,0,1:T(8,128)(2,1)S(1)} %fusion), channel_id=1, source_target_pairs={{0,2},{1,3},{2,0},{3,1},{4,6},{5,7},{6,4},{7,5},{8,10},{9,11},{10,... | collective-permute-start | bytes 786440 | tf_op jit(solution)/shard_map/ppermute | solution.py:244
  59.5 6.8 %collective-permute-done.6 = bf16[4,16,8,256]{3,2,0,1:T(8,128)(2,1)S(1)} collective-permute-done((bf16[4,16,8,256]{3,2,0,1:T(8,128)(2,1)S(1)}, bf16[4,16,8,256]{3,2,0,1:T(8,128)(2,1)S(1)}, u32[]{:S(2)}, u32[]{:S(2)}) %collective-permute-start.6) | collective-permute-done | bytes 262176 | tf_op jit(solution)/shard_map/ppermute | solution.py:244
  66.3 0.1 bitcast_add_fusion
  66.5 1.8 %collective-permute-start.7 = (bf16[16,8,256]{2,1,0:T(8,128)(2,1)S(1)}, bf16[16,8,256]{2,1,0:T(8,128)(2,1)S(1)}, u32[]{:S(2)}, u32[]{:S(2)}) collective-permute-start(bf16[16,8,256]{2,1,0:T(8,128)(2,1)S(1)} %get-tuple-element.27), channel_id=1, source_target_pairs={{0,4},{1,5},{2,6},{3,7},{4,8},{5,9},{6,10},{7,11},{8,12},{9,13},{1... | collective-permute-start | bytes 196616 | tf_op jit(solution)/shard_map/ppermute | solution.py:250
  68.3 2.6 %collective-permute-start.8 = (bf16[16,8,256]{2,1,0:T(8,128)(2,1)S(1)}, bf16[16,8,256]{2,1,0:T(8,128)(2,1)S(1)}, u32[]{:S(2)}, u32[]{:S(2)}) collective-permute-start(bf16[16,8,256]{2,1,0:T(8,128)(2,1)S(1)} %get-tuple-element.29), channel_id=1, source_target_pairs={{0,8},{1,9},{2,10},{3,11},{4,12},{5,13},{6,14},{7,15},{8,0},{9,1},... | collective-permute-start | bytes 196616 | tf_op jit(solution)/shard_map/ppermute | solution.py:250
  70.9 1.3 %collective-permute-start.9 = (bf16[16,8,256]{2,1,0:T(8,128)(2,1)S(1)}, bf16[16,8,256]{2,1,0:T(8,128)(2,1)S(1)}, u32[]{:S(2)}, u32[]{:S(2)}) collective-permute-start(bf16[16,8,256]{2,1,0:T(8,128)(2,1)S(1)} %get-tuple-element.28), channel_id=1, source_target_pairs={{0,12},{1,13},{2,14},{3,15},{4,0},{5,1},{6,2},{7,3},{8,4},{9,5},{1... | collective-permute-start | bytes 196616 | tf_op jit(solution)/shard_map/ppermute | solution.py:250
  72.2 1.2 %collective-permute-done.7 = bf16[16,8,256]{2,1,0:T(8,128)(2,1)S(1)} collective-permute-done((bf16[16,8,256]{2,1,0:T(8,128)(2,1)S(1)}, bf16[16,8,256]{2,1,0:T(8,128)(2,1)S(1)}, u32[]{:S(2)}, u32[]{:S(2)}) %collective-permute-start.7) | collective-permute-done | bytes 65568 | tf_op jit(solution)/shard_map/ppermute | solution.py:250
  73.4 2.1 %collective-permute-done.8 = bf16[16,8,256]{2,1,0:T(8,128)(2,1)S(1)} collective-permute-done((bf16[16,8,256]{2,1,0:T(8,128)(2,1)S(1)}, bf16[16,8,256]{2,1,0:T(8,128)(2,1)S(1)}, u32[]{:S(2)}, u32[]{:S(2)}) %collective-permute-start.8) | collective-permute-done | bytes 65568 | tf_op jit(solution)/shard_map/ppermute | solution.py:250
  75.5 0.0 collective-permute-done.9
  75.5 0.1 reshape.21
  75.6 0.7 copy.13
  (9 shorter events, 0.2 us)
Async XLA Ops:
  0.0 7.9 %collective-permute-start = (bf16[32,2,128,128]{3,2,1,0:T(8,128)(2,1)}, bf16[32,2,128,128]{3,2,1,0:T(8,128)(2,1)}, u32[]{:S(2)}, u32[]{:S(2)}) collective-permute-start(bf16[32,2,128,128]{3,2,1,0:T(8,128)(2,1)} %own_ref.1), channel_id=1, source_target_pairs={{0,1},{1,0},{2,3},{3,2},{4,5},{5,4},{6,7},{7,6},{8,9},{9,8},{10,11... | collective-permute-start | bytes 6291464 | tf_op jit(solution)/shard_map/ppermute | solution.py:277
  0.5 1.6 %copy-start.2 = (bf16[32,2,128,128]{3,2,1,0:T(8,128)(2,1)S(1)}, bf16[32,2,128,128]{3,2,1,0:T(8,128)(2,1)}, u32[]{:S(2)}) copy-start(bf16[32,2,128,128]{3,2,1,0:T(8,128)(2,1)} %green_ref.1) | copy-start | bytes 6291460
  2.0 5.5 %copy-start.8 = (bf16[2,128,128]{2,1,0:T(8,128)(2,1)S(1)}, bf16[2,128,128]{2,1,0:T(8,128)(2,1)}, u32[]{:S(2)}) copy-start(bf16[2,128,128]{2,1,0:T(8,128)(2,1)} %param.7) | copy-start | bytes 196612
  2.1 36.3 %collective-permute-start.1 = (bf16[16,2,128,128]{3,2,1,0:T(8,128)(2,1)S(1)}, bf16[16,2,128,128]{3,2,1,0:T(8,128)(2,1)}, u32[]{:S(2)}, u32[]{:S(2)}) collective-permute-start(bf16[16,2,128,128]{3,2,1,0:T(8,128)(2,1)S(1)} %shard_map.57), channel_id=1, source_target_pairs={{0,2},{1,3},{2,4},{3,5},{4,6},{5,7},{6,8},{7,9},{8,10},{9,11},{10,... | collective-permute-start | bytes 3145736 | tf_op jit(solution)/shard_map/ppermute | solution.py:267
  7.9 9.7 %copy-start.3 = (bf16[32,2,128,128]{3,2,1,0:T(8,128)(2,1)S(1)}, bf16[32,2,128,128]{3,2,1,0:T(8,128)(2,1)}, u32[]{:S(2)}) copy-start(bf16[32,2,128,128]{3,2,1,0:T(8,128)(2,1)} %green_ref.1) | copy-start | bytes 6291460
  7.9 1.7 %copy-start.4 = (bf16[32,2,128,128]{3,2,1,0:T(8,128)(2,1)S(1)}, bf16[32,2,128,128]{3,2,1,0:T(8,128)(2,1)}, u32[]{:S(2)}) copy-start(bf16[32,2,128,128]{3,2,1,0:T(8,128)(2,1)} %own_ref.1) | copy-start | bytes 6291460
  15.3 2.4 %copy-start = (bf16[80,128,256]{2,1,0:T(8,128)(2,1)}, bf16[80,128,256]{2,1,0:T(8,128)(2,1)S(1)}, u32[]{:S(2)}) copy-start(bf16[80,128,256]{2,1,0:T(8,128)(2,1)S(1)} %shard_map.55.proj_ref) | copy-start | bytes 15728644
  17.6 5.1 %copy-start.9 = (s32[2]{0:T(128)S(1)}, s32[2]{0:T(128)}, u32[]{:S(2)}) copy-start(s32[2]{0:T(128)} %param.9) | copy-start | bytes 28
  17.7 5.2 %copy-start.5 = (s32[16]{0:T(128)S(1)}, s32[16]{0:T(128)}, u32[]{:S(2)}) copy-start(s32[16]{0:T(128)} %shifts_ref.9) | copy-start | bytes 196
  18.9 0.7 copy-start.6
  19.5 28.3 %collective-permute-start.4 = (bf16[8,2,128,128]{3,2,1,0:T(8,128)(2,1)}, bf16[8,2,128,128]{3,2,1,0:T(8,128)(2,1)}, u32[]{:S(2)}, u32[]{:S(2)}) collective-permute-start(bf16[8,2,128,128]{3,2,1,0:T(8,128)(2,1)} %get-tuple-element.23), channel_id=1, source_target_pairs={{0,2},{1,3},{2,4},{3,5},{4,6},{5,7},{6,8},{7,9},{8,10},{9,11},{10,... | collective-permute-start | bytes 1572872 | tf_op jit(solution)/shard_map/ppermute | solution.py:281
  22.9 2.5 %copy-start.1 = (bf16[80,128,256]{2,1,0:T(8,128)(2,1)S(1)}, bf16[80,128,256]{2,1,0:T(8,128)(2,1)}, u32[]{:S(2)}) copy-start(bf16[80,128,256]{2,1,0:T(8,128)(2,1)} %copy-done) | copy-start | bytes 15728644
  35.6 8.9 %copy-start.7 = (bf16[2,2,128,128]{3,2,1,0:T(8,128)(2,1)S(1)}, bf16[2,2,128,128]{3,2,1,0:T(8,128)(2,1)}, u32[]{:S(2)}) copy-start(bf16[2,2,128,128]{3,2,1,0:T(8,128)(2,1)} %copy-done.6) | copy-start | bytes 393220
  35.6 15.7 %collective-permute-start.3 = (bf16[6,2,128,128]{3,2,1,0:T(8,128)(2,1)S(1)}, bf16[6,2,128,128]{3,2,1,0:T(8,128)(2,1)S(1)}, u32[]{:S(2)}, u32[]{:S(2)}) collective-permute-start(bf16[6,2,128,128]{3,2,1,0:T(8,128)(2,1)S(1)} %get-tuple-element.22), channel_id=1, source_target_pairs={{0,2},{1,3},{2,4},{3,5},{4,6},{5,7},{6,8},{7,9},{8,10},{9,11},{10,... | collective-permute-start | bytes 1179656 | tf_op jit(solution)/shard_map/ppermute | solution.py:292
  44.5 9.9 %collective-permute-start.2 = (bf16[2,2,128,128]{3,2,1,0:T(8,128)(2,1)S(1)}, bf16[2,2,128,128]{3,2,1,0:T(8,128)(2,1)S(1)}, u32[]{:S(2)}, u32[]{:S(2)}) collective-permute-start(bf16[2,2,128,128]{3,2,1,0:T(8,128)(2,1)S(1)} %copy-done.7), channel_id=1, source_target_pairs={{0,2},{1,3},{2,4},{3,5},{4,6},{5,7},{6,8},{7,9},{8,10},{9,11},{10,... | collective-permute-start | bytes 393224 | tf_op jit(solution)/shard_map/ppermute | solution.py:292
  55.8 2.0 %collective-permute-start.5 = (bf16[16,64,256]{2,1,0:T(8,128)(2,1)S(1)}, bf16[16,64,256]{2,1,0:T(8,128)(2,1)S(1)}, u32[]{:S(2)}, u32[]{:S(2)}) collective-permute-start(bf16[16,64,256]{2,1,0:T(8,128)(2,1)S(1)} %get-tuple-element.26), channel_id=1, source_target_pairs={{0,1},{1,0},{2,3},{3,2},{4,5},{5,4},{6,7},{7,6},{8,9},{9,8},{10,11... | collective-permute-start | bytes 1572872 | tf_op jit(solution)/shard_map/ppermute | solution.py:239
  57.9 8.4 %collective-permute-start.6 = (bf16[4,16,8,256]{3,2,0,1:T(8,128)(2,1)S(1)}, bf16[4,16,8,256]{3,2,0,1:T(8,128)(2,1)S(1)}, u32[]{:S(2)}, u32[]{:S(2)}) collective-permute-start(bf16[4,16,8,256]{3,2,0,1:T(8,128)(2,1)S(1)} %fusion), channel_id=1, source_target_pairs={{0,2},{1,3},{2,0},{3,1},{4,6},{5,7},{6,4},{7,5},{8,10},{9,11},{10,... | collective-permute-start | bytes 786440 | tf_op jit(solution)/shard_map/ppermute | solution.py:244
  66.5 7.0 %collective-permute-start.7 = (bf16[16,8,256]{2,1,0:T(8,128)(2,1)S(1)}, bf16[16,8,256]{2,1,0:T(8,128)(2,1)S(1)}, u32[]{:S(2)}, u32[]{:S(2)}) collective-permute-start(bf16[16,8,256]{2,1,0:T(8,128)(2,1)S(1)} %get-tuple-element.27), channel_id=1, source_target_pairs={{0,4},{1,5},{2,6},{3,7},{4,8},{5,9},{6,10},{7,11},{8,12},{9,13},{1... | collective-permute-start | bytes 196616 | tf_op jit(solution)/shard_map/ppermute | solution.py:250
  68.3 7.2 %collective-permute-start.8 = (bf16[16,8,256]{2,1,0:T(8,128)(2,1)S(1)}, bf16[16,8,256]{2,1,0:T(8,128)(2,1)S(1)}, u32[]{:S(2)}, u32[]{:S(2)}) collective-permute-start(bf16[16,8,256]{2,1,0:T(8,128)(2,1)S(1)} %get-tuple-element.29), channel_id=1, source_target_pairs={{0,8},{1,9},{2,10},{3,11},{4,12},{5,13},{6,14},{7,15},{8,0},{9,1},... | collective-permute-start | bytes 196616 | tf_op jit(solution)/shard_map/ppermute | solution.py:250
  70.9 4.6 %collective-permute-start.9 = (bf16[16,8,256]{2,1,0:T(8,128)(2,1)S(1)}, bf16[16,8,256]{2,1,0:T(8,128)(2,1)S(1)}, u32[]{:S(2)}, u32[]{:S(2)}) collective-permute-start(bf16[16,8,256]{2,1,0:T(8,128)(2,1)S(1)} %get-tuple-element.28), channel_id=1, source_target_pairs={{0,12},{1,13},{2,14},{3,15},{4,0},{5,1},{6,2},{7,3},{8,4},{9,5},{1... | collective-permute-start | bytes 196616 | tf_op jit(solution)/shard_map/ppermute | solution.py:250

commit v9 on v8

--- a/solution.py
+++ b/solution.py
@@ -240,14 +240,21 @@
     both = keep + got.astype(jnp.float32)
     both = both.reshape(photons, 2, planes, share, width)
     both = jnp.transpose(both, (1, 2, 0, 3, 4))
-    send = pick(both, 1 - chip).astype(jnp.bfloat16)
-    got = lax.ppermute(send, "energy", [(i, i ^ 2) for i in range(devices)])
-    both = pick(both, chip) + got.astype(jnp.float32)
-    total = pick(both, plane)
-    for step in range(1, planes):
-        send = pick(both, (plane + step) % planes).astype(jnp.bfloat16)
+    theirs, mine = pick(both, 1 - chip), pick(both, chip)
+    steps = sorted(range(1, planes), key=lambda k: -min(k, planes - k)) + [0]
+    sums = []
+    for part in (steps[: planes // 2], steps[planes // 2 :]):
+        at = [(plane + step) % planes for step in part]
+        send = jnp.stack([pick(theirs, k) for k in at]).astype(jnp.bfloat16)
+        got = lax.ppermute(send, "energy", [(i, i ^ 2) for i in range(devices)])
+        sums += [pick(mine, k) + got[n].astype(jnp.float32) for n, k in enumerate(at)]
+        mine = lax.optimization_barrier(mine)
+    total = sums[-1]
+    for step, block in zip(steps[:-1], sums):
         route = [(i, (i + 4 * step) % devices) for i in range(devices)]
-        total = total + lax.ppermute(send, "energy", route).astype(jnp.float32)
+        total = total + lax.ppermute(block.astype(jnp.bfloat16), "energy", route).astype(
+            jnp.float32
+        )
     return total
 
 

time: 76.7 us -> 75.1 us (0.979)
  waiting for transfers between devices: 12 us -> 8.68 us
  starting transfers between devices: 22.8 us -> 24.3 us
    ppermute x1 -> x2, waiting for transfers between devices: 6.83 us -> 4.19 us  [reduced(): got = lax.ppermute(send, 'energy', [(i, i ^ 2) for i in range(devices)])]
    ppermute x3, starting transfers between devices: 5.76 us -> 6.73 us  [reduced(): lax.ppermute(block.astype(jnp.bfloat16), 'energy', route)]
    ppermute x1 -> x2, starting transfers between devices: 1.58 us -> 2.16 us  [reduced(): got = lax.ppermute(send, 'energy', [(i, i ^ 2) for i in range(devices)])]
  transfers between devices with their start and end apart: 10 -> 11, of which waited for: 4 -> 4; matrix products, arithmetic and copies ran while one was open for 0% -> 1% of each run, Pallas kernels for 39% -> 40%
where the time goes in v9:
time: 75.1 us; the launch traced here: 74.7 us
  Pallas kernels  31 us (41%)
  starting transfers between devices  24.3 us (32%)
  local copies, waits for them, and re-layouts  9.94 us (13%)
  waiting for transfers between devices  8.68 us (12%)
    pallas_call x5, Pallas kernels, products(): pl.pallas_call(kernel, out_shape=out_shape, grid=(energies // step,), in_...  24.1 us
    unnamed x22, local copies, waits for them, and re-layouts  9.06 us
    ppermute x3, starting transfers between devices, reduced(): lax.ppermute(block.astype(jnp.bfloat16), 'energy', route)  6.73 us
    ppermute x2, starting transfers between devices, on_device(): far.append(lax.ppermute(pieces[k + 2], 'energy', up))  6.23 us
    pallas_call x1, Pallas kernels, project(): pl.pallas_call(functools.partial(project_kernel, steps), out_shape=jax.Sh...  5.62 us
    ppermute x1, starting transfers between devices, on_device(): far = [lax.ppermute(pieces[0], 'energy', up)]  5.41 us
    ppermute x2, waiting for transfers between devices, reduced(): got = lax.ppermute(send, 'energy', [(i, i ^ 2) for i in range(devices)])  4.19 us
    ppermute x1, starting transfers between devices, on_device(): far.append(lax.ppermute(pieces[1], 'energy', up))  3.25 us
  transfers between devices with their start and end apart: 11, of which 4 were waited for; matrix products, arithmetic and copies ran while one was open for 1% of the time, Pallas kernels for 40%

profile of v9, /device:TPU:0, one launch (start us, length us, event | category | flops | bytes accessed | tf_op | source)
XLA Modules:
  0.0 74.7 jit_solution(1428373828053943781)
XLA Ops:
  0.0 0.5 collective-permute-start
  0.5 0.0 copy-start.2
  0.5 1.6 %copy-done.2 = bf16[32,2,128,128]{3,2,1,0:T(8,128)(2,1)S(1)} copy-done((bf16[32,2,128,128]{3,2,1,0:T(8,128)(2,1)S(1)}, bf16[32,2,128,128]{3,2,1,0:T(8,128)(2,1)}, u32[]{:S(2)}) %copy-start.2) | copy-done | bytes 2097176
  2.0 0.0 copy-start.8
  2.0 0.1 shard_map.57
  2.1 5.4 %collective-permute-start.1 = (bf16[16,2,128,128]{3,2,1,0:T(8,128)(2,1)S(1)}, bf16[16,2,128,128]{3,2,1,0:T(8,128)(2,1)}, u32[]{:S(2)}, u32[]{:S(2)}) collective-permute-start(bf16[16,2,128,128]{3,2,1,0:T(8,128)(2,1)S(1)} %shard_map.57), channel_id=1, source_target_pairs={{0,2},{1,3},{2,4},{3,5},{4,6},{5,7},{6,8},{7,9},{8,10},{9,11},{10,... | collective-permute-start | bytes 3145736 | tf_op jit(solution)/shard_map/ppermute | solution.py:274
  7.5 0.0 copy-done.8
  7.6 0.1 copy.16
  7.7 0.1 copy.15
  7.9 0.0 copy-start.3
  7.9 0.0 collective-permute-done.other_ref
  7.9 0.0 copy-start.4
  7.9 1.7 %copy-done.4 = bf16[32,2,128,128]{3,2,1,0:T(8,128)(2,1)S(1)} copy-done((bf16[32,2,128,128]{3,2,1,0:T(8,128)(2,1)S(1)}, bf16[32,2,128,128]{3,2,1,0:T(8,128)(2,1)}, u32[]{:S(2)}) %copy-start.4) | copy-done | bytes 2097176
  9.7 5.6 %shard_map.55.proj_ref = bf16[80,128,256]{2,1,0:T(8,128)(2,1)S(1)} custom-call(bf16[128,256]{1,0:T(8,128)(2,1)S(1)} %pad_maximum_fusion.2.left_ref, bf16[256,256]{1,0:T(8,128)(2,1)S(1)} %maximum_maximum_fusion.right_ref, bf16[32,2,128,128]{3,2,1,0:T(8,128)(2,1)S(1)} %copy-done.4, bf16[32,2,128,128]{3,2,1,0:T(8,128)(2,1)} %collective-permute-done.other_ref), custom_call_target="tpu_custom_call" | custom-call | tf_op jit(solution)/shard_map/pallas_call | solution.py:88
  15.3 0.0 copy-start
  15.3 2.3 %copy-done = bf16[80,128,256]{2,1,0:T(8,128)(2,1)} copy-done((bf16[80,128,256]{2,1,0:T(8,128)(2,1)}, bf16[80,128,256]{2,1,0:T(8,128)(2,1)S(1)}, u32[]{:S(2)}) %copy-start) | copy-done | bytes 5242904
  17.6 0.0 copy-done.3
  17.6 0.0 copy-start.9
  17.6 0.0 copy-start.5
  17.6 1.2 %shard_map.56 = (bf16[8,2,128,128]{3,2,1,0:T(8,128)(2,1)}, bf16[6,2,128,128]{3,2,1,0:T(8,128)(2,1)S(1)}, bf16[2,2,128,128]{3,2,1,0:T(8,128)(2,1)S(1)}) custom-call(bf16[32,2,128,128]{3,2,1,0:T(8,128)(2,1)S(1)} %copy-done.3), custom_call_target="tpu_custom_call" | custom-call | tf_op jit(solution)/shard_map/pallas_call | solution.py:39
  18.9 0.0 copy-start.6
  18.9 0.6 copy-done.6
  19.5 3.3 %collective-permute-start.4 = (bf16[8,2,128,128]{3,2,1,0:T(8,128)(2,1)}, bf16[8,2,128,128]{3,2,1,0:T(8,128)(2,1)}, u32[]{:S(2)}, u32[]{:S(2)}) collective-permute-start(bf16[8,2,128,128]{3,2,1,0:T(8,128)(2,1)} %get-tuple-element.23), channel_id=1, source_target_pairs={{0,2},{1,3},{2,4},{3,5},{4,6},{5,7},{6,8},{7,9},{8,10},{9,11},{10,... | collective-permute-start | bytes 1572872 | tf_op jit(solution)/shard_map/ppermute | solution.py:288
  22.8 0.0 copy-done.9
  22.8 0.1 pad_add_fusion.facts_ref
  22.9 0.0 copy-done.5
  22.9 0.0 copy-start.1
  22.9 2.5 %copy-done.1 = bf16[80,128,256]{2,1,0:T(8,128)(2,1)S(1)} copy-done((bf16[80,128,256]{2,1,0:T(8,128)(2,1)S(1)}, bf16[80,128,256]{2,1,0:T(8,128)(2,1)}, u32[]{:S(2)}) %copy-start.1) | copy-done | bytes 5242904
  25.4 10.2 %shard_map.58.before_ref = f32[16,128,256]{2,1,0:T(8,128)S(1)} custom-call(s32[16]{0:T(128)S(1)} %copy-done.5, s32[5]{0:T(128)S(1)} %pad_add_fusion.facts_ref, bf16[80,128,256]{2,1,0:T(8,128)(2,1)S(1)} %copy-done.1, bf16[32,2,128,128]{3,2,1,0:T(8,128)(2,1)S(1)} %copy-done.3), custom_call_target="tpu_custom_call" | custom-call | tf_op jit(solution)/shard_map/pallas_call | solution.py:219
  35.6 0.0 copy-start.7
  35.6 2.8 %collective-permute-start.3 = (bf16[6,2,128,128]{3,2,1,0:T(8,128)(2,1)S(1)}, bf16[6,2,128,128]{3,2,1,0:T(8,128)(2,1)S(1)}, u32[]{:S(2)}, u32[]{:S(2)}) collective-permute-start(bf16[6,2,128,128]{3,2,1,0:T(8,128)(2,1)S(1)} %get-tuple-element.22), channel_id=1, source_target_pairs={{0,2},{1,3},{2,4},{3,5},{4,6},{5,7},{6,8},{7,9},{8,10},{9,11},{10,... | collective-permute-start | bytes 1179656 | tf_op jit(solution)/shard_map/ppermute | solution.py:299
  38.4 0.0 collective-permute-done.1.green_ref
  38.4 6.0 %shard_map.59.before_ref = f32[16,128,256]{2,1,0:T(8,128)S(1)} custom-call(s32[16]{0:T(128)S(1)} %copy-done.5, s32[5]{0:T(128)S(1)} %pad_add_fusion.facts_ref, bf16[80,128,256]{2,1,0:T(8,128)(2,1)S(1)} %copy-done.1, bf16[16,2,128,128]{3,2,1,0:T(8,128)(2,1)} %collective-permute-done.1.green_ref, f32[16,128,256]{2,1,0:T(8,128)S(1)} %shard_map.58.before_ref), custom_call_target="tpu_custom_call" | custom-call | tf_op jit(solution)/shard_map/pallas_call | solution.py:219
  44.4 0.0 copy-done.7
  44.5 3.4 %collective-permute-start.2 = (bf16[2,2,128,128]{3,2,1,0:T(8,128)(2,1)S(1)}, bf16[2,2,128,128]{3,2,1,0:T(8,128)(2,1)S(1)}, u32[]{:S(2)}, u32[]{:S(2)}) collective-permute-start(bf16[2,2,128,128]{3,2,1,0:T(8,128)(2,1)S(1)} %copy-done.7), channel_id=1, source_target_pairs={{0,2},{1,3},{2,4},{3,5},{4,6},{5,7},{6,8},{7,9},{8,10},{9,11},{10,... | collective-permute-start | bytes 393224 | tf_op jit(solution)/shard_map/ppermute | solution.py:299
  47.9 0.0 collective-permute-done.4.green_ref
  47.9 3.4 %shard_map.60.before_ref = f32[16,128,256]{2,1,0:T(8,128)S(1)} custom-call(s32[16]{0:T(128)S(1)} %copy-done.5, s32[5]{0:T(128)S(1)} %pad_add_fusion.facts_ref, bf16[80,128,256]{2,1,0:T(8,128)(2,1)S(1)} %copy-done.1, bf16[8,2,128,128]{3,2,1,0:T(8,128)(2,1)} %collective-permute-done.4.green_ref, f32[16,128,256]{2,1,0:T(8,128)S(1)} %shard_map.59.before_ref), custom_call_target="tpu_custom_call" | custom-call | tf_op jit(solution)/shard_map/pallas_call | solution.py:219
  51.3 0.0 collective-permute-done.3.green_ref
  51.3 3.0 %shard_map.61.before_ref = f32[16,128,256]{2,1,0:T(8,128)S(1)} custom-call(s32[16]{0:T(128)S(1)} %copy-done.5, s32[5]{0:T(128)S(1)} %pad_add_fusion.facts_ref, bf16[80,128,256]{2,1,0:T(8,128)(2,1)S(1)} %copy-done.1, bf16[6,2,128,128]{3,2,1,0:T(8,128)(2,1)S(1)} %collective-permute-done.3.green_ref, f32[16,128,256]{2,1,0:T(8,128)S(1)} %shard_map.60.before_ref), custom_call_target="tpu_custom_call" | custom-call | tf_op jit(solution)/shard_map/pallas_call | solution.py:219
  54.3 0.0 collective-permute-done.2.green_ref
  54.3 1.4 %shard_map.62 = (f32[16,64,256]{2,1,0:T(8,128)S(1)}, bf16[16,64,256]{2,1,0:T(8,128)(2,1)S(1)}) custom-call(s32[16]{0:T(128)S(1)} %copy-done.5, s32[5]{0:T(128)S(1)} %pad_add_fusion.facts_ref, s32[1]{0:T(128)} %bitcast.2.core_ref, bf16[80,128,256]{2,1,0:T(8,128)(2,1)S(1)} %copy-done.1, bf16[2,2,128,128]{3,2,1,0:T(8,128)(2,1)S(1)} %collective-permute-done.2.green_ref, ...), custom_call_target="tpu_custom_call" | custom-call | tf_op jit(solution)/shard_map/pallas_call | solution.py:219
  55.8 0.1 collective-permute-start.5
  56.0 1.8 %collective-permute-done.5 = bf16[16,64,256]{2,1,0:T(8,128)(2,1)S(1)} collective-permute-done((bf16[16,64,256]{2,1,0:T(8,128)(2,1)S(1)}, bf16[16,64,256]{2,1,0:T(8,128)(2,1)S(1)}, u32[]{:S(2)}, u32[]{:S(2)}) %collective-permute-start.5) | collective-permute-done | bytes 524320 | tf_op jit(solution)/shard_map/ppermute | solution.py:239
  57.7 0.1 convert_add_fusion
  57.9 0.1 fusion.10
  58.0 1.6 %collective-permute-start.7 = (bf16[2,16,8,256]{3,2,1,0:T(8,128)(2,1)S(1)}, bf16[2,16,8,256]{3,2,1,0:T(8,128)(2,1)S(1)}, u32[]{:S(2)}, u32[]{:S(2)}) collective-permute-start(bf16[2,16,8,256]{3,2,1,0:T(8,128)(2,1)S(1)} %pad_maximum_fusion.1), channel_id=1, source_target_pairs={{0,2},{1,3},{2,0},{3,1},{4,6},{5,7},{6,4},{7,5},{8,10},{9,11},{10,... | collective-permute-start | bytes 393224 | tf_op jit(solution)/shard_map/ppermute | solution.py:249
  59.5 0.6 collective-permute-start.6
  60.2 4.2 %collective-permute-done.7 = bf16[2,16,8,256]{3,2,1,0:T(8,128)(2,1)S(1)} collective-permute-done((bf16[2,16,8,256]{3,2,1,0:T(8,128)(2,1)S(1)}, bf16[2,16,8,256]{3,2,1,0:T(8,128)(2,1)S(1)}, u32[]{:S(2)}, u32[]{:S(2)}) %collective-permute-start.7) | collective-permute-done | bytes 131104 | tf_op jit(solution)/shard_map/ppermute | solution.py:249
  64.4 2.9 %collective-permute-start.8 = (bf16[16,8,256]{2,1,0:T(8,128)(2,1)S(1)}, bf16[16,8,256]{2,1,0:T(8,128)(2,1)S(1)}, u32[]{:S(2)}, u32[]{:S(2)}) collective-permute-start(bf16[16,8,256]{2,1,0:T(8,128)(2,1)S(1)} %get-tuple-element.27), channel_id=1, source_target_pairs={{0,8},{1,9},{2,10},{3,11},{4,12},{5,13},{6,14},{7,15},{8,0},{9,1},... | collective-permute-start | bytes 196616 | tf_op jit(solution)/shard_map/ppermute | solution.py:255
  67.2 1.6 %collective-permute-start.9 = (bf16[16,8,256]{2,1,0:T(8,128)(2,1)S(1)}, bf16[16,8,256]{2,1,0:T(8,128)(2,1)S(1)}, u32[]{:S(2)}, u32[]{:S(2)}) collective-permute-start(bf16[16,8,256]{2,1,0:T(8,128)(2,1)S(1)} %get-tuple-element.28), channel_id=1, source_target_pairs={{0,4},{1,5},{2,6},{3,7},{4,8},{5,9},{6,10},{7,11},{8,12},{9,13},{1... | collective-permute-start | bytes 196616 | tf_op jit(solution)/shard_map/ppermute | solution.py:255
  68.8 0.0 collective-permute-done.6
  68.8 2.3 %collective-permute-start.10 = (bf16[16,8,256]{2,1,0:T(8,128)(2,1)S(1)}, bf16[16,8,256]{2,1,0:T(8,128)(2,1)S(1)}, u32[]{:S(2)}, u32[]{:S(2)}) collective-permute-start(bf16[16,8,256]{2,1,0:T(8,128)(2,1)S(1)} %fusion.7), channel_id=1, source_target_pairs={{0,12},{1,13},{2,14},{3,15},{4,0},{5,1},{6,2},{7,3},{8,4},{9,5},{1... | collective-permute-start | bytes 196616 | tf_op jit(solution)/shard_map/ppermute | solution.py:255
  71.1 0.0 collective-permute-done.8
  71.2 2.3 %collective-permute-done.9 = bf16[16,8,256]{2,1,0:T(8,128)(2,1)S(1)} collective-permute-done((bf16[16,8,256]{2,1,0:T(8,128)(2,1)S(1)}, bf16[16,8,256]{2,1,0:T(8,128)(2,1)S(1)}, u32[]{:S(2)}, u32[]{:S(2)}) %collective-permute-start.9) | collective-permute-done | bytes 65568 | tf_op jit(solution)/shard_map/ppermute | solution.py:255
  73.4 0.4 collective-permute-done.10
  73.9 0.1 reshape.52
  74.0 0.7 copy.14
  (12 shorter events, 0.2 us)
Async XLA Ops:
  0.0 7.9 %collective-permute-start = (bf16[32,2,128,128]{3,2,1,0:T(8,128)(2,1)}, bf16[32,2,128,128]{3,2,1,0:T(8,128)(2,1)}, u32[]{:S(2)}, u32[]{:S(2)}) collective-permute-start(bf16[32,2,128,128]{3,2,1,0:T(8,128)(2,1)} %own_ref.1), channel_id=1, source_target_pairs={{0,1},{1,0},{2,3},{3,2},{4,5},{5,4},{6,7},{7,6},{8,9},{9,8},{10,11... | collective-permute-start | bytes 6291464 | tf_op jit(solution)/shard_map/ppermute | solution.py:284
  0.5 1.6 %copy-start.2 = (bf16[32,2,128,128]{3,2,1,0:T(8,128)(2,1)S(1)}, bf16[32,2,128,128]{3,2,1,0:T(8,128)(2,1)}, u32[]{:S(2)}) copy-start(bf16[32,2,128,128]{3,2,1,0:T(8,128)(2,1)} %green_ref.1) | copy-start | bytes 6291460
  2.0 5.5 %copy-start.8 = (bf16[2,128,128]{2,1,0:T(8,128)(2,1)S(1)}, bf16[2,128,128]{2,1,0:T(8,128)(2,1)}, u32[]{:S(2)}) copy-start(bf16[2,128,128]{2,1,0:T(8,128)(2,1)} %param.7) | copy-start | bytes 196612
  2.1 36.3 %collective-permute-start.1 = (bf16[16,2,128,128]{3,2,1,0:T(8,128)(2,1)S(1)}, bf16[16,2,128,128]{3,2,1,0:T(8,128)(2,1)}, u32[]{:S(2)}, u32[]{:S(2)}) collective-permute-start(bf16[16,2,128,128]{3,2,1,0:T(8,128)(2,1)S(1)} %shard_map.57), channel_id=1, source_target_pairs={{0,2},{1,3},{2,4},{3,5},{4,6},{5,7},{6,8},{7,9},{8,10},{9,11},{10,... | collective-permute-start | bytes 3145736 | tf_op jit(solution)/shard_map/ppermute | solution.py:274
  7.9 9.7 %copy-start.3 = (bf16[32,2,128,128]{3,2,1,0:T(8,128)(2,1)S(1)}, bf16[32,2,128,128]{3,2,1,0:T(8,128)(2,1)}, u32[]{:S(2)}) copy-start(bf16[32,2,128,128]{3,2,1,0:T(8,128)(2,1)} %green_ref.1) | copy-start | bytes 6291460
  7.9 1.7 %copy-start.4 = (bf16[32,2,128,128]{3,2,1,0:T(8,128)(2,1)S(1)}, bf16[32,2,128,128]{3,2,1,0:T(8,128)(2,1)}, u32[]{:S(2)}) copy-start(bf16[32,2,128,128]{3,2,1,0:T(8,128)(2,1)} %own_ref.1) | copy-start | bytes 6291460
  15.3 2.3 %copy-start = (bf16[80,128,256]{2,1,0:T(8,128)(2,1)}, bf16[80,128,256]{2,1,0:T(8,128)(2,1)S(1)}, u32[]{:S(2)}) copy-start(bf16[80,128,256]{2,1,0:T(8,128)(2,1)S(1)} %shard_map.55.proj_ref) | copy-start | bytes 15728644
  17.6 5.1 %copy-start.9 = (s32[2]{0:T(128)S(1)}, s32[2]{0:T(128)}, u32[]{:S(2)}) copy-start(s32[2]{0:T(128)} %param.9) | copy-start | bytes 28
  17.6 5.2 %copy-start.5 = (s32[16]{0:T(128)S(1)}, s32[16]{0:T(128)}, u32[]{:S(2)}) copy-start(s32[16]{0:T(128)} %shifts_ref.9) | copy-start | bytes 196
  18.9 0.7 copy-start.6
  19.5 28.4 %collective-permute-start.4 = (bf16[8,2,128,128]{3,2,1,0:T(8,128)(2,1)}, bf16[8,2,128,128]{3,2,1,0:T(8,128)(2,1)}, u32[]{:S(2)}, u32[]{:S(2)}) collective-permute-start(bf16[8,2,128,128]{3,2,1,0:T(8,128)(2,1)} %get-tuple-element.23), channel_id=1, source_target_pairs={{0,2},{1,3},{2,4},{3,5},{4,6},{5,7},{6,8},{7,9},{8,10},{9,11},{10,... | collective-permute-start | bytes 1572872 | tf_op jit(solution)/shard_map/ppermute | solution.py:288
  22.9 2.5 %copy-start.1 = (bf16[80,128,256]{2,1,0:T(8,128)(2,1)S(1)}, bf16[80,128,256]{2,1,0:T(8,128)(2,1)}, u32[]{:S(2)}) copy-start(bf16[80,128,256]{2,1,0:T(8,128)(2,1)} %copy-done) | copy-start | bytes 15728644
  35.6 8.9 %copy-start.7 = (bf16[2,2,128,128]{3,2,1,0:T(8,128)(2,1)S(1)}, bf16[2,2,128,128]{3,2,1,0:T(8,128)(2,1)}, u32[]{:S(2)}) copy-start(bf16[2,2,128,128]{3,2,1,0:T(8,128)(2,1)} %copy-done.6) | copy-start | bytes 393220
  35.6 15.7 %collective-permute-start.3 = (bf16[6,2,128,128]{3,2,1,0:T(8,128)(2,1)S(1)}, bf16[6,2,128,128]{3,2,1,0:T(8,128)(2,1)S(1)}, u32[]{:S(2)}, u32[]{:S(2)}) collective-permute-start(bf16[6,2,128,128]{3,2,1,0:T(8,128)(2,1)S(1)} %get-tuple-element.22), channel_id=1, source_target_pairs={{0,2},{1,3},{2,4},{3,5},{4,6},{5,7},{6,8},{7,9},{8,10},{9,11},{10,... | collective-permute-start | bytes 1179656 | tf_op jit(solution)/shard_map/ppermute | solution.py:299
  44.5 9.9 %collective-permute-start.2 = (bf16[2,2,128,128]{3,2,1,0:T(8,128)(2,1)S(1)}, bf16[2,2,128,128]{3,2,1,0:T(8,128)(2,1)S(1)}, u32[]{:S(2)}, u32[]{:S(2)}) collective-permute-start(bf16[2,2,128,128]{3,2,1,0:T(8,128)(2,1)S(1)} %copy-done.7), channel_id=1, source_target_pairs={{0,2},{1,3},{2,4},{3,5},{4,6},{5,7},{6,8},{7,9},{8,10},{9,11},{10,... | collective-permute-start | bytes 393224 | tf_op jit(solution)/shard_map/ppermute | solution.py:299
  55.8 2.0 %collective-permute-start.5 = (bf16[16,64,256]{2,1,0:T(8,128)(2,1)S(1)}, bf16[16,64,256]{2,1,0:T(8,128)(2,1)S(1)}, u32[]{:S(2)}, u32[]{:S(2)}) collective-permute-start(bf16[16,64,256]{2,1,0:T(8,128)(2,1)S(1)} %get-tuple-element.26), channel_id=1, source_target_pairs={{0,1},{1,0},{2,3},{3,2},{4,5},{5,4},{6,7},{7,6},{8,9},{9,8},{10,11... | collective-permute-start | bytes 1572872 | tf_op jit(solution)/shard_map/ppermute | solution.py:239
  58.0 6.4 %collective-permute-start.7 = (bf16[2,16,8,256]{3,2,1,0:T(8,128)(2,1)S(1)}, bf16[2,16,8,256]{3,2,1,0:T(8,128)(2,1)S(1)}, u32[]{:S(2)}, u32[]{:S(2)}) collective-permute-start(bf16[2,16,8,256]{3,2,1,0:T(8,128)(2,1)S(1)} %pad_maximum_fusion.1), channel_id=1, source_target_pairs={{0,2},{1,3},{2,0},{3,1},{4,6},{5,7},{6,4},{7,5},{8,10},{9,11},{10,... | collective-permute-start | bytes 393224 | tf_op jit(solution)/shard_map/ppermute | solution.py:249
  59.5 9.3 %collective-permute-start.6 = (bf16[2,16,8,256]{3,2,1,0:T(8,128)(2,1)S(1)}, bf16[2,16,8,256]{3,2,1,0:T(8,128)(2,1)S(1)}, u32[]{:S(2)}, u32[]{:S(2)}) collective-permute-start(bf16[2,16,8,256]{3,2,1,0:T(8,128)(2,1)S(1)} %pad_maximum_fusion), channel_id=1, source_target_pairs={{0,2},{1,3},{2,0},{3,1},{4,6},{5,7},{6,4},{7,5},{8,10},{9,11},{10,... | collective-permute-start | bytes 393224 | tf_op jit(solution)/shard_map/ppermute | solution.py:249
  64.4 6.8 %collective-permute-start.8 = (bf16[16,8,256]{2,1,0:T(8,128)(2,1)S(1)}, bf16[16,8,256]{2,1,0:T(8,128)(2,1)S(1)}, u32[]{:S(2)}, u32[]{:S(2)}) collective-permute-start(bf16[16,8,256]{2,1,0:T(8,128)(2,1)S(1)} %get-tuple-element.27), channel_id=1, source_target_pairs={{0,8},{1,9},{2,10},{3,11},{4,12},{5,13},{6,14},{7,15},{8,0},{9,1},... | collective-permute-start | bytes 196616 | tf_op jit(solution)/shard_map/ppermute | solution.py:255
  67.2 6.2 %collective-permute-start.9 = (bf16[16,8,256]{2,1,0:T(8,128)(2,1)S(1)}, bf16[16,8,256]{2,1,0:T(8,128)(2,1)S(1)}, u32[]{:S(2)}, u32[]{:S(2)}) collective-permute-start(bf16[16,8,256]{2,1,0:T(8,128)(2,1)S(1)} %get-tuple-element.28), channel_id=1, source_target_pairs={{0,4},{1,5},{2,6},{3,7},{4,8},{5,9},{6,10},{7,11},{8,12},{9,13},{1... | collective-permute-start | bytes 196616 | tf_op jit(solution)/shard_map/ppermute | solution.py:255
  68.8 5.0 %collective-permute-start.10 = (bf16[16,8,256]{2,1,0:T(8,128)(2,1)S(1)}, bf16[16,8,256]{2,1,0:T(8,128)(2,1)S(1)}, u32[]{:S(2)}, u32[]{:S(2)}) collective-permute-start(bf16[16,8,256]{2,1,0:T(8,128)(2,1)S(1)} %fusion.7), channel_id=1, source_target_pairs={{0,12},{1,13},{2,14},{3,15},{4,0},{5,1},{6,2},{7,3},{8,4},{9,5},{1... | collective-permute-start | bytes 196616 | tf_op jit(solution)/shard_map/ppermute | solution.py:255

commit v10 on v9

--- a/solution.py
+++ b/solution.py
@@ -12,7 +12,7 @@
 WIDE = 16
 PAIR = 2
 GROUPS = 1
-PARTS = (16, 8, 6, 2)
+PARTS = (20, 6, 4, 2)
 MIB = 1 << 20
 
 

time: 75.1 us -> 74.6 us (level)
  starting transfers between devices: 24.3 us -> 23.1 us
    ppermute x3, starting transfers between devices: 6.73 us -> 5.66 us  [reduced(): lax.ppermute(block.astype(jnp.bfloat16), 'energy', route)]
  transfers between devices with their start and end apart: 11 -> 11, of which waited for: 4 -> 5; matrix products, arithmetic and copies ran while one was open for 1% -> 1% of each run, Pallas kernels for 40% -> 41%
where the time goes in v10:
time: 74.6 us; the launch traced here: 74.2 us
  Pallas kernels  31.6 us (42%)
  starting transfers between devices  23.1 us (31%)
  local copies, waits for them, and re-layouts  9.99 us (13%)
  waiting for transfers between devices  8.77 us (12%)
    pallas_call x5, Pallas kernels, products(): pl.pallas_call(kernel, out_shape=out_shape, grid=(energies // step,), in_...  24.7 us
    unnamed x22, local copies, waits for them, and re-layouts  9.1 us
    ppermute x2, starting transfers between devices, on_device(): far.append(lax.ppermute(pieces[k + 2], 'energy', up))  6.15 us
    ppermute x3, starting transfers between devices, reduced(): lax.ppermute(block.astype(jnp.bfloat16), 'energy', route)  5.66 us
    pallas_call x1, Pallas kernels, project(): pl.pallas_call(functools.partial(project_kernel, steps), out_shape=jax.Sh...  5.62 us
    ppermute x1, starting transfers between devices, on_device(): far = [lax.ppermute(pieces[0], 'energy', up)]  5.5 us
    ppermute x2, waiting for transfers between devices, reduced(): got = lax.ppermute(send, 'energy', [(i, i ^ 2) for i in range(devices)])  4.19 us
    ppermute x1, starting transfers between devices, on_device(): far.append(lax.ppermute(pieces[1], 'energy', up))  3.11 us
  transfers between devices with their start and end apart: 11, of which 5 were waited for; matrix products, arithmetic and copies ran while one was open for 1% of the time, Pallas kernels for 41%

profile of v10, /device:TPU:0, one launch (start us, length us, event | category | flops | bytes accessed | tf_op | source)
XLA Modules:
  0.0 74.2 jit_solution(16344436788743649477)
XLA Ops:
  0.0 0.5 collective-permute-start
  0.5 0.0 copy-start.2
  0.5 1.6 %copy-done.2 = bf16[32,2,128,128]{3,2,1,0:T(8,128)(2,1)S(1)} copy-done((bf16[32,2,128,128]{3,2,1,0:T(8,128)(2,1)S(1)}, bf16[32,2,128,128]{3,2,1,0:T(8,128)(2,1)}, u32[]{:S(2)}) %copy-start.2) | copy-done | bytes 2097176
  2.0 0.0 copy-start.8
  2.0 0.1 shard_map.57
  2.2 5.5 %collective-permute-start.1 = (bf16[20,2,128,128]{3,2,1,0:T(8,128)(2,1)S(1)}, bf16[20,2,128,128]{3,2,1,0:T(8,128)(2,1)}, u32[]{:S(2)}, u32[]{:S(2)}) collective-permute-start(bf16[20,2,128,128]{3,2,1,0:T(8,128)(2,1)S(1)} %shard_map.57), channel_id=1, source_target_pairs={{0,2},{1,3},{2,4},{3,5},{4,6},{5,7},{6,8},{7,9},{8,10},{9,11},{10,... | collective-permute-start | bytes 3932168 | tf_op jit(solution)/shard_map/ppermute | solution.py:274
  7.7 0.0 copy-done.8
  7.7 0.1 copy.16
  7.8 0.1 copy.15
  8.0 0.0 copy-start.3
  8.0 0.0 collective-permute-done.other_ref
  8.0 0.0 copy-start.4
  8.0 1.7 %copy-done.4 = bf16[32,2,128,128]{3,2,1,0:T(8,128)(2,1)S(1)} copy-done((bf16[32,2,128,128]{3,2,1,0:T(8,128)(2,1)S(1)}, bf16[32,2,128,128]{3,2,1,0:T(8,128)(2,1)}, u32[]{:S(2)}) %copy-start.4) | copy-done | bytes 2097176
  9.8 5.6 %shard_map.55.proj_ref = bf16[80,128,256]{2,1,0:T(8,128)(2,1)S(1)} custom-call(bf16[128,256]{1,0:T(8,128)(2,1)S(1)} %pad_maximum_fusion.2.left_ref, bf16[256,256]{1,0:T(8,128)(2,1)S(1)} %maximum_maximum_fusion.right_ref, bf16[32,2,128,128]{3,2,1,0:T(8,128)(2,1)S(1)} %copy-done.4, bf16[32,2,128,128]{3,2,1,0:T(8,128)(2,1)} %collective-permute-done.other_ref), custom_call_target="tpu_custom_call" | custom-call | tf_op jit(solution)/shard_map/pallas_call | solution.py:88
  15.4 0.0 copy-start
  15.4 2.3 %copy-done = bf16[80,128,256]{2,1,0:T(8,128)(2,1)} copy-done((bf16[80,128,256]{2,1,0:T(8,128)(2,1)}, bf16[80,128,256]{2,1,0:T(8,128)(2,1)S(1)}, u32[]{:S(2)}) %copy-start) | copy-done | bytes 5242904
  17.7 0.0 copy-done.3
  17.7 0.0 copy-start.9
  17.7 0.0 copy-start.5
  17.8 1.2 %shard_map.56 = (bf16[6,2,128,128]{3,2,1,0:T(8,128)(2,1)}, bf16[4,2,128,128]{3,2,1,0:T(8,128)(2,1)S(1)}, bf16[2,2,128,128]{3,2,1,0:T(8,128)(2,1)S(1)}) custom-call(bf16[32,2,128,128]{3,2,1,0:T(8,128)(2,1)S(1)} %copy-done.3), custom_call_target="tpu_custom_call" | custom-call | tf_op jit(solution)/shard_map/pallas_call | solution.py:39
  18.9 0.0 copy-start.6
  18.9 0.7 copy-done.6
  19.6 3.1 %collective-permute-start.4 = (bf16[6,2,128,128]{3,2,1,0:T(8,128)(2,1)}, bf16[6,2,128,128]{3,2,1,0:T(8,128)(2,1)}, u32[]{:S(2)}, u32[]{:S(2)}) collective-permute-start(bf16[6,2,128,128]{3,2,1,0:T(8,128)(2,1)} %get-tuple-element.23), channel_id=1, source_target_pairs={{0,2},{1,3},{2,4},{3,5},{4,6},{5,7},{6,8},{7,9},{8,10},{9,11},{10,... | collective-permute-start | bytes 1179656 | tf_op jit(solution)/shard_map/ppermute | solution.py:288
  22.7 0.0 copy-done.9
  22.7 0.1 pad_add_fusion.facts_ref
  22.8 0.0 copy-done.5
  22.8 0.0 copy-start.1
  22.8 2.5 %copy-done.1 = bf16[80,128,256]{2,1,0:T(8,128)(2,1)S(1)} copy-done((bf16[80,128,256]{2,1,0:T(8,128)(2,1)S(1)}, bf16[80,128,256]{2,1,0:T(8,128)(2,1)}, u32[]{:S(2)}) %copy-start.1) | copy-done | bytes 5242904
  25.3 0.0 copy-start.7
  25.3 10.2 %shard_map.58.before_ref = f32[16,128,256]{2,1,0:T(8,128)S(1)} custom-call(s32[16]{0:T(128)S(1)} %copy-done.5, s32[5]{0:T(128)S(1)} %pad_add_fusion.facts_ref, bf16[80,128,256]{2,1,0:T(8,128)(2,1)S(1)} %copy-done.1, bf16[32,2,128,128]{3,2,1,0:T(8,128)(2,1)S(1)} %copy-done.3), custom_call_target="tpu_custom_call" | custom-call | tf_op jit(solution)/shard_map/pallas_call | solution.py:219
  35.5 0.0 copy-done.7
  35.6 2.7 %collective-permute-start.3 = (bf16[4,2,128,128]{3,2,1,0:T(8,128)(2,1)S(1)}, bf16[4,2,128,128]{3,2,1,0:T(8,128)(2,1)S(1)}, u32[]{:S(2)}, u32[]{:S(2)}) collective-permute-start(bf16[4,2,128,128]{3,2,1,0:T(8,128)(2,1)S(1)} %copy-done.7), channel_id=1, source_target_pairs={{0,2},{1,3},{2,4},{3,5},{4,6},{5,7},{6,8},{7,9},{8,10},{9,11},{10,... | collective-permute-start | bytes 786440 | tf_op jit(solution)/shard_map/ppermute | solution.py:299
  38.3 0.0 collective-permute-done.1.green_ref
  38.3 7.7 %shard_map.59.before_ref = f32[16,128,256]{2,1,0:T(8,128)S(1)} custom-call(s32[16]{0:T(128)S(1)} %copy-done.5, s32[5]{0:T(128)S(1)} %pad_add_fusion.facts_ref, bf16[80,128,256]{2,1,0:T(8,128)(2,1)S(1)} %copy-done.1, bf16[20,2,128,128]{3,2,1,0:T(8,128)(2,1)} %collective-permute-done.1.green_ref, f32[16,128,256]{2,1,0:T(8,128)S(1)} %shard_map.58.before_ref), custom_call_target="tpu_custom_call" | custom-call | tf_op jit(solution)/shard_map/pallas_call | solution.py:219
  46.0 3.4 %collective-permute-start.2 = (bf16[2,2,128,128]{3,2,1,0:T(8,128)(2,1)S(1)}, bf16[2,2,128,128]{3,2,1,0:T(8,128)(2,1)S(1)}, u32[]{:S(2)}, u32[]{:S(2)}) collective-permute-start(bf16[2,2,128,128]{3,2,1,0:T(8,128)(2,1)S(1)} %get-tuple-element.21), channel_id=1, source_target_pairs={{0,2},{1,3},{2,4},{3,5},{4,6},{5,7},{6,8},{7,9},{8,10},{9,11},{10,... | collective-permute-start | bytes 393224 | tf_op jit(solution)/shard_map/ppermute | solution.py:299
  49.5 0.0 collective-permute-done.4.green_ref
  49.5 3.5 %shard_map.60.before_ref = f32[16,128,256]{2,1,0:T(8,128)S(1)} custom-call(s32[16]{0:T(128)S(1)} %copy-done.5, s32[5]{0:T(128)S(1)} %pad_add_fusion.facts_ref, bf16[80,128,256]{2,1,0:T(8,128)(2,1)S(1)} %copy-done.1, bf16[6,2,128,128]{3,2,1,0:T(8,128)(2,1)} %collective-permute-done.4.green_ref, f32[16,128,256]{2,1,0:T(8,128)S(1)} %shard_map.59.before_ref), custom_call_target="tpu_custom_call" | custom-call | tf_op jit(solution)/shard_map/pallas_call | solution.py:219
  53.0 0.0 collective-permute-done.3.green_ref
  53.0 1.8 %shard_map.61.before_ref = f32[16,128,256]{2,1,0:T(8,128)S(1)} custom-call(s32[16]{0:T(128)S(1)} %copy-done.5, s32[5]{0:T(128)S(1)} %pad_add_fusion.facts_ref, bf16[80,128,256]{2,1,0:T(8,128)(2,1)S(1)} %copy-done.1, bf16[4,2,128,128]{3,2,1,0:T(8,128)(2,1)S(1)} %collective-permute-done.3.green_ref, f32[16,128,256]{2,1,0:T(8,128)S(1)} %shard_map.60.before_ref), custom_call_target="tpu_custom_call" | custom-call | tf_op jit(solution)/shard_map/pallas_call | solution.py:219
  54.8 0.0 collective-permute-done.2.green_ref
  54.9 1.4 %shard_map.62 = (f32[16,64,256]{2,1,0:T(8,128)S(1)}, bf16[16,64,256]{2,1,0:T(8,128)(2,1)S(1)}) custom-call(s32[16]{0:T(128)S(1)} %copy-done.5, s32[5]{0:T(128)S(1)} %pad_add_fusion.facts_ref, s32[1]{0:T(128)} %bitcast.2.core_ref, bf16[80,128,256]{2,1,0:T(8,128)(2,1)S(1)} %copy-done.1, bf16[2,2,128,128]{3,2,1,0:T(8,128)(2,1)S(1)} %collective-permute-done.2.green_ref, ...), custom_call_target="tpu_custom_call" | custom-call | tf_op jit(solution)/shard_map/pallas_call | solution.py:219
  56.3 0.1 collective-permute-start.5
  56.5 1.8 %collective-permute-done.5 = bf16[16,64,256]{2,1,0:T(8,128)(2,1)S(1)} collective-permute-done((bf16[16,64,256]{2,1,0:T(8,128)(2,1)S(1)}, bf16[16,64,256]{2,1,0:T(8,128)(2,1)S(1)}, u32[]{:S(2)}, u32[]{:S(2)}) %collective-permute-start.5) | collective-permute-done | bytes 524320 | tf_op jit(solution)/shard_map/ppermute | solution.py:239
  58.2 0.1 convert_add_fusion
  58.4 0.1 fusion.10
  58.5 1.6 %collective-permute-start.7 = (bf16[2,16,8,256]{3,2,1,0:T(8,128)(2,1)S(1)}, bf16[2,16,8,256]{3,2,1,0:T(8,128)(2,1)S(1)}, u32[]{:S(2)}, u32[]{:S(2)}) collective-permute-start(bf16[2,16,8,256]{3,2,1,0:T(8,128)(2,1)S(1)} %pad_maximum_fusion.1), channel_id=1, source_target_pairs={{0,2},{1,3},{2,0},{3,1},{4,6},{5,7},{6,4},{7,5},{8,10},{9,11},{10,... | collective-permute-start | bytes 393224 | tf_op jit(solution)/shard_map/ppermute | solution.py:249
  60.1 0.6 collective-permute-start.6
  60.7 4.2 %collective-permute-done.7 = bf16[2,16,8,256]{3,2,1,0:T(8,128)(2,1)S(1)} collective-permute-done((bf16[2,16,8,256]{3,2,1,0:T(8,128)(2,1)S(1)}, bf16[2,16,8,256]{3,2,1,0:T(8,128)(2,1)S(1)}, u32[]{:S(2)}, u32[]{:S(2)}) %collective-permute-start.7) | collective-permute-done | bytes 131104 | tf_op jit(solution)/shard_map/ppermute | solution.py:249
  64.9 1.8 %collective-permute-start.8 = (bf16[16,8,256]{2,1,0:T(8,128)(2,1)S(1)}, bf16[16,8,256]{2,1,0:T(8,128)(2,1)S(1)}, u32[]{:S(2)}, u32[]{:S(2)}) collective-permute-start(bf16[16,8,256]{2,1,0:T(8,128)(2,1)S(1)} %get-tuple-element.27), channel_id=1, source_target_pairs={{0,8},{1,9},{2,10},{3,11},{4,12},{5,13},{6,14},{7,15},{8,0},{9,1},... | collective-permute-start | bytes 196616 | tf_op jit(solution)/shard_map/ppermute | solution.py:255
  66.7 1.6 %collective-permute-start.9 = (bf16[16,8,256]{2,1,0:T(8,128)(2,1)S(1)}, bf16[16,8,256]{2,1,0:T(8,128)(2,1)S(1)}, u32[]{:S(2)}, u32[]{:S(2)}) collective-permute-start(bf16[16,8,256]{2,1,0:T(8,128)(2,1)S(1)} %get-tuple-element.28), channel_id=1, source_target_pairs={{0,4},{1,5},{2,6},{3,7},{4,8},{5,9},{6,10},{7,11},{8,12},{9,13},{1... | collective-permute-start | bytes 196616 | tf_op jit(solution)/shard_map/ppermute | solution.py:255
  68.3 0.0 collective-permute-done.6
  68.3 2.3 %collective-permute-start.10 = (bf16[16,8,256]{2,1,0:T(8,128)(2,1)S(1)}, bf16[16,8,256]{2,1,0:T(8,128)(2,1)S(1)}, u32[]{:S(2)}, u32[]{:S(2)}) collective-permute-start(bf16[16,8,256]{2,1,0:T(8,128)(2,1)S(1)} %fusion.7), channel_id=1, source_target_pairs={{0,12},{1,13},{2,14},{3,15},{4,0},{5,1},{6,2},{7,3},{8,4},{9,5},{1... | collective-permute-start | bytes 196616 | tf_op jit(solution)/shard_map/ppermute | solution.py:255
  70.6 1.6 %collective-permute-done.8 = bf16[16,8,256]{2,1,0:T(8,128)(2,1)S(1)} collective-permute-done((bf16[16,8,256]{2,1,0:T(8,128)(2,1)S(1)}, bf16[16,8,256]{2,1,0:T(8,128)(2,1)S(1)}, u32[]{:S(2)}, u32[]{:S(2)}) %collective-permute-start.8) | collective-permute-done | bytes 65568 | tf_op jit(solution)/shard_map/ppermute | solution.py:255
  72.2 0.7 collective-permute-done.9
  72.9 0.5 collective-permute-done.10
  73.4 0.1 reshape.52
  73.5 0.7 copy.14
  (12 shorter events, 0.2 us)
Async XLA Ops:
  0.0 8.0 %collective-permute-start = (bf16[32,2,128,128]{3,2,1,0:T(8,128)(2,1)}, bf16[32,2,128,128]{3,2,1,0:T(8,128)(2,1)}, u32[]{:S(2)}, u32[]{:S(2)}) collective-permute-start(bf16[32,2,128,128]{3,2,1,0:T(8,128)(2,1)} %own_ref.1), channel_id=1, source_target_pairs={{0,1},{1,0},{2,3},{3,2},{4,5},{5,4},{6,7},{7,6},{8,9},{9,8},{10,11... | collective-permute-start | bytes 6291464 | tf_op jit(solution)/shard_map/ppermute | solution.py:284
  0.5 1.6 %copy-start.2 = (bf16[32,2,128,128]{3,2,1,0:T(8,128)(2,1)S(1)}, bf16[32,2,128,128]{3,2,1,0:T(8,128)(2,1)}, u32[]{:S(2)}) copy-start(bf16[32,2,128,128]{3,2,1,0:T(8,128)(2,1)} %green_ref.1) | copy-start | bytes 6291460
  2.0 5.6 %copy-start.8 = (bf16[2,128,128]{2,1,0:T(8,128)(2,1)S(1)}, bf16[2,128,128]{2,1,0:T(8,128)(2,1)}, u32[]{:S(2)}) copy-start(bf16[2,128,128]{2,1,0:T(8,128)(2,1)} %param.7) | copy-start | bytes 196612
  2.2 36.1 %collective-permute-start.1 = (bf16[20,2,128,128]{3,2,1,0:T(8,128)(2,1)S(1)}, bf16[20,2,128,128]{3,2,1,0:T(8,128)(2,1)}, u32[]{:S(2)}, u32[]{:S(2)}) collective-permute-start(bf16[20,2,128,128]{3,2,1,0:T(8,128)(2,1)S(1)} %shard_map.57), channel_id=1, source_target_pairs={{0,2},{1,3},{2,4},{3,5},{4,6},{5,7},{6,8},{7,9},{8,10},{9,11},{10,... | collective-permute-start | bytes 3932168 | tf_op jit(solution)/shard_map/ppermute | solution.py:274
  8.0 9.7 %copy-start.3 = (bf16[32,2,128,128]{3,2,1,0:T(8,128)(2,1)S(1)}, bf16[32,2,128,128]{3,2,1,0:T(8,128)(2,1)}, u32[]{:S(2)}) copy-start(bf16[32,2,128,128]{3,2,1,0:T(8,128)(2,1)} %green_ref.1) | copy-start | bytes 6291460
  8.0 1.7 %copy-start.4 = (bf16[32,2,128,128]{3,2,1,0:T(8,128)(2,1)S(1)}, bf16[32,2,128,128]{3,2,1,0:T(8,128)(2,1)}, u32[]{:S(2)}) copy-start(bf16[32,2,128,128]{3,2,1,0:T(8,128)(2,1)} %own_ref.1) | copy-start | bytes 6291460
  15.4 2.3 %copy-start = (bf16[80,128,256]{2,1,0:T(8,128)(2,1)}, bf16[80,128,256]{2,1,0:T(8,128)(2,1)S(1)}, u32[]{:S(2)}) copy-start(bf16[80,128,256]{2,1,0:T(8,128)(2,1)S(1)} %shard_map.55.proj_ref) | copy-start | bytes 15728644
  17.7 5.0 %copy-start.9 = (s32[2]{0:T(128)S(1)}, s32[2]{0:T(128)}, u32[]{:S(2)}) copy-start(s32[2]{0:T(128)} %param.9) | copy-start | bytes 28
  17.7 5.1 %copy-start.5 = (s32[16]{0:T(128)S(1)}, s32[16]{0:T(128)}, u32[]{:S(2)}) copy-start(s32[16]{0:T(128)} %shifts_ref.9) | copy-start | bytes 196
  18.9 0.7 copy-start.6
  19.6 29.8 %collective-permute-start.4 = (bf16[6,2,128,128]{3,2,1,0:T(8,128)(2,1)}, bf16[6,2,128,128]{3,2,1,0:T(8,128)(2,1)}, u32[]{:S(2)}, u32[]{:S(2)}) collective-permute-start(bf16[6,2,128,128]{3,2,1,0:T(8,128)(2,1)} %get-tuple-element.23), channel_id=1, source_target_pairs={{0,2},{1,3},{2,4},{3,5},{4,6},{5,7},{6,8},{7,9},{8,10},{9,11},{10,... | collective-permute-start | bytes 1179656 | tf_op jit(solution)/shard_map/ppermute | solution.py:288
  22.8 2.5 %copy-start.1 = (bf16[80,128,256]{2,1,0:T(8,128)(2,1)S(1)}, bf16[80,128,256]{2,1,0:T(8,128)(2,1)}, u32[]{:S(2)}) copy-start(bf16[80,128,256]{2,1,0:T(8,128)(2,1)} %copy-done) | copy-start | bytes 15728644
  25.3 10.2 %copy-start.7 = (bf16[4,2,128,128]{3,2,1,0:T(8,128)(2,1)S(1)}, bf16[4,2,128,128]{3,2,1,0:T(8,128)(2,1)}, u32[]{:S(2)}) copy-start(bf16[4,2,128,128]{3,2,1,0:T(8,128)(2,1)} %copy-done.6) | copy-start | bytes 786436
  35.6 17.4 %collective-permute-start.3 = (bf16[4,2,128,128]{3,2,1,0:T(8,128)(2,1)S(1)}, bf16[4,2,128,128]{3,2,1,0:T(8,128)(2,1)S(1)}, u32[]{:S(2)}, u32[]{:S(2)}) collective-permute-start(bf16[4,2,128,128]{3,2,1,0:T(8,128)(2,1)S(1)} %copy-done.7), channel_id=1, source_target_pairs={{0,2},{1,3},{2,4},{3,5},{4,6},{5,7},{6,8},{7,9},{8,10},{9,11},{10,... | collective-permute-start | bytes 786440 | tf_op jit(solution)/shard_map/ppermute | solution.py:299
  46.0 8.8 %collective-permute-start.2 = (bf16[2,2,128,128]{3,2,1,0:T(8,128)(2,1)S(1)}, bf16[2,2,128,128]{3,2,1,0:T(8,128)(2,1)S(1)}, u32[]{:S(2)}, u32[]{:S(2)}) collective-permute-start(bf16[2,2,128,128]{3,2,1,0:T(8,128)(2,1)S(1)} %get-tuple-element.21), channel_id=1, source_target_pairs={{0,2},{1,3},{2,4},{3,5},{4,6},{5,7},{6,8},{7,9},{8,10},{9,11},{10,... | collective-permute-start | bytes 393224 | tf_op jit(solution)/shard_map/ppermute | solution.py:299
  56.3 2.0 %collective-permute-start.5 = (bf16[16,64,256]{2,1,0:T(8,128)(2,1)S(1)}, bf16[16,64,256]{2,1,0:T(8,128)(2,1)S(1)}, u32[]{:S(2)}, u32[]{:S(2)}) collective-permute-start(bf16[16,64,256]{2,1,0:T(8,128)(2,1)S(1)} %get-tuple-element.26), channel_id=1, source_target_pairs={{0,1},{1,0},{2,3},{3,2},{4,5},{5,4},{6,7},{7,6},{8,9},{9,8},{10,11... | collective-permute-start | bytes 1572872 | tf_op jit(solution)/shard_map/ppermute | solution.py:239
  58.5 6.4 %collective-permute-start.7 = (bf16[2,16,8,256]{3,2,1,0:T(8,128)(2,1)S(1)}, bf16[2,16,8,256]{3,2,1,0:T(8,128)(2,1)S(1)}, u32[]{:S(2)}, u32[]{:S(2)}) collective-permute-start(bf16[2,16,8,256]{3,2,1,0:T(8,128)(2,1)S(1)} %pad_maximum_fusion.1), channel_id=1, source_target_pairs={{0,2},{1,3},{2,0},{3,1},{4,6},{5,7},{6,4},{7,5},{8,10},{9,11},{10,... | collective-permute-start | bytes 393224 | tf_op jit(solution)/shard_map/ppermute | solution.py:249
  60.1 8.2 %collective-permute-start.6 = (bf16[2,16,8,256]{3,2,1,0:T(8,128)(2,1)S(1)}, bf16[2,16,8,256]{3,2,1,0:T(8,128)(2,1)S(1)}, u32[]{:S(2)}, u32[]{:S(2)}) collective-permute-start(bf16[2,16,8,256]{3,2,1,0:T(8,128)(2,1)S(1)} %pad_maximum_fusion), channel_id=1, source_target_pairs={{0,2},{1,3},{2,0},{3,1},{4,6},{5,7},{6,4},{7,5},{8,10},{9,11},{10,... | collective-permute-start | bytes 393224 | tf_op jit(solution)/shard_map/ppermute | solution.py:249
  64.9 7.3 %collective-permute-start.8 = (bf16[16,8,256]{2,1,0:T(8,128)(2,1)S(1)}, bf16[16,8,256]{2,1,0:T(8,128)(2,1)S(1)}, u32[]{:S(2)}, u32[]{:S(2)}) collective-permute-start(bf16[16,8,256]{2,1,0:T(8,128)(2,1)S(1)} %get-tuple-element.27), channel_id=1, source_target_pairs={{0,8},{1,9},{2,10},{3,11},{4,12},{5,13},{6,14},{7,15},{8,0},{9,1},... | collective-permute-start | bytes 196616 | tf_op jit(solution)/shard_map/ppermute | solution.py:255
  66.7 6.2 %collective-permute-start.9 = (bf16[16,8,256]{2,1,0:T(8,128)(2,1)S(1)}, bf16[16,8,256]{2,1,0:T(8,128)(2,1)S(1)}, u32[]{:S(2)}, u32[]{:S(2)}) collective-permute-start(bf16[16,8,256]{2,1,0:T(8,128)(2,1)S(1)} %get-tuple-element.28), channel_id=1, source_target_pairs={{0,4},{1,5},{2,6},{3,7},{4,8},{5,9},{6,10},{7,11},{8,12},{9,13},{1... | collective-permute-start | bytes 196616 | tf_op jit(solution)/shard_map/ppermute | solution.py:255
  68.3 5.1 %collective-permute-start.10 = (bf16[16,8,256]{2,1,0:T(8,128)(2,1)S(1)}, bf16[16,8,256]{2,1,0:T(8,128)(2,1)S(1)}, u32[]{:S(2)}, u32[]{:S(2)}) collective-permute-start(bf16[16,8,256]{2,1,0:T(8,128)(2,1)S(1)} %fusion.7), channel_id=1, source_target_pairs={{0,12},{1,13},{2,14},{3,15},{4,0},{5,1},{6,2},{7,3},{8,4},{9,5},{1... | collective-permute-start | bytes 196616 | tf_op jit(solution)/shard_map/ppermute | solution.py:255

commit v11 on v9

--- a/solution.py
+++ b/solution.py
@@ -236,11 +236,18 @@
     index = lax.axis_index("energy")
     plane, chip = index // 4, (index // 2) % 2
     photons, half, width = keep.shape
-    got = lax.ppermute(send, "energy", [(i, i ^ 1) for i in range(devices)])
-    both = keep + got.astype(jnp.float32)
-    both = both.reshape(photons, 2, planes, share, width)
-    both = jnp.transpose(both, (1, 2, 0, 3, 4))
-    theirs, mine = pick(both, 1 - chip), pick(both, chip)
+    rows = half // 2
+
+    def over_cores(chip):
+        mine = lax.dynamic_slice_in_dim(keep, chip * rows, rows, 1)
+        part = lax.dynamic_slice_in_dim(send, chip * rows, rows, 1)
+        got = lax.ppermute(part, "energy", [(i, i ^ 1) for i in range(devices)])
+        both = (mine + got.astype(jnp.float32)).reshape(photons, planes, share, width)
+        return jnp.transpose(both, (1, 0, 2, 3))
+
+    theirs = over_cores(1 - chip)
+    keep = lax.optimization_barrier(keep)
+    mine = over_cores(chip)
     steps = sorted(range(1, planes), key=lambda k: -min(k, planes - k)) + [0]
     sums = []
     for part in (steps[: planes // 2], steps[planes // 2 :]):

time: 75.1 us -> 74.9 us (level)
  starting transfers between devices: 24.3 us -> 22.3 us
  local copies, waits for them, and re-layouts: 9.94 us -> 11.8 us
    ppermute x3, starting transfers between devices: 6.73 us -> 4.46 us  [reduced(): lax.ppermute(block.astype(jnp.bfloat16), 'energy', route)]
    unnamed x22 -> x20, local copies, waits for them, and re-layouts: 9.06 us -> 10.9 us
    ppermute x1 -> x2, waiting for transfers between devices: 1.75 us -> 1.03 us  [over_cores(): got = lax.ppermute(part, 'energy', [(i, i ^ 1) for i in range(devices)])]
  transfers between devices with their start and end apart: 11 -> 12, of which waited for: 4 -> 4; matrix products, arithmetic and copies ran while one was open for 1% -> 1% of each run, Pallas kernels for 40% -> 40%
where the time goes in v11:
time: 74.9 us; the launch traced here: 74.5 us
  Pallas kernels  31 us (41%)
  starting transfers between devices  22.3 us (30%)
  local copies, waits for them, and re-layouts  11.8 us (16%)
  waiting for transfers between devices  8.51 us (11%)
    pallas_call x5, Pallas kernels, products(): pl.pallas_call(kernel, out_shape=out_shape, grid=(energies // step,), in_...  24 us
    unnamed x20, local copies, waits for them, and re-layouts  10.9 us
    ppermute x2, starting transfers between devices, on_device(): far.append(lax.ppermute(pieces[k + 2], 'energy', up))  6.1 us
    pallas_call x1, Pallas kernels, project(): pl.pallas_call(functools.partial(project_kernel, steps), out_shape=jax.Sh...  5.62 us
    ppermute x1, starting transfers between devices, on_device(): far = [lax.ppermute(pieces[0], 'energy', up)]  5.41 us
    ppermute x3, starting transfers between devices, reduced(): lax.ppermute(block.astype(jnp.bfloat16), 'energy', route)  4.46 us
    ppermute x2, waiting for transfers between devices, reduced(): got = lax.ppermute(send, 'energy', [(i, i ^ 2) for i in range(devices)])  4.09 us
    ppermute x3, waiting for transfers between devices, reduced(): lax.ppermute(block.astype(jnp.bfloat16), 'energy', route)  3.39 us
  transfers between devices with their start and end apart: 12, of which 4 were waited for; matrix products, arithmetic and copies ran while one was open for 1% of the time, Pallas kernels for 40%

profile of v11, /device:TPU:0, one launch (start us, length us, event | category | flops | bytes accessed | tf_op | source)
XLA Modules:
  0.0 74.5 jit_solution(14333420576657894527)
XLA Ops:
  0.0 0.5 collective-permute-start
  0.5 0.0 copy-start.3
  0.5 1.6 %copy-done.3 = bf16[32,2,128,128]{3,2,1,0:T(8,128)(2,1)S(1)} copy-done((bf16[32,2,128,128]{3,2,1,0:T(8,128)(2,1)S(1)}, bf16[32,2,128,128]{3,2,1,0:T(8,128)(2,1)}, u32[]{:S(2)}) %copy-start.3) | copy-done | bytes 2097176
  2.0 0.0 copy-start.7
  2.0 0.1 shard_map.57
  2.1 5.4 %collective-permute-start.1 = (bf16[16,2,128,128]{3,2,1,0:T(8,128)(2,1)S(1)}, bf16[16,2,128,128]{3,2,1,0:T(8,128)(2,1)}, u32[]{:S(2)}, u32[]{:S(2)}) collective-permute-start(bf16[16,2,128,128]{3,2,1,0:T(8,128)(2,1)S(1)} %shard_map.57), channel_id=1, source_target_pairs={{0,2},{1,3},{2,4},{3,5},{4,6},{5,7},{6,8},{7,9},{8,10},{9,11},{10,... | collective-permute-start | bytes 3145736 | tf_op jit(solution)/shard_map/ppermute | solution.py:281
  7.5 0.0 copy-done.7
  7.5 0.1 copy.16
  7.7 0.1 copy.15
  7.9 0.0 copy-start.4
  7.9 0.0 collective-permute-done.other_ref
  7.9 0.0 copy-start.5
  7.9 1.7 %copy-done.5 = bf16[32,2,128,128]{3,2,1,0:T(8,128)(2,1)S(1)} copy-done((bf16[32,2,128,128]{3,2,1,0:T(8,128)(2,1)S(1)}, bf16[32,2,128,128]{3,2,1,0:T(8,128)(2,1)}, u32[]{:S(2)}) %copy-start.5) | copy-done | bytes 2097176
  9.7 5.6 %shard_map.55.proj_ref = bf16[80,128,256]{2,1,0:T(8,128)(2,1)S(1)} custom-call(bf16[128,256]{1,0:T(8,128)(2,1)S(1)} %pad_maximum_fusion.2.left_ref, bf16[256,256]{1,0:T(8,128)(2,1)S(1)} %maximum_maximum_fusion.right_ref, bf16[32,2,128,128]{3,2,1,0:T(8,128)(2,1)S(1)} %copy-done.5, bf16[32,2,128,128]{3,2,1,0:T(8,128)(2,1)} %collective-permute-done.other_ref), custom_call_target="tpu_custom_call" | custom-call | tf_op jit(solution)/shard_map/pallas_call | solution.py:88
  15.3 0.0 copy-start
  15.3 2.3 %copy-done = bf16[80,128,256]{2,1,0:T(8,128)(2,1)} copy-done((bf16[80,128,256]{2,1,0:T(8,128)(2,1)}, bf16[80,128,256]{2,1,0:T(8,128)(2,1)S(1)}, u32[]{:S(2)}) %copy-start) | copy-done | bytes 5242904
  17.6 0.0 copy-done.4
  17.6 0.0 copy-start.8
  17.6 0.0 copy-start.6
  17.6 1.4 %shard_map.56 = (bf16[8,2,128,128]{3,2,1,0:T(8,128)(2,1)}, bf16[6,2,128,128]{3,2,1,0:T(8,128)(2,1)}, bf16[2,2,128,128]{3,2,1,0:T(8,128)(2,1)}) custom-call(bf16[32,2,128,128]{3,2,1,0:T(8,128)(2,1)S(1)} %copy-done.4), custom_call_target="tpu_custom_call" | custom-call | tf_op jit(solution)/shard_map/pallas_call | solution.py:39
  19.0 3.3 %collective-permute-start.4 = (bf16[8,2,128,128]{3,2,1,0:T(8,128)(2,1)}, bf16[8,2,128,128]{3,2,1,0:T(8,128)(2,1)}, u32[]{:S(2)}, u32[]{:S(2)}) collective-permute-start(bf16[8,2,128,128]{3,2,1,0:T(8,128)(2,1)} %get-tuple-element.23), channel_id=1, source_target_pairs={{0,2},{1,3},{2,4},{3,5},{4,6},{5,7},{6,8},{7,9},{8,10},{9,11},{10,... | collective-permute-start | bytes 1572872 | tf_op jit(solution)/shard_map/ppermute | solution.py:295
  22.3 0.0 copy-done.8
  22.3 0.1 pad_add_fusion.facts_ref
  22.4 0.0 copy-done.6
  22.4 0.0 copy-start.1
  22.4 2.5 %copy-done.1 = bf16[80,128,256]{2,1,0:T(8,128)(2,1)S(1)} copy-done((bf16[80,128,256]{2,1,0:T(8,128)(2,1)S(1)}, bf16[80,128,256]{2,1,0:T(8,128)(2,1)}, u32[]{:S(2)}) %copy-start.1) | copy-done | bytes 5242904
  24.9 10.2 %shard_map.58.before_ref = f32[16,128,256]{2,1,0:T(8,128)S(1)} custom-call(s32[16]{0:T(128)S(1)} %copy-done.6, s32[5]{0:T(128)S(1)} %pad_add_fusion.facts_ref, bf16[80,128,256]{2,1,0:T(8,128)(2,1)S(1)} %copy-done.1, bf16[32,2,128,128]{3,2,1,0:T(8,128)(2,1)S(1)} %copy-done.4), custom_call_target="tpu_custom_call" | custom-call | tf_op jit(solution)/shard_map/pallas_call | solution.py:219
  35.1 2.7 %collective-permute-start.3 = (bf16[6,2,128,128]{3,2,1,0:T(8,128)(2,1)}, bf16[6,2,128,128]{3,2,1,0:T(8,128)(2,1)S(1)}, u32[]{:S(2)}, u32[]{:S(2)}) collective-permute-start(bf16[6,2,128,128]{3,2,1,0:T(8,128)(2,1)} %get-tuple-element.22), channel_id=1, source_target_pairs={{0,2},{1,3},{2,4},{3,5},{4,6},{5,7},{6,8},{7,9},{8,10},{9,11},{10,... | collective-permute-start | bytes 1179656 | tf_op jit(solution)/shard_map/ppermute | solution.py:306
  37.8 0.0 collective-permute-done.1.green_ref
  37.8 5.9 %shard_map.59.before_ref = f32[16,128,256]{2,1,0:T(8,128)S(1)} custom-call(s32[16]{0:T(128)S(1)} %copy-done.6, s32[5]{0:T(128)S(1)} %pad_add_fusion.facts_ref, bf16[80,128,256]{2,1,0:T(8,128)(2,1)S(1)} %copy-done.1, bf16[16,2,128,128]{3,2,1,0:T(8,128)(2,1)} %collective-permute-done.1.green_ref, f32[16,128,256]{2,1,0:T(8,128)S(1)} %shard_map.58.before_ref), custom_call_target="tpu_custom_call" | custom-call | tf_op jit(solution)/shard_map/pallas_call | solution.py:219
  43.7 3.4 %collective-permute-start.2 = (bf16[2,2,128,128]{3,2,1,0:T(8,128)(2,1)}, bf16[2,2,128,128]{3,2,1,0:T(8,128)(2,1)S(1)}, u32[]{:S(2)}, u32[]{:S(2)}) collective-permute-start(bf16[2,2,128,128]{3,2,1,0:T(8,128)(2,1)} %get-tuple-element.21), channel_id=1, source_target_pairs={{0,2},{1,3},{2,4},{3,5},{4,6},{5,7},{6,8},{7,9},{8,10},{9,11},{10,... | collective-permute-start | bytes 393224 | tf_op jit(solution)/shard_map/ppermute | solution.py:306
  47.2 0.0 collective-permute-done.4.green_ref
  47.2 0.0 copy-start.2
  47.2 2.5 %copy-done.2 = bf16[80,128,256]{2,1,0:T(8,128)(2,1)S(1)} copy-done((bf16[80,128,256]{2,1,0:T(8,128)(2,1)S(1)}, bf16[80,128,256]{2,1,0:T(8,128)(2,1)}, u32[]{:S(2)}) %copy-start.2) | copy-done | bytes 5242904
  49.7 3.4 %shard_map.60.before_ref = f32[16,128,256]{2,1,0:T(8,128)S(1)} custom-call(s32[16]{0:T(128)S(1)} %copy-done.6, s32[5]{0:T(128)S(1)} %pad_add_fusion.facts_ref, bf16[80,128,256]{2,1,0:T(8,128)(2,1)S(1)} %copy-done.2, bf16[8,2,128,128]{3,2,1,0:T(8,128)(2,1)} %collective-permute-done.4.green_ref, f32[16,128,256]{2,1,0:T(8,128)S(1)} %shard_map.59.before_ref), custom_call_target="tpu_custom_call" | custom-call | tf_op jit(solution)/shard_map/pallas_call | solution.py:219
  53.1 0.0 collective-permute-done.3.green_ref
  53.1 3.0 %shard_map.61.before_ref = f32[16,128,256]{2,1,0:T(8,128)S(1)} custom-call(s32[16]{0:T(128)S(1)} %copy-done.6, s32[5]{0:T(128)S(1)} %pad_add_fusion.facts_ref, bf16[80,128,256]{2,1,0:T(8,128)(2,1)S(1)} %copy-done.2, bf16[6,2,128,128]{3,2,1,0:T(8,128)(2,1)S(1)} %collective-permute-done.3.green_ref, f32[16,128,256]{2,1,0:T(8,128)S(1)} %shard_map.60.before_ref), custom_call_target="tpu_custom_call" | custom-call | tf_op jit(solution)/shard_map/pallas_call | solution.py:219
  56.1 0.0 collective-permute-done.2.green_ref
  56.1 1.4 %shard_map.62 = (f32[16,64,256]{2,1,0:T(8,128)S(1)}, bf16[16,64,256]{2,1,0:T(8,128)(2,1)S(1)}) custom-call(s32[16]{0:T(128)S(1)} %copy-done.6, s32[5]{0:T(128)S(1)} %pad_add_fusion.facts_ref, s32[1]{0:T(128)} %bitcast.2.core_ref, bf16[80,128,256]{2,1,0:T(8,128)(2,1)S(1)} %copy-done.2, bf16[2,2,128,128]{3,2,1,0:T(8,128)(2,1)S(1)} %collective-permute-done.2.green_ref, ...), custom_call_target="tpu_custom_call" | custom-call | tf_op jit(solution)/shard_map/pallas_call | solution.py:219
  57.6 0.1 collective-permute-start.6
  57.8 0.4 collective-permute-start.5
  58.2 1.0 %collective-permute-done.6 = bf16[16,32,256]{2,1,0:T(8,128)(2,1)S(1)} collective-permute-done((bf16[16,32,256]{2,1,0:T(8,128)(2,1)S(1)}, bf16[16,32,256]{2,1,0:T(8,128)(2,1)S(1)}, u32[]{:S(2)}, u32[]{:S(2)}) %collective-permute-start.6) | collective-permute-done | bytes 262176 | tf_op jit(solution)/shard_map/ppermute | solution.py:244
  59.2 0.1 add_bitcast_fusion
  59.4 1.6 %collective-permute-start.8 = (bf16[2,16,8,256]{3,2,1,0:T(8,128)(2,1)S(1)}, bf16[2,16,8,256]{3,2,1,0:T(8,128)(2,1)S(1)}, u32[]{:S(2)}, u32[]{:S(2)}) collective-permute-start(bf16[2,16,8,256]{3,2,1,0:T(8,128)(2,1)S(1)} %pad_maximum_fusion.1), channel_id=1, source_target_pairs={{0,2},{1,3},{2,0},{3,1},{4,6},{5,7},{6,4},{7,5},{8,10},{9,11},{10,... | collective-permute-start | bytes 393224 | tf_op jit(solution)/shard_map/ppermute | solution.py:256
  61.0 0.6 collective-permute-start.7
  61.5 0.0 collective-permute-done.5
  61.5 0.1 copy_bitcast_fusion
  61.6 0.1 add_bitcast_fusion.1
  61.7 4.1 %collective-permute-done.8 = bf16[2,16,8,256]{3,2,1,0:T(8,128)(2,1)S(1)} collective-permute-done((bf16[2,16,8,256]{3,2,1,0:T(8,128)(2,1)S(1)}, bf16[2,16,8,256]{3,2,1,0:T(8,128)(2,1)S(1)}, u32[]{:S(2)}, u32[]{:S(2)}) %collective-permute-start.8) | collective-permute-done | bytes 131104 | tf_op jit(solution)/shard_map/ppermute | solution.py:256
  65.8 1.6 %collective-permute-start.10 = (bf16[16,8,256]{2,1,0:T(8,128)(2,1)S(1)}, bf16[16,8,256]{2,1,0:T(8,128)(2,1)S(1)}, u32[]{:S(2)}, u32[]{:S(2)}) collective-permute-start(bf16[16,8,256]{2,1,0:T(8,128)(2,1)S(1)} %get-tuple-element.28), channel_id=1, source_target_pairs={{0,4},{1,5},{2,6},{3,7},{4,8},{5,9},{6,10},{7,11},{8,12},{9,13},{1... | collective-permute-start | bytes 196616 | tf_op jit(solution)/shard_map/ppermute | solution.py:262
  67.4 1.0 %collective-permute-start.9 = (bf16[16,8,256]{2,1,0:T(8,128)(2,1)S(1)}, bf16[16,8,256]{2,1,0:T(8,128)(2,1)S(1)}, u32[]{:S(2)}, u32[]{:S(2)}) collective-permute-start(bf16[16,8,256]{2,1,0:T(8,128)(2,1)S(1)} %get-tuple-element.27), channel_id=1, source_target_pairs={{0,8},{1,9},{2,10},{3,11},{4,12},{5,13},{6,14},{7,15},{8,0},{9,1},... | collective-permute-start | bytes 196616 | tf_op jit(solution)/shard_map/ppermute | solution.py:262
  68.5 0.0 collective-permute-done.7
  68.5 1.8 %collective-permute-start.11 = (bf16[16,8,256]{2,1,0:T(8,128)(2,1)S(1)}, bf16[16,8,256]{2,1,0:T(8,128)(2,1)S(1)}, u32[]{:S(2)}, u32[]{:S(2)}) collective-permute-start(bf16[16,8,256]{2,1,0:T(8,128)(2,1)S(1)} %fusion.7), channel_id=1, source_target_pairs={{0,12},{1,13},{2,14},{3,15},{4,0},{5,1},{6,2},{7,3},{8,4},{9,5},{1... | collective-permute-start | bytes 196616 | tf_op jit(solution)/shard_map/ppermute | solution.py:262
  70.3 1.8 %collective-permute-done.10 = bf16[16,8,256]{2,1,0:T(8,128)(2,1)S(1)} collective-permute-done((bf16[16,8,256]{2,1,0:T(8,128)(2,1)S(1)}, bf16[16,8,256]{2,1,0:T(8,128)(2,1)S(1)}, u32[]{:S(2)}, u32[]{:S(2)}) %collective-permute-start.10) | collective-permute-done | bytes 65568 | tf_op jit(solution)/shard_map/ppermute | solution.py:262
  72.1 1.6 %collective-permute-done.9 = bf16[16,8,256]{2,1,0:T(8,128)(2,1)S(1)} collective-permute-done((bf16[16,8,256]{2,1,0:T(8,128)(2,1)S(1)}, bf16[16,8,256]{2,1,0:T(8,128)(2,1)S(1)}, u32[]{:S(2)}, u32[]{:S(2)}) %collective-permute-start.9) | collective-permute-done | bytes 65568 | tf_op jit(solution)/shard_map/ppermute | solution.py:262
  73.7 0.0 collective-permute-done.11
  73.7 0.1 reshape.44
  73.8 0.7 copy.14
  (13 shorter events, 0.3 us)
Async XLA Ops:
  0.0 7.9 %collective-permute-start = (bf16[32,2,128,128]{3,2,1,0:T(8,128)(2,1)}, bf16[32,2,128,128]{3,2,1,0:T(8,128)(2,1)}, u32[]{:S(2)}, u32[]{:S(2)}) collective-permute-start(bf16[32,2,128,128]{3,2,1,0:T(8,128)(2,1)} %own_ref.1), channel_id=1, source_target_pairs={{0,1},{1,0},{2,3},{3,2},{4,5},{5,4},{6,7},{7,6},{8,9},{9,8},{10,11... | collective-permute-start | bytes 6291464 | tf_op jit(solution)/shard_map/ppermute | solution.py:291
  0.5 1.6 %copy-start.3 = (bf16[32,2,128,128]{3,2,1,0:T(8,128)(2,1)S(1)}, bf16[32,2,128,128]{3,2,1,0:T(8,128)(2,1)}, u32[]{:S(2)}) copy-start(bf16[32,2,128,128]{3,2,1,0:T(8,128)(2,1)} %green_ref.1) | copy-start | bytes 6291460
  2.0 5.5 %copy-start.7 = (bf16[2,128,128]{2,1,0:T(8,128)(2,1)S(1)}, bf16[2,128,128]{2,1,0:T(8,128)(2,1)}, u32[]{:S(2)}) copy-start(bf16[2,128,128]{2,1,0:T(8,128)(2,1)} %param.7) | copy-start | bytes 196612
  2.1 35.7 %collective-permute-start.1 = (bf16[16,2,128,128]{3,2,1,0:T(8,128)(2,1)S(1)}, bf16[16,2,128,128]{3,2,1,0:T(8,128)(2,1)}, u32[]{:S(2)}, u32[]{:S(2)}) collective-permute-start(bf16[16,2,128,128]{3,2,1,0:T(8,128)(2,1)S(1)} %shard_map.57), channel_id=1, source_target_pairs={{0,2},{1,3},{2,4},{3,5},{4,6},{5,7},{6,8},{7,9},{8,10},{9,11},{10,... | collective-permute-start | bytes 3145736 | tf_op jit(solution)/shard_map/ppermute | solution.py:281
  7.9 9.7 %copy-start.4 = (bf16[32,2,128,128]{3,2,1,0:T(8,128)(2,1)S(1)}, bf16[32,2,128,128]{3,2,1,0:T(8,128)(2,1)}, u32[]{:S(2)}) copy-start(bf16[32,2,128,128]{3,2,1,0:T(8,128)(2,1)} %green_ref.1) | copy-start | bytes 6291460
  7.9 1.7 %copy-start.5 = (bf16[32,2,128,128]{3,2,1,0:T(8,128)(2,1)S(1)}, bf16[32,2,128,128]{3,2,1,0:T(8,128)(2,1)}, u32[]{:S(2)}) copy-start(bf16[32,2,128,128]{3,2,1,0:T(8,128)(2,1)} %own_ref.1) | copy-start | bytes 6291460
  15.3 2.3 %copy-start = (bf16[80,128,256]{2,1,0:T(8,128)(2,1)}, bf16[80,128,256]{2,1,0:T(8,128)(2,1)S(1)}, u32[]{:S(2)}) copy-start(bf16[80,128,256]{2,1,0:T(8,128)(2,1)S(1)} %shard_map.55.proj_ref) | copy-start | bytes 15728644
  17.6 4.7 %copy-start.8 = (s32[2]{0:T(128)S(1)}, s32[2]{0:T(128)}, u32[]{:S(2)}) copy-start(s32[2]{0:T(128)} %param.9) | copy-start | bytes 28
  17.6 4.7 %copy-start.6 = (s32[16]{0:T(128)S(1)}, s32[16]{0:T(128)}, u32[]{:S(2)}) copy-start(s32[16]{0:T(128)} %shifts_ref.9) | copy-start | bytes 196
  19.0 28.2 %collective-permute-start.4 = (bf16[8,2,128,128]{3,2,1,0:T(8,128)(2,1)}, bf16[8,2,128,128]{3,2,1,0:T(8,128)(2,1)}, u32[]{:S(2)}, u32[]{:S(2)}) collective-permute-start(bf16[8,2,128,128]{3,2,1,0:T(8,128)(2,1)} %get-tuple-element.23), channel_id=1, source_target_pairs={{0,2},{1,3},{2,4},{3,5},{4,6},{5,7},{6,8},{7,9},{8,10},{9,11},{10,... | collective-permute-start | bytes 1572872 | tf_op jit(solution)/shard_map/ppermute | solution.py:295
  22.4 2.5 %copy-start.1 = (bf16[80,128,256]{2,1,0:T(8,128)(2,1)S(1)}, bf16[80,128,256]{2,1,0:T(8,128)(2,1)}, u32[]{:S(2)}) copy-start(bf16[80,128,256]{2,1,0:T(8,128)(2,1)} %copy-done) | copy-start | bytes 15728644
  35.1 18.0 %collective-permute-start.3 = (bf16[6,2,128,128]{3,2,1,0:T(8,128)(2,1)}, bf16[6,2,128,128]{3,2,1,0:T(8,128)(2,1)S(1)}, u32[]{:S(2)}, u32[]{:S(2)}) collective-permute-start(bf16[6,2,128,128]{3,2,1,0:T(8,128)(2,1)} %get-tuple-element.22), channel_id=1, source_target_pairs={{0,2},{1,3},{2,4},{3,5},{4,6},{5,7},{6,8},{7,9},{8,10},{9,11},{10,... | collective-permute-start | bytes 1179656 | tf_op jit(solution)/shard_map/ppermute | solution.py:306
  43.7 12.4 %collective-permute-start.2 = (bf16[2,2,128,128]{3,2,1,0:T(8,128)(2,1)}, bf16[2,2,128,128]{3,2,1,0:T(8,128)(2,1)S(1)}, u32[]{:S(2)}, u32[]{:S(2)}) collective-permute-start(bf16[2,2,128,128]{3,2,1,0:T(8,128)(2,1)} %get-tuple-element.21), channel_id=1, source_target_pairs={{0,2},{1,3},{2,4},{3,5},{4,6},{5,7},{6,8},{7,9},{8,10},{9,11},{10,... | collective-permute-start | bytes 393224 | tf_op jit(solution)/shard_map/ppermute | solution.py:306
  47.2 2.5 %copy-start.2 = (bf16[80,128,256]{2,1,0:T(8,128)(2,1)S(1)}, bf16[80,128,256]{2,1,0:T(8,128)(2,1)}, u32[]{:S(2)}) copy-start(bf16[80,128,256]{2,1,0:T(8,128)(2,1)} %copy-done) | copy-start | bytes 15728644
  57.6 1.6 %collective-permute-start.6 = (bf16[16,32,256]{2,1,0:T(8,128)(2,1)S(1)}, bf16[16,32,256]{2,1,0:T(8,128)(2,1)S(1)}, u32[]{:S(2)}, u32[]{:S(2)}) collective-permute-start(bf16[16,32,256]{2,1,0:T(8,128)(2,1)S(1)} %get-tuple-element.29), channel_id=1, source_target_pairs={{0,1},{1,0},{2,3},{3,2},{4,5},{5,4},{6,7},{7,6},{8,9},{9,8},{10,11... | collective-permute-start | bytes 786440 | tf_op jit(solution)/shard_map/ppermute | solution.py:244
  57.8 3.8 %collective-permute-start.5 = (bf16[16,32,256]{2,1,0:T(8,128)(2,1)S(1)}, bf16[16,32,256]{2,1,0:T(8,128)(2,1)S(1)}, u32[]{:S(2)}, u32[]{:S(2)}) collective-permute-start(bf16[16,32,256]{2,1,0:T(8,128)(2,1)S(1)} %get-tuple-element.30), channel_id=1, source_target_pairs={{0,1},{1,0},{2,3},{3,2},{4,5},{5,4},{6,7},{7,6},{8,9},{9,8},{10,11... | collective-permute-start | bytes 786440 | tf_op jit(solution)/shard_map/ppermute | solution.py:244
  59.4 6.4 %collective-permute-start.8 = (bf16[2,16,8,256]{3,2,1,0:T(8,128)(2,1)S(1)}, bf16[2,16,8,256]{3,2,1,0:T(8,128)(2,1)S(1)}, u32[]{:S(2)}, u32[]{:S(2)}) collective-permute-start(bf16[2,16,8,256]{3,2,1,0:T(8,128)(2,1)S(1)} %pad_maximum_fusion.1), channel_id=1, source_target_pairs={{0,2},{1,3},{2,0},{3,1},{4,6},{5,7},{6,4},{7,5},{8,10},{9,11},{10,... | collective-permute-start | bytes 393224 | tf_op jit(solution)/shard_map/ppermute | solution.py:256
  61.0 7.5 %collective-permute-start.7 = (bf16[2,16,8,256]{3,2,1,0:T(8,128)(2,1)S(1)}, bf16[2,16,8,256]{3,2,1,0:T(8,128)(2,1)S(1)}, u32[]{:S(2)}, u32[]{:S(2)}) collective-permute-start(bf16[2,16,8,256]{3,2,1,0:T(8,128)(2,1)S(1)} %pad_maximum_fusion), channel_id=1, source_target_pairs={{0,2},{1,3},{2,0},{3,1},{4,6},{5,7},{6,4},{7,5},{8,10},{9,11},{10,... | collective-permute-start | bytes 393224 | tf_op jit(solution)/shard_map/ppermute | solution.py:256
  65.8 6.3 %collective-permute-start.10 = (bf16[16,8,256]{2,1,0:T(8,128)(2,1)S(1)}, bf16[16,8,256]{2,1,0:T(8,128)(2,1)S(1)}, u32[]{:S(2)}, u32[]{:S(2)}) collective-permute-start(bf16[16,8,256]{2,1,0:T(8,128)(2,1)S(1)} %get-tuple-element.28), channel_id=1, source_target_pairs={{0,4},{1,5},{2,6},{3,7},{4,8},{5,9},{6,10},{7,11},{8,12},{9,13},{1... | collective-permute-start | bytes 196616 | tf_op jit(solution)/shard_map/ppermute | solution.py:262
  67.4 6.2 %collective-permute-start.9 = (bf16[16,8,256]{2,1,0:T(8,128)(2,1)S(1)}, bf16[16,8,256]{2,1,0:T(8,128)(2,1)S(1)}, u32[]{:S(2)}, u32[]{:S(2)}) collective-permute-start(bf16[16,8,256]{2,1,0:T(8,128)(2,1)S(1)} %get-tuple-element.27), channel_id=1, source_target_pairs={{0,8},{1,9},{2,10},{3,11},{4,12},{5,13},{6,14},{7,15},{8,0},{9,1},... | collective-permute-start | bytes 196616 | tf_op jit(solution)/shard_map/ppermute | solution.py:262
  68.5 5.2 %collective-permute-start.11 = (bf16[16,8,256]{2,1,0:T(8,128)(2,1)S(1)}, bf16[16,8,256]{2,1,0:T(8,128)(2,1)S(1)}, u32[]{:S(2)}, u32[]{:S(2)}) collective-permute-start(bf16[16,8,256]{2,1,0:T(8,128)(2,1)S(1)} %fusion.7), channel_id=1, source_target_pairs={{0,12},{1,13},{2,14},{3,15},{4,0},{5,1},{6,2},{7,3},{8,4},{9,5},{1... | collective-permute-start | bytes 196616 | tf_op jit(solution)/shard_map/ppermute | solution.py:262

commit v12 on v9

--- a/solution.py
+++ b/solution.py
@@ -283,13 +283,14 @@
     )
     proj = project(left, right, lesser, lax.ppermute(lesser, "energy", across))
 
-    rest, proj = lax.optimization_barrier((greater, proj))
-    pieces += list(cut(rest, sizes[0], sizes[1:], 8))
-    far.append(lax.ppermute(pieces[1], "energy", up))
-
     limit = jnp.where(core == 0, 2 * e_dev, e_dev)
     facts = jnp.stack([window[0], window[1], index * e_dev, limit, jnp.int32(e_dev)])
     facts = facts.astype(jnp.int32)
+    facts = facts + proj[-1, 0, 0].astype(jnp.int32)
+    rest, facts = lax.optimization_barrier((greater, facts))
+    pieces += list(cut(rest, sizes[0], sizes[1:], 8))
+    far.append(lax.ppermute(pieces[1], "energy", up))
+
     result = products(shifts, facts, proj, greater)
     core = core[None]
     first = 0

time: 75.1 us -> 75.1 us (level)
  Pallas kernels: 31 us -> 29.7 us
    pallas_call x2, Pallas kernels: 1.3 us -> 0.5 us  [cut(): pl.pallas_call(functools.partial(cut_kernel, first, sizes), out_shape=[pl...]
    ppermute x3, starting transfers between devices: 6.73 us -> 7.5 us  [reduced(): lax.ppermute(block.astype(jnp.bfloat16), 'energy', route)]
    ppermute x1, starting transfers between devices: 3.25 us -> 2.49 us  [on_device(): far.append(lax.ppermute(pieces[1], 'energy', up))]
    unnamed x22 -> x18, local copies, waits for them, and re-layouts: 9.06 us -> 8.41 us
  transfers between devices with their start and end apart: 11 -> 11, of which waited for: 4 -> 4; matrix products, arithmetic and copies ran while one was open for 1% -> 1% of each run, Pallas kernels for 40% -> 38%
where the time goes in v12:
time: 75.1 us; the launch traced here: 74.7 us
  Pallas kernels  29.7 us (40%)
  starting transfers between devices  24.9 us (33%)
  local copies, waits for them, and re-layouts  9.88 us (13%)
  waiting for transfers between devices  8.68 us (12%)
  between operations  1.16 us (2%)
    pallas_call x5, Pallas kernels, products(): pl.pallas_call(kernel, out_shape=out_shape, grid=(energies // step,), in_...  23.6 us
    unnamed x18, local copies, waits for them, and re-layouts  8.41 us
    ppermute x3, starting transfers between devices, reduced(): lax.ppermute(block.astype(jnp.bfloat16), 'energy', route)  7.5 us
    ppermute x2, starting transfers between devices, on_device(): far.append(lax.ppermute(pieces[k + 2], 'energy', up))  6.83 us
    pallas_call x1, Pallas kernels, project(): pl.pallas_call(functools.partial(project_kernel, steps), out_shape=jax.Sh...  5.63 us
    ppermute x1, starting transfers between devices, on_device(): far = [lax.ppermute(pieces[0], 'energy', up)]  5.41 us
    ppermute x2, waiting for transfers between devices, reduced(): got = lax.ppermute(send, 'energy', [(i, i ^ 2) for i in range(devices)])  4.19 us
    ppermute x3, waiting for transfers between devices, reduced(): lax.ppermute(block.astype(jnp.bfloat16), 'energy', route)  2.72 us
  transfers between devices with their start and end apart: 11, of which 4 were waited for; matrix products, arithmetic and copies ran while one was open for 1% of the time, Pallas kernels for 38%

profile of v12, /device:TPU:0, one launch (start us, length us, event | category | flops | bytes accessed | tf_op | source)
XLA Modules:
  0.0 74.7 jit_solution(5087084202665867071)
XLA Ops:
  0.0 0.5 collective-permute-start
  0.5 0.0 copy-start.2
  0.5 1.6 %copy-done.2 = bf16[32,2,128,128]{3,2,1,0:T(8,128)(2,1)S(1)} copy-done((bf16[32,2,128,128]{3,2,1,0:T(8,128)(2,1)S(1)}, bf16[32,2,128,128]{3,2,1,0:T(8,128)(2,1)}, u32[]{:S(2)}) %copy-start.2) | copy-done | bytes 2097176
  2.0 0.0 copy-start.6
  2.0 0.1 shard_map.57
  2.1 5.4 %collective-permute-start.1 = (bf16[16,2,128,128]{3,2,1,0:T(8,128)(2,1)S(1)}, bf16[16,2,128,128]{3,2,1,0:T(8,128)(2,1)}, u32[]{:S(2)}, u32[]{:S(2)}) collective-permute-start(bf16[16,2,128,128]{3,2,1,0:T(8,128)(2,1)S(1)} %shard_map.57), channel_id=1, source_target_pairs={{0,2},{1,3},{2,4},{3,5},{4,6},{5,7},{6,8},{7,9},{8,10},{9,11},{10,... | collective-permute-start | bytes 3145736 | tf_op jit(solution)/shard_map/ppermute | solution.py:274
  7.5 0.0 copy-done.6
  7.6 0.1 copy.16
  7.7 0.1 copy.15
  7.9 0.0 copy-start.3
  7.9 0.0 collective-permute-done.other_ref
  7.9 0.0 copy-start.4
  8.0 1.7 %copy-done.4 = bf16[32,2,128,128]{3,2,1,0:T(8,128)(2,1)S(1)} copy-done((bf16[32,2,128,128]{3,2,1,0:T(8,128)(2,1)S(1)}, bf16[32,2,128,128]{3,2,1,0:T(8,128)(2,1)}, u32[]{:S(2)}) %copy-start.4) | copy-done | bytes 2097176
  9.7 0.0 copy-start.7
  9.7 5.6 %shard_map.55.proj_ref = bf16[80,128,256]{2,1,0:T(8,128)(2,1)S(1)} custom-call(bf16[128,256]{1,0:T(8,128)(2,1)S(1)} %pad_maximum_fusion.2.left_ref, bf16[256,256]{1,0:T(8,128)(2,1)S(1)} %maximum_maximum_fusion.right_ref, bf16[32,2,128,128]{3,2,1,0:T(8,128)(2,1)S(1)} %copy-done.4, bf16[32,2,128,128]{3,2,1,0:T(8,128)(2,1)} %collective-permute-done.other_ref), custom_call_target="tpu_custom_call" | custom-call | tf_op jit(solution)/shard_map/pallas_call | solution.py:88
  15.3 0.0 copy-start.5
  15.3 0.6 slice.43
  15.9 0.0 copy-start
  15.9 2.4 %copy-done = bf16[80,128,256]{2,1,0:T(8,128)(2,1)} copy-done((bf16[80,128,256]{2,1,0:T(8,128)(2,1)}, bf16[80,128,256]{2,1,0:T(8,128)(2,1)S(1)}, u32[]{:S(2)}) %copy-start) | copy-done | bytes 5242904
  19.0 0.0 copy-done.7
  19.0 0.1 add_add_fusion.facts_ref
  19.1 0.0 copy-done.3
  19.1 0.4 shard_map.56
  19.5 2.5 %collective-permute-start.4 = (bf16[8,2,128,128]{3,2,1,0:T(8,128)(2,1)S(1)}, bf16[8,2,128,128]{3,2,1,0:T(8,128)(2,1)S(1)}, u32[]{:S(2)}, u32[]{:S(2)}) collective-permute-start(bf16[8,2,128,128]{3,2,1,0:T(8,128)(2,1)S(1)} %get-tuple-element.23), channel_id=1, source_target_pairs={{0,2},{1,3},{2,4},{3,5},{4,6},{5,7},{6,8},{7,9},{8,10},{9,11},{10,... | collective-permute-start | bytes 1572872 | tf_op jit(solution)/shard_map/ppermute | solution.py:292
  22.0 0.0 copy-done.5
  22.0 0.0 copy-start.1
  22.0 2.5 %copy-done.1 = bf16[80,128,256]{2,1,0:T(8,128)(2,1)S(1)} copy-done((bf16[80,128,256]{2,1,0:T(8,128)(2,1)S(1)}, bf16[80,128,256]{2,1,0:T(8,128)(2,1)}, u32[]{:S(2)}) %copy-start.1) | copy-done | bytes 5242904
  24.5 10.2 %shard_map.58.before_ref = f32[16,128,256]{2,1,0:T(8,128)S(1)} custom-call(s32[16]{0:T(128)S(1)} %copy-done.5, s32[5]{0:T(128)S(1)} %add_add_fusion.facts_ref, bf16[80,128,256]{2,1,0:T(8,128)(2,1)S(1)} %copy-done.1, bf16[32,2,128,128]{3,2,1,0:T(8,128)(2,1)S(1)} %copy-done.3), custom_call_target="tpu_custom_call" | custom-call | tf_op jit(solution)/shard_map/pallas_call | solution.py:219
  34.7 3.4 %collective-permute-start.3 = (bf16[6,2,128,128]{3,2,1,0:T(8,128)(2,1)S(1)}, bf16[6,2,128,128]{3,2,1,0:T(8,128)(2,1)S(1)}, u32[]{:S(2)}, u32[]{:S(2)}) collective-permute-start(bf16[6,2,128,128]{3,2,1,0:T(8,128)(2,1)S(1)} %get-tuple-element.22), channel_id=1, source_target_pairs={{0,2},{1,3},{2,4},{3,5},{4,6},{5,7},{6,8},{7,9},{8,10},{9,11},{10,... | collective-permute-start | bytes 1179656 | tf_op jit(solution)/shard_map/ppermute | solution.py:300
  38.2 0.0 collective-permute-done.1.green_ref
  38.2 6.0 %shard_map.59.before_ref = f32[16,128,256]{2,1,0:T(8,128)S(1)} custom-call(s32[16]{0:T(128)S(1)} %copy-done.5, s32[5]{0:T(128)S(1)} %add_add_fusion.facts_ref, bf16[80,128,256]{2,1,0:T(8,128)(2,1)S(1)} %copy-done.1, bf16[16,2,128,128]{3,2,1,0:T(8,128)(2,1)} %collective-permute-done.1.green_ref, f32[16,128,256]{2,1,0:T(8,128)S(1)} %shard_map.58.before_ref), custom_call_target="tpu_custom_call" | custom-call | tf_op jit(solution)/shard_map/pallas_call | solution.py:219
  44.2 3.4 %collective-permute-start.2 = (bf16[2,2,128,128]{3,2,1,0:T(8,128)(2,1)S(1)}, bf16[2,2,128,128]{3,2,1,0:T(8,128)(2,1)S(1)}, u32[]{:S(2)}, u32[]{:S(2)}) collective-permute-start(bf16[2,2,128,128]{3,2,1,0:T(8,128)(2,1)S(1)} %get-tuple-element.21), channel_id=1, source_target_pairs={{0,2},{1,3},{2,4},{3,5},{4,6},{5,7},{6,8},{7,9},{8,10},{9,11},{10,... | collective-permute-start | bytes 393224 | tf_op jit(solution)/shard_map/ppermute | solution.py:300
  47.6 0.0 collective-permute-done.4.green_ref
  47.6 2.9 %shard_map.60.before_ref = f32[16,128,256]{2,1,0:T(8,128)S(1)} custom-call(s32[16]{0:T(128)S(1)} %copy-done.5, s32[5]{0:T(128)S(1)} %add_add_fusion.facts_ref, bf16[80,128,256]{2,1,0:T(8,128)(2,1)S(1)} %copy-done.1, bf16[8,2,128,128]{3,2,1,0:T(8,128)(2,1)S(1)} %collective-permute-done.4.green_ref, f32[16,128,256]{2,1,0:T(8,128)S(1)} %shard_map.59.before_ref), custom_call_target="tpu_custom_call" | custom-call | tf_op jit(solution)/shard_map/pallas_call | solution.py:219
  50.5 0.0 collective-permute-done.3.green_ref
  50.6 3.0 %shard_map.61.before_ref = f32[16,128,256]{2,1,0:T(8,128)S(1)} custom-call(s32[16]{0:T(128)S(1)} %copy-done.5, s32[5]{0:T(128)S(1)} %add_add_fusion.facts_ref, bf16[80,128,256]{2,1,0:T(8,128)(2,1)S(1)} %copy-done.1, bf16[6,2,128,128]{3,2,1,0:T(8,128)(2,1)S(1)} %collective-permute-done.3.green_ref, f32[16,128,256]{2,1,0:T(8,128)S(1)} %shard_map.60.before_ref), custom_call_target="tpu_custom_call" | custom-call | tf_op jit(solution)/shard_map/pallas_call | solution.py:219
  53.6 0.0 collective-permute-done.2.green_ref
  53.6 1.4 %shard_map.62 = (f32[16,64,256]{2,1,0:T(8,128)S(1)}, bf16[16,64,256]{2,1,0:T(8,128)(2,1)S(1)}) custom-call(s32[16]{0:T(128)S(1)} %copy-done.5, s32[5]{0:T(128)S(1)} %add_add_fusion.facts_ref, s32[1]{0:T(128)} %bitcast.13.core_ref, bf16[80,128,256]{2,1,0:T(8,128)(2,1)S(1)} %copy-done.1, bf16[2,2,128,128]{3,2,1,0:T(8,128)(2,1)S(1)} %collective-permute-done.2.green_ref, ...), custom_call_target="tpu_custom_call" | custom-call | tf_op jit(solution)/shard_map/pallas_call | solution.py:219
  55.0 0.1 collective-permute-start.5
  55.2 1.8 %collective-permute-done.5 = bf16[16,64,256]{2,1,0:T(8,128)(2,1)S(1)} collective-permute-done((bf16[16,64,256]{2,1,0:T(8,128)(2,1)S(1)}, bf16[16,64,256]{2,1,0:T(8,128)(2,1)S(1)}, u32[]{:S(2)}, u32[]{:S(2)}) %collective-permute-start.5) | collective-permute-done | bytes 524320 | tf_op jit(solution)/shard_map/ppermute | solution.py:239
  57.0 0.1 convert_add_fusion
  57.1 0.1 fusion.10
  57.2 1.7 %collective-permute-start.7 = (bf16[2,16,8,256]{3,2,1,0:T(8,128)(2,1)S(1)}, bf16[2,16,8,256]{3,2,1,0:T(8,128)(2,1)S(1)}, u32[]{:S(2)}, u32[]{:S(2)}) collective-permute-start(bf16[2,16,8,256]{3,2,1,0:T(8,128)(2,1)S(1)} %pad_maximum_fusion.1), channel_id=1, source_target_pairs={{0,2},{1,3},{2,0},{3,1},{4,6},{5,7},{6,4},{7,5},{8,10},{9,11},{10,... | collective-permute-start | bytes 393224 | tf_op jit(solution)/shard_map/ppermute | solution.py:249
  58.9 0.5 collective-permute-start.6
  59.4 4.2 %collective-permute-done.7 = bf16[2,16,8,256]{3,2,1,0:T(8,128)(2,1)S(1)} collective-permute-done((bf16[2,16,8,256]{3,2,1,0:T(8,128)(2,1)S(1)}, bf16[2,16,8,256]{3,2,1,0:T(8,128)(2,1)S(1)}, u32[]{:S(2)}, u32[]{:S(2)}) %collective-permute-start.7) | collective-permute-done | bytes 131104 | tf_op jit(solution)/shard_map/ppermute | solution.py:249
  63.6 3.6 %collective-permute-start.8 = (bf16[16,8,256]{2,1,0:T(8,128)(2,1)S(1)}, bf16[16,8,256]{2,1,0:T(8,128)(2,1)S(1)}, u32[]{:S(2)}, u32[]{:S(2)}) collective-permute-start(bf16[16,8,256]{2,1,0:T(8,128)(2,1)S(1)} %get-tuple-element.27), channel_id=1, source_target_pairs={{0,8},{1,9},{2,10},{3,11},{4,12},{5,13},{6,14},{7,15},{8,0},{9,1},... | collective-permute-start | bytes 196616 | tf_op jit(solution)/shard_map/ppermute | solution.py:255
  67.3 1.6 %collective-permute-start.9 = (bf16[16,8,256]{2,1,0:T(8,128)(2,1)S(1)}, bf16[16,8,256]{2,1,0:T(8,128)(2,1)S(1)}, u32[]{:S(2)}, u32[]{:S(2)}) collective-permute-start(bf16[16,8,256]{2,1,0:T(8,128)(2,1)S(1)} %get-tuple-element.28), channel_id=1, source_target_pairs={{0,4},{1,5},{2,6},{3,7},{4,8},{5,9},{6,10},{7,11},{8,12},{9,13},{1... | collective-permute-start | bytes 196616 | tf_op jit(solution)/shard_map/ppermute | solution.py:255
  68.8 0.0 collective-permute-done.6
  68.8 2.3 %collective-permute-start.10 = (bf16[16,8,256]{2,1,0:T(8,128)(2,1)S(1)}, bf16[16,8,256]{2,1,0:T(8,128)(2,1)S(1)}, u32[]{:S(2)}, u32[]{:S(2)}) collective-permute-start(bf16[16,8,256]{2,1,0:T(8,128)(2,1)S(1)} %fusion.7), channel_id=1, source_target_pairs={{0,12},{1,13},{2,14},{3,15},{4,0},{5,1},{6,2},{7,3},{8,4},{9,5},{1... | collective-permute-start | bytes 196616 | tf_op jit(solution)/shard_map/ppermute | solution.py:255
  71.2 0.0 collective-permute-done.8
  71.2 2.3 %collective-permute-done.9 = bf16[16,8,256]{2,1,0:T(8,128)(2,1)S(1)} collective-permute-done((bf16[16,8,256]{2,1,0:T(8,128)(2,1)S(1)}, bf16[16,8,256]{2,1,0:T(8,128)(2,1)S(1)}, u32[]{:S(2)}, u32[]{:S(2)}) %collective-permute-start.9) | collective-permute-done | bytes 65568 | tf_op jit(solution)/shard_map/ppermute | solution.py:255
  73.4 0.4 collective-permute-done.10
  73.9 0.1 reshape.55
  74.0 0.7 copy.14
  (12 shorter events, 0.2 us)
Async XLA Ops:
  0.0 7.9 %collective-permute-start = (bf16[32,2,128,128]{3,2,1,0:T(8,128)(2,1)}, bf16[32,2,128,128]{3,2,1,0:T(8,128)(2,1)}, u32[]{:S(2)}, u32[]{:S(2)}) collective-permute-start(bf16[32,2,128,128]{3,2,1,0:T(8,128)(2,1)} %own_ref.1), channel_id=1, source_target_pairs={{0,1},{1,0},{2,3},{3,2},{4,5},{5,4},{6,7},{7,6},{8,9},{9,8},{10,11... | collective-permute-start | bytes 6291464 | tf_op jit(solution)/shard_map/ppermute | solution.py:284
  0.5 1.6 %copy-start.2 = (bf16[32,2,128,128]{3,2,1,0:T(8,128)(2,1)S(1)}, bf16[32,2,128,128]{3,2,1,0:T(8,128)(2,1)}, u32[]{:S(2)}) copy-start(bf16[32,2,128,128]{3,2,1,0:T(8,128)(2,1)} %green_ref.1) | copy-start | bytes 6291460
  2.0 5.5 %copy-start.6 = (bf16[2,128,128]{2,1,0:T(8,128)(2,1)S(1)}, bf16[2,128,128]{2,1,0:T(8,128)(2,1)}, u32[]{:S(2)}) copy-start(bf16[2,128,128]{2,1,0:T(8,128)(2,1)} %param.7) | copy-start | bytes 196612
  2.1 36.0 %collective-permute-start.1 = (bf16[16,2,128,128]{3,2,1,0:T(8,128)(2,1)S(1)}, bf16[16,2,128,128]{3,2,1,0:T(8,128)(2,1)}, u32[]{:S(2)}, u32[]{:S(2)}) collective-permute-start(bf16[16,2,128,128]{3,2,1,0:T(8,128)(2,1)S(1)} %shard_map.57), channel_id=1, source_target_pairs={{0,2},{1,3},{2,4},{3,5},{4,6},{5,7},{6,8},{7,9},{8,10},{9,11},{10,... | collective-permute-start | bytes 3145736 | tf_op jit(solution)/shard_map/ppermute | solution.py:274
  7.9 11.2 %copy-start.3 = (bf16[32,2,128,128]{3,2,1,0:T(8,128)(2,1)S(1)}, bf16[32,2,128,128]{3,2,1,0:T(8,128)(2,1)}, u32[]{:S(2)}) copy-start(bf16[32,2,128,128]{3,2,1,0:T(8,128)(2,1)} %green_ref.1) | copy-start | bytes 6291460
  7.9 1.7 %copy-start.4 = (bf16[32,2,128,128]{3,2,1,0:T(8,128)(2,1)S(1)}, bf16[32,2,128,128]{3,2,1,0:T(8,128)(2,1)}, u32[]{:S(2)}) copy-start(bf16[32,2,128,128]{3,2,1,0:T(8,128)(2,1)} %own_ref.1) | copy-start | bytes 6291460
  9.7 9.3 %copy-start.7 = (s32[2]{0:T(128)S(1)}, s32[2]{0:T(128)}, u32[]{:S(2)}) copy-start(s32[2]{0:T(128)} %param.9) | copy-start | bytes 28
  15.3 6.7 %copy-start.5 = (s32[16]{0:T(128)S(1)}, s32[16]{0:T(128)}, u32[]{:S(2)}) copy-start(s32[16]{0:T(128)} %shifts_ref.9) | copy-start | bytes 196
  15.9 2.4 %copy-start = (bf16[80,128,256]{2,1,0:T(8,128)(2,1)}, bf16[80,128,256]{2,1,0:T(8,128)(2,1)S(1)}, u32[]{:S(2)}) copy-start(bf16[80,128,256]{2,1,0:T(8,128)(2,1)S(1)} %shard_map.55.proj_ref) | copy-start | bytes 15728644
  19.5 28.1 %collective-permute-start.4 = (bf16[8,2,128,128]{3,2,1,0:T(8,128)(2,1)S(1)}, bf16[8,2,128,128]{3,2,1,0:T(8,128)(2,1)S(1)}, u32[]{:S(2)}, u32[]{:S(2)}) collective-permute-start(bf16[8,2,128,128]{3,2,1,0:T(8,128)(2,1)S(1)} %get-tuple-element.23), channel_id=1, source_target_pairs={{0,2},{1,3},{2,4},{3,5},{4,6},{5,7},{6,8},{7,9},{8,10},{9,11},{10,... | collective-permute-start | bytes 1572872 | tf_op jit(solution)/shard_map/ppermute | solution.py:292
  22.0 2.5 %copy-start.1 = (bf16[80,128,256]{2,1,0:T(8,128)(2,1)S(1)}, bf16[80,128,256]{2,1,0:T(8,128)(2,1)}, u32[]{:S(2)}) copy-start(bf16[80,128,256]{2,1,0:T(8,128)(2,1)} %copy-done) | copy-start | bytes 15728644
  34.7 15.8 %collective-permute-start.3 = (bf16[6,2,128,128]{3,2,1,0:T(8,128)(2,1)S(1)}, bf16[6,2,128,128]{3,2,1,0:T(8,128)(2,1)S(1)}, u32[]{:S(2)}, u32[]{:S(2)}) collective-permute-start(bf16[6,2,128,128]{3,2,1,0:T(8,128)(2,1)S(1)} %get-tuple-element.22), channel_id=1, source_target_pairs={{0,2},{1,3},{2,4},{3,5},{4,6},{5,7},{6,8},{7,9},{8,10},{9,11},{10,... | collective-permute-start | bytes 1179656 | tf_op jit(solution)/shard_map/ppermute | solution.py:300
  44.2 9.4 %collective-permute-start.2 = (bf16[2,2,128,128]{3,2,1,0:T(8,128)(2,1)S(1)}, bf16[2,2,128,128]{3,2,1,0:T(8,128)(2,1)S(1)}, u32[]{:S(2)}, u32[]{:S(2)}) collective-permute-start(bf16[2,2,128,128]{3,2,1,0:T(8,128)(2,1)S(1)} %get-tuple-element.21), channel_id=1, source_target_pairs={{0,2},{1,3},{2,4},{3,5},{4,6},{5,7},{6,8},{7,9},{8,10},{9,11},{10,... | collective-permute-start | bytes 393224 | tf_op jit(solution)/shard_map/ppermute | solution.py:300
  55.0 2.0 %collective-permute-start.5 = (bf16[16,64,256]{2,1,0:T(8,128)(2,1)S(1)}, bf16[16,64,256]{2,1,0:T(8,128)(2,1)S(1)}, u32[]{:S(2)}, u32[]{:S(2)}) collective-permute-start(bf16[16,64,256]{2,1,0:T(8,128)(2,1)S(1)} %get-tuple-element.26), channel_id=1, source_target_pairs={{0,1},{1,0},{2,3},{3,2},{4,5},{5,4},{6,7},{7,6},{8,9},{9,8},{10,11... | collective-permute-start | bytes 1572872 | tf_op jit(solution)/shard_map/ppermute | solution.py:239
  57.2 6.4 %collective-permute-start.7 = (bf16[2,16,8,256]{3,2,1,0:T(8,128)(2,1)S(1)}, bf16[2,16,8,256]{3,2,1,0:T(8,128)(2,1)S(1)}, u32[]{:S(2)}, u32[]{:S(2)}) collective-permute-start(bf16[2,16,8,256]{3,2,1,0:T(8,128)(2,1)S(1)} %pad_maximum_fusion.1), channel_id=1, source_target_pairs={{0,2},{1,3},{2,0},{3,1},{4,6},{5,7},{6,4},{7,5},{8,10},{9,11},{10,... | collective-permute-start | bytes 393224 | tf_op jit(solution)/shard_map/ppermute | solution.py:249
  58.9 10.0 %collective-permute-start.6 = (bf16[2,16,8,256]{3,2,1,0:T(8,128)(2,1)S(1)}, bf16[2,16,8,256]{3,2,1,0:T(8,128)(2,1)S(1)}, u32[]{:S(2)}, u32[]{:S(2)}) collective-permute-start(bf16[2,16,8,256]{3,2,1,0:T(8,128)(2,1)S(1)} %pad_maximum_fusion), channel_id=1, source_target_pairs={{0,2},{1,3},{2,0},{3,1},{4,6},{5,7},{6,4},{7,5},{8,10},{9,11},{10,... | collective-permute-start | bytes 393224 | tf_op jit(solution)/shard_map/ppermute | solution.py:249
  63.6 7.5 %collective-permute-start.8 = (bf16[16,8,256]{2,1,0:T(8,128)(2,1)S(1)}, bf16[16,8,256]{2,1,0:T(8,128)(2,1)S(1)}, u32[]{:S(2)}, u32[]{:S(2)}) collective-permute-start(bf16[16,8,256]{2,1,0:T(8,128)(2,1)S(1)} %get-tuple-element.27), channel_id=1, source_target_pairs={{0,8},{1,9},{2,10},{3,11},{4,12},{5,13},{6,14},{7,15},{8,0},{9,1},... | collective-permute-start | bytes 196616 | tf_op jit(solution)/shard_map/ppermute | solution.py:255
  67.3 6.2 %collective-permute-start.9 = (bf16[16,8,256]{2,1,0:T(8,128)(2,1)S(1)}, bf16[16,8,256]{2,1,0:T(8,128)(2,1)S(1)}, u32[]{:S(2)}, u32[]{:S(2)}) collective-permute-start(bf16[16,8,256]{2,1,0:T(8,128)(2,1)S(1)} %get-tuple-element.28), channel_id=1, source_target_pairs={{0,4},{1,5},{2,6},{3,7},{4,8},{5,9},{6,10},{7,11},{8,12},{9,13},{1... | collective-permute-start | bytes 196616 | tf_op jit(solution)/shard_map/ppermute | solution.py:255
  68.8 5.0 %collective-permute-start.10 = (bf16[16,8,256]{2,1,0:T(8,128)(2,1)S(1)}, bf16[16,8,256]{2,1,0:T(8,128)(2,1)S(1)}, u32[]{:S(2)}, u32[]{:S(2)}) collective-permute-start(bf16[16,8,256]{2,1,0:T(8,128)(2,1)S(1)} %fusion.7), channel_id=1, source_target_pairs={{0,12},{1,13},{2,14},{3,15},{4,0},{5,1},{6,2},{7,3},{8,4},{9,5},{1... | collective-permute-start | bytes 196616 | tf_op jit(solution)/shard_map/ppermute | solution.py:255

commit v13 on v9

--- a/solution.py
+++ b/solution.py
@@ -8,7 +8,7 @@
 from jax.experimental.pallas import tpu as pltpu
 from jax.sharding import PartitionSpec as P
 
-STEP = 8
+STEP = 16
 WIDE = 16
 PAIR = 2
 GROUPS = 1

time: 75.1 us -> 75.1 us (level)
  transfers between devices with their start and end apart: 11 -> 11, of which waited for: 4 -> 4; matrix products, arithmetic and copies ran while one was open for 1% -> 1% of each run, Pallas kernels for 40% -> 39%
where the time goes in v13:
time: 75.1 us; the launch traced here: 74.7 us
  Pallas kernels  30.3 us (40%)
  starting transfers between devices  25 us (33%)
  local copies, waits for them, and re-layouts  9.94 us (13%)
  waiting for transfers between devices  8.68 us (12%)
    pallas_call x5, Pallas kernels, products(): pl.pallas_call(kernel, out_shape=out_shape, grid=(energies // step,), in_...  23.4 us
    unnamed x22, local copies, waits for them, and re-layouts  9.06 us
    ppermute x3, starting transfers between devices, reduced(): lax.ppermute(block.astype(jnp.bfloat16), 'energy', route)  7.26 us
    ppermute x2, starting transfers between devices, on_device(): far.append(lax.ppermute(pieces[k + 2], 'energy', up))  6.41 us
    pallas_call x1, Pallas kernels, project(): pl.pallas_call(functools.partial(project_kernel, steps), out_shape=jax.Sh...  5.62 us
    ppermute x1, starting transfers between devices, on_device(): far = [lax.ppermute(pieces[0], 'energy', up)]  5.41 us
    ppermute x2, waiting for transfers between devices, reduced(): got = lax.ppermute(send, 'energy', [(i, i ^ 2) for i in range(devices)])  4.19 us
    ppermute x1, starting transfers between devices, on_device(): far.append(lax.ppermute(pieces[1], 'energy', up))  3.25 us
  transfers between devices with their start and end apart: 11, of which 4 were waited for; matrix products, arithmetic and copies ran while one was open for 1% of the time, Pallas kernels for 39%

profile of v13, /device:TPU:0, one launch (start us, length us, event | category | flops | bytes accessed | tf_op | source)
XLA Modules:
  0.0 74.7 jit_solution(1302715127641455022)
XLA Ops:
  0.0 0.5 collective-permute-start
  0.5 0.0 copy-start.2
  0.5 1.6 %copy-done.2 = bf16[32,2,128,128]{3,2,1,0:T(8,128)(2,1)S(1)} copy-done((bf16[32,2,128,128]{3,2,1,0:T(8,128)(2,1)S(1)}, bf16[32,2,128,128]{3,2,1,0:T(8,128)(2,1)}, u32[]{:S(2)}) %copy-start.2) | copy-done | bytes 2097176
  2.0 0.0 copy-start.8
  2.0 0.1 shard_map.57
  2.1 5.4 %collective-permute-start.1 = (bf16[16,2,128,128]{3,2,1,0:T(8,128)(2,1)S(1)}, bf16[16,2,128,128]{3,2,1,0:T(8,128)(2,1)}, u32[]{:S(2)}, u32[]{:S(2)}) collective-permute-start(bf16[16,2,128,128]{3,2,1,0:T(8,128)(2,1)S(1)} %shard_map.57), channel_id=1, source_target_pairs={{0,2},{1,3},{2,4},{3,5},{4,6},{5,7},{6,8},{7,9},{8,10},{9,11},{10,... | collective-permute-start | bytes 3145736 | tf_op jit(solution)/shard_map/ppermute | solution.py:274
  7.5 0.0 copy-done.8
  7.6 0.1 copy.16
  7.7 0.1 copy.15
  7.9 0.0 copy-start.3
  7.9 0.0 collective-permute-done.other_ref
  7.9 0.0 copy-start.4
  7.9 1.7 %copy-done.4 = bf16[32,2,128,128]{3,2,1,0:T(8,128)(2,1)S(1)} copy-done((bf16[32,2,128,128]{3,2,1,0:T(8,128)(2,1)S(1)}, bf16[32,2,128,128]{3,2,1,0:T(8,128)(2,1)}, u32[]{:S(2)}) %copy-start.4) | copy-done | bytes 2097176
  9.7 5.6 %shard_map.55.proj_ref = bf16[80,128,256]{2,1,0:T(8,128)(2,1)S(1)} custom-call(bf16[128,256]{1,0:T(8,128)(2,1)S(1)} %pad_maximum_fusion.2.left_ref, bf16[256,256]{1,0:T(8,128)(2,1)S(1)} %maximum_maximum_fusion.right_ref, bf16[32,2,128,128]{3,2,1,0:T(8,128)(2,1)S(1)} %copy-done.4, bf16[32,2,128,128]{3,2,1,0:T(8,128)(2,1)} %collective-permute-done.other_ref), custom_call_target="tpu_custom_call" | custom-call | tf_op jit(solution)/shard_map/pallas_call | solution.py:88
  15.3 0.0 copy-start
  15.3 2.3 %copy-done = bf16[80,128,256]{2,1,0:T(8,128)(2,1)} copy-done((bf16[80,128,256]{2,1,0:T(8,128)(2,1)}, bf16[80,128,256]{2,1,0:T(8,128)(2,1)S(1)}, u32[]{:S(2)}) %copy-start) | copy-done | bytes 5242904
  17.6 0.0 copy-done.3
  17.6 0.0 copy-start.9
  17.6 0.0 copy-start.5
  17.6 1.2 %shard_map.56 = (bf16[8,2,128,128]{3,2,1,0:T(8,128)(2,1)}, bf16[6,2,128,128]{3,2,1,0:T(8,128)(2,1)S(1)}, bf16[2,2,128,128]{3,2,1,0:T(8,128)(2,1)S(1)}) custom-call(bf16[32,2,128,128]{3,2,1,0:T(8,128)(2,1)S(1)} %copy-done.3), custom_call_target="tpu_custom_call" | custom-call | tf_op jit(solution)/shard_map/pallas_call | solution.py:39
  18.9 0.0 copy-start.6
  18.9 0.6 copy-done.6
  19.5 3.3 %collective-permute-start.4 = (bf16[8,2,128,128]{3,2,1,0:T(8,128)(2,1)}, bf16[8,2,128,128]{3,2,1,0:T(8,128)(2,1)}, u32[]{:S(2)}, u32[]{:S(2)}) collective-permute-start(bf16[8,2,128,128]{3,2,1,0:T(8,128)(2,1)} %get-tuple-element.23), channel_id=1, source_target_pairs={{0,2},{1,3},{2,4},{3,5},{4,6},{5,7},{6,8},{7,9},{8,10},{9,11},{10,... | collective-permute-start | bytes 1572872 | tf_op jit(solution)/shard_map/ppermute | solution.py:288
  22.8 0.0 copy-done.9
  22.8 0.1 pad_add_fusion.facts_ref
  22.9 0.0 copy-done.5
  22.9 0.0 copy-start.1
  22.9 2.5 %copy-done.1 = bf16[80,128,256]{2,1,0:T(8,128)(2,1)S(1)} copy-done((bf16[80,128,256]{2,1,0:T(8,128)(2,1)S(1)}, bf16[80,128,256]{2,1,0:T(8,128)(2,1)}, u32[]{:S(2)}) %copy-start.1) | copy-done | bytes 5242904
  25.4 9.8 %shard_map.58.before_ref = f32[16,128,256]{2,1,0:T(8,128)S(1)} custom-call(s32[16]{0:T(128)S(1)} %copy-done.5, s32[5]{0:T(128)S(1)} %pad_add_fusion.facts_ref, bf16[80,128,256]{2,1,0:T(8,128)(2,1)S(1)} %copy-done.1, bf16[32,2,128,128]{3,2,1,0:T(8,128)(2,1)S(1)} %copy-done.3), custom_call_target="tpu_custom_call" | custom-call | tf_op jit(solution)/shard_map/pallas_call | solution.py:219
  35.1 0.0 copy-start.7
  35.1 2.8 %collective-permute-start.3 = (bf16[6,2,128,128]{3,2,1,0:T(8,128)(2,1)S(1)}, bf16[6,2,128,128]{3,2,1,0:T(8,128)(2,1)S(1)}, u32[]{:S(2)}, u32[]{:S(2)}) collective-permute-start(bf16[6,2,128,128]{3,2,1,0:T(8,128)(2,1)S(1)} %get-tuple-element.22), channel_id=1, source_target_pairs={{0,2},{1,3},{2,4},{3,5},{4,6},{5,7},{6,8},{7,9},{8,10},{9,11},{10,... | collective-permute-start | bytes 1179656 | tf_op jit(solution)/shard_map/ppermute | solution.py:299
  38.0 0.0 collective-permute-done.1.green_ref
  38.0 5.8 %shard_map.59.before_ref = f32[16,128,256]{2,1,0:T(8,128)S(1)} custom-call(s32[16]{0:T(128)S(1)} %copy-done.5, s32[5]{0:T(128)S(1)} %pad_add_fusion.facts_ref, bf16[80,128,256]{2,1,0:T(8,128)(2,1)S(1)} %copy-done.1, bf16[16,2,128,128]{3,2,1,0:T(8,128)(2,1)} %collective-permute-done.1.green_ref, f32[16,128,256]{2,1,0:T(8,128)S(1)} %shard_map.58.before_ref), custom_call_target="tpu_custom_call" | custom-call | tf_op jit(solution)/shard_map/pallas_call | solution.py:219
  43.7 0.0 copy-done.7
  43.7 3.6 %collective-permute-start.2 = (bf16[2,2,128,128]{3,2,1,0:T(8,128)(2,1)S(1)}, bf16[2,2,128,128]{3,2,1,0:T(8,128)(2,1)S(1)}, u32[]{:S(2)}, u32[]{:S(2)}) collective-permute-start(bf16[2,2,128,128]{3,2,1,0:T(8,128)(2,1)S(1)} %copy-done.7), channel_id=1, source_target_pairs={{0,2},{1,3},{2,4},{3,5},{4,6},{5,7},{6,8},{7,9},{8,10},{9,11},{10,... | collective-permute-start | bytes 393224 | tf_op jit(solution)/shard_map/ppermute | solution.py:299
  47.3 0.0 collective-permute-done.4.green_ref
  47.4 3.4 %shard_map.60.before_ref = f32[16,128,256]{2,1,0:T(8,128)S(1)} custom-call(s32[16]{0:T(128)S(1)} %copy-done.5, s32[5]{0:T(128)S(1)} %pad_add_fusion.facts_ref, bf16[80,128,256]{2,1,0:T(8,128)(2,1)S(1)} %copy-done.1, bf16[8,2,128,128]{3,2,1,0:T(8,128)(2,1)} %collective-permute-done.4.green_ref, f32[16,128,256]{2,1,0:T(8,128)S(1)} %shard_map.59.before_ref), custom_call_target="tpu_custom_call" | custom-call | tf_op jit(solution)/shard_map/pallas_call | solution.py:219
  50.8 0.0 collective-permute-done.3.green_ref
  50.8 3.0 %shard_map.61.before_ref = f32[16,128,256]{2,1,0:T(8,128)S(1)} custom-call(s32[16]{0:T(128)S(1)} %copy-done.5, s32[5]{0:T(128)S(1)} %pad_add_fusion.facts_ref, bf16[80,128,256]{2,1,0:T(8,128)(2,1)S(1)} %copy-done.1, bf16[6,2,128,128]{3,2,1,0:T(8,128)(2,1)S(1)} %collective-permute-done.3.green_ref, f32[16,128,256]{2,1,0:T(8,128)S(1)} %shard_map.60.before_ref), custom_call_target="tpu_custom_call" | custom-call | tf_op jit(solution)/shard_map/pallas_call | solution.py:219
  53.8 0.0 collective-permute-done.2.green_ref
  53.8 1.4 %shard_map.62 = (f32[16,64,256]{2,1,0:T(8,128)S(1)}, bf16[16,64,256]{2,1,0:T(8,128)(2,1)S(1)}) custom-call(s32[16]{0:T(128)S(1)} %copy-done.5, s32[5]{0:T(128)S(1)} %pad_add_fusion.facts_ref, s32[1]{0:T(128)} %bitcast.2.core_ref, bf16[80,128,256]{2,1,0:T(8,128)(2,1)S(1)} %copy-done.1, bf16[2,2,128,128]{3,2,1,0:T(8,128)(2,1)S(1)} %collective-permute-done.2.green_ref, ...), custom_call_target="tpu_custom_call" | custom-call | tf_op jit(solution)/shard_map/pallas_call | solution.py:219
  55.2 0.1 collective-permute-start.5
  55.5 1.8 %collective-permute-done.5 = bf16[16,64,256]{2,1,0:T(8,128)(2,1)S(1)} collective-permute-done((bf16[16,64,256]{2,1,0:T(8,128)(2,1)S(1)}, bf16[16,64,256]{2,1,0:T(8,128)(2,1)S(1)}, u32[]{:S(2)}, u32[]{:S(2)}) %collective-permute-start.5) | collective-permute-done | bytes 524320 | tf_op jit(solution)/shard_map/ppermute | solution.py:239
  57.2 0.1 convert_add_fusion
  57.3 0.1 fusion.10
  57.4 1.6 %collective-permute-start.7 = (bf16[2,16,8,256]{3,2,1,0:T(8,128)(2,1)S(1)}, bf16[2,16,8,256]{3,2,1,0:T(8,128)(2,1)S(1)}, u32[]{:S(2)}, u32[]{:S(2)}) collective-permute-start(bf16[2,16,8,256]{3,2,1,0:T(8,128)(2,1)S(1)} %pad_maximum_fusion.1), channel_id=1, source_target_pairs={{0,2},{1,3},{2,0},{3,1},{4,6},{5,7},{6,4},{7,5},{8,10},{9,11},{10,... | collective-permute-start | bytes 393224 | tf_op jit(solution)/shard_map/ppermute | solution.py:249
  59.0 0.6 collective-permute-start.6
  59.6 4.2 %collective-permute-done.7 = bf16[2,16,8,256]{3,2,1,0:T(8,128)(2,1)S(1)} collective-permute-done((bf16[2,16,8,256]{3,2,1,0:T(8,128)(2,1)S(1)}, bf16[2,16,8,256]{3,2,1,0:T(8,128)(2,1)S(1)}, u32[]{:S(2)}, u32[]{:S(2)}) %collective-permute-start.7) | collective-permute-done | bytes 131104 | tf_op jit(solution)/shard_map/ppermute | solution.py:249
  63.9 3.4 %collective-permute-start.8 = (bf16[16,8,256]{2,1,0:T(8,128)(2,1)S(1)}, bf16[16,8,256]{2,1,0:T(8,128)(2,1)S(1)}, u32[]{:S(2)}, u32[]{:S(2)}) collective-permute-start(bf16[16,8,256]{2,1,0:T(8,128)(2,1)S(1)} %get-tuple-element.27), channel_id=1, source_target_pairs={{0,8},{1,9},{2,10},{3,11},{4,12},{5,13},{6,14},{7,15},{8,0},{9,1},... | collective-permute-start | bytes 196616 | tf_op jit(solution)/shard_map/ppermute | solution.py:255
  67.2 1.6 %collective-permute-start.9 = (bf16[16,8,256]{2,1,0:T(8,128)(2,1)S(1)}, bf16[16,8,256]{2,1,0:T(8,128)(2,1)S(1)}, u32[]{:S(2)}, u32[]{:S(2)}) collective-permute-start(bf16[16,8,256]{2,1,0:T(8,128)(2,1)S(1)} %get-tuple-element.28), channel_id=1, source_target_pairs={{0,4},{1,5},{2,6},{3,7},{4,8},{5,9},{6,10},{7,11},{8,12},{9,13},{1... | collective-permute-start | bytes 196616 | tf_op jit(solution)/shard_map/ppermute | solution.py:255
  68.8 0.0 collective-permute-done.6
  68.8 2.3 %collective-permute-start.10 = (bf16[16,8,256]{2,1,0:T(8,128)(2,1)S(1)}, bf16[16,8,256]{2,1,0:T(8,128)(2,1)S(1)}, u32[]{:S(2)}, u32[]{:S(2)}) collective-permute-start(bf16[16,8,256]{2,1,0:T(8,128)(2,1)S(1)} %fusion.7), channel_id=1, source_target_pairs={{0,12},{1,13},{2,14},{3,15},{4,0},{5,1},{6,2},{7,3},{8,4},{9,5},{1... | collective-permute-start | bytes 196616 | tf_op jit(solution)/shard_map/ppermute | solution.py:255
  71.1 0.0 collective-permute-done.8
  71.2 2.3 %collective-permute-done.9 = bf16[16,8,256]{2,1,0:T(8,128)(2,1)S(1)} collective-permute-done((bf16[16,8,256]{2,1,0:T(8,128)(2,1)S(1)}, bf16[16,8,256]{2,1,0:T(8,128)(2,1)S(1)}, u32[]{:S(2)}, u32[]{:S(2)}) %collective-permute-start.9) | collective-permute-done | bytes 65568 | tf_op jit(solution)/shard_map/ppermute | solution.py:255
  73.4 0.4 collective-permute-done.10
  73.9 0.1 reshape.52
  74.0 0.7 copy.14
  (12 shorter events, 0.2 us)
Async XLA Ops:
  0.0 7.9 %collective-permute-start = (bf16[32,2,128,128]{3,2,1,0:T(8,128)(2,1)}, bf16[32,2,128,128]{3,2,1,0:T(8,128)(2,1)}, u32[]{:S(2)}, u32[]{:S(2)}) collective-permute-start(bf16[32,2,128,128]{3,2,1,0:T(8,128)(2,1)} %own_ref.1), channel_id=1, source_target_pairs={{0,1},{1,0},{2,3},{3,2},{4,5},{5,4},{6,7},{7,6},{8,9},{9,8},{10,11... | collective-permute-start | bytes 6291464 | tf_op jit(solution)/shard_map/ppermute | solution.py:284
  0.5 1.6 %copy-start.2 = (bf16[32,2,128,128]{3,2,1,0:T(8,128)(2,1)S(1)}, bf16[32,2,128,128]{3,2,1,0:T(8,128)(2,1)}, u32[]{:S(2)}) copy-start(bf16[32,2,128,128]{3,2,1,0:T(8,128)(2,1)} %green_ref.1) | copy-start | bytes 6291460
  2.0 5.5 %copy-start.8 = (bf16[2,128,128]{2,1,0:T(8,128)(2,1)S(1)}, bf16[2,128,128]{2,1,0:T(8,128)(2,1)}, u32[]{:S(2)}) copy-start(bf16[2,128,128]{2,1,0:T(8,128)(2,1)} %param.7) | copy-start | bytes 196612
  2.1 35.8 %collective-permute-start.1 = (bf16[16,2,128,128]{3,2,1,0:T(8,128)(2,1)S(1)}, bf16[16,2,128,128]{3,2,1,0:T(8,128)(2,1)}, u32[]{:S(2)}, u32[]{:S(2)}) collective-permute-start(bf16[16,2,128,128]{3,2,1,0:T(8,128)(2,1)S(1)} %shard_map.57), channel_id=1, source_target_pairs={{0,2},{1,3},{2,4},{3,5},{4,6},{5,7},{6,8},{7,9},{8,10},{9,11},{10,... | collective-permute-start | bytes 3145736 | tf_op jit(solution)/shard_map/ppermute | solution.py:274
  7.9 9.7 %copy-start.3 = (bf16[32,2,128,128]{3,2,1,0:T(8,128)(2,1)S(1)}, bf16[32,2,128,128]{3,2,1,0:T(8,128)(2,1)}, u32[]{:S(2)}) copy-start(bf16[32,2,128,128]{3,2,1,0:T(8,128)(2,1)} %green_ref.1) | copy-start | bytes 6291460
  7.9 1.7 %copy-start.4 = (bf16[32,2,128,128]{3,2,1,0:T(8,128)(2,1)S(1)}, bf16[32,2,128,128]{3,2,1,0:T(8,128)(2,1)}, u32[]{:S(2)}) copy-start(bf16[32,2,128,128]{3,2,1,0:T(8,128)(2,1)} %own_ref.1) | copy-start | bytes 6291460
  15.3 2.3 %copy-start = (bf16[80,128,256]{2,1,0:T(8,128)(2,1)}, bf16[80,128,256]{2,1,0:T(8,128)(2,1)S(1)}, u32[]{:S(2)}) copy-start(bf16[80,128,256]{2,1,0:T(8,128)(2,1)S(1)} %shard_map.55.proj_ref) | copy-start | bytes 15728644
  17.6 5.1 %copy-start.9 = (s32[2]{0:T(128)S(1)}, s32[2]{0:T(128)}, u32[]{:S(2)}) copy-start(s32[2]{0:T(128)} %param.9) | copy-start | bytes 28
  17.6 5.2 %copy-start.5 = (s32[16]{0:T(128)S(1)}, s32[16]{0:T(128)}, u32[]{:S(2)}) copy-start(s32[16]{0:T(128)} %shifts_ref.9) | copy-start | bytes 196
  18.9 0.7 copy-start.6
  19.5 27.8 %collective-permute-start.4 = (bf16[8,2,128,128]{3,2,1,0:T(8,128)(2,1)}, bf16[8,2,128,128]{3,2,1,0:T(8,128)(2,1)}, u32[]{:S(2)}, u32[]{:S(2)}) collective-permute-start(bf16[8,2,128,128]{3,2,1,0:T(8,128)(2,1)} %get-tuple-element.23), channel_id=1, source_target_pairs={{0,2},{1,3},{2,4},{3,5},{4,6},{5,7},{6,8},{7,9},{8,10},{9,11},{10,... | collective-permute-start | bytes 1572872 | tf_op jit(solution)/shard_map/ppermute | solution.py:288
  22.9 2.5 %copy-start.1 = (bf16[80,128,256]{2,1,0:T(8,128)(2,1)S(1)}, bf16[80,128,256]{2,1,0:T(8,128)(2,1)}, u32[]{:S(2)}) copy-start(bf16[80,128,256]{2,1,0:T(8,128)(2,1)} %copy-done) | copy-start | bytes 15728644
  35.1 8.6 %copy-start.7 = (bf16[2,2,128,128]{3,2,1,0:T(8,128)(2,1)S(1)}, bf16[2,2,128,128]{3,2,1,0:T(8,128)(2,1)}, u32[]{:S(2)}) copy-start(bf16[2,2,128,128]{3,2,1,0:T(8,128)(2,1)} %copy-done.6) | copy-start | bytes 393220
  35.1 15.6 %collective-permute-start.3 = (bf16[6,2,128,128]{3,2,1,0:T(8,128)(2,1)S(1)}, bf16[6,2,128,128]{3,2,1,0:T(8,128)(2,1)S(1)}, u32[]{:S(2)}, u32[]{:S(2)}) collective-permute-start(bf16[6,2,128,128]{3,2,1,0:T(8,128)(2,1)S(1)} %get-tuple-element.22), channel_id=1, source_target_pairs={{0,2},{1,3},{2,4},{3,5},{4,6},{5,7},{6,8},{7,9},{8,10},{9,11},{10,... | collective-permute-start | bytes 1179656 | tf_op jit(solution)/shard_map/ppermute | solution.py:299
  43.7 10.1 %collective-permute-start.2 = (bf16[2,2,128,128]{3,2,1,0:T(8,128)(2,1)S(1)}, bf16[2,2,128,128]{3,2,1,0:T(8,128)(2,1)S(1)}, u32[]{:S(2)}, u32[]{:S(2)}) collective-permute-start(bf16[2,2,128,128]{3,2,1,0:T(8,128)(2,1)S(1)} %copy-done.7), channel_id=1, source_target_pairs={{0,2},{1,3},{2,4},{3,5},{4,6},{5,7},{6,8},{7,9},{8,10},{9,11},{10,... | collective-permute-start | bytes 393224 | tf_op jit(solution)/shard_map/ppermute | solution.py:299
  55.2 2.0 %collective-permute-start.5 = (bf16[16,64,256]{2,1,0:T(8,128)(2,1)S(1)}, bf16[16,64,256]{2,1,0:T(8,128)(2,1)S(1)}, u32[]{:S(2)}, u32[]{:S(2)}) collective-permute-start(bf16[16,64,256]{2,1,0:T(8,128)(2,1)S(1)} %get-tuple-element.26), channel_id=1, source_target_pairs={{0,1},{1,0},{2,3},{3,2},{4,5},{5,4},{6,7},{7,6},{8,9},{9,8},{10,11... | collective-permute-start | bytes 1572872 | tf_op jit(solution)/shard_map/ppermute | solution.py:239
  57.4 6.4 %collective-permute-start.7 = (bf16[2,16,8,256]{3,2,1,0:T(8,128)(2,1)S(1)}, bf16[2,16,8,256]{3,2,1,0:T(8,128)(2,1)S(1)}, u32[]{:S(2)}, u32[]{:S(2)}) collective-permute-start(bf16[2,16,8,256]{3,2,1,0:T(8,128)(2,1)S(1)} %pad_maximum_fusion.1), channel_id=1, source_target_pairs={{0,2},{1,3},{2,0},{3,1},{4,6},{5,7},{6,4},{7,5},{8,10},{9,11},{10,... | collective-permute-start | bytes 393224 | tf_op jit(solution)/shard_map/ppermute | solution.py:249
  59.0 9.8 %collective-permute-start.6 = (bf16[2,16,8,256]{3,2,1,0:T(8,128)(2,1)S(1)}, bf16[2,16,8,256]{3,2,1,0:T(8,128)(2,1)S(1)}, u32[]{:S(2)}, u32[]{:S(2)}) collective-permute-start(bf16[2,16,8,256]{3,2,1,0:T(8,128)(2,1)S(1)} %pad_maximum_fusion), channel_id=1, source_target_pairs={{0,2},{1,3},{2,0},{3,1},{4,6},{5,7},{6,4},{7,5},{8,10},{9,11},{10,... | collective-permute-start | bytes 393224 | tf_op jit(solution)/shard_map/ppermute | solution.py:249
  63.9 7.3 %collective-permute-start.8 = (bf16[16,8,256]{2,1,0:T(8,128)(2,1)S(1)}, bf16[16,8,256]{2,1,0:T(8,128)(2,1)S(1)}, u32[]{:S(2)}, u32[]{:S(2)}) collective-permute-start(bf16[16,8,256]{2,1,0:T(8,128)(2,1)S(1)} %get-tuple-element.27), channel_id=1, source_target_pairs={{0,8},{1,9},{2,10},{3,11},{4,12},{5,13},{6,14},{7,15},{8,0},{9,1},... | collective-permute-start | bytes 196616 | tf_op jit(solution)/shard_map/ppermute | solution.py:255
  67.2 6.2 %collective-permute-start.9 = (bf16[16,8,256]{2,1,0:T(8,128)(2,1)S(1)}, bf16[16,8,256]{2,1,0:T(8,128)(2,1)S(1)}, u32[]{:S(2)}, u32[]{:S(2)}) collective-permute-start(bf16[16,8,256]{2,1,0:T(8,128)(2,1)S(1)} %get-tuple-element.28), channel_id=1, source_target_pairs={{0,4},{1,5},{2,6},{3,7},{4,8},{5,9},{6,10},{7,11},{8,12},{9,13},{1... | collective-permute-start | bytes 196616 | tf_op jit(solution)/shard_map/ppermute | solution.py:255
  68.8 5.0 %collective-permute-start.10 = (bf16[16,8,256]{2,1,0:T(8,128)(2,1)S(1)}, bf16[16,8,256]{2,1,0:T(8,128)(2,1)S(1)}, u32[]{:S(2)}, u32[]{:S(2)}) collective-permute-start(bf16[16,8,256]{2,1,0:T(8,128)(2,1)S(1)} %fusion.7), channel_id=1, source_target_pairs={{0,12},{1,13},{2,14},{3,15},{4,0},{5,1},{6,2},{7,3},{8,4},{9,5},{1... | collective-permute-start | bytes 196616 | tf_op jit(solution)/shard_map/ppermute | solution.py:255
